TPU v7x, 32 devices: a whole 2x2x4 slice. The times are simulated.
32 devices in a mesh: section: 2 (over core), wide: 4 (over z), narrow: 4 (over y, x).
Axes of the slice: x: 2, y: 2, z: 4, core: 2. Of those that a mesh axis runs over, the one named last changes fastest.
Arguments:
- inputs: bfloat16 [2, 4096, 1152], P(None, ('wide', 'narrow')), may hold values from -6 to 6
- cotangent: bfloat16 [2, 4096, 1152], P(None, ('wide', 'narrow')), may hold values from -6 to 6
- lengths: int32 [2, 4], P(None, 'wide'), may hold values from 256 to 1024, as said below
- norm_gains: bfloat16 [2, 4, 1152], P('section', None, 'wide'), may hold values from 0.25 to 1.75
- head_gains: bfloat16 [2, 2, 256], P('section', None, 'wide'), may hold values from 0.25 to 1.75
- w_q: bfloat16 [2, 1152, 1024], P('section', 'wide', 'narrow'), may hold values from -0.1875 to 0.1875
- w_kv: bfloat16 [2, 1152, 512], P('section', 'wide'), may hold values from -0.1875 to 0.1875
- w_o: bfloat16 [2, 1024, 1152], P('section', 'narrow', 'wide'), may hold values from -0.1875 to 0.1875
- w_gate_up: bfloat16 [2, 1152, 2, 6912], P('section', 'wide', None, 'narrow'), may hold values from -0.1875 to 0.1875
- w_down: bfloat16 [2, 6912, 1152], P('section', 'narrow', 'wide'), may hold values from -0.078125 to 0.078125
Outputs:
- section_out: bfloat16 [2, 2, 4096, 1152], P('section', None, ('wide', 'narrow'))
- input_grad: float32 [2, 2, 4096, 1152], P('section', None, ('wide', 'narrow'))
- grad_norm_gains: float32 [2, 4, 1152], P('section', None, 'wide')
- grad_head_gains: float32 [2, 2, 256], P('section', None, 'wide')
- grad_w_q: float32 [2, 1152, 1024], P('section', 'wide', 'narrow')
- grad_w_kv: float32 [2, 1152, 512], P('section', 'wide')
- grad_w_o: float32 [2, 1024, 1152], P('section', 'narrow', 'wide')
- grad_w_gate_up: float32 [2, 1152, 2, 6912], P('section', 'wide', None, 'narrow')
- grad_w_down: float32 [2, 6912, 1152], P('section', 'narrow', 'wide')
Inputs may be any that keep to these rules, and one draw needn't show every extreme that they name: `lengths`: in every micro-batch the sequence of one wide index, drawn from the seed, has exactly 1024 tokens, and that of another exactly 256.
All inputs are finite; a program needn't handle non-finite values.
Results may differ from a plain program's by a relative error of at most 0.033.
Values may be sent and summed in bfloat16 or wider, within the bound.
A program may use at most 256 MiB of HBM per device.

v0:
```python
import jax
import jax.numpy as jnp
from jax import lax
from jax.sharding import PartitionSpec as P

WINDOW = 512
SEQ = 1024


EPSILON = 1e-06
NEGATIVE = -1e30
ROPE_BASE = 10000.0


def shifted(shard, axis, by):
    length = lax.axis_size(axis)
    pairs = [(i, i + by) for i in range(length) if 0 <= i + by < length]
    return lax.ppermute(shard, axis, pairs)


def normed(operand, gain_vec):
    return (
        operand
        * lax.rsqrt(jnp.mean(operand * operand, axis=-1, keepdims=True) + EPSILON)
        * gain_vec
    )


def tables(row_count, head_width):
    half_width = head_width // 2
    positions = jnp.arange(row_count, dtype=jnp.float32)
    frequency = ROPE_BASE ** (-jnp.arange(half_width, dtype=jnp.float32) * (2.0 / head_width))
    angles = positions[:, None] * frequency[None, :]
    return (jnp.cos(angles), jnp.sin(angles))


def rotate(operand, cosine, sine_table):
    half_width = operand.shape[-1] // 2
    front_half = operand[..., :half_width]
    back_half = operand[..., half_width:]
    return jnp.concatenate(
        [
            front_half * cosine - back_half * sine_table,
            back_half * cosine + front_half * sine_table,
        ],
        axis=-1,
    )


def shape_heads(q_raw, kv_raw, head_gain, cosine, sine_table):
    head_width = head_gain.shape[-1]
    queries = q_raw.reshape(q_raw.shape[0], -1, head_width)
    q_rot = rotate(normed(queries, head_gain[0]), cosine[:, None, :], sine_table[:, None, :])
    k_rot = rotate(normed(kv_raw[:, :head_width], head_gain[1]), cosine, sine_table)
    return (q_rot, k_rot)


def padded(key_rows):
    return jnp.concatenate(
        [jnp.zeros((WINDOW, key_rows.shape[1]), key_rows.dtype), key_rows], axis=0
    )


def block_scores(q_block, k_block, offset, seq_length, scaling):
    scores = (
        jnp.einsum("qhd,kd->hqk", q_block, k_block, preferred_element_type=jnp.float32) * scaling
    )
    rows_at = offset + jnp.arange(WINDOW, dtype=jnp.int32)[:, None]
    cols_at = offset - WINDOW + jnp.arange(2 * WINDOW, dtype=jnp.int32)[None, :]
    visible = (
        (cols_at <= rows_at)
        & (rows_at - cols_at < WINDOW)
        & (cols_at >= 0)
        & ((cols_at < seq_length) | (cols_at == rows_at))
    )
    return jnp.where(visible[None], scores, NEGATIVE)


def attend_forward(q_bf, k_bf, v_bf, seq_length, scaling):
    key_rows = padded(k_bf)
    value_rows = padded(v_bf)
    outputs = []
    log_parts = []
    for block_index in range(SEQ // WINDOW):
        offset = block_index * WINDOW
        scores = block_scores(
            q_bf[offset : offset + WINDOW],
            key_rows[offset : offset + 2 * WINDOW],
            offset,
            seq_length,
            scaling,
        )
        maximum = jnp.max(scores, axis=-1, keepdims=True)
        exponent = jnp.exp(scores - maximum)
        row_total = jnp.sum(exponent, axis=-1, keepdims=True)
        probabilities = (exponent / row_total).astype(jnp.bfloat16)
        outputs.append(
            jnp.einsum(
                "hqk,kd->qhd",
                probabilities,
                value_rows[offset : offset + 2 * WINDOW],
                preferred_element_type=jnp.float32,
            )
        )
        log_parts.append(maximum + jnp.log(row_total))
    return (jnp.concatenate(outputs, axis=0), jnp.concatenate(log_parts, axis=1))


def attend_backward(q_bf, k_bf, v_bf, log_totals, grad_out, seq_length, scaling):
    key_rows = padded(k_bf)
    value_rows = padded(v_bf)
    grad_keys = jnp.zeros(key_rows.shape, jnp.float32)
    grad_values = jnp.zeros(value_rows.shape, jnp.float32)
    grad_queries = []
    for block_index in range(SEQ // WINDOW):
        offset = block_index * WINDOW
        q_block = q_bf[offset : offset + WINDOW]
        k_block = key_rows[offset : offset + 2 * WINDOW]
        v_block = value_rows[offset : offset + 2 * WINDOW]
        g_block = grad_out[offset : offset + WINDOW]
        scores = block_scores(q_block, k_block, offset, seq_length, scaling)
        probabilities = jnp.exp(scores - log_totals[:, offset : offset + WINDOW])
        grad_probs = jnp.einsum("qhd,kd->hqk", g_block, v_block, preferred_element_type=jnp.float32)
        row_dots = jnp.sum(probabilities * grad_probs, axis=-1, keepdims=True)
        grad_scores = (probabilities * (grad_probs - row_dots)).astype(jnp.bfloat16)
        grad_queries.append(
            jnp.einsum("hqk,kd->qhd", grad_scores, k_block, preferred_element_type=jnp.float32)
            * scaling
        )
        grad_keys = grad_keys.at[offset : offset + 2 * WINDOW].add(
            jnp.einsum("hqk,qhd->kd", grad_scores, q_block, preferred_element_type=jnp.float32)
            * scaling
        )
        grad_values = grad_values.at[offset : offset + 2 * WINDOW].add(
            jnp.einsum(
                "hqk,qhd->kd",
                probabilities.astype(jnp.bfloat16),
                g_block,
                preferred_element_type=jnp.float32,
            )
        )
    return (jnp.concatenate(grad_queries, axis=0), grad_keys[WINDOW:], grad_values[WINDOW:])


def gather_rows(normed_rows):
    return lax.all_gather(normed_rows, "narrow", axis=0, tiled=True)


def gather_grads(grad_rows):
    return lax.all_gather(grad_rows, "narrow", axis=0, tiled=True)


def reduce_parts(left_rows, right_matrix, row_count, active):
    out_width = right_matrix.shape[-1]

    def term(offset, row_span):

        def term_compute():
            return jnp.dot(left_rows, right_matrix, preferred_element_type=jnp.float32)

        def term_nothing():
            return jnp.zeros((row_span, out_width), jnp.float32)

        return lax.cond(active, term_compute, term_nothing)

    return lax.psum_scatter(
        term(jnp.int32(0), row_count * lax.axis_size("narrow")).astype(jnp.bfloat16),
        "narrow",
        scatter_dimension=0,
        tiled=True,
    ).astype(jnp.float32)


def reduce_grad_parts(term, row_count):
    return lax.psum_scatter(
        term(jnp.int32(0), row_count * lax.axis_size("narrow")).astype(jnp.bfloat16),
        "narrow",
        scatter_dimension=0,
        tiled=True,
    ).astype(jnp.float32)


def reduce_weights(gradients):
    summed = (
        lax.psum_scatter(
            gradients[0].astype(jnp.bfloat16), "wide", scatter_dimension=1, tiled=True
        ).astype(jnp.float32),
        lax.psum_scatter(
            gradients[1].astype(jnp.bfloat16), "wide", scatter_dimension=1, tiled=True
        ).astype(jnp.float32),
        lax.psum_scatter(
            gradients[2].astype(jnp.bfloat16), "wide", scatter_dimension=0, tiled=True
        ).astype(jnp.float32),
        lax.psum_scatter(
            gradients[3].astype(jnp.bfloat16), "wide", scatter_dimension=0, tiled=True
        ).astype(jnp.float32),
        lax.psum_scatter(
            gradients[4].astype(jnp.bfloat16), "wide", scatter_dimension=1, tiled=True
        ).astype(jnp.float32),
        lax.psum_scatter(
            gradients[5].astype(jnp.bfloat16), "wide", scatter_dimension=0, tiled=True
        ).astype(jnp.float32),
        lax.psum_scatter(
            gradients[6].astype(jnp.bfloat16), "wide", scatter_dimension=1, tiled=True
        ).astype(jnp.float32),
    )
    shared = (
        lax.psum(summed[0].astype(jnp.bfloat16), "narrow").astype(jnp.float32),
        lax.psum(summed[1].astype(jnp.bfloat16), "narrow").astype(jnp.float32),
        lax.psum(summed[3].astype(jnp.bfloat16), "narrow").astype(jnp.float32),
    )
    return (shared[0], shared[1], summed[2], shared[2], summed[4], summed[5], summed[6])


def layer_forward(layer_in, seq_length, gathered, cosine, sine_table, active):
    norm_gain, head_gain, w_query, w_keyval, w_out, w_gateup, w_downp = gathered
    gains = norm_gain.astype(jnp.float32)
    head_gains_f = head_gain.astype(jnp.float32)
    row_count = layer_in.shape[0]
    head_width = head_gain.shape[-1]
    per_width = w_query.shape[1]
    per_heads = per_width // head_width
    scaling = head_width ** (-0.5)
    normed_in = normed(layer_in, gains[0]).astype(jnp.bfloat16)
    seq_rows = gather_rows(normed_in)
    seq_len = seq_rows.shape[0]

    def attention_part():
        q_raw = jnp.dot(seq_rows, w_query, preferred_element_type=jnp.float32)
        kv_raw = jnp.dot(seq_rows, w_keyval, preferred_element_type=jnp.float32)
        q_rot, k_rot = shape_heads(q_raw, kv_raw, head_gains_f, cosine, sine_table)
        attn_out, log_totals = attend_forward(
            q_rot.astype(jnp.bfloat16),
            k_rot.astype(jnp.bfloat16),
            kv_raw[:, head_width:].astype(jnp.bfloat16),
            seq_length,
            scaling,
        )
        return (
            q_raw,
            kv_raw,
            log_totals,
            attn_out.reshape(seq_len, per_width).astype(jnp.bfloat16),
        )

    def attention_none():
        return (
            jnp.zeros((seq_len, per_width), jnp.float32),
            jnp.zeros((seq_len, 2 * head_width), jnp.float32),
            jnp.zeros((per_heads, seq_len, 1), jnp.float32),
            jnp.zeros((seq_len, per_width), jnp.bfloat16),
        )

    q_raw, kv_raw, log_totals, attn_bf = lax.cond(active, attention_part, attention_none)
    branch_a = reduce_parts(attn_bf, w_out, row_count, active)
    hidden_res = layer_in + normed(branch_a, gains[1])
    normed_mid = normed(hidden_res, gains[2]).astype(jnp.bfloat16)
    mid_rows = gather_rows(normed_mid)

    def feed_part():
        gate_up = jnp.einsum("sd,dcf->scf", mid_rows, w_gateup, preferred_element_type=jnp.float32)
        return geglu(gate_up).astype(jnp.bfloat16)

    def feed_none():
        return jnp.zeros((seq_len, w_gateup.shape[2]), jnp.bfloat16)

    product = lax.cond(active, feed_part, feed_none)
    branch_f = reduce_parts(product, w_downp, row_count, active)
    layer_out = hidden_res + normed(branch_f, gains[3])
    kept = (
        layer_in,
        seq_rows,
        q_raw,
        kv_raw,
        log_totals,
        attn_bf,
        branch_a,
        hidden_res,
        mid_rows,
        branch_f,
    )
    return (layer_out, kept)


def geglu(gate_up):
    return jax.nn.gelu(gate_up[:, 0], approximate=True) * gate_up[:, 1]


def layer_backward(grad_out, seq_length, gathered, kept, cosine, sine_table, active):
    norm_gain, head_gain, w_query, w_keyval, w_out, w_gateup, w_downp = gathered
    (
        layer_in,
        seq_rows,
        q_raw,
        kv_raw,
        log_totals,
        attn_bf,
        branch_a,
        hidden_res,
        mid_rows,
        branch_f,
    ) = kept
    gains = norm_gain.astype(jnp.float32)
    head_gains_f = head_gain.astype(jnp.float32)
    row_count = layer_in.shape[0]
    seq_len = seq_rows.shape[0]
    model_width = layer_in.shape[1]
    head_width = head_gain.shape[-1]
    per_width = w_query.shape[1]
    scaling = head_width ** (-0.5)
    unused_post, post_pull = jax.vjp(normed, branch_f, gains[3])
    grad_f, grad_g3 = post_pull(grad_out)
    grad_f_rows = gather_grads(grad_f.astype(jnp.bfloat16))

    def feed_part():
        gate_up = jnp.einsum("sd,dcf->scf", mid_rows, w_gateup, preferred_element_type=jnp.float32)
        product, geglu_pull = jax.vjp(geglu, gate_up)
        grad_product = jnp.einsum(
            "sd,fd->sf", grad_f_rows, w_downp, preferred_element_type=jnp.float32
        )
        down_grad = jnp.einsum(
            "sf,sd->fd",
            product.astype(jnp.bfloat16),
            grad_f_rows,
            preferred_element_type=jnp.float32,
        )
        (grad_gate_up,) = geglu_pull(grad_product)
        gu_bf = grad_gate_up.astype(jnp.bfloat16)
        gateup_grad = jnp.einsum("sd,scf->dcf", mid_rows, gu_bf, preferred_element_type=jnp.float32)
        return (gu_bf, gateup_grad, down_grad)

    def feed_none():
        return (
            jnp.zeros((seq_len, 2, w_gateup.shape[2]), jnp.bfloat16),
            jnp.zeros(w_gateup.shape, jnp.float32),
            jnp.zeros(w_downp.shape, jnp.float32),
        )

    grad_gu_bf, grad_w_gate_up, grad_w_down = lax.cond(active, feed_part, feed_none)

    def mid_term(offset, row_span):

        def mid_compute():
            return jnp.einsum(
                "scf,dcf->sd", grad_gu_bf, w_gateup, preferred_element_type=jnp.float32
            )

        def mid_nothing():
            return jnp.zeros((row_span, model_width), jnp.float32)

        return lax.cond(active, mid_compute, mid_nothing)

    grad_mid = reduce_grad_parts(mid_term, row_count)
    unused_mid, mid_pull = jax.vjp(normed, hidden_res, gains[2])
    grad_res_part, grad_g2 = mid_pull(grad_mid)
    grad_res = grad_out + grad_res_part
    unused_attn, attn_pull = jax.vjp(normed, branch_a, gains[1])
    grad_a, grad_g1 = attn_pull(grad_res)
    grad_a_rows = gather_grads(grad_a.astype(jnp.bfloat16))

    def attention_part():
        grad_attn = jnp.einsum(
            "sd,ed->se", grad_a_rows, w_out, preferred_element_type=jnp.float32
        ).astype(jnp.bfloat16)
        out_grad = jnp.einsum("se,sd->ed", attn_bf, grad_a_rows, preferred_element_type=jnp.float32)
        (q_rot, k_rot), shape_pull = jax.vjp(
            lambda q_in, kv_in, gain_in: shape_heads(q_in, kv_in, gain_in, cosine, sine_table),
            q_raw,
            kv_raw,
            head_gains_f,
        )
        grad_q_rot, grad_k_rot, grad_values = attend_backward(
            q_rot.astype(jnp.bfloat16),
            k_rot.astype(jnp.bfloat16),
            kv_raw[:, head_width:].astype(jnp.bfloat16),
            log_totals,
            grad_attn.reshape(q_rot.shape),
            seq_length,
            scaling,
        )
        grad_q_raw, grad_kv_raw, grad_head = shape_pull((grad_q_rot, grad_k_rot))
        grad_q_bf = grad_q_raw.astype(jnp.bfloat16)
        grad_kv_bf = jnp.concatenate([grad_kv_raw[:, :head_width], grad_values], axis=1).astype(
            jnp.bfloat16
        )
        query_grad = jnp.einsum(
            "sd,se->de", seq_rows, grad_q_bf, preferred_element_type=jnp.float32
        )
        keyval_grad = jnp.einsum(
            "sd,se->de", seq_rows, grad_kv_bf, preferred_element_type=jnp.float32
        )
        return (grad_q_bf, grad_kv_bf, out_grad, query_grad, keyval_grad, grad_head)

    def attention_none():
        return (
            jnp.zeros((seq_len, per_width), jnp.bfloat16),
            jnp.zeros((seq_len, 2 * head_width), jnp.bfloat16),
            jnp.zeros(w_out.shape, jnp.float32),
            jnp.zeros(w_query.shape, jnp.float32),
            jnp.zeros(w_keyval.shape, jnp.float32),
            jnp.zeros(head_gain.shape, jnp.float32),
        )

    grad_q_bf, grad_kv_bf, grad_w_out, grad_w_query, grad_w_keyval, grad_head = lax.cond(
        active, attention_part, attention_none
    )

    def in_term(offset, row_span):

        def in_compute():
            from_queries = jnp.einsum(
                "se,de->sd", grad_q_bf, w_query, preferred_element_type=jnp.float32
            )
            return from_queries + jnp.einsum(
                "se,de->sd", grad_kv_bf, w_keyval, preferred_element_type=jnp.float32
            )

        def in_nothing():
            return jnp.zeros((row_span, model_width), jnp.float32)

        return lax.cond(active, in_compute, in_nothing)

    grad_in_normed = reduce_grad_parts(in_term, row_count)
    unused_in, in_pull = jax.vjp(normed, layer_in, gains[0])
    grad_in_part, grad_g0 = in_pull(grad_in_normed)
    grad_in = grad_res + grad_in_part
    gradients = (
        jnp.stack([grad_g0, grad_g1, grad_g2, grad_g3]),
        grad_head,
        grad_w_query,
        grad_w_keyval,
        grad_w_out,
        grad_w_gate_up,
        grad_w_down,
    )
    return (grad_in, gradients)


def on_device(
    inputs, cotangent, lengths, norm_gains, head_gains, w_q, w_kv, w_o, w_gate_up, w_down
):
    section_index = lax.axis_index("section")
    narrow_index = lax.axis_index("narrow")
    gathered = (
        lax.all_gather(norm_gains[0], "wide", axis=1, tiled=True),
        lax.all_gather(head_gains[0], "wide", axis=1, tiled=True),
        lax.all_gather(w_q[0], "wide", axis=0, tiled=True),
        lax.all_gather(w_kv[0], "wide", axis=0, tiled=True),
        lax.all_gather(w_o[0], "wide", axis=1, tiled=True),
        lax.all_gather(w_gate_up[0], "wide", axis=0, tiled=True),
        lax.all_gather(w_down[0], "wide", axis=1, tiled=True),
    )
    micro_count, row_count, model_width = inputs.shape
    seq_len = row_count * lax.axis_size("narrow")
    head_width = gathered[1].shape[-1]
    per_width = gathered[2].shape[1]
    per_heads = per_width // head_width
    cosine, sine_table = tables(seq_len, head_width)
    seq_lengths = lengths[:, 0]
    positions = narrow_index * row_count + jnp.arange(row_count, dtype=jnp.int32)
    zero_rows = jnp.zeros((row_count, model_width), jnp.float32)
    blank = (
        zero_rows,
        jnp.zeros((seq_len, model_width), jnp.bfloat16),
        jnp.zeros((seq_len, per_width), jnp.float32),
        jnp.zeros((seq_len, 2 * head_width), jnp.float32),
        jnp.zeros((per_heads, seq_len, 1), jnp.float32),
        jnp.zeros((seq_len, per_width), jnp.bfloat16),
        zero_rows,
        zero_rows,
        jnp.zeros((seq_len, model_width), jnp.bfloat16),
        zero_rows,
    )
    kept_start = jax.tree.map(
        lambda member: jnp.zeros((micro_count,) + member.shape, member.dtype), blank
    )
    out_start = jnp.zeros((micro_count, row_count, model_width), jnp.bfloat16)

    def put_slot(whole, member, slot_index, active):
        previous = lax.dynamic_index_in_dim(whole, slot_index, 0, keepdims=False)
        return lax.dynamic_update_index_in_dim(
            whole, jnp.where(active, member, previous), slot_index, 0
        )

    def forward_step(carry, step_index):
        arrived, kept_store, out_store = carry
        micro_index = jnp.clip(step_index - section_index, 0, micro_count - 1)
        active = (step_index >= section_index) & (step_index - section_index < micro_count)
        own_input = lax.dynamic_index_in_dim(inputs, micro_index, 0, keepdims=False)
        layer_in = jnp.where(section_index == 0, own_input, arrived).astype(jnp.float32)
        seq_length = seq_lengths[micro_index]
        layer_out, kept = layer_forward(layer_in, seq_length, gathered, cosine, sine_table, active)
        layer_bf = layer_out.astype(jnp.bfloat16)
        kept_store = jax.tree.map(
            lambda whole, member: put_slot(whole, member, micro_index, active), kept_store, kept
        )
        out_store = put_slot(out_store, layer_bf, micro_index, active)
        arrived = shifted(layer_bf, "section", 1)
        return ((arrived, kept_store, out_store), None)

    first_arrived = jnp.zeros((row_count, model_width), jnp.bfloat16)
    (unused_arrived, kept_store, out_store), unused_steps = lax.scan(
        forward_step,
        (first_arrived, kept_start, out_start),
        jnp.arange(micro_count + 1, dtype=jnp.int32),
    )
    shard_blocks = (norm_gains[0], head_gains[0], w_q[0], w_kv[0], w_o[0], w_gate_up[0], w_down[0])
    grad_blank = tuple((jnp.zeros(member.shape, jnp.float32) for member in shard_blocks))

    def backward_step(carry, step_index):
        arrived, grad_total, grad_store = carry
        raw_index = micro_count - step_index - section_index
        active = (raw_index >= 0) & (raw_index < micro_count)
        micro_index = jnp.clip(raw_index, 0, micro_count - 1)
        seq_length = seq_lengths[micro_index]
        real_rows = (positions < seq_length).astype(jnp.float32)
        own_grad = (
            lax.dynamic_index_in_dim(cotangent, micro_index, 0, keepdims=False).astype(jnp.float32)
            * real_rows[:, None]
        )
        grad_out = jnp.where(section_index == 1, own_grad, arrived.astype(jnp.float32))
        kept = jax.tree.map(
            lambda whole: lax.dynamic_index_in_dim(whole, micro_index, 0, keepdims=False),
            kept_store,
        )
        grad_in, gradients = layer_backward(
            grad_out, seq_length, gathered, kept, cosine, sine_table, active
        )
        gradients = tuple(
            (jnp.where(active, member, jnp.zeros_like(member)) for member in gradients)
        )
        gradients = reduce_weights(gradients)
        grad_total = jax.tree.map(jnp.add, grad_total, gradients)
        grad_store = put_slot(grad_store, grad_in, micro_index, active)
        arrived = shifted(grad_in.astype(jnp.bfloat16), "section", -1)
        return ((arrived, grad_total, grad_store), None)

    grad_start = jnp.zeros((micro_count, row_count, model_width), jnp.float32)
    (unused_back, grad_total, grad_store), unused_back_steps = lax.scan(
        backward_step,
        (first_arrived, grad_blank, grad_start),
        jnp.arange(micro_count + 1, dtype=jnp.int32),
    )
    return (
        out_store[None],
        grad_store[None],
        grad_total[0][None],
        grad_total[1][None],
        grad_total[2][None],
        grad_total[3][None],
        grad_total[4][None],
        grad_total[5][None],
        grad_total[6][None],
    )


def solution(mesh):
    return jax.shard_map(
        on_device,
        mesh=mesh,
        in_specs=(
            P(None, ("wide", "narrow"), None),
            P(None, ("wide", "narrow"), None),
            P(None, "wide"),
            P("section", None, "wide"),
            P("section", None, "wide"),
            P("section", "wide", "narrow"),
            P("section", "wide", None),
            P("section", "narrow", "wide"),
            P("section", "wide", None, "narrow"),
            P("section", "narrow", "wide"),
        ),
        out_specs=(
            P("section", None, ("wide", "narrow"), None),
            P("section", None, ("wide", "narrow"), None),
            P("section", None, "wide"),
            P("section", None, "wide"),
            P("section", "wide", "narrow"),
            P("section", "wide", None),
            P("section", "narrow", "wide"),
            P("section", "wide", None, "narrow"),
            P("section", "narrow", "wide"),
        ),
        check_vma=False,
    )
```

profile of v0, /device:TPU:0, one launch (start us, length us, event | category | flops | bytes accessed | tf_op | source)
XLA Modules:
  0.0 3598.2 jit_solution(16897730218027055424)
XLA Ops:
  9.5 21.8 all-gather.4
  32.5 23.4 all-gather
  73.0 23.7 all-gather.1
  121.2 141.9 %all-gather.17.cloned.1.call-done = bf16[1,1152,2,1728]{3,2,0,1:T(2,128)(2,1)} async-done(((bf16[1,288,2,1728]{3,2,0,1:T(2,128)(2,1)}), bf16[1,1152,2,1728]{3,2,0,1:T(2,128)(2,1)}) %all-gather.17.cloned.1.call-update) | async-done | bytes 7962640 | tf_op jit(solution)/shard_map/all_gather | solution.py:450
  263.1 22.9 copy.73
  310.2 706.0 %while.71 = (s32[]{:T(128)}, bf16[256,1152]{1,0:T(8,128)(2,1)S(1)}, f32[2,256,1152]{2,1,0:T(8,128)S(1)}, bf16[2,1024,1152]{2,1,0:T(8,128)(2,1)}, f32[2,1024,256]...) while((s32[]{:T(128)}, bf16[256,1152]{1,0:T(8,128)(2,1)S(1)}, ...), condition=%wide.region_21.22_spmd.clone.clone.clone, body=%wide.region_0.21_spmd.clone.clone.clone.sunk | while | flops 15781444608 | bytes 320482752 | solution.py:502
  338.3 35.9 all-gather.21.cloned.1.call-done
  374.2 25.8 conditional.44
  404.2 37.5 %reduce-scatter.27.cloned.1.call-done = bf16[256,1152]{1,0:T(8,128)(2,1)} async-done(((bf16[1024,1152]{1,0:T(8,128)(2,1)}), bf16[256,1152]{1,0:T(8,128)(2,1)}) %reduce-scatter.27.cloned.1.call-update) | async-done | bytes 589840 | tf_op jit(solution)/shard_map/while/body/eval_jaxpr/reduce_scatter | solution.py:166
  446.5 37.6 %all-gather.23.cloned.1.call-done = bf16[1024,1152]{1,0:T(8,128)(2,1)} async-done(((bf16[256,1152]{1,0:T(8,128)(2,1)}), bf16[1024,1152]{1,0:T(8,128)(2,1)}) %all-gather.23.cloned.1.call-update) | async-done | bytes 2359312 | tf_op jit(solution)/shard_map/while/body/eval_jaxpr/all_gather | solution.py:146
  567.0 36.8 %all-gather.21.cloned.1.call-done = bf16[1024,1152]{1,0:T(8,128)(2,1)} async-done(((bf16[256,1152]{1,0:T(8,128)(2,1)}), bf16[1024,1152]{1,0:T(8,128)(2,1)}) %all-gather.21.cloned.1.call-update) | async-done | bytes 2359312 | tf_op jit(solution)/shard_map/while/body/eval_jaxpr/all_gather | solution.py:146
  603.8 25.8 conditional.44
  633.8 37.5 %reduce-scatter.27.cloned.1.call-done = bf16[256,1152]{1,0:T(8,128)(2,1)} async-done(((bf16[1024,1152]{1,0:T(8,128)(2,1)}), bf16[256,1152]{1,0:T(8,128)(2,1)}) %reduce-scatter.27.cloned.1.call-update) | async-done | bytes 589840 | tf_op jit(solution)/shard_map/while/body/eval_jaxpr/reduce_scatter | solution.py:166
  676.1 37.6 %all-gather.23.cloned.1.call-done = bf16[1024,1152]{1,0:T(8,128)(2,1)} async-done(((bf16[256,1152]{1,0:T(8,128)(2,1)}), bf16[1024,1152]{1,0:T(8,128)(2,1)}) %all-gather.23.cloned.1.call-update) | async-done | bytes 2359312 | tf_op jit(solution)/shard_map/while/body/eval_jaxpr/all_gather | solution.py:146
  796.6 36.8 %all-gather.21.cloned.1.call-done = bf16[1024,1152]{1,0:T(8,128)(2,1)} async-done(((bf16[256,1152]{1,0:T(8,128)(2,1)}), bf16[1024,1152]{1,0:T(8,128)(2,1)}) %all-gather.21.cloned.1.call-update) | async-done | bytes 2359312 | tf_op jit(solution)/shard_map/while/body/eval_jaxpr/all_gather | solution.py:146
  838.6 61.8 %reduce-scatter.27.cloned.1.call-done = bf16[256,1152]{1,0:T(8,128)(2,1)} async-done(((bf16[1024,1152]{1,0:T(8,128)(2,1)}), bf16[256,1152]{1,0:T(8,128)(2,1)}) %reduce-scatter.27.cloned.1.call-update) | async-done | bytes 589840 | tf_op jit(solution)/shard_map/while/body/eval_jaxpr/reduce_scatter | solution.py:166
  905.2 37.6 %all-gather.23.cloned.1.call-done = bf16[1024,1152]{1,0:T(8,128)(2,1)} async-done(((bf16[256,1152]{1,0:T(8,128)(2,1)}), bf16[1024,1152]{1,0:T(8,128)(2,1)}) %all-gather.23.cloned.1.call-update) | async-done | bytes 2359312 | tf_op jit(solution)/shard_map/while/body/eval_jaxpr/all_gather | solution.py:146
  981.9 24.0 reduce-scatter.29.cloned.1.call-done
  1019.3 2567.7 %while.72 = (s32[]{:T(128)}, bf16[256,1152]{1,0:T(8,128)(2,1)}, f32[4,288]{1,0:T(4,128)}, f32[2,64]{1,0:T(2,128)}, f32[288,256]{1,0:T(8,128)}, /*index=5*/f32[28...) while((s32[]{:T(128)}, bf16[256,1152]{1,0:T(8,128)(2,1)}, ...), condition=%wide.region_63.64_spmd.clone.clone.clone.clone, body=%wide.region_22.63_spmd.clone.clone.clone.clone.sunk | while | flops 40278130688 | bytes 579084160 | solution.py:539
  1038.0 37.6 %all-gather.25.cloned.1.call-done = bf16[1024,1152]{1,0:T(8,128)(2,1)} async-done(((bf16[256,1152]{1,0:T(8,128)(2,1)}), bf16[1024,1152]{1,0:T(8,128)(2,1)}) %all-gather.25.cloned.1.call-update) | async-done | bytes 2359312 | tf_op jit(solution)/shard_map/while/body/eval_jaxpr/all_gather | solution.py:150
  1096.0 122.7 %reduce-scatter.31.cloned.1.call-done = bf16[256,1152]{1,0:T(8,128)(2,1)} async-done(((bf16[1024,1152]{1,0:T(8,128)(2,1)}), bf16[256,1152]{1,0:T(8,128)(2,1)}) %reduce-scatter.31.cloned.1.call-update) | async-done | bytes 589840 | tf_op jit(solution)/shard_map/while/body/eval_jaxpr/reduce_scatter | solution.py:175
  1228.3 36.0 %all-gather.27.cloned.1.call-done = bf16[1024,1152]{1,0:T(8,128)(2,1)} async-done(((bf16[256,1152]{1,0:T(8,128)(2,1)}), bf16[1024,1152]{1,0:T(8,128)(2,1)}) %all-gather.27.cloned.1.call-update) | async-done | bytes 2359312 | tf_op jit(solution)/shard_map/while/body/eval_jaxpr/all_gather | solution.py:150
  1298.9 26.0 reduce-scatter.41.cloned.1.call-done
  1333.8 67.8 %reduce-scatter.45.cloned.1.call-done = bf16[288,1728]{1,0:T(8,128)(2,1)} async-done(((bf16[1152,1728]{1,0:T(8,128)(2,1)}), bf16[288,1728]{1,0:T(8,128)(2,1)}) %reduce-scatter.45.cloned.1.call-update) | async-done | bytes 995344 | tf_op jit(solution)/shard_map/while
  1407.2 284.2 %all-reduce.25.cloned.1.call-done = bf16[1152,2,1728]{2,1,0:T(2,128)(2,1)} async-done(((bf16[1152,2,1728]{2,1,0:T(2,128)(2,1)}), bf16[1152,2,1728]{2,1,0:T(2,128)(2,1)}) %all-reduce.25.cloned.1.call-update) | async-done | bytes 7962640 | tf_op jit(solution)/shard_map/while
  1713.5 21.3 reduce-scatter.43.cloned.1.call-done
  1760.9 41.4 %all-reduce.23.cloned.1.call-done = bf16[288,512]{1,0:T(8,128)(2,1)} async-done(((bf16[288,512]{1,0:T(8,128)(2,1)}), bf16[288,512]{1,0:T(8,128)(2,1)}) %all-reduce.23.cloned.1.call-update) | async-done | bytes 294928 | tf_op jit(solution)/shard_map/while/body/eval_jaxpr/psum | solution.py:210
  1804.2 38.5 %reduce-scatter.33.cloned.1.call-done = bf16[256,1152]{1,0:T(8,128)(2,1)} async-done(((bf16[1024,1152]{1,0:T(8,128)(2,1)}), bf16[256,1152]{1,0:T(8,128)(2,1)}) %reduce-scatter.33.cloned.1.call-update) | async-done | bytes 589840 | tf_op jit(solution)/shard_map/while/body/eval_jaxpr/reduce_scatter | solution.py:175
  1892.3 34.0 all-gather.25.cloned.1.call-done
  1926.3 90.1 %conditional.48 = (bf16[1024,2,1728]{0,2,1:T(8,128)(2,1)}, bf16[1728,1152]{1,0:T(8,128)(2,1)}, bf16[1152,2,1728]{2,1,0:T(2,128)(2,1)}) conditional(s32[]{:T(128)} %convert_element_type.633, () %tuple.326, (bf16[2,1024,1152]{2,1,0:T(8,128)(2,1)}, s32[]{:T(128)}, bf16[1152,2,1728]{0,2,1:T(8,128)(2,1)}, bf16[1024,1152]{1,0:T(8,128)(2,1)}, ...), branch_computations={%region_25.25_spmd, %region_26.26_spmd} | conditional | flops 24524881920 | bytes 159548512 | solution.py:339
  1980.0 22.9 copy.94
  2034.1 35.6 reduce-scatter.31.cloned.1.call-done
  2079.2 36.0 %all-gather.27.cloned.1.call-done = bf16[1024,1152]{1,0:T(8,128)(2,1)} async-done(((bf16[256,1152]{1,0:T(8,128)(2,1)}), bf16[1024,1152]{1,0:T(8,128)(2,1)}) %all-gather.27.cloned.1.call-update) | async-done | bytes 2359312 | tf_op jit(solution)/shard_map/while/body/eval_jaxpr/all_gather | solution.py:150
  2115.2 30.7 conditional.50
  2190.1 63.3 %reduce-scatter.45.cloned.1.call-done = bf16[288,1728]{1,0:T(8,128)(2,1)} async-done(((bf16[1152,1728]{1,0:T(8,128)(2,1)}), bf16[288,1728]{1,0:T(8,128)(2,1)}) %reduce-scatter.45.cloned.1.call-update) | async-done | bytes 995344 | tf_op jit(solution)/shard_map/while
  2259.7 283.2 %all-reduce.25.cloned.1.call-done = bf16[1152,2,1728]{2,1,0:T(2,128)(2,1)} async-done(((bf16[1152,2,1728]{2,1,0:T(2,128)(2,1)}), bf16[1152,2,1728]{2,1,0:T(2,128)(2,1)}) %all-reduce.25.cloned.1.call-update) | async-done | bytes 7962640 | tf_op jit(solution)/shard_map/while
  2612.6 41.1 %all-reduce.23.cloned.1.call-done = bf16[288,512]{1,0:T(8,128)(2,1)} async-done(((bf16[288,512]{1,0:T(8,128)(2,1)}), bf16[288,512]{1,0:T(8,128)(2,1)}) %all-reduce.23.cloned.1.call-update) | async-done | bytes 294928 | tf_op jit(solution)/shard_map/while/body/eval_jaxpr/psum | solution.py:210
  2655.7 38.4 %reduce-scatter.33.cloned.1.call-done = bf16[256,1152]{1,0:T(8,128)(2,1)} async-done(((bf16[1024,1152]{1,0:T(8,128)(2,1)}), bf16[256,1152]{1,0:T(8,128)(2,1)}) %reduce-scatter.33.cloned.1.call-update) | async-done | bytes 589840 | tf_op jit(solution)/shard_map/while/body/eval_jaxpr/reduce_scatter | solution.py:175
  2744.9 34.0 all-gather.25.cloned.1.call-done
  2778.9 90.2 %conditional.48 = (bf16[1024,2,1728]{0,2,1:T(8,128)(2,1)}, bf16[1728,1152]{1,0:T(8,128)(2,1)}, bf16[1152,2,1728]{2,1,0:T(2,128)(2,1)}) conditional(s32[]{:T(128)} %convert_element_type.633, () %tuple.326, (bf16[2,1024,1152]{2,1,0:T(8,128)(2,1)}, s32[]{:T(128)}, bf16[1152,2,1728]{0,2,1:T(8,128)(2,1)}, bf16[1024,1152]{1,0:T(8,128)(2,1)}, ...), branch_computations={%region_25.25_spmd, %region_26.26_spmd} | conditional | flops 24524881920 | bytes 159548512 | solution.py:339
  2832.9 22.9 copy.94
  2886.9 35.6 reduce-scatter.31.cloned.1.call-done
  2932.1 36.0 %all-gather.27.cloned.1.call-done = bf16[1024,1152]{1,0:T(8,128)(2,1)} async-done(((bf16[256,1152]{1,0:T(8,128)(2,1)}), bf16[1024,1152]{1,0:T(8,128)(2,1)}) %all-gather.27.cloned.1.call-update) | async-done | bytes 2359312 | tf_op jit(solution)/shard_map/while/body/eval_jaxpr/all_gather | solution.py:150
  2968.1 30.7 conditional.50
  3043.0 63.3 %reduce-scatter.45.cloned.1.call-done = bf16[288,1728]{1,0:T(8,128)(2,1)} async-done(((bf16[1152,1728]{1,0:T(8,128)(2,1)}), bf16[288,1728]{1,0:T(8,128)(2,1)}) %reduce-scatter.45.cloned.1.call-update) | async-done | bytes 995344 | tf_op jit(solution)/shard_map/while
  3112.6 283.2 %all-reduce.25.cloned.1.call-done = bf16[1152,2,1728]{2,1,0:T(2,128)(2,1)} async-done(((bf16[1152,2,1728]{2,1,0:T(2,128)(2,1)}), bf16[1152,2,1728]{2,1,0:T(2,128)(2,1)}) %all-reduce.25.cloned.1.call-update) | async-done | bytes 7962640 | tf_op jit(solution)/shard_map/while
  3465.2 41.1 %all-reduce.23.cloned.1.call-done = bf16[288,512]{1,0:T(8,128)(2,1)} async-done(((bf16[288,512]{1,0:T(8,128)(2,1)}), bf16[288,512]{1,0:T(8,128)(2,1)}) %all-reduce.23.cloned.1.call-update) | async-done | bytes 294928 | tf_op jit(solution)/shard_map/while/body/eval_jaxpr/psum | solution.py:210
  3508.3 38.4 %reduce-scatter.33.cloned.1.call-done = bf16[256,1152]{1,0:T(8,128)(2,1)} async-done(((bf16[1024,1152]{1,0:T(8,128)(2,1)}), bf16[256,1152]{1,0:T(8,128)(2,1)}) %reduce-scatter.33.cloned.1.call-update) | async-done | bytes 589840 | tf_op jit(solution)/shard_map/while/body/eval_jaxpr/reduce_scatter | solution.py:175
  (899 shorter events, 1266.2 us)
Async XLA Ops:
  7.2 107.6 %all-gather.19.cloned.1.call-start = ((), (), s32[]{:S(2)}) async-start(), calls=%async_computation.12 | async-start | bytes 5160960 | tf_op jit(solution)/shard_map/all_gather | solution.py:451
  7.9 255.2 %all-gather.17.cloned.1.call-start = ((), (), s32[]{:S(2)}) async-start(), calls=%async_computation.11 | async-start | bytes 10321920 | tf_op jit(solution)/shard_map/all_gather | solution.py:450
  8.7 284.7 %all-gather.15.cloned.1.call-start = ((), (), s32[]{:S(2)}) async-start(), calls=%async_computation.10 | async-start | bytes 1474560 | tf_op jit(solution)/shard_map/all_gather | solution.py:448
  337.4 104.3 %reduce-scatter.27.cloned.1.call-start = ((), (), s32[]{:S(2)}) async-start(), calls=%async_computation.14 | async-start | bytes 2949120 | tf_op jit(solution)/shard_map/while/body/eval_jaxpr/reduce_scatter | solution.py:166
  404.1 80.0 %all-gather.23.cloned.1.call-start = ((), (), s32[]{:S(2)}) async-start(), calls=%async_computation.15 | async-start | bytes 2949120 | tf_op jit(solution)/shard_map/while/body/eval_jaxpr/all_gather | solution.py:146
  446.5 101.3 %reduce-scatter.29.cloned.1.call-start = ((), (), s32[]{:S(2)}) async-start(), calls=%async_computation.16 | async-start | bytes 2949120 | tf_op jit(solution)/shard_map/while/body/eval_jaxpr/reduce_scatter | solution.py:166
  566.2 105.1 %reduce-scatter.27.cloned.1.call-start = ((), (), s32[]{:S(2)}) async-start(), calls=%async_computation.14 | async-start | bytes 2949120 | tf_op jit(solution)/shard_map/while/body/eval_jaxpr/reduce_scatter | solution.py:166
  633.7 80.0 %all-gather.23.cloned.1.call-start = ((), (), s32[]{:S(2)}) async-start(), calls=%async_computation.15 | async-start | bytes 2949120 | tf_op jit(solution)/shard_map/while/body/eval_jaxpr/all_gather | solution.py:146
  676.1 101.3 %reduce-scatter.29.cloned.1.call-start = ((), (), s32[]{:S(2)}) async-start(), calls=%async_computation.16 | async-start | bytes 2949120 | tf_op jit(solution)/shard_map/while/body/eval_jaxpr/reduce_scatter | solution.py:166
  795.8 104.6 %reduce-scatter.27.cloned.1.call-start = ((), (), s32[]{:S(2)}) async-start(), calls=%async_computation.14 | async-start | bytes 2949120 | tf_op jit(solution)/shard_map/while/body/eval_jaxpr/reduce_scatter | solution.py:166
  838.6 104.2 %all-gather.23.cloned.1.call-start = ((), (), s32[]{:S(2)}) async-start(), calls=%async_computation.15 | async-start | bytes 2949120 | tf_op jit(solution)/shard_map/while/body/eval_jaxpr/all_gather | solution.py:146
  905.2 100.7 %reduce-scatter.29.cloned.1.call-start = ((), (), s32[]{:S(2)}) async-start(), calls=%async_computation.16 | async-start | bytes 2949120 | tf_op jit(solution)/shard_map/while/body/eval_jaxpr/reduce_scatter | solution.py:166
  1026.5 49.1 %all-gather.25.cloned.1.call-start = ((), (), s32[]{:S(2)}) async-start(), calls=%async_computation.17 | async-start | bytes 2949120 | tf_op jit(solution)/shard_map/while/body/eval_jaxpr/all_gather | solution.py:150
  1038.0 180.8 %reduce-scatter.31.cloned.1.call-start = ((), (), s32[]{:S(2)}) async-start(), calls=%async_computation.18 | async-start | bytes 2949120 | tf_op jit(solution)/shard_map/while/body/eval_jaxpr/reduce_scatter | solution.py:175
  1094.1 170.2 %all-gather.27.cloned.1.call-start = ((), (), s32[]{:S(2)}) async-start(), calls=%async_computation.19 | async-start | bytes 2949120 | tf_op jit(solution)/shard_map/while/body/eval_jaxpr/all_gather | solution.py:150
  1226.6 98.3 %reduce-scatter.41.cloned.1.call-start = ((), (), s32[]{:S(2)}) async-start(), calls=%async_computation.24 | async-start | bytes 1474560 | tf_op jit(solution)/shard_map/while/body/eval_jaxpr/reduce_scatter | solution.py:194
  1277.4 124.2 %reduce-scatter.45.cloned.1.call-start = ((), (), s32[]{:S(2)}) async-start(), calls=%async_computation.28 | async-start | bytes 5160960 | tf_op jit(solution)/shard_map/while
  1286.7 404.7 %all-reduce.25.cloned.1.call-start = ((), (), s32[]{:S(2)}) async-start(), calls=%async_computation.27 | async-start | bytes 16515072 | tf_op jit(solution)/shard_map/while
  1295.7 416.5 %reduce-scatter.37.cloned.1.call-start = ((), (), s32[]{:S(2)}) async-start(), calls=%async_computation.22 | async-start | bytes 81920 | tf_op jit(solution)/shard_map/while
  1296.6 438.3 %reduce-scatter.43.cloned.1.call-start = ((), (), s32[]{:S(2)}) async-start(), calls=%async_computation.26 | async-start | bytes 737280 | tf_op jit(solution)/shard_map/while
  1297.8 459.7 %reduce-scatter.39.cloned.1.call-start = ((), (), s32[]{:S(2)}) async-start(), calls=%async_computation.23 | async-start | bytes 737280 | tf_op jit(solution)/shard_map/while/body/eval_jaxpr/reduce_scatter | solution.py:191
  1298.9 503.5 %all-reduce.23.cloned.1.call-start = ((), (), s32[]{:S(2)}) async-start(), calls=%async_computation.25 | async-start | bytes 589824 | tf_op jit(solution)/shard_map/while/body/eval_jaxpr/psum | solution.py:210
  1325.0 517.7 %reduce-scatter.33.cloned.1.call-start = ((), (), s32[]{:S(2)}) async-start(), calls=%async_computation.20 | async-start | bytes 2949120 | tf_op jit(solution)/shard_map/while/body/eval_jaxpr/reduce_scatter | solution.py:175
  1326.7 541.7 %reduce-scatter.35.cloned.1.call-start = ((), (), s32[]{:S(2)}) async-start(), calls=%async_computation.21 | async-start | bytes 368640 | tf_op jit(solution)/shard_map/while
  1880.8 45.5 %all-gather.25.cloned.1.call-start = ((), (), s32[]{:S(2)}) async-start(), calls=%async_computation.17 | async-start | bytes 2949120 | tf_op jit(solution)/shard_map/while/body/eval_jaxpr/all_gather | solution.py:150
  1892.2 177.5 %reduce-scatter.31.cloned.1.call-start = ((), (), s32[]{:S(2)}) async-start(), calls=%async_computation.18 | async-start | bytes 2949120 | tf_op jit(solution)/shard_map/while/body/eval_jaxpr/reduce_scatter | solution.py:175
  2032.2 83.1 %all-gather.27.cloned.1.call-start = ((), (), s32[]{:S(2)}) async-start(), calls=%async_computation.19 | async-start | bytes 2949120 | tf_op jit(solution)/shard_map/while/body/eval_jaxpr/all_gather | solution.py:150
  2077.6 98.9 %reduce-scatter.41.cloned.1.call-start = ((), (), s32[]{:S(2)}) async-start(), calls=%async_computation.24 | async-start | bytes 1474560 | tf_op jit(solution)/shard_map/while/body/eval_jaxpr/reduce_scatter | solution.py:194
  2147.2 106.1 %reduce-scatter.45.cloned.1.call-start = ((), (), s32[]{:S(2)}) async-start(), calls=%async_computation.28 | async-start | bytes 5160960 | tf_op jit(solution)/shard_map/while
  2158.6 384.3 %all-reduce.25.cloned.1.call-start = ((), (), s32[]{:S(2)}) async-start(), calls=%async_computation.27 | async-start | bytes 16515072 | tf_op jit(solution)/shard_map/while
  2168.5 395.3 %reduce-scatter.37.cloned.1.call-start = ((), (), s32[]{:S(2)}) async-start(), calls=%async_computation.22 | async-start | bytes 81920 | tf_op jit(solution)/shard_map/while
  2169.4 417.0 %reduce-scatter.43.cloned.1.call-start = ((), (), s32[]{:S(2)}) async-start(), calls=%async_computation.26 | async-start | bytes 737280 | tf_op jit(solution)/shard_map/while
  2171.7 437.3 %reduce-scatter.39.cloned.1.call-start = ((), (), s32[]{:S(2)}) async-start(), calls=%async_computation.23 | async-start | bytes 737280 | tf_op jit(solution)/shard_map/while/body/eval_jaxpr/reduce_scatter | solution.py:191
  2173.8 479.9 %all-reduce.23.cloned.1.call-start = ((), (), s32[]{:S(2)}) async-start(), calls=%async_computation.25 | async-start | bytes 589824 | tf_op jit(solution)/shard_map/while/body/eval_jaxpr/psum | solution.py:210
  2176.6 517.6 %reduce-scatter.33.cloned.1.call-start = ((), (), s32[]{:S(2)}) async-start(), calls=%async_computation.20 | async-start | bytes 2949120 | tf_op jit(solution)/shard_map/while/body/eval_jaxpr/reduce_scatter | solution.py:175
  2182.9 537.0 %reduce-scatter.35.cloned.1.call-start = ((), (), s32[]{:S(2)}) async-start(), calls=%async_computation.21 | async-start | bytes 368640 | tf_op jit(solution)/shard_map/while
  2733.4 45.5 %all-gather.25.cloned.1.call-start = ((), (), s32[]{:S(2)}) async-start(), calls=%async_computation.17 | async-start | bytes 2949120 | tf_op jit(solution)/shard_map/while/body/eval_jaxpr/all_gather | solution.py:150
  2744.9 177.6 %reduce-scatter.31.cloned.1.call-start = ((), (), s32[]{:S(2)}) async-start(), calls=%async_computation.18 | async-start | bytes 2949120 | tf_op jit(solution)/shard_map/while/body/eval_jaxpr/reduce_scatter | solution.py:175
  2885.0 83.1 %all-gather.27.cloned.1.call-start = ((), (), s32[]{:S(2)}) async-start(), calls=%async_computation.19 | async-start | bytes 2949120 | tf_op jit(solution)/shard_map/while/body/eval_jaxpr/all_gather | solution.py:150
  2930.4 99.0 %reduce-scatter.41.cloned.1.call-start = ((), (), s32[]{:S(2)}) async-start(), calls=%async_computation.24 | async-start | bytes 1474560 | tf_op jit(solution)/shard_map/while/body/eval_jaxpr/reduce_scatter | solution.py:194
  3000.0 106.2 %reduce-scatter.45.cloned.1.call-start = ((), (), s32[]{:S(2)}) async-start(), calls=%async_computation.28 | async-start | bytes 5160960 | tf_op jit(solution)/shard_map/while
  3011.4 384.4 %all-reduce.25.cloned.1.call-start = ((), (), s32[]{:S(2)}) async-start(), calls=%async_computation.27 | async-start | bytes 16515072 | tf_op jit(solution)/shard_map/while
  3021.3 395.2 %reduce-scatter.37.cloned.1.call-start = ((), (), s32[]{:S(2)}) async-start(), calls=%async_computation.22 | async-start | bytes 81920 | tf_op jit(solution)/shard_map/while
  3022.2 416.8 %reduce-scatter.43.cloned.1.call-start = ((), (), s32[]{:S(2)}) async-start(), calls=%async_computation.26 | async-start | bytes 737280 | tf_op jit(solution)/shard_map/while
  3024.5 437.1 %reduce-scatter.39.cloned.1.call-start = ((), (), s32[]{:S(2)}) async-start(), calls=%async_computation.23 | async-start | bytes 737280 | tf_op jit(solution)/shard_map/while/body/eval_jaxpr/reduce_scatter | solution.py:191
  3026.6 479.7 %all-reduce.23.cloned.1.call-start = ((), (), s32[]{:S(2)}) async-start(), calls=%async_computation.25 | async-start | bytes 589824 | tf_op jit(solution)/shard_map/while/body/eval_jaxpr/psum | solution.py:210
  3029.4 517.3 %reduce-scatter.33.cloned.1.call-start = ((), (), s32[]{:S(2)}) async-start(), calls=%async_computation.20 | async-start | bytes 2949120 | tf_op jit(solution)/shard_map/while/body/eval_jaxpr/reduce_scatter | solution.py:175
  3035.7 536.7 %reduce-scatter.35.cloned.1.call-start = ((), (), s32[]{:S(2)}) async-start(), calls=%async_computation.21 | async-start | bytes 368640 | tf_op jit(solution)/shard_map/while
  (137 other events, 1659.5 us)
Sparse Core Ops, SparseCore 0:
  9.6 105.1 all-gather.18
  116.4 146.7 all-gather.16
  264.7 28.6 all-gather.14
  337.6 36.5 all-gather.20
  404.3 37.3 reduce-scatter.26
  446.6 37.4 all-gather.22
  510.3 37.3 reduce-scatter.28
  566.3 37.4 all-gather.20
  633.8 37.3 reduce-scatter.26
  676.2 37.4 all-gather.22
  739.9 37.3 reduce-scatter.28
  795.9 37.4 all-gather.20
  838.7 61.6 reduce-scatter.26
  905.3 37.4 all-gather.22
  946.8 59.1 reduce-scatter.28
  1038.1 37.4 all-gather.24
  1094.2 124.4 reduce-scatter.30
  1226.8 37.4 all-gather.26
  1277.6 47.3 reduce-scatter.40
  1327.1 74.4 reduce-scatter.44
  1404.3 287.0 all-reduce.24
  1714.6 20.2 reduce-scatter.42
  1737.1 20.3 reduce-scatter.38
  1760.7 41.5 all-reduce.22
  1805.2 37.3 reduce-scatter.32
  1848.4 19.8 reduce-scatter.34
  1892.4 33.8 all-gather.24
  2032.3 37.3 reduce-scatter.30
  2077.7 37.4 all-gather.26
  2147.3 29.1 reduce-scatter.40
  2178.9 74.4 reduce-scatter.44
  2255.8 287.0 all-reduce.24
  2566.2 20.2 reduce-scatter.42
  2588.7 20.2 reduce-scatter.38
  2612.1 41.5 all-reduce.22
  2656.7 37.3 reduce-scatter.32
  2699.9 19.8 reduce-scatter.34
  2745.0 33.8 all-gather.24
  2885.1 37.3 reduce-scatter.30
  2930.6 37.4 all-gather.26
  3000.2 29.1 reduce-scatter.40
  3031.7 74.4 reduce-scatter.44
  3108.7 287.0 all-reduce.24
  3418.8 20.2 reduce-scatter.42
  3441.2 20.2 reduce-scatter.38
  3464.6 41.5 all-reduce.22
  3509.3 37.3 reduce-scatter.32
  3552.5 19.8 reduce-scatter.34
  (3 shorter events, 53.8 us)
where the time goes:
time: 3610 us; the launch traced here: 3600 us
  waiting for transfers between devices  2490 us (69%)
  local copies, waits for them, and re-layouts  328 us (9%)
  other arithmetic  325 us (9%)
  matrix products  262 us (7%)
  blocking collectives  113 us (3%)
  loops' own time  54.9 us (2%)
    while x63, waiting for transfers between devices  1190 us
    reduce_scatter x6, waiting for transfers between devices, reduce_grad_parts(): lax.psum_scatter(term(jnp.int32(0), row_count * lax.axis_size('narrow'))....  309 us
    all_gather x6, waiting for transfers between devices, gather_rows(): return lax.all_gather(normed_rows, 'narrow', axis=0, tiled=True)  222 us
    all_gather x6, waiting for transfers between devices, gather_grads(): return lax.all_gather(grad_rows, 'narrow', axis=0, tiled=True)  214 us
    reduce_scatter x6, waiting for transfers between devices, reduce_parts(): lax.psum_scatter(term(jnp.int32(0), row_count * lax.axis_size('narrow'))....  163 us
    all_gather x1, waiting for transfers between devices, on_device(): lax.all_gather(w_gate_up[0], 'wide', axis=0, tiled=True)  142 us
    psum x3, waiting for transfers between devices, reduce_weights(): lax.psum(summed[3].astype(jnp.bfloat16), 'narrow').astype(jnp.float32)  124 us
  transfers between devices with their start and end apart: 57, of which 51 were waited for; matrix products, arithmetic and copies ran while one was open for 10% of the time, Pallas kernels for 0%

commit v1 on v0

v1 whole, which is shorter than its diff:
```python
import functools

import jax
import jax.numpy as jnp
from jax import lax
from jax.experimental import pallas as pl
from jax.experimental.pallas import tpu as pltpu
from jax.sharding import PartitionSpec as P

WINDOW = 512
EPSILON = 1e-06
NEGATIVE = -1e30
ROPE_BASE = 10000.0
MESH = pl.DeviceIdType.MESH
MIB = 2**20
GAIN_ROWS = 16
F32 = jnp.float32
BF16 = jnp.bfloat16


def dot(a, b, dims):
    return lax.dot_general(a, b, ((dims[0], dims[1]), ((), ())), preferred_element_type=F32)


def nn(a, b):
    return dot(a, b, ((1,), (0,)))


def nt(a, b):
    return dot(a, b, ((1,), (1,)))


def tn(a, b):
    return dot(a, b, ((0,), (0,)))


def normed(operand, gain_vec):
    return (
        operand
        * lax.rsqrt(jnp.mean(operand * operand, axis=-1, keepdims=True) + EPSILON)
        * gain_vec
    )


def geglu(gate, up):
    return jax.nn.gelu(gate, approximate=True) * up


def neighbours():
    me = lax.axis_index("narrow")
    return me, jnp.bitwise_xor(me, 1), jnp.bitwise_xor(me, 2)


def meet(nx, ny):
    barrier = pltpu.get_barrier_semaphore()
    for other in (nx, ny):
        pl.semaphore_signal(barrier, inc=1, device_id={"narrow": other}, device_id_type=MESH)
    pl.semaphore_wait(barrier, 2)


def remote(src, dst, send_sem, recv_sem, other):
    return pltpu.make_async_remote_copy(
        src_ref=src,
        dst_ref=dst,
        send_sem=send_sem,
        recv_sem=recv_sem,
        device_id={"narrow": other},
        device_id_type=MESH,
    )


def gather_kernel(a_ref, o_ref, local_sem, send, recv):
    me, nx, ny = neighbours()
    half = a_ref.shape[0] // 2
    first, second = pl.ds(0, half), pl.ds(half, half)
    meet(nx, ny)
    to_x1 = remote(a_ref.at[first], o_ref.at[me, first], send.at[0], recv.at[0], nx)
    to_y2 = remote(a_ref.at[second], o_ref.at[me, second], send.at[1], recv.at[1], ny)
    to_x2 = remote(a_ref.at[second], o_ref.at[me, second], send.at[2], recv.at[2], nx)
    to_y1 = remote(a_ref.at[first], o_ref.at[me, first], send.at[3], recv.at[3], ny)
    for copy in (to_x1, to_y2, to_x2, to_y1):
        copy.start()
    own = pltpu.make_async_copy(a_ref, o_ref.at[me], local_sem)
    own.start()
    to_x1.wait_recv()
    on_y = remote(o_ref.at[nx, first], o_ref.at[nx, first], send.at[4], recv.at[4], ny)
    on_y.start()
    to_y2.wait_recv()
    on_x = remote(o_ref.at[ny, second], o_ref.at[ny, second], send.at[5], recv.at[5], nx)
    on_x.start()
    for copy in (to_x2, to_y1, on_y, on_x):
        copy.wait_recv()
    for copy in (to_x1, to_y2, to_x2, to_y1, on_y, on_x):
        copy.wait_send()
    own.wait()


def gather_rows(rows, collective_id):
    count, width = rows.shape
    gathered = pl.pallas_call(
        gather_kernel,
        out_shape=jax.ShapeDtypeStruct((4, count, width), rows.dtype),
        in_specs=[pl.BlockSpec(memory_space=pltpu.VMEM)],
        out_specs=pl.BlockSpec(memory_space=pltpu.VMEM),
        scratch_shapes=[
            pltpu.SemaphoreType.DMA,
            pltpu.SemaphoreType.DMA((6,)),
            pltpu.SemaphoreType.DMA((6,)),
        ],
        compiler_params=pltpu.CompilerParams(
            collective_id=collective_id, has_side_effects=True, vmem_limit_bytes=32 * MIB
        ),
    )(rows)
    return gathered.reshape(4 * count, width)


def reduce_kernel(p_ref, o_ref, land, passing, send, recv):
    me, nx, ny = neighbours()
    diag = jnp.bitwise_xor(me, 3)
    half = p_ref.shape[1] // 2
    first, second = pl.ds(0, half), pl.ds(half, half)
    meet(nx, ny)
    copies = [
        remote(p_ref.at[diag, first], land.at[0], send.at[0], recv.at[0], nx),
        remote(p_ref.at[diag, second], land.at[1], send.at[1], recv.at[1], ny),
        remote(p_ref.at[nx, first], land.at[2], send.at[2], recv.at[2], nx),
        remote(p_ref.at[ny, second], land.at[3], send.at[3], recv.at[3], ny),
    ]
    for copy in copies:
        copy.start()
    copies[0].wait_recv()
    passing[0] = (p_ref[ny, first, :].astype(F32) + land[0].astype(F32)).astype(BF16)
    copies.append(remote(passing.at[0], land.at[4], send.at[4], recv.at[4], ny))
    copies[4].start()
    copies[1].wait_recv()
    passing[1] = (p_ref[nx, second, :].astype(F32) + land[1].astype(F32)).astype(BF16)
    copies.append(remote(passing.at[1], land.at[5], send.at[5], recv.at[5], nx))
    copies[5].start()
    for copy in copies[2:]:
        copy.wait_recv()
    o_ref[first, :] = p_ref[me, first, :].astype(F32) + land[2].astype(F32) + land[4].astype(F32)
    o_ref[second, :] = p_ref[me, second, :].astype(F32) + land[3].astype(F32) + land[5].astype(F32)
    for copy in copies:
        copy.wait_send()


def reduce_rows(parts, collective_id):
    count, width = parts.shape[0] // 4, parts.shape[1]
    return pl.pallas_call(
        reduce_kernel,
        out_shape=jax.ShapeDtypeStruct((count, width), F32),
        in_specs=[pl.BlockSpec(memory_space=pltpu.VMEM)],
        out_specs=pl.BlockSpec(memory_space=pltpu.VMEM),
        scratch_shapes=[
            pltpu.VMEM((6, count // 2, width), BF16),
            pltpu.VMEM((2, count // 2, width), BF16),
            pltpu.SemaphoreType.DMA((6,)),
            pltpu.SemaphoreType.DMA((6,)),
        ],
        compiler_params=pltpu.CompilerParams(
            collective_id=collective_id, has_side_effects=True, vmem_limit_bytes=32 * MIB
        ),
    )(parts.reshape(4, count, width))


def tables(positions, head_width):
    half_width = head_width // 2
    frequency = ROPE_BASE ** (-jnp.arange(half_width, dtype=F32) * (2.0 / head_width))
    angles = positions.astype(F32)[:, None] * frequency[None, :]
    return (jnp.cos(angles), jnp.sin(angles))


def rotate(operand, cosine, sine_table):
    half_width = operand.shape[-1] // 2
    front_half = operand[..., :half_width]
    back_half = operand[..., half_width:]
    return jnp.concatenate(
        [
            front_half * cosine - back_half * sine_table,
            back_half * cosine + front_half * sine_table,
        ],
        axis=-1,
    )


def shape_heads(q_raw, k_raw, head_gain, cosine, sine_table):
    head_width = head_gain.shape[-1]
    queries = q_raw.reshape(q_raw.shape[0], -1, head_width)
    q_rot = rotate(normed(queries, head_gain[0]), cosine[:, None, :], sine_table[:, None, :])
    k_rot = rotate(normed(k_raw, head_gain[1]), cosine, sine_table)
    return (q_rot, k_rot)


def window_of(rows, start):
    padded = jnp.concatenate([jnp.zeros((WINDOW, rows.shape[1]), rows.dtype), rows], axis=0)
    return lax.dynamic_slice_in_dim(padded, start, rows.shape[0] // 4 + WINDOW, 0)


def scores_of(q_bf, k_win, start, length, scaling):
    scores = jnp.einsum("qhd,kd->hqk", q_bf, k_win, preferred_element_type=F32) * scaling
    rows_at = start + jnp.arange(q_bf.shape[0], dtype=jnp.int32)[:, None]
    cols_at = start - WINDOW + jnp.arange(k_win.shape[0], dtype=jnp.int32)[None, :]
    visible = (
        (cols_at <= rows_at)
        & (rows_at - cols_at < WINDOW)
        & (cols_at >= 0)
        & ((cols_at < length) | (cols_at == rows_at))
    )
    return jnp.where(visible[None], scores, NEGATIVE)


def attention_forward(x, length, weights, start, trig):
    gains, head_gains, w_q, w_ot, w_kv = weights[:5]
    head_width = head_gains.shape[-1]
    scaling = head_width ** (-0.5)
    rows = x.shape[0]
    xn = normed(x, gains[0]).astype(BF16)
    q_raw = nn(xn, w_q)
    kv_raw = nn(xn, w_kv)
    q_rot, k_rot = shape_heads(q_raw, kv_raw[:, :head_width], head_gains, *trig)
    q_bf = q_rot.astype(BF16)
    kv_own = jnp.concatenate([k_rot, kv_raw[:, head_width:]], axis=1).astype(BF16)
    kv_win = window_of(gather_rows(kv_own, 0), start)
    k_win, v_win = kv_win[:, :head_width], kv_win[:, head_width:]
    scores = scores_of(q_bf, k_win, start, length, scaling)
    maximum = jnp.max(scores, axis=-1, keepdims=True)
    exponent = jnp.exp(scores - maximum)
    row_total = jnp.sum(exponent, axis=-1, keepdims=True)
    probs = (exponent / row_total).astype(BF16)
    o_bf = jnp.einsum("hqk,kd->qhd", probs, v_win, preferred_element_type=F32)
    o_bf = o_bf.reshape(rows, -1).astype(BF16)
    a = nt(o_bf, w_ot)
    h = x + normed(a, gains[1])
    kept = (x, xn, q_raw, kv_raw[:, :head_width], q_bf, k_win, v_win, maximum + jnp.log(row_total), o_bf, a)
    return h, kept


def attention_backward(dh, length, weights, kept, start, trig):
    gains, head_gains, w_q, w_ot, w_kv = weights[:5]
    x, xn, q_raw, k_raw, q_bf, k_win, v_win, log_totals, o_bf, a = kept
    head_width = head_gains.shape[-1]
    scaling = head_width ** (-0.5)
    rows = x.shape[0]
    _, pull = jax.vjp(normed, a, gains[1])
    da, dg1 = pull(dh)
    da = da.astype(BF16)
    do = nn(da, w_ot).astype(BF16)
    d_w_ot = tn(da, o_bf)
    do = do.reshape(q_bf.shape)
    scores = scores_of(q_bf, k_win, start, length, scaling)
    probs = jnp.exp(scores - log_totals)
    dp = jnp.einsum("qhd,kd->hqk", do, v_win, preferred_element_type=F32)
    ds = (probs * (dp - jnp.sum(probs * dp, axis=-1, keepdims=True))).astype(BF16)
    dqr = jnp.einsum("hqk,kd->qhd", ds, k_win, preferred_element_type=F32) * scaling
    dkr = jnp.einsum("hqk,qhd->kd", ds, q_bf, preferred_element_type=F32) * scaling
    dv = jnp.einsum("hqk,qhd->kd", probs.astype(BF16), do, preferred_element_type=F32)
    dkv_win = jnp.concatenate([dkr, dv], axis=1).astype(BF16)
    dkv_all = jnp.zeros((4 * rows + WINDOW, 2 * head_width), BF16)
    dkv_all = lax.dynamic_update_slice_in_dim(dkv_all, dkv_win, start, 0)
    dkv = reduce_rows(dkv_all[WINDOW:], 1)
    _, pull = jax.vjp(lambda q, k, g: shape_heads(q, k, g, *trig), q_raw, k_raw, head_gains)
    dq, dk, d_head = pull((dqr, dkv[:, :head_width]))
    dq = dq.astype(BF16)
    dkv = jnp.concatenate([dk, dkv[:, head_width:]], axis=1).astype(BF16)
    dxn = nt(dq, w_q) + nt(dkv, w_kv)
    d_w_q = tn(xn, dq)
    d_w_kv = tn(xn, dkv)
    _, pull = jax.vjp(normed, x, gains[0])
    dx, dg0 = pull(dxn)
    return dh + dx, (dg0, dg1, d_head, d_w_q, d_w_ot, d_w_kv)


def feed_forward(h, weights):
    gains, w_gate, w_up, w_dt = weights[0], *weights[5:]
    hn = normed(h, gains[2]).astype(BF16)
    rows = gather_rows(hn, 2)
    gate = nn(rows, w_gate)
    up = nn(rows, w_up)
    act = geglu(gate, up).astype(BF16)
    f = reduce_rows(nt(act, w_dt).astype(BF16), 3)
    out = h + normed(f, gains[3])
    return out, (h, rows, gate.astype(BF16), up.astype(BF16), f)


def feed_backward(dy, weights, kept):
    gains, w_gate, w_up, w_dt = weights[0], *weights[5:]
    h, rows, gate, up, f = kept
    _, pull = jax.vjp(normed, f, gains[3])
    df, dg3 = pull(dy)
    df_rows = gather_rows(df.astype(BF16), 2)
    act, pull = jax.vjp(geglu, gate.astype(F32), up.astype(F32))
    d_w_dt = tn(df_rows, act.astype(BF16)).astype(BF16)
    dgate, dup = pull(nn(df_rows, w_dt))
    dgate, dup = dgate.astype(BF16), dup.astype(BF16)
    dhn = reduce_rows((nt(dgate, w_gate) + nt(dup, w_up)).astype(BF16), 3)
    d_w_gate = tn(rows, dgate).astype(BF16)
    d_w_up = tn(rows, dup).astype(BF16)
    _, pull = jax.vjp(normed, h, gains[2])
    dh, dg2 = pull(dhn)
    return dy + dh, (dg2, dg3, d_w_gate, d_w_up, d_w_dt)


def on_device(
    inputs, cotangent, lengths, norm_gains, head_gains, w_q, w_kv, w_o, w_gate_up, w_down
):
    core = lax.axis_index("section")
    narrow = lax.axis_index("narrow")
    n_narrow = lax.axis_size("narrow")
    is_zero = core == 0
    rows, model = inputs.shape[1], inputs.shape[2]
    block = w_q.shape[1]
    head_width = w_q.shape[2]
    n_wide = lax.axis_size("wide")
    hidden = w_down.shape[1]
    kv_part = w_kv.shape[2] // n_narrow

    def swap(value):
        return lax.ppermute(value, "section", [(0, 1), (1, 0)])

    def by_core(first, second):
        return jnp.where(is_zero, first, second)

    kv_own = lax.dynamic_slice_in_dim(w_kv[0], narrow * kv_part, kv_part, 1)
    pack_width = 2 * head_width + kv_part
    pack = jnp.concatenate([w_q[0], w_o[0].T, kv_own], axis=1)
    gain_rows = jnp.zeros((GAIN_ROWS, pack_width), BF16)
    gain_rows = lax.dynamic_update_slice(gain_rows, norm_gains[0], (0, 0))
    gain_rows = lax.dynamic_update_slice(gain_rows, head_gains[0], (4, 0))
    pack = jnp.concatenate([pack, gain_rows], axis=0)
    pack = lax.all_gather(pack, "wide", axis=0)
    pack = lax.all_gather(pack, "narrow", axis=0)
    pack_peer = swap(pack)

    def unpack(whole):
        body = whole[:, :, :block]
        tail = whole[0, :, block:]

        def columns(first, last):
            return body[..., first:last].transpose(1, 2, 0, 3).reshape(model, -1)

        norm_part = tail[:, :4, :block].transpose(1, 0, 2).reshape(4, model).astype(F32)
        head_part = tail[:, 4:6, : head_width // n_wide].transpose(1, 0, 2).reshape(2, head_width)
        return (
            norm_part,
            head_part.astype(F32),
            columns(0, head_width),
            columns(head_width, 2 * head_width),
            columns(2 * head_width, pack_width),
        )

    attention_own, attention_peer = unpack(pack), unpack(pack_peer)

    w_gate, w_up = w_gate_up[0, :, 0], w_gate_up[0, :, 1]
    came = swap(by_core(w_up, w_gate))
    stays = by_core(w_gate, w_up)
    role = [by_core(stays, came), by_core(came, stays)]
    role = [lax.all_gather(member, "wide", axis=0, tiled=True) for member in role]
    role_peer = [swap(member) for member in role]
    down_own = lax.all_gather(w_down[0].T, "wide", axis=0, tiled=True)
    down_peer = swap(down_own)
    layers = []
    for section in range(2):
        mine = is_zero if section == 0 else jnp.logical_not(is_zero)
        attention = jax.tree.map(
            lambda own, peer: jnp.where(mine, own, peer), attention_own, attention_peer
        )
        layers.append(
            (
                *attention,
                by_core(role[section], role_peer[section]),
                by_core(role_peer[section], role[section]),
                jnp.where(mine, down_own, down_peer),
            )
        )

    start = narrow * rows
    positions = start + jnp.arange(rows, dtype=jnp.int32)
    trig = tables(positions, head_width)
    length = lax.dynamic_index_in_dim(lengths[:, 0], core, 0, keepdims=False)

    x = lax.dynamic_index_in_dim(inputs, core, 0, keepdims=False).astype(F32)
    outs, kept = [], []
    for section in range(2):
        h, kept_a = attention_forward(x, length, layers[section], start, trig)
        x, kept_f = feed_forward(h, layers[section])
        outs.append(x.astype(BF16))
        kept.append((kept_a, kept_f))
        x = outs[-1].astype(F32)

    real = (positions < length).astype(F32)[:, None]
    dy = lax.dynamic_index_in_dim(cotangent, core, 0, keepdims=False).astype(F32) * real
    dxs, grads = [None, None], [None, None]
    for section in (1, 0):
        dh, grads_f = feed_backward(dy, layers[section], kept[section][1])
        dx, grads_a = attention_backward(
            dh, length, layers[section], kept[section][0], start, trig
        )
        dxs[section] = dx
        grads[section] = (grads_a, grads_f)
        dy = dx.astype(BF16).astype(F32)

    role_sums = [None, None]
    for section in (1, 0):
        d_gate, d_up = grads[section][1][2:4]
        total = by_core(d_gate, d_up) + swap(by_core(d_up, d_gate))
        role_sums[section] = lax.psum_scatter(total, "wide", scatter_dimension=0, tiled=True)
    came = swap(by_core(role_sums[1], role_sums[0]))
    stays = by_core(role_sums[0], role_sums[1])
    grad_gate_up = jnp.stack([by_core(stays, came), by_core(came, stays)], axis=1).astype(F32)

    d_downs = [grads[section][1][4] for section in range(2)]
    down_sum = by_core(*d_downs) + swap(by_core(*d_downs[::-1]))
    down_sum = lax.psum_scatter(down_sum, "wide", scatter_dimension=0, tiled=True)
    grad_down = down_sum.T.astype(F32)

    packs = []
    for section in range(2):
        dg0, dg1, d_head, d_w_q, d_w_ot, d_w_kv = grads[section][0]
        dg2, dg3 = grads[section][1][:2]

        def blocks(member):
            return member.astype(BF16).reshape(n_wide, block, n_narrow, -1).transpose(2, 0, 1, 3)

        body = jnp.concatenate([blocks(d_w_q), blocks(d_w_ot), blocks(d_w_kv)], axis=3)
        norm_part = jnp.stack([dg0, dg1, dg2, dg3]).astype(BF16)
        norm_part = norm_part.reshape(4, n_wide, block).transpose(1, 0, 2)
        head_part = d_head.astype(BF16).reshape(2, n_wide, head_width // n_wide).transpose(1, 0, 2)
        tail = jnp.zeros((n_wide, GAIN_ROWS, pack_width), BF16)
        tail = lax.dynamic_update_slice(tail, norm_part, (0, 0, 0))
        tail = lax.dynamic_update_slice(tail, head_part, (0, 4, 0))
        tail = jnp.broadcast_to(tail[None], (n_narrow, *tail.shape))
        packs.append(jnp.concatenate([body, tail], axis=2))
    pack_sum = by_core(*packs) + swap(by_core(*packs[::-1]))
    pack_sum = lax.psum_scatter(pack_sum, "narrow", scatter_dimension=0, tiled=False)
    pack_sum = lax.psum_scatter(pack_sum, "wide", scatter_dimension=0, tiled=False)
    grad_q = pack_sum[:block, :head_width].astype(F32)
    grad_o = pack_sum[:block, head_width : 2 * head_width].T.astype(F32)
    grad_kv = lax.all_gather(
        pack_sum[:block, 2 * head_width :], "narrow", axis=1, tiled=True
    ).astype(F32)
    grad_norm = pack_sum[block : block + 4, :block].astype(F32)
    grad_head = pack_sum[block + 4 : block + 6, : head_width // n_wide].astype(F32)

    def by_section(first, second):
        stays, came = by_core(first, second), swap(by_core(second, first))
        return jnp.stack([by_core(stays, came), by_core(came, stays)])

    return (
        by_section(*outs)[None],
        by_section(*dxs)[None],
        grad_norm[None],
        grad_head[None],
        grad_q[None],
        grad_kv[None],
        grad_o[None],
        grad_gate_up[None],
        grad_down[None],
    )


def solution(mesh):
    return jax.shard_map(
        on_device,
        mesh=mesh,
        in_specs=(
            P(None, ("wide", "narrow"), None),
            P(None, ("wide", "narrow"), None),
            P(None, "wide"),
            P("section", None, "wide"),
            P("section", None, "wide"),
            P("section", "wide", "narrow"),
            P("section", "wide", None),
            P("section", "narrow", "wide"),
            P("section", "wide", None, "narrow"),
            P("section", "narrow", "wide"),
        ),
        out_specs=(
            P("section", None, ("wide", "narrow"), None),
            P("section", None, ("wide", "narrow"), None),
            P("section", None, "wide"),
            P("section", None, "wide"),
            P("section", "wide", "narrow"),
            P("section", "wide", None),
            P("section", "narrow", "wide"),
            P("section", "wide", None, "narrow"),
            P("section", "narrow", "wide"),
        ),
        check_vma=False,
    )
```

time: 3610 us -> 1260 us (0.35)
  waiting for transfers between devices: 2490 us -> 571 us
  other arithmetic: 325 us -> 75.9 us
  Pallas kernels: 0 us -> 202 us
  local copies, waits for them, and re-layouts: 328 us -> 162 us
  blocking collectives: 113 us -> 9.08 us
  loops' own time: 54.9 us -> 0 us
  matrix products: 262 us -> 210 us
    while x63 -> x0, waiting for transfers between devices: 1190 us -> none
    reduce_scatter x18 -> x3, waiting for transfers between devices: 567 us -> 138 us  [the longest x2 113 us: on_device(): lax.psum_scatter(total, 'wide', scatter_dimension=0, tiled=True)]
    all_gather x15 -> x5, waiting for transfers between devices: 603 us -> 326 us  [the longest x2 148 us: on_device(): lax.all_gather(member, 'wide', axis=0, tiled=True)]
    pallas_call x0 -> x12, Pallas kernels: none -> 202 us  [the longest x6 103 us: gather_rows(): pl.pallas_call(gather_kernel, out_shape=jax.ShapeDtypeStruct((4, count, w...]
    psum x3 -> x0, waiting for transfers between devices: 124 us -> none  [reduce_weights(): lax.psum(summed[3].astype(jnp.bfloat16), 'narrow').astype(jnp.float32)]
    convert_element_type x53 -> x14, other arithmetic: 121 us -> 4.8 us  [the longest x1 1.23 us: on_device(): real = (positions < length).astype(F32)[:, None]]
    dynamic_slice x41 -> x2, local copies, waits for them, and re-layouts: 82.2 us -> 0.6 us  [the longest x1 0.59 us: on_device(): length = lax.dynamic_index_in_dim(lengths[:, 0], core, 0, keepdims=False)]
    all_gather x4 -> x1, blocking collectives: 83.6 us -> 9.08 us  [on_device(): lax.all_gather(pack_sum[:block, 2 * head_width:], 'narrow', axis=1, tiled...]
  transfers between devices with their start and end apart: 57 -> 22, of which waited for: 51 -> 14; matrix products, arithmetic and copies ran while one was open for 10% -> 17% of each run, Pallas kernels for 0% -> 7%
where the time goes in v1:
time: 1260 us; the launch traced here: 1250 us
  waiting for transfers between devices  571 us (45%)
  matrix products  210 us (17%)
  Pallas kernels  202 us (16%)
  local copies, waits for them, and re-layouts  162 us (13%)
  other arithmetic  75.9 us (6%)
  between operations  16.9 us (1%)
    dot_general x36, matrix products, dot(): lax.dot_general(a, b, ((dims[0], dims[1]), ((), ())), preferred_element_t...  198 us
    all_gather x2, waiting for transfers between devices, on_device(): lax.all_gather(member, 'wide', axis=0, tiled=True)  148 us
    reduce_scatter x2, waiting for transfers between devices, on_device(): lax.psum_scatter(total, 'wide', scatter_dimension=0, tiled=True)  113 us
    pallas_call x6, Pallas kernels, gather_rows(): pl.pallas_call(gather_kernel, out_shape=jax.ShapeDtypeStruct((4, count, w...  103 us
    pallas_call x6, Pallas kernels, reduce_rows(): pl.pallas_call(reduce_kernel, out_shape=jax.ShapeDtypeStruct((count, widt...  99.2 us
    all_gather x1, waiting for transfers between devices, on_device(): down_own = lax.all_gather(w_down[0].T, 'wide', axis=0, tiled=True)  77.1 us
    unnamed x12, waiting for transfers between devices  74.1 us
    all_gather x1, waiting for transfers between devices, on_device(): pack = lax.all_gather(pack, 'narrow', axis=0)  61.2 us
  transfers between devices with their start and end apart: 22, of which 14 were waited for; matrix products, arithmetic and copies ran while one was open for 17% of the time, Pallas kernels for 7%

profile of v1, /device:TPU:0, one launch (start us, length us, event | category | flops | bytes accessed | tf_op | source)
XLA Modules:
  0.0 1249.6 jit_solution(5708879028195960774)
XLA Ops:
  11.5 39.6 %all-gather.14.cloned.1.call-done = bf16[1216,640]{1,0:T(8,128)(2,1)} async-done(((bf16[304,640]{1,0:T(8,128)(2,1)}), bf16[1216,640]{1,0:T(8,128)(2,1)}) %all-gather.14.cloned.1.call-update) | async-done | bytes 1556496 | tf_op jit(solution)/shard_map/all_gather | solution.py:330
  60.3 61.2 %all-gather.16.cloned.1.call-done = bf16[16,304,640]{2,1,0:T(8,128)(2,1)} async-done(((bf16[4,304,640]{2,1,0:T(8,128)(2,1)}), bf16[16,304,640]{2,1,0:T(8,128)(2,1)}) %all-gather.16.cloned.1.call-update) | async-done | bytes 6225936 | tf_op jit(solution)/shard_map/all_gather | solution.py:331
  125.7 77.1 %all-gather.10.cloned.1.call-done = bf16[1152,1728]{1,0:T(8,128)(2,1)} async-done(((bf16[288,1728]{1,0:T(8,128)(2,1)}), bf16[1152,1728]{1,0:T(8,128)(2,1)}) %all-gather.10.cloned.1.call-update) | async-done | bytes 3981328 | tf_op jit(solution)/shard_map/all_gather | solution.py:359
  202.8 6.5 copy.150
  209.3 73.8 %all-gather.8.cloned.1.call-done = bf16[1152,1728]{1,0:T(8,128)(2,1)} async-done(((bf16[288,1728]{1,0:T(8,128)(2,1)}), bf16[1152,1728]{1,0:T(8,128)(2,1)}) %all-gather.8.cloned.1.call-update) | async-done | bytes 3981328 | tf_op jit(solution)/shard_map/all_gather | solution.py:357
  283.0 6.3 copy.147
  289.4 73.9 %all-gather.12.cloned.1.call-done = bf16[1152,1728]{1,0:T(8,128)(2,1)} async-done(((bf16[288,1728]{1,0:T(8,128)(2,1)}), bf16[1152,1728]{1,0:T(8,128)(2,1)}) %all-gather.12.cloned.1.call-update) | async-done | bytes 3981328 | tf_op jit(solution)/shard_map/all_gather | solution.py:357
  363.3 6.4 copy.159
  377.8 6.6 select_bitcast_fusion
  390.7 12.7 %shard_map.169 = bf16[4,256,512]{2,1,0:T(8,128)(2,1)S(1)} custom-call(bf16[256,512]{1,0:T(8,128)(2,1)S(1)} %pad_maximum_fusion.11.a_ref), custom_call_target="tpu_custom_call" | custom-call | tf_op jit(solution)/shard_map/pallas_call | solution.py:100
  419.4 21.5 %shard_map.170 = bf16[4,256,1152]{2,1,0:T(8,128)(2,1)S(1)} custom-call(bf16[256,1152]{1,0:T(8,128)(2,1)S(1)} %multiply_convert_fusion.3.a_ref), custom_call_target="tpu_custom_call" | custom-call | tf_op jit(solution)/shard_map/pallas_call | solution.py:100
  440.9 7.9 fusion.78
  448.9 7.5 fusion.76
  456.4 9.5 convolution_convert_fusion.11
  465.8 22.0 %shard_map.171 = f32[256,1152]{1,0:T(8,128)S(1)} custom-call(bf16[4,256,1152]{2,1,0:T(8,128)(2,1)S(1)} %bitcast.372), custom_call_target="tpu_custom_call" | custom-call | tf_op jit(solution)/shard_map/pallas_call | solution.py:149
  504.0 11.9 shard_map.172
  529.1 21.6 %shard_map.173 = bf16[4,256,1152]{2,1,0:T(8,128)(2,1)S(1)} custom-call(bf16[256,1152]{1,0:T(8,128)(2,1)S(1)} %multiply_convert_fusion.2.a_ref), custom_call_target="tpu_custom_call" | custom-call | tf_op jit(solution)/shard_map/pallas_call | solution.py:100
  550.8 10.0 fusion.82
  560.8 7.2 fusion.80
  568.0 12.4 convolution_convert_fusion.10
  580.4 20.2 %shard_map.174 = f32[256,1152]{1,0:T(8,128)S(1)} custom-call(bf16[4,256,1152]{2,1,0:T(8,128)(2,1)S(1)} %bitcast.373), custom_call_target="tpu_custom_call" | custom-call | tf_op jit(solution)/shard_map/pallas_call | solution.py:149
  602.0 19.1 %shard_map.175 = bf16[4,256,1152]{2,1,0:T(8,128)(2,1)S(1)} custom-call(bf16[256,1152]{1,0:T(8,128)(2,1)S(1)} %fusion.124.a_ref), custom_call_target="tpu_custom_call" | custom-call | tf_op jit(solution)/shard_map/pallas_call | solution.py:100
  621.1 16.8 %fusion.9 = (bf16[1024,1728]{0,1:T(8,128)(2,1)}, bf16[1024,1728]{0,1:T(8,128)(2,1)}) fusion(f32[1024,1728]{0,1:T(8,128)} %fusion.82, f32[1024,1728]{0,1:T(8,128)} %fusion.80, bf16[1024,1152]{1,0:T(8,128)(2,1)S(1)} %bitcast.364, bf16[1152,1728]{0,1:T(8,128)(2,1)} %copy.150, bf16[1152,1728]{0,1:T(8,128)(2,1)} %collective-permute-done.3, pred[]{:T(512)S(6)} %not.3), kind=kOutput, calls=%fused_computation.31 | convolution fusion | flops 4128399360 | bytes 31555584 | tf_op jit(solution)/shard_map/dot_general | solution.py:22
  637.9 8.7 fusion.81
  652.5 19.3 %shard_map.176 = f32[256,1152]{1,0:T(8,128)S(1)} custom-call(bf16[4,256,1152]{2,1,0:T(8,128)(2,1)S(1)} %bitcast.356), custom_call_target="tpu_custom_call" | custom-call | tf_op jit(solution)/shard_map/pallas_call | solution.py:149
  689.3 9.3 shard_map.177
  707.2 16.5 %shard_map.178 = bf16[4,256,1152]{2,1,0:T(8,128)(2,1)S(1)} custom-call(bf16[256,1152]{1,0:T(8,128)(2,1)S(1)} %fusion.129.a_ref), custom_call_target="tpu_custom_call" | custom-call | tf_op jit(solution)/shard_map/pallas_call | solution.py:100
  723.8 15.7 %fusion.6 = (bf16[1024,1728]{0,1:T(8,128)(2,1)S(1)}, bf16[1024,1728]{0,1:T(8,128)(2,1)}) fusion(f32[1024,1728]{0,1:T(8,128)} %copy-done.155, f32[1024,1728]{0,1:T(8,128)} %fusion.76, bf16[1024,1152]{1,0:T(8,128)(2,1)S(1)} %bitcast.370, bf16[1152,1728]{0,1:T(8,128)(2,1)S(1)} %copy-done.63, bf16[1152,1728]{0,1:T(8,128)(2,1)} %collective-permute-done.3, ...), kind=kOutput, calls=%fused_computation.28 | convolution fusion | flops 4128399360 | bytes 31555584 | tf_op jit(solution)/shard_map/dot_general | solution.py:22
  739.5 9.9 fusion.77
  755.5 18.6 %shard_map.179 = f32[256,1152]{1,0:T(8,128)S(1)} custom-call(bf16[4,256,1152]{2,1,0:T(8,128)(2,1)S(1)} %bitcast.357), custom_call_target="tpu_custom_call" | custom-call | tf_op jit(solution)/shard_map/pallas_call | solution.py:149
  789.6 10.0 shard_map.180
  865.1 6.5 broadcast_select_fusion
  871.7 10.1 collective-permute-done.7
  887.7 6.9 convolution_convert_fusion.3
  899.9 6.7 collective-permute-done.9
  909.1 6.4 copy.212
  917.2 6.9 convolution_convert_fusion.5
  929.4 6.7 collective-permute-done.8
  938.5 6.4 copy.210
  945.2 12.3 convolution_convert_fusion.1
  957.6 14.0 %broadcast_select_fusion.2 = (bf16[1152,1728]{0,1:T(8,128)(2,1)}, bf16[1152,1728]{0,1:T(8,128)(2,1)S(1)}) fusion(bf16[1152,1728]{0,1:T(8,128)(2,1)S(1)} %convolution_convert_fusion.1, pred[]{:T(512)S(6)} %eq.8, bf16[1024,1152]{1,0:T(8,128)(2,1)S(1)} %bitcast.365, f32[1024,1728]{0,1:T(8,128)} %fusion.82, f32[1024,1728]{0,1:T(8,128)} %fusion.80), kind=kOutput, calls=%fused_computation.72 | convolution fusion | flops 4105617408 | bytes 28459008 | tf_op jit(solution)/shard_map/dot_general | solution.py:22
  971.6 7.1 collective-permute-done.11
  981.2 6.4 copy.214
  997.4 34.7 %reduce-scatter.18.cloned.1.call-done = bf16[288,1728]{1,0:T(8,128)(2,1)} async-done(((bf16[1152,1728]{1,0:T(8,128)(2,1)}), bf16[288,1728]{1,0:T(8,128)(2,1)}) %reduce-scatter.18.cloned.1.call-update) | async-done | bytes 995344 | tf_op jit(solution)/shard_map/reduce_scatter | solution.py:406
  1032.1 78.7 %reduce-scatter.16.cloned.1.call-done = bf16[288,1728]{1,0:T(8,128)(2,1)} async-done(((bf16[1152,1728]{1,0:T(8,128)(2,1)}), bf16[288,1728]{1,0:T(8,128)(2,1)}) %reduce-scatter.16.cloned.1.call-update) | async-done | bytes 995344 | tf_op jit(solution)/shard_map/reduce_scatter | solution.py:406
  1116.1 73.2 %reduce-scatter.20.cloned.1.call-done = bf16[288,1728]{1,0:T(8,128)(2,1)} async-done(((bf16[1152,1728]{1,0:T(8,128)(2,1)}), bf16[288,1728]{1,0:T(8,128)(2,1)}) %reduce-scatter.20.cloned.1.call-update) | async-done | bytes 995344
  1202.6 24.8 %reduce-scatter.14.cloned.1.call-done = bf16[1,304,640]{2,1,0:T(8,128)(2,1)} async-done(((bf16[4,304,640]{2,1,0:T(8,128)(2,1)}), bf16[1,304,640]{2,1,0:T(8,128)(2,1)}) %reduce-scatter.14.cloned.1.call-update) | async-done | bytes 389136 | tf_op jit(solution)/shard_map/reduce_scatter | solution.py:435
  1232.6 9.1 all_gather.31
  (583 shorter events, 256.3 us)
Async XLA Ops:
  7.2 44.8 %copy-start.48 = (bf16[1,288,2,1728]{3,2,1,0:T(2,128)(2,1)S(1)}, bf16[1,288,2,1728]{3,2,1,0:T(2,128)(2,1)}, u32[]{:S(2)}) copy-start(bf16[1,288,2,1728]{3,2,1,0:T(2,128)(2,1)} %param.18) | copy-start | bytes 5971972
  7.2 43.9 %all-gather.14.cloned.1.call-start = ((), (), s32[]{:S(2)}) async-start(), calls=%async_computation.9 | async-start | bytes 1945600 | tf_op jit(solution)/shard_map/all_gather | solution.py:330
  11.5 110.0 %all-gather.16.cloned.1.call-start = ((), (), s32[]{:S(2)}) async-start(), calls=%async_computation.10 | async-start | bytes 7782400 | tf_op jit(solution)/shard_map/all_gather | solution.py:331
  51.2 151.6 %all-gather.10.cloned.1.call-start = ((), (), s32[]{:S(2)}) async-start(), calls=%async_computation.6 | async-start | bytes 5160960 | tf_op jit(solution)/shard_map/all_gather | solution.py:359
  51.9 231.1 %all-gather.8.cloned.1.call-start = ((), (), s32[]{:S(2)}) async-start(), calls=%async_computation.5 | async-start | bytes 5160960 | tf_op jit(solution)/shard_map/all_gather | solution.py:357
  55.2 2.7 collective-permute-start.1
  59.2 62.4 %copy-start.154 = (s32[2,1]{0,1:T(1,128)S(1)}, s32[2,1]{0,1:T(1,128)}, u32[]{:S(2)}) copy-start(s32[2,1]{0,1:T(1,128)} %param.12) | copy-start | bytes 28
  59.2 63.0 %copy-start.49 = (bf16[2,256,1152]{2,1,0:T(8,128)(2,1)S(1)}, bf16[2,256,1152]{2,1,0:T(8,128)(2,1)}, u32[]{:S(2)}) copy-start(bf16[2,256,1152]{2,1,0:T(8,128)(2,1)} %param.10) | copy-start | bytes 3538948
  60.3 303.0 %all-gather.12.cloned.1.call-start = ((), (), s32[]{:S(2)}) async-start(), calls=%async_computation.7 | async-start | bytes 5160960 | tf_op jit(solution)/shard_map/all_gather | solution.py:357
  121.5 249.1 %collective-permute-start = (bf16[4,4,304,640]{3,2,1,0:T(8,128)(2,1)}, bf16[4,4,304,640]{3,2,1,0:T(8,128)(2,1)}, u32[]{:S(2)}, u32[]{:S(2)}) collective-permute-start(bf16[4,4,304,640]{3,2,1,0:T(8,128)(2,1)} %bitcast.398), channel_id=1, source_target_pairs={{0,16},{16,0},{1,17},{17,1},{2,18},{18,2},{3,19},{19,3},{4,20},{20... | collective-permute-start | bytes 18677768 | tf_op jit(solution)/shard_map/ppermute | solution.py:318
  121.5 873.5 %reduce-scatter.22.cloned.1.call-start = ((), (), s32[]{:S(2)}) async-start(), calls=%async_computation.14 | async-start | bytes 7782400
  122.4 86.9 %copy-start.136 = (f32[256]{0:T(256)}, f32[256]{0:T(256)S(1)}, u32[]{:S(2)}) copy-start(f32[256]{0:T(256)S(1)} %fusion.120) | copy-start | bytes 3076
  122.4 262.0 %copy-start.148 = (f32[128]{0:T(128)}, f32[128]{0:T(128)S(1)}, u32[]{:S(2)}) copy-start(f32[128]{0:T(128)S(1)} %multiply_power_fusion) | copy-start | bytes 1540
  123.6 260.8 %copy-start.106 = (f32[256]{0:T(256)}, f32[256]{0:T(256)S(1)}, u32[]{:S(2)}) copy-start(f32[256]{0:T(256)S(1)} %get-tuple-element.170) | copy-start | bytes 3076
  124.3 252.6 %copy-start.118 = (f32[256]{0:T(256)}, f32[256]{0:T(256)S(1)}, u32[]{:S(2)}) copy-start(f32[256]{0:T(256)S(1)} %fusion.226) | copy-start | bytes 3076
  209.3 247.1 %collective-permute-start.3 = (bf16[1152,1728]{0,1:T(8,128)(2,1)}, bf16[1152,1728]{0,1:T(8,128)(2,1)}, u32[]{:S(2)}, u32[]{:S(2)}) collective-permute-start(bf16[1152,1728]{0,1:T(8,128)(2,1)} %copy.150), channel_id=1, source_target_pairs={{0,16},{16,0},{1,17},{17,1},{2,18},{18,2},{3,19},{19,3},{4,20},{20... | collective-permute-start | bytes 11943944 | tf_op jit(solution)/shard_map/ppermute | solution.py:318
  289.4 151.5 %collective-permute-start.2 = (bf16[1152,1728]{0,1:T(8,128)(2,1)}, bf16[1152,1728]{0,1:T(8,128)(2,1)}, u32[]{:S(2)}, u32[]{:S(2)}) collective-permute-start(bf16[1152,1728]{0,1:T(8,128)(2,1)} %copy.147), channel_id=1, source_target_pairs={{0,16},{16,0},{1,17},{17,1},{2,18},{18,2},{3,19},{19,3},{4,20},{20... | collective-permute-start | bytes 11943944 | tf_op jit(solution)/shard_map/ppermute | solution.py:318
  369.7 181.1 %collective-permute-start.4 = (bf16[1152,1728]{0,1:T(8,128)(2,1)}, bf16[1152,1728]{0,1:T(8,128)(2,1)}, u32[]{:S(2)}, u32[]{:S(2)}) collective-permute-start(bf16[1152,1728]{0,1:T(8,128)(2,1)} %copy.159), channel_id=1, source_target_pairs={{0,16},{16,0},{1,17},{17,1},{2,18},{18,2},{3,19},{19,3},{4,20},{20... | collective-permute-start | bytes 11943944 | tf_op jit(solution)/shard_map/ppermute | solution.py:318
  372.4 37.1 %copy-start.95 = (f32[1152]{0:T(1024)}, f32[1152]{0:T(1024)S(1)}, u32[]{:S(2)}) copy-start(f32[1152]{0:T(1024)S(1)} %mul.1102) | copy-start | bytes 13828
  385.1 33.0 %copy-start.100 = (f32[1152]{0:T(1024)}, f32[1152]{0:T(1024)S(1)}, u32[]{:S(2)}) copy-start(f32[1152]{0:T(1024)S(1)} %mul.1138) | copy-start | bytes 13828
  390.5 21.7 %copy-start.114 = (f32[256]{0:T(256)}, f32[256]{0:T(256)S(1)}, u32[]{:S(2)}) copy-start(f32[256]{0:T(256)S(1)} %mul.1124) | copy-start | bytes 3076
  418.5 22.3 %copy-start.142 = (f32[256]{0:T(256)}, f32[256]{0:T(256)S(1)}, u32[]{:S(2)}) copy-start(f32[256]{0:T(256)S(1)} %get-tuple-element.95) | copy-start | bytes 3076
  418.6 70.1 %copy-start.15 = (f32[256,1152]{1,0:T(8,128)}, f32[256,1152]{1,0:T(8,128)S(1)}, u32[]{:S(2)}) copy-start(f32[256,1152]{1,0:T(8,128)S(1)} %get-tuple-element.96) | copy-start | bytes 3538948
  418.6 22.3 %copy-start.134 = (f32[256]{0:T(256)}, f32[256]{0:T(256)S(1)}, u32[]{:S(2)}) copy-start(f32[256]{0:T(256)S(1)} %fusion.230) | copy-start | bytes 3076
  419.2 21.7 %copy-start.28 = (bf16[1152,1728]{0,1:T(8,128)(2,1)S(1)}, bf16[1152,1728]{0,1:T(8,128)(2,1)}, u32[]{:S(2)}) copy-start(bf16[1152,1728]{0,1:T(8,128)(2,1)} %copy.147) | copy-start | bytes 11943940
  465.8 22.7 %copy-start.111 = (f32[4,288]{1,0:T(4,128)S(1)}, f32[4,288]{1,0:T(4,128)}, u32[]{:S(2)}) copy-start(f32[4,288]{1,0:T(4,128)} %get-tuple-element.72) | copy-start | bytes 13828
  519.9 81.4 %copy-start.98 = (f32[1152]{0:T(1024)}, f32[1152]{0:T(1024)S(1)}, u32[]{:S(2)}) copy-start(f32[1152]{0:T(1024)S(1)} %mul.1206) | copy-start | bytes 13828
  528.9 143.2 %copy-start.13 = (f32[256,1152]{1,0:T(8,128)}, f32[256,1152]{1,0:T(8,128)S(1)}, u32[]{:S(2)}) copy-start(f32[256,1152]{1,0:T(8,128)S(1)} %get-tuple-element.92) | copy-start | bytes 3538948
  528.9 21.9 %copy-start.30 = (bf16[1152,1728]{0,1:T(8,128)(2,1)S(1)}, bf16[1152,1728]{0,1:T(8,128)(2,1)}, u32[]{:S(2)}) copy-start(bf16[1152,1728]{0,1:T(8,128)(2,1)} %copy.159) | copy-start | bytes 11943940
  580.4 20.4 %copy-start.66 = (bf16[2,256,1152]{2,1,0:T(8,128)(2,1)S(1)}, bf16[2,256,1152]{2,1,0:T(8,128)(2,1)}, u32[]{:S(2)}) copy-start(bf16[2,256,1152]{2,1,0:T(8,128)(2,1)} %param.11) | copy-start | bytes 3538948
  580.4 20.4 %copy-start.126 = (f32[256]{0:T(256)S(1)}, f32[256]{0:T(256)}, u32[]{:S(2)}) copy-start(f32[256]{0:T(256)} %compare_convert_fusion) | copy-start | bytes 3076
  600.8 20.3 %copy-start.122 = (f32[256]{0:T(256)}, f32[256]{0:T(256)S(1)}, u32[]{:S(2)}) copy-start(f32[256]{0:T(256)S(1)} %fusion.236) | copy-start | bytes 3076
  755.5 19.5 %copy-start.27 = (f32[256,1152]{1,0:T(8,128)S(1)}, f32[256,1152]{1,0:T(8,128)}, u32[]{:S(2)}) copy-start(f32[256,1152]{1,0:T(8,128)} %copy-done.26) | copy-start | bytes 3538948
  755.5 19.5 %copy-start.101 = (f32[1152]{0:T(1024)S(1)}, f32[1152]{0:T(1024)}, u32[]{:S(2)}) copy-start(f32[1152]{0:T(1024)} %copy-done.100) | copy-start | bytes 13828
  755.5 19.5 %copy-start.131 = (f32[256]{0:T(256)S(1)}, f32[256]{0:T(256)}, u32[]{:S(2)}) copy-start(f32[256]{0:T(256)} %copy-done.130) | copy-start | bytes 3076
  871.6 10.1 collective-permute-start.7
  886.1 146.0 %reduce-scatter.18.cloned.1.call-start = ((), (), s32[]{:S(2)}) async-start(), calls=%async_computation.12 | async-start | bytes 5160960 | tf_op jit(solution)/shard_map/reduce_scatter | solution.py:406
  899.7 6.9 collective-permute-start.9
  915.5 195.3 %reduce-scatter.16.cloned.1.call-start = ((), (), s32[]{:S(2)}) async-start(), calls=%async_computation.11 | async-start | bytes 5160960 | tf_op jit(solution)/shard_map/reduce_scatter | solution.py:406
  929.1 6.9 collective-permute-start.8
  945.0 244.4 %reduce-scatter.20.cloned.1.call-start = ((), (), s32[]{:S(2)}) async-start(), calls=%async_computation.13 | async-start | bytes 5160960
  971.6 7.1 collective-permute-start.11
  987.6 239.7 %reduce-scatter.14.cloned.1.call-start = ((), (), s32[]{:S(2)}) async-start(), calls=%async_computation.8 | async-start | bytes 1945600 | tf_op jit(solution)/shard_map/reduce_scatter | solution.py:435
  989.6 4.5 collective-permute-start.5
  993.9 119.2 %collective-permute-start.6 = (f32[256,1152]{1,0:T(8,128)}, f32[256,1152]{1,0:T(8,128)}, u32[]{:S(2)}, u32[]{:S(2)}) collective-permute-start(f32[256,1152]{1,0:T(8,128)} %get-tuple-element.81), channel_id=1, source_target_pairs={{0,16},{16,0},{1,17},{17,1},{2,18},{18,2},{3,19},{19,3},{4,20},{20... | collective-permute-start | bytes 3538952 | tf_op jit(solution)/shard_map/ppermute | solution.py:318
  995.1 118.0 %copy-start.34 = (f32[256,1152]{1,0:T(8,128)S(1)}, f32[256,1152]{1,0:T(8,128)}, u32[]{:S(2)}) copy-start(f32[256,1152]{1,0:T(8,128)} %get-tuple-element.85) | copy-start | bytes 3538948
  1113.1 82.3 %collective-permute-start.10 = (bf16[288,1728]{1,0:T(8,128)(2,1)}, bf16[288,1728]{1,0:T(8,128)(2,1)}, u32[]{:S(2)}, u32[]{:S(2)}) collective-permute-start(bf16[288,1728]{1,0:T(8,128)(2,1)} %broadcast_select_fusion.23), channel_id=1, source_target_pairs={{0,16},{16,0},{1,17},{17,1},{2,18},{18,2},{3,19},{19,3},{4,20},{20... | collective-permute-start | bytes 2985992 | tf_op jit(solution)/shard_map/ppermute | solution.py:318
  1197.4 45.2 %copy-start.1 = (bf16[1,288,512]{2,1,0:T(8,128)(2,1)S(1)}, bf16[1,288,512]{2,1,0:T(8,128)(2,1)}, u32[]{:S(2)}) copy-start(bf16[1,288,512]{2,1,0:T(8,128)(2,1)} %param.16) | copy-start | bytes 884740
  (132 other events, 577.9 us)
Sparse Core Ops, SparseCore 0:
  11.6 39.5 all-gather.13
  53.0 68.4 all-gather.15
  123.1 79.6 all-gather.9
  204.8 78.2 all-gather.7
  285.0 78.2 all-gather.11
  886.2 67.1 reduce-scatter.21
  956.4 75.6 reduce-scatter.17
  1034.5 76.2 reduce-scatter.15
  1113.1 76.1 reduce-scatter.19
  1191.6 35.6 reduce-scatter.13

commit v2 on v1

--- a/solution.py
+++ b/solution.py
@@ -138,17 +138,19 @@
     copies[5].start()
     for copy in copies[2:]:
         copy.wait_recv()
-    o_ref[first, :] = p_ref[me, first, :].astype(F32) + land[2].astype(F32) + land[4].astype(F32)
-    o_ref[second, :] = p_ref[me, second, :].astype(F32) + land[3].astype(F32) + land[5].astype(F32)
+    one = p_ref[me, first, :].astype(F32) + land[2].astype(F32) + land[4].astype(F32)
+    two = p_ref[me, second, :].astype(F32) + land[3].astype(F32) + land[5].astype(F32)
+    o_ref[first, :] = one.astype(o_ref.dtype)
+    o_ref[second, :] = two.astype(o_ref.dtype)
     for copy in copies:
         copy.wait_send()
 
 
-def reduce_rows(parts, collective_id):
+def reduce_rows(parts, collective_id, dtype=F32):
     count, width = parts.shape[0] // 4, parts.shape[1]
     return pl.pallas_call(
         reduce_kernel,
-        out_shape=jax.ShapeDtypeStruct((count, width), F32),
+        out_shape=jax.ShapeDtypeStruct((count, width), dtype),
         in_specs=[pl.BlockSpec(memory_space=pltpu.VMEM)],
         out_specs=pl.BlockSpec(memory_space=pltpu.VMEM),
         scratch_shapes=[
@@ -270,34 +272,613 @@
     return dh + dx, (dg0, dg1, d_head, d_w_q, d_w_ot, d_w_kv)
 
 
+GELU_SCALE = 0.7978845608028654
+GELU_CUBE = 0.044715
+
+
+def vmem_spec():
+    return pl.BlockSpec(memory_space=pltpu.VMEM)
+
+
+def any_spec():
+    return pl.BlockSpec(memory_space=pl.ANY)
+
+
+def rows_of(block, count):
+    return pl.ds(pl.multiple_of(block * count, count), count)
+
+
+def columns_of(tile, width, offset=0):
+    return pl.ds(pl.multiple_of(tile * width + offset, 128), width)
+
+
+def inverse_rms(value):
+    return lax.rsqrt(jnp.mean(value * value, axis=-1, keepdims=True) + EPSILON)
+
+
+def normed_gradient(value, gain, grad):
+    inverse = inverse_rms(value)
+    unit = value * inverse
+    scaled = grad * gain
+    by_value = inverse * (scaled - unit * jnp.mean(scaled * unit, axis=-1, keepdims=True))
+    return by_value, jnp.sum(grad * unit, axis=0, keepdims=True)
+
+
+class Spread:
+    def __init__(self, rows_ref, count, send, recv):
+        self.me, self.nx, self.ny = neighbours()
+        self.far = jnp.bitwise_xor(self.me, 3)
+        half = count // 2
+
+        def part(block, which):
+            return rows_ref.at[pl.ds(pl.multiple_of(block * count + which * half, half), half)]
+
+        def copy(block, which, at, other):
+            ref = part(block, which)
+            return remote(ref, ref, send.at[at], recv.at[at], other)
+
+        self.to_x1 = copy(self.me, 0, 0, self.nx)
+        self.to_y2 = copy(self.me, 1, 1, self.ny)
+        self.to_x2 = copy(self.me, 1, 2, self.nx)
+        self.to_y1 = copy(self.me, 0, 3, self.ny)
+        self.on_y = copy(self.nx, 0, 4, self.ny)
+        self.on_x = copy(self.ny, 1, 5, self.nx)
+
+    def start(self):
+        for copy in (self.to_x1, self.to_y2, self.to_x2, self.to_y1):
+            copy.start()
+
+    def pass_on(self):
+        self.to_x1.wait_recv()
+        self.on_y.start()
+        self.to_y2.wait_recv()
+        self.on_x.start()
+
+    def x_here(self):
+        self.to_x2.wait_recv()
+
+    def y_here(self):
+        self.to_y1.wait_recv()
+
+    def far_here(self):
+        self.on_y.wait_recv()
+        self.on_x.wait_recv()
+
+    def finish(self):
+        for copy in (self.to_x1, self.to_y2, self.to_x2, self.to_y1, self.on_y, self.on_x):
+            copy.wait_send()
+
+
+class Fold:
+    def __init__(self, parts_ref, count, land, passing, send, recv):
+        self.me, self.nx, self.ny = neighbours()
+        self.far = jnp.bitwise_xor(self.me, 3)
+        self.parts, self.count, self.land, self.passing = parts_ref, count, land, passing
+        half = count // 2
+
+        def copy(src, at, other):
+            return remote(src, land.at[at], send.at[at], recv.at[at], other)
+
+        self.far_x = copy(self.part(self.far, 0), 0, self.nx)
+        self.far_y = copy(self.part(self.far, 1), 1, self.ny)
+        self.near_x = copy(self.part(self.nx, 0), 2, self.nx)
+        self.near_y = copy(self.part(self.ny, 1), 3, self.ny)
+        self.on_y = copy(passing.at[0], 4, self.ny)
+        self.on_x = copy(passing.at[1], 5, self.nx)
+
+    def part(self, block, which):
+        half = self.count // 2
+        return self.parts.at[pl.ds(pl.multiple_of(block * self.count + which * half, half), half)]
+
+    def send_far(self):
+        self.far_x.start()
+        self.far_y.start()
+
+    def send_near(self):
+        self.near_x.start()
+        self.near_y.start()
+
+    def pass_on(self):
+        self.far_x.wait_recv()
+        self.passing[0] = (self.part(self.ny, 0)[...].astype(F32) + self.land[0].astype(F32)).astype(BF16)
+        self.on_y.start()
+        self.far_y.wait_recv()
+        self.passing[1] = (self.part(self.nx, 1)[...].astype(F32) + self.land[1].astype(F32)).astype(BF16)
+        self.on_x.start()
+
+    def total(self, own):
+        half = self.count // 2
+        for copy in (self.near_x, self.near_y, self.on_y, self.on_x):
+            copy.wait_recv()
+        first = own[:half] + (self.land[2].astype(F32) + self.land[4].astype(F32))
+        second = own[half:] + (self.land[3].astype(F32) + self.land[5].astype(F32))
+        return jnp.concatenate([first, second], axis=0)
+
+    def finish(self):
+        for copy in (self.far_x, self.far_y, self.near_x, self.near_y, self.on_y, self.on_x):
+            copy.wait_send()
+
+
+def greet(*others):
+    barrier = pltpu.get_barrier_semaphore()
+    for other in others:
+        pl.semaphore_signal(barrier, inc=1, device_id=other, device_id_type=MESH)
+    return lambda: pl.semaphore_wait(barrier, len(others))
+
+
+def spread_spec():
+    return [pltpu.SemaphoreType.DMA((6,)), pltpu.SemaphoreType.DMA((6,))]
+
+
+def fold_spec(count, width):
+    return [
+        pltpu.VMEM((6, count // 2, width), BF16),
+        pltpu.VMEM((2, count // 2, width), BF16),
+        pltpu.SemaphoreType.DMA((6,)),
+        pltpu.SemaphoreType.DMA((6,)),
+    ]
+
+
+def params(collective_id, mib):
+    return pltpu.CompilerParams(
+        collective_id=collective_id, has_side_effects=True, vmem_limit_bytes=mib * MIB
+    )
+
+
+TILE = 256
+
+
+def up_kernel(
+    h_ref, gain_ref, w_ref, rows_out, gu_out, act_out, rows, w, gu, act, load, store, send, recv
+):
+    count = h_ref.shape[0]
+    hidden = act.shape[1]
+    weights = pltpu.make_async_copy(w_ref, w, load)
+    weights.start()
+    me, nx, ny = neighbours()
+    met = greet({"narrow": nx}, {"narrow": ny})
+    value = h_ref[...]
+    rows[rows_of(me, count), :] = (value * inverse_rms(value) * gain_ref[...]).astype(BF16)
+    spread = Spread(rows, count, send, recv)
+    met()
+    spread.start()
+    weights.wait()
+
+    def one(block, at):
+        here = rows_of(block, count)
+
+        def tile(j, _):
+            left = rows[here, :]
+            gate = nn(left, w[:, columns_of(j, TILE)])
+            up = nn(left, w[:, columns_of(j, TILE, hidden)])
+            inner = jnp.tanh(GELU_SCALE * (gate + GELU_CUBE * (gate * gate * gate)))
+            gu[here, columns_of(j, TILE)] = gate.astype(BF16)
+            gu[here, columns_of(j, TILE, hidden)] = up.astype(BF16)
+            act[here, columns_of(j, TILE)] = (0.5 * gate * (1.0 + inner) * up).astype(BF16)
+            return 0
+
+        lax.fori_loop(0, hidden // TILE, tile, 0)
+        copies = [
+            pltpu.make_async_copy(ref.at[here], out.at[here], store.at[k, at])
+            for k, (ref, out) in enumerate(((gu, gu_out), (act, act_out), (rows, rows_out)))
+        ]
+        for copy in copies:
+            copy.start()
+        return copies
+
+    copies = one(me, 0)
+    spread.pass_on()
+    spread.x_here()
+    copies += one(nx, 1)
+    spread.y_here()
+    copies += one(ny, 2)
+    spread.far_here()
+    copies += one(spread.far, 3)
+    spread.finish()
+    for copy in copies:
+        copy.wait()
+
+
+def feed_up(h, gain, w_gu, collective_id):
+    count, model = h.shape
+    hidden = w_gu.shape[1] // 2
+    total = 4 * count
+    shapes = [(total, model), (total, 2 * hidden), (total, hidden)]
+    return pl.pallas_call(
+        up_kernel,
+        out_shape=[jax.ShapeDtypeStruct(shape, BF16) for shape in shapes],
+        in_specs=[vmem_spec(), vmem_spec(), any_spec()],
+        out_specs=[any_spec()] * 3,
+        scratch_shapes=[
+            pltpu.VMEM((total, model), BF16),
+            pltpu.VMEM(w_gu.shape, BF16),
+            pltpu.VMEM((total, 2 * hidden), BF16),
+            pltpu.VMEM((total, hidden), BF16),
+            pltpu.SemaphoreType.DMA,
+            pltpu.SemaphoreType.DMA((3, 4)),
+            *spread_spec(),
+        ],
+        compiler_params=params(collective_id, 48),
+    )(h, gain, w_gu)
+
+
+def down_kernel(
+    h_ref, gain_ref, act_ref, w_ref, x_out, f_out, act, w, parts, load, land, passing, send, recv
+):
+    count, model = h_ref.shape
+    me, nx, ny = neighbours()
+    met = greet({"narrow": nx}, {"narrow": ny})
+    far = jnp.bitwise_xor(me, 3)
+    weights = pltpu.make_async_copy(w_ref, w, load.at[0])
+    weights.start()
+    arrivals = []
+    for at, block in enumerate((far, nx, ny, me)):
+        here = rows_of(block, count)
+        arrivals.append(pltpu.make_async_copy(act_ref.at[here], act.at[here], load.at[1 + at]))
+        arrivals[-1].start()
+    fold = Fold(parts, count, land, passing, send, recv)
+    weights.wait()
+    met()
+
+    def one(block, at):
+        arrivals[at].wait()
+        return nt(act[rows_of(block, count), :], w[...])
+
+    parts[rows_of(far, count), :] = one(far, 0).astype(BF16)
+    fold.send_far()
+    parts[rows_of(nx, count), :] = one(nx, 1).astype(BF16)
+    parts[rows_of(ny, count), :] = one(ny, 2).astype(BF16)
+    fold.send_near()
+    f_out[...] = one(me, 3)
+    fold.pass_on()
+    total = fold.total(f_out[...])
+    f_out[...] = total
+    x_out[...] = (h_ref[...] + total * inverse_rms(total) * gain_ref[...]).astype(BF16)
+    fold.finish()
+
+
+def feed_down(h, gain, act, w_dt, collective_id):
+    count, model = h.shape
+    return pl.pallas_call(
+        down_kernel,
+        out_shape=[
+            jax.ShapeDtypeStruct((count, model), BF16),
+            jax.ShapeDtypeStruct((count, model), F32),
+        ],
+        in_specs=[vmem_spec(), vmem_spec(), any_spec(), any_spec()],
+        out_specs=[vmem_spec(), vmem_spec()],
+        scratch_shapes=[
+            pltpu.VMEM(act.shape, BF16),
+            pltpu.VMEM(w_dt.shape, BF16),
+            pltpu.VMEM((4 * count, model), BF16),
+            pltpu.SemaphoreType.DMA((5,)),
+            *fold_spec(count, model),
+        ],
+        compiler_params=params(collective_id, 40),
+    )(h, gain, act, w_dt)
+
+
+def swap_sum(make, tiles, ours, theirs, came, send, recv, out, out_sems):
+    other = {"section": 1 - lax.axis_index("section")}
+    sends = []
+    for at, (first, width) in enumerate(tiles):
+        columns = pl.ds(first, width)
+        theirs[:, columns] = make(False, first, width).astype(BF16)
+        copy = pltpu.make_async_remote_copy(
+            src_ref=theirs.at[:, columns],
+            dst_ref=came.at[:, columns],
+            send_sem=send.at[at],
+            recv_sem=recv.at[at],
+            device_id=other,
+            device_id_type=MESH,
+        )
+        copy.start()
+        sends.append(copy)
+    stores = []
+    for at, (first, width) in enumerate(tiles):
+        columns = pl.ds(first, width)
+        own = make(True, first, width)
+        sends[at].wait_recv()
+        ours[:, columns] = (own + came[:, columns].astype(F32)).astype(BF16)
+        copy = pltpu.make_async_copy(ours.at[:, columns], out.at[:, columns], out_sems.at[at])
+        copy.start()
+        stores.append(copy)
+    return sends, stores
+
+
+def column_tiles(width):
+    return [(first, min(TILE, width - first)) for first in range(0, width, TILE)]
+
+
+def back_up_kernel(
+    dy_ref, f_ref, gain_ref, gu_ref, act_ref, w_ref, dgu_out, dw_out, dgain_out,
+    df, gu, act, w, ours, theirs, came, load, store, send, recv, swap_send, swap_recv, out_sems,
+):
+    count, model = dy_ref.shape
+    hidden = act.shape[1]
+    me, nx, ny = neighbours()
+    core = lax.axis_index("section")
+    met = greet({"narrow": nx}, {"narrow": ny}, {"section": 1 - core})
+    far = jnp.bitwise_xor(me, 3)
+    weights = pltpu.make_async_copy(w_ref, w, load.at[0, 0])
+    weights.start()
+    arrivals = []
+    for at, block in enumerate((me, nx, ny, far)):
+        here = rows_of(block, count)
+        pair = [
+            pltpu.make_async_copy(gu_ref.at[here], gu.at[here], load.at[1, at]),
+            pltpu.make_async_copy(act_ref.at[here], act.at[here], load.at[2, at]),
+        ]
+        for copy in pair:
+            copy.start()
+        arrivals.append(pair)
+    by_value, by_gain = normed_gradient(f_ref[...], gain_ref[...], dy_ref[...])
+    df[rows_of(me, count), :] = by_value.astype(BF16)
+    spread = Spread(df, count, send, recv)
+    met()
+    spread.start()
+    dgain_out[...] = by_gain
+    weights.wait()
+
+    def one(block, at):
+        here = rows_of(block, count)
+        for copy in arrivals[at]:
+            copy.wait()
+
+        def tile(j, _):
+            dact = nn(df[here, :], w[:, columns_of(j, TILE)])
+            gate = gu[here, columns_of(j, TILE)].astype(F32)
+            up = gu[here, columns_of(j, TILE, hidden)].astype(F32)
+            square = gate * gate
+            inner = jnp.tanh(GELU_SCALE * gate * (1.0 + GELU_CUBE * square))
+            half = 0.5 * (1.0 + inner)
+            slope = half + 0.5 * GELU_SCALE * gate * (1.0 - inner * inner) * (
+                1.0 + 3.0 * GELU_CUBE * square
+            )
+            gu[here, columns_of(j, TILE)] = (dact * up * slope).astype(BF16)
+            gu[here, columns_of(j, TILE, hidden)] = (dact * gate * half).astype(BF16)
+            return 0
+
+        lax.fori_loop(0, hidden // TILE, tile, 0)
+        copy = pltpu.make_async_copy(gu.at[here], dgu_out.at[here], store.at[at])
+        copy.start()
+        return copy
+
+    copies = [one(me, 0)]
+    spread.pass_on()
+    spread.x_here()
+    copies.append(one(nx, 1))
+    spread.y_here()
+    copies.append(one(ny, 2))
+    spread.far_here()
+    copies.append(one(far, 3))
+
+    def make(mine, first, width):
+        side = core if mine else 1 - core
+        start = pl.multiple_of(side * (hidden // 2) + first, 128)
+        return tn(df[...], act[:, pl.ds(start, width)])
+
+    sends, stores = swap_sum(
+        make, column_tiles(hidden // 2), ours, theirs, came, swap_send, swap_recv, dw_out, out_sems
+    )
+    spread.finish()
+    for copy in sends:
+        copy.wait_send()
+    for copy in copies + stores:
+        copy.wait()
+
+
+def feed_back_up(dy, f, gain, gu, act, w_dt, collective_id):
+    count, model = dy.shape
+    total, hidden = act.shape
+    tiles = len(column_tiles(hidden // 2))
+    return pl.pallas_call(
+        back_up_kernel,
+        out_shape=[
+            jax.ShapeDtypeStruct(gu.shape, BF16),
+            jax.ShapeDtypeStruct((model, hidden // 2), BF16),
+            jax.ShapeDtypeStruct((1, model), F32),
+        ],
+        in_specs=[vmem_spec()] * 3 + [any_spec()] * 3,
+        out_specs=[any_spec(), any_spec(), vmem_spec()],
+        scratch_shapes=[
+            pltpu.VMEM((total, model), BF16),
+            pltpu.VMEM(gu.shape, BF16),
+            pltpu.VMEM(act.shape, BF16),
+            pltpu.VMEM(w_dt.shape, BF16),
+            pltpu.VMEM((model, hidden // 2), BF16),
+            pltpu.VMEM((model, hidden // 2), BF16),
+            pltpu.VMEM((model, hidden // 2), BF16),
+            pltpu.SemaphoreType.DMA((3, 4)),
+            pltpu.SemaphoreType.DMA((4,)),
+            *spread_spec(),
+            pltpu.SemaphoreType.DMA((tiles,)),
+            pltpu.SemaphoreType.DMA((tiles,)),
+            pltpu.SemaphoreType.DMA((tiles,)),
+        ],
+        compiler_params=params(collective_id, 48),
+    )(dy, f, gain, gu, act, w_dt)
+
+
+def back_down_kernel(
+    dy_ref, h_ref, gain_ref, dgu_ref, rows_ref, w_ref, dh_out, dw_out, dgain_out,
+    dgu, rows, w, parts, ours, theirs, came, load, land, passing, send, recv, swap_send, swap_recv, out_sems,
+):
+    count, model = dy_ref.shape
+    hidden = dgu.shape[1] // 2
+    me, nx, ny = neighbours()
+    core = lax.axis_index("section")
+    met = greet({"narrow": nx}, {"narrow": ny}, {"section": 1 - core})
+    far = jnp.bitwise_xor(me, 3)
+    weights = pltpu.make_async_copy(w_ref, w, load.at[0])
+    weights.start()
+    arrivals = []
+    for at, block in enumerate((far, nx, ny, me)):
+        here = rows_of(block, count)
+        arrivals.append(pltpu.make_async_copy(dgu_ref.at[here], dgu.at[here], load.at[1 + at]))
+        arrivals[-1].start()
+    kept = pltpu.make_async_copy(rows_ref, rows, load.at[5])
+    kept.start()
+    fold = Fold(parts, count, land, passing, send, recv)
+    weights.wait()
+    met()
+    step = model // 3
+
+    def one(block, at, out, here):
+        arrivals[at].wait()
+
+        def tile(j, _):
+            part = nt(dgu[rows_of(block, count), :], w[pl.ds(pl.multiple_of(j * step, step), step), :])
+            out[here, columns_of(j, step)] = part.astype(out.dtype)
+            return 0
+
+        lax.fori_loop(0, 3, tile, 0)
+
+    one(far, 0, parts, rows_of(far, count))
+    fold.send_far()
+    one(nx, 1, parts, rows_of(nx, count))
+    one(ny, 2, parts, rows_of(ny, count))
+    fold.send_near()
+    one(me, 3, dh_out, pl.ds(0, count))
+    fold.pass_on()
+    kept.wait()
+
+    def make(mine, first, width):
+        side = core if mine else 1 - core
+        start = pl.multiple_of(side * hidden + first, 128)
+        return tn(rows[...], dgu[:, pl.ds(start, width)])
+
+    sends, stores = swap_sum(
+        make, column_tiles(hidden), ours, theirs, came, swap_send, swap_recv, dw_out, out_sems
+    )
+    total = fold.total(dh_out[...])
+    by_value, by_gain = normed_gradient(h_ref[...], gain_ref[...], total)
+    dh_out[...] = dy_ref[...] + by_value
+    dgain_out[...] = by_gain
+    fold.finish()
+    for copy in sends:
+        copy.wait_send()
+    for copy in stores:
+        copy.wait()
+
+
+def feed_back_down(dy, h, gain, dgu, rows, w_gu, collective_id):
+    count, model = dy.shape
+    total, hidden = dgu.shape[0], dgu.shape[1] // 2
+    tiles = len(column_tiles(hidden))
+    return pl.pallas_call(
+        back_down_kernel,
+        out_shape=[
+            jax.ShapeDtypeStruct((count, model), F32),
+            jax.ShapeDtypeStruct((model, hidden), BF16),
+            jax.ShapeDtypeStruct((1, model), F32),
+        ],
+        in_specs=[vmem_spec()] * 3 + [any_spec()] * 3,
+        out_specs=[vmem_spec(), any_spec(), vmem_spec()],
+        scratch_shapes=[
+            pltpu.VMEM(dgu.shape, BF16),
+            pltpu.VMEM(rows.shape, BF16),
+            pltpu.VMEM(w_gu.shape, BF16),
+            pltpu.VMEM((total, model), BF16),
+            pltpu.VMEM((model, hidden), BF16),
+            pltpu.VMEM((model, hidden), BF16),
+            pltpu.VMEM((model, hidden), BF16),
+            pltpu.SemaphoreType.DMA((6,)),
+            *fold_spec(count, model),
+            pltpu.SemaphoreType.DMA((tiles,)),
+            pltpu.SemaphoreType.DMA((tiles,)),
+            pltpu.SemaphoreType.DMA((tiles,)),
+        ],
+        compiler_params=params(collective_id, 56),
+    )(dy, h, gain, dgu, rows, w_gu)
+
+
+def pack_kernel(p_ref, o_ref, local, send, recv, peer_send, peer_recv):
+    count = p_ref.shape[0]
+    core = lax.axis_index("section")
+    me, nx, ny = neighbours()
+    met = greet({"narrow": nx}, {"narrow": ny}, {"section": 1 - core})
+    side = o_ref.at[core]
+    own = pltpu.make_async_copy(p_ref, side.at[rows_of(me, count)], local)
+    own.start()
+    spread = Spread(side, count, send, recv)
+    own.wait()
+    met()
+    spread.start()
+    copies = []
+
+    def across(block, at):
+        ref = side.at[rows_of(block, count)]
+        copy = pltpu.make_async_remote_copy(
+            src_ref=ref,
+            dst_ref=ref,
+            send_sem=peer_send.at[at],
+            recv_sem=peer_recv.at[at],
+            device_id={"section": 1 - core},
+            device_id_type=MESH,
+        )
+        copy.start()
+        copies.append(copy)
+
+    across(me, 0)
+    spread.pass_on()
+    spread.x_here()
+    across(nx, 1)
+    spread.y_here()
+    across(ny, 2)
+    spread.far_here()
+    across(spread.far, 3)
+    for copy in copies:
+        copy.wait_recv()
+    spread.finish()
+    for copy in copies:
+        copy.wait_send()
+
+
+def gather_pack(pack, collective_id):
+    count, width = pack.shape
+    return pl.pallas_call(
+        pack_kernel,
+        out_shape=jax.ShapeDtypeStruct((2, 4 * count, width), pack.dtype),
+        in_specs=[vmem_spec()],
+        out_specs=vmem_spec(),
+        scratch_shapes=[
+            pltpu.SemaphoreType.DMA,
+            *spread_spec(),
+            pltpu.SemaphoreType.DMA((4,)),
+            pltpu.SemaphoreType.DMA((4,)),
+        ],
+        compiler_params=params(collective_id, 24),
+    )(pack)
+
+
+def after(value, *others):
+    return pl.pallas_call(
+        lambda *refs: None,
+        out_shape=jax.ShapeDtypeStruct(value.shape, value.dtype),
+        in_specs=[any_spec()] * (1 + len(others)),
+        out_specs=any_spec(),
+        input_output_aliases={0: 0},
+    )(value, *others)
+
+
 def feed_forward(h, weights):
-    gains, w_gate, w_up, w_dt = weights[0], *weights[5:]
-    hn = normed(h, gains[2]).astype(BF16)
-    rows = gather_rows(hn, 2)
-    gate = nn(rows, w_gate)
-    up = nn(rows, w_up)
-    act = geglu(gate, up).astype(BF16)
-    f = reduce_rows(nt(act, w_dt).astype(BF16), 3)
-    out = h + normed(f, gains[3])
-    return out, (h, rows, gate.astype(BF16), up.astype(BF16), f)
+    gains, w_gu, w_dt = weights[0], *weights[5:]
+    rows, gu, act = feed_up(h, gains[2:3], w_gu, 2)
+    out, f = feed_down(h, gains[3:4], act, w_dt, 3)
+    return out, (h, rows, gu, act, f)
+
+
+def scatter(member):
+    return lax.psum_scatter(member, "wide", scatter_dimension=0, tiled=True)
 
 
 def feed_backward(dy, weights, kept):
-    gains, w_gate, w_up, w_dt = weights[0], *weights[5:]
-    h, rows, gate, up, f = kept
-    _, pull = jax.vjp(normed, f, gains[3])
-    df, dg3 = pull(dy)
-    df_rows = gather_rows(df.astype(BF16), 2)
-    act, pull = jax.vjp(geglu, gate.astype(F32), up.astype(F32))
-    d_w_dt = tn(df_rows, act.astype(BF16)).astype(BF16)
-    dgate, dup = pull(nn(df_rows, w_dt))
-    dgate, dup = dgate.astype(BF16), dup.astype(BF16)
-    dhn = reduce_rows((nt(dgate, w_gate) + nt(dup, w_up)).astype(BF16), 3)
-    d_w_gate = tn(rows, dgate).astype(BF16)
-    d_w_up = tn(rows, dup).astype(BF16)
-    _, pull = jax.vjp(normed, h, gains[2])
-    dh, dg2 = pull(dhn)
-    return dy + dh, (dg2, dg3, d_w_gate, d_w_up, d_w_dt)
+    gains, w_gu, w_dt = weights[0], *weights[5:]
+    h, rows, gu, act, f = kept
+    dgu, d_w_dt, dg3 = feed_back_up(dy, f, gains[3:4], gu, act, w_dt, 4)
+    dh, d_w_gu, dg2 = feed_back_down(dy, h, gains[2:3], dgu, rows, w_gu, 5)
+    return dh, (dg2[0], dg3[0], scatter(d_w_gu), scatter(d_w_dt))
 
 
 def on_device(
@@ -320,23 +901,38 @@
     def by_core(first, second):
         return jnp.where(is_zero, first, second)
 
+    half = block // 2
+
+    def by_halves(member):
+        keep = lax.dynamic_slice_in_dim(member, core * half, half, 0)
+        give = lax.dynamic_slice_in_dim(member, (1 - core) * half, half, 0)
+        came = swap(give)
+        return by_core(keep, came), by_core(came, keep)
+
+    pad = -hidden % TILE
     kv_own = lax.dynamic_slice_in_dim(w_kv[0], narrow * kv_part, kv_part, 1)
     pack_width = 2 * head_width + kv_part
-    pack = jnp.concatenate([w_q[0], w_o[0].T, kv_own], axis=1)
     gain_rows = jnp.zeros((GAIN_ROWS, pack_width), BF16)
     gain_rows = lax.dynamic_update_slice(gain_rows, norm_gains[0], (0, 0))
     gain_rows = lax.dynamic_update_slice(gain_rows, head_gains[0], (4, 0))
-    pack = jnp.concatenate([pack, gain_rows], axis=0)
-    pack = lax.all_gather(pack, "wide", axis=0)
-    pack = lax.all_gather(pack, "narrow", axis=0)
-    pack_peer = swap(pack)
-
-    def unpack(whole):
-        body = whole[:, :, :block]
-        tail = whole[0, :, block:]
+    gains_came = swap(gain_rows)
+    gain_rows = (by_core(gain_rows, gains_came), by_core(gains_came, gain_rows))
+    pack = by_halves(jnp.concatenate([w_q[0], w_o[0].T, kv_own], axis=1))
+    pack = jnp.concatenate([pack[0], gain_rows[0], pack[1], gain_rows[1]], axis=0)
+    pack = lax.all_gather(pack, "wide", axis=0).reshape(n_wide, 2, half + GAIN_ROWS, pack_width)
+
+    gate_up = jnp.pad(w_gate_up[0], ((0, 0), (0, 0), (0, pad))).reshape(block, -1)
+    gate_up = [lax.all_gather(m, ("wide", "section"), axis=0, tiled=True) for m in by_halves(gate_up)]
+    down = jnp.pad(w_down[0].T, ((0, 0), (0, pad)))
+    down = [lax.all_gather(m, ("wide", "section"), axis=0, tiled=True) for m in by_halves(down)]
+
+    def unpack(section):
+        whole = gather_pack(pack[:, section].reshape(-1, pack_width), 6)
+        whole = whole.reshape(2, n_narrow, n_wide, half + GAIN_ROWS, pack_width)
+        body, tail = whole[:, :, :, :half], whole[0, 0, :, half:]
 
         def columns(first, last):
-            return body[..., first:last].transpose(1, 2, 0, 3).reshape(model, -1)
+            return body[..., first:last].transpose(2, 0, 3, 1, 4).reshape(model, -1)
 
         norm_part = tail[:, :4, :block].transpose(1, 0, 2).reshape(4, model).astype(F32)
         head_part = tail[:, 4:6, : head_width // n_wide].transpose(1, 0, 2).reshape(2, head_width)
@@ -348,30 +944,7 @@
             columns(2 * head_width, pack_width),
         )
 
-    attention_own, attention_peer = unpack(pack), unpack(pack_peer)
-
-    w_gate, w_up = w_gate_up[0, :, 0], w_gate_up[0, :, 1]
-    came = swap(by_core(w_up, w_gate))
-    stays = by_core(w_gate, w_up)
-    role = [by_core(stays, came), by_core(came, stays)]
-    role = [lax.all_gather(member, "wide", axis=0, tiled=True) for member in role]
-    role_peer = [swap(member) for member in role]
-    down_own = lax.all_gather(w_down[0].T, "wide", axis=0, tiled=True)
-    down_peer = swap(down_own)
-    layers = []
-    for section in range(2):
-        mine = is_zero if section == 0 else jnp.logical_not(is_zero)
-        attention = jax.tree.map(
-            lambda own, peer: jnp.where(mine, own, peer), attention_own, attention_peer
-        )
-        layers.append(
-            (
-                *attention,
-                by_core(role[section], role_peer[section]),
-                by_core(role_peer[section], role[section]),
-                jnp.where(mine, down_own, down_peer),
-            )
-        )
+    layers = [(*unpack(section), gate_up[section], down[section]) for section in range(2)]
 
     start = narrow * rows
     positions = start + jnp.arange(rows, dtype=jnp.int32)
@@ -391,7 +964,11 @@
     dy = lax.dynamic_index_in_dim(cotangent, core, 0, keepdims=False).astype(F32) * real
     dxs, grads = [None, None], [None, None]
     for section in (1, 0):
+        if section == 0:
+            dy = after(dy, grads[1][1][3])
         dh, grads_f = feed_backward(dy, layers[section], kept[section][1])
+        if section == 0:
+            dh = after(dh, grads[1][1][2])
         dx, grads_a = attention_backward(
             dh, length, layers[section], kept[section][0], start, trig
         )
@@ -399,19 +976,16 @@
         grads[section] = (grads_a, grads_f)
         dy = dx.astype(BF16).astype(F32)
 
-    role_sums = [None, None]
-    for section in (1, 0):
-        d_gate, d_up = grads[section][1][2:4]
-        total = by_core(d_gate, d_up) + swap(by_core(d_up, d_gate))
-        role_sums[section] = lax.psum_scatter(total, "wide", scatter_dimension=0, tiled=True)
-    came = swap(by_core(role_sums[1], role_sums[0]))
-    stays = by_core(role_sums[0], role_sums[1])
-    grad_gate_up = jnp.stack([by_core(stays, came), by_core(came, stays)], axis=1).astype(F32)
-
-    d_downs = [grads[section][1][4] for section in range(2)]
-    down_sum = by_core(*d_downs) + swap(by_core(*d_downs[::-1]))
-    down_sum = lax.psum_scatter(down_sum, "wide", scatter_dimension=0, tiled=True)
-    grad_down = down_sum.T.astype(F32)
+    sums = [[grads[section][1][k] for k in (2, 3)] for section in range(2)]
+
+    def own_section(k):
+        first, second = sums[0][k], sums[1][k]
+        came = swap(by_core(second, first))
+        stays = by_core(first, second)
+        return by_core(stays, came).astype(F32), by_core(came, stays).astype(F32)
+
+    grad_gate_up = jnp.stack(own_section(0), axis=1)[:, :, :hidden]
+    grad_down = jnp.concatenate(own_section(1), axis=1)[:, :hidden].T
 
     packs = []
     for section in range(2):
@@ -431,8 +1005,9 @@
         tail = jnp.broadcast_to(tail[None], (n_narrow, *tail.shape))
         packs.append(jnp.concatenate([body, tail], axis=2))
     pack_sum = by_core(*packs) + swap(by_core(*packs[::-1]))
-    pack_sum = lax.psum_scatter(pack_sum, "narrow", scatter_dimension=0, tiled=False)
-    pack_sum = lax.psum_scatter(pack_sum, "wide", scatter_dimension=0, tiled=False)
+    pack_sum = after(pack_sum, grads[0][1][3])
+    pack_sum = reduce_rows(pack_sum.reshape(-1, pack_width), 7, BF16)
+    pack_sum = scatter(pack_sum)
     grad_q = pack_sum[:block, :head_width].astype(F32)
     grad_o = pack_sum[:block, head_width : 2 * head_width].T.astype(F32)
     grad_kv = lax.all_gather(

time: 1260 us -> 780 us (0.62)
  waiting for transfers between devices: 571 us -> 63.3 us
  Pallas kernels: 202 us -> 427 us
  matrix products: 210 us -> 40.6 us
  other arithmetic: 75.9 us -> 57.3 us
    pallas_call x0 -> x13, Pallas kernels: none -> 330 us  [the longest x2 84.6 us: feed_back_down(): pl.pallas_call(back_down_kernel, out_shape=[jax.ShapeDtypeStruct((count,...]
    all_gather x5, waiting for transfers between devices: 326 us -> 32 us  [the longest x1 28.4 us: on_device(): lax.all_gather(pack, 'wide', axis=0)]
    dot_general x36 -> x18, matrix products: 198 us -> 26.7 us  [dot(): lax.dot_general(a, b, ((dims[0], dims[1]), ((), ())), preferred_element_t...]
    reduce_scatter x3 -> x5, waiting for transfers between devices: 138 us -> 18.3 us  [scatter(): return lax.psum_scatter(member, 'wide', scatter_dimension=0, tiled=True)]
    pallas_call x6 -> x2, Pallas kernels: 103 us -> 21.8 us  [gather_rows(): pl.pallas_call(gather_kernel, out_shape=jax.ShapeDtypeStruct((4, count, w...]
    unnamed x12 -> x10, waiting for transfers between devices: 74.1 us -> 0.67 us
    unnamed x326 -> x346, local copies, waits for them, and re-layouts: 57.3 us -> 81.3 us
    pallas_call x6 -> x3, Pallas kernels: 99.2 us -> 75.4 us  [reduce_rows(): pl.pallas_call(reduce_kernel, out_shape=jax.ShapeDtypeStruct((count, widt...]
  transfers between devices with their start and end apart: 22 -> 19, of which waited for: 14 -> 6; matrix products, arithmetic and copies ran while one was open for 17% -> 25% of each run, Pallas kernels for 7% -> 47%
where the time goes in v2:
time: 780 us; the launch traced here: 774 us
  Pallas kernels  427 us (55%)
  local copies, waits for them, and re-layouts  155 us (20%)
  waiting for transfers between devices  63.3 us (8%)
  other arithmetic  57.3 us (7%)
  matrix products  40.6 us (5%)
  between operations  16.8 us (2%)
  blocking collectives  9.09 us (1%)
    pallas_call x2, Pallas kernels, feed_back_down(): pl.pallas_call(back_down_kernel, out_shape=[jax.ShapeDtypeStruct((count,...  84.6 us
    unnamed x346, local copies, waits for them, and re-layouts  81.3 us
    pallas_call x2, Pallas kernels, feed_back_up(): pl.pallas_call(back_up_kernel, out_shape=[jax.ShapeDtypeStruct(gu.shape,...  75.5 us
    pallas_call x3, Pallas kernels, reduce_rows(): pl.pallas_call(reduce_kernel, out_shape=jax.ShapeDtypeStruct((count, widt...  75.4 us
    pallas_call x2, Pallas kernels, gather_pack(): pl.pallas_call(pack_kernel, out_shape=jax.ShapeDtypeStruct((2, 4 * count,...  63.3 us
    pallas_call x2, Pallas kernels, feed_up(): pl.pallas_call(up_kernel, out_shape=[jax.ShapeDtypeStruct(shape, BF16) fo...  58.6 us
    pallas_call x2, Pallas kernels, feed_down(): pl.pallas_call(down_kernel, out_shape=[jax.ShapeDtypeStruct((count, model...  47.5 us
    reshape x12, local copies, waits for them, and re-layouts, blocks(): member.astype(BF16).reshape(n_wide, block, n_narrow, -1)  32.7 us
  transfers between devices with their start and end apart: 19, of which 6 were waited for; matrix products, arithmetic and copies ran while one was open for 25% of the time, Pallas kernels for 47%

profile of v2, /device:TPU:0, one launch (start us, length us, event | category | flops | bytes accessed | tf_op | source)
XLA Modules:
  0.0 773.5 jit_solution(18379757246996094428)
XLA Ops:
  11.2 3.2 pad.49
  28.2 28.4 %all-gather.15.cloned.1.call-done = bf16[1280,640]{1,0:T(8,128)(2,1)} async-done(((bf16[320,640]{1,0:T(8,128)(2,1)}), bf16[1280,640]{1,0:T(8,128)(2,1)}) %all-gather.15.cloned.1.call-update) | async-done | bytes 1638416 | tf_op jit(solution)/shard_map/all_gather | solution.py:922
  58.2 31.9 %shard_map.169 = bf16[2,2560,640]{2,1,0:T(8,128)(2,1)S(1)} custom-call(bf16[640,640]{1,0:T(8,128)(2,1)S(1)} %bitcast.334), custom_call_target="tpu_custom_call" | custom-call | tf_op jit(solution)/shard_map/pallas_call | solution.py:840
  90.1 2.6 copy-done.3
  99.1 5.1 fusion.179
  104.3 31.5 %shard_map.173 = bf16[2,2560,640]{2,1,0:T(8,128)(2,1)S(1)} custom-call(bf16[640,640]{1,0:T(8,128)(2,1)S(1)} %bitcast.333), custom_call_target="tpu_custom_call" | custom-call | tf_op jit(solution)/shard_map/pallas_call | solution.py:840
  137.0 2.7 fusion.178
  141.3 3.5 copy.117
  146.8 4.3 copy.57
  151.1 2.9 multiply_reduce_fusion.11
  155.7 11.6 %shard_map.170 = bf16[4,256,512]{2,1,0:T(8,128)(2,1)S(1)} custom-call(bf16[256,512]{1,0:T(8,128)(2,1)S(1)} %pad_maximum_fusion.14.a_ref), custom_call_target="tpu_custom_call" | custom-call | tf_op jit(solution)/shard_map/pallas_call | solution.py:100
  171.5 3.3 copy.121
  175.4 3.5 copy.122
  180.9 4.8 copy.68
  186.3 3.5 copy.123
  199.1 30.0 %shard_map.171 = (bf16[1024,1152]{1,0:T(8,128)(2,1)S(1)}, bf16[1024,3584]{1,0:T(8,128)(2,1)}, bf16[1024,1792]{1,0:T(8,128)(2,1)}) custom-call(f32[256,1152]{1,0:T(8,128)S(1)} %fusion.23.h_ref, f32[1,1152]{1,0:T(1,128)S(1)} %slice.235.gain_ref, bf16[1152,3584]{1,0:T(8,128)(2,1)} %all-gather.7.cloned.1.call-done.w_ref), custom_call_target="tpu_custom_call" | custom-call | tf_op jit(solution)/shard_map/pallas_call | solution.py:487
  234.9 22.4 %shard_map.172 = (bf16[256,1152]{1,0:T(8,128)(2,1)S(1)}, f32[256,1152]{1,0:T(8,128)S(1)}) custom-call(f32[256,1152]{1,0:T(8,128)S(1)} %fusion.23.h_ref, f32[1,1152]{1,0:T(1,128)S(1)} %slice.233.gain_ref, bf16[1024,1792]{1,0:T(8,128)(2,1)S(1)} %copy-done.9, bf16[1152,1792]{1,0:T(8,128)(2,1)S(1)} %copy-done.7), custom_call_target="tpu_custom_call" | custom-call | tf_op jit(solution)/shard_map/pallas_call | solution.py:542
  261.0 10.2 %shard_map.174 = bf16[4,256,512]{2,1,0:T(8,128)(2,1)S(1)} custom-call(bf16[256,512]{1,0:T(8,128)(2,1)S(1)} %pad_maximum_fusion.15.a_ref), custom_call_target="tpu_custom_call" | custom-call | tf_op jit(solution)/shard_map/pallas_call | solution.py:100
  280.3 28.5 %shard_map.175 = (bf16[1024,1152]{1,0:T(8,128)(2,1)S(1)}, bf16[1024,3584]{1,0:T(8,128)(2,1)}, bf16[1024,1792]{1,0:T(8,128)(2,1)}) custom-call(f32[256,1152]{1,0:T(8,128)S(1)} %convert_add_fusion.h_ref, f32[1,1152]{1,0:T(1,128)S(1)} %slice.258.gain_ref, bf16[1152,3584]{1,0:T(8,128)(2,1)} %all-gather.11.cloned.1.call-done.w_ref), custom_call_target="tpu_custom_call" | custom-call | tf_op jit(solution)/shard_map/pallas_call | solution.py:487
  310.2 3.5 all-gather.13.cloned.1.call-done.w_ref
  318.0 25.1 %shard_map.176 = (bf16[256,1152]{1,0:T(8,128)(2,1)S(1)}, f32[256,1152]{1,0:T(8,128)S(1)}) custom-call(f32[256,1152]{1,0:T(8,128)S(1)} %convert_add_fusion.h_ref, f32[1,1152]{1,0:T(1,128)S(1)} %slice.256.gain_ref, bf16[1024,1792]{1,0:T(8,128)(2,1)S(1)} %copy-done.10, bf16[1152,1792]{1,0:T(8,128)(2,1)S(1)} %copy-done.8), custom_call_target="tpu_custom_call" | custom-call | tf_op jit(solution)/shard_map/pallas_call | solution.py:542
  343.9 37.9 %shard_map.177 = (bf16[1024,3584]{1,0:T(8,128)(2,1)}, bf16[1152,896]{1,0:T(8,128)(2,1)S(1)}, f32[1,1152]{1,0:T(1,128)S(1)}) custom-call(f32[256,1152]{1,0:T(8,128)S(1)} %convert_multiply_fusion.5.dy_ref, f32[256,1152]{1,0:T(8,128)S(1)} %get-tuple-element.35.f_ref, f32[1,1152]{1,0:T(1,128)S(1)} %slice.256.gain_ref, ...), custom_call_target="tpu_custom_call" | custom-call | tf_op jit(solution)/shard_map/pallas_call | solution.py:675
  383.2 42.5 %shard_map.178 = (f32[256,1152]{1,0:T(8,128)}, bf16[1152,1792]{1,0:T(8,128)(2,1)}, f32[1,1152]{1,0:T(1,128)}) custom-call(f32[256,1152]{1,0:T(8,128)} %copy-done.11, f32[256,1152]{1,0:T(8,128)} %copy-done.5, f32[1,1152]{1,0:T(1,128)} %copy-done.24, bf16[1024,3584]{1,0:T(8,128)(2,1)} %get-tuple-element.37.dgu_ref, bf16[1024,1152]{1,0:T(8,128)(2,1)} %copy-done.17, ...), custom_call_target="tpu_custom_call" | custom-call | tf_op jit(solution)/shard_map/pallas_call | solution.py:769
  434.0 3.0 fusion.3
  440.9 2.3 copy.79
  444.6 10.6 %shard_map.179 = f32[256,512]{1,0:T(8,128)S(1)} custom-call(bf16[4,256,512]{2,1,0:T(8,128)(2,1)S(1)} %bitcast.331), custom_call_target="tpu_custom_call" | custom-call | tf_op jit(solution)/shard_map/pallas_call | solution.py:151
  468.1 37.6 %shard_map.181 = (bf16[1024,3584]{1,0:T(8,128)(2,1)}, bf16[1152,896]{1,0:T(8,128)(2,1)}, f32[1,1152]{1,0:T(1,128)S(1)}) custom-call(f32[256,1152]{1,0:T(8,128)S(1)} %copy-done.6, f32[256,1152]{1,0:T(8,128)S(1)} %copy-done.22, f32[1,1152]{1,0:T(1,128)S(1)} %slice.233.gain_ref, bf16[1024,3584]{1,0:T(8,128)(2,1)} %get-tuple-element.42.gu_ref, ...), custom_call_target="tpu_custom_call" | custom-call | tf_op jit(solution)/shard_map/pallas_call | solution.py:675
  508.4 3.2 reshape.612
  511.6 3.6 copy.158
  516.1 3.0 reshape.613
  519.1 3.5 copy.157
  526.2 42.1 %shard_map.182 = (f32[256,1152]{1,0:T(8,128)}, bf16[1152,1792]{1,0:T(8,128)(2,1)}, f32[1,1152]{1,0:T(1,128)}) custom-call(f32[256,1152]{1,0:T(8,128)} %shard_map.180.dy_ref, f32[256,1152]{1,0:T(8,128)} %copy-done.4, f32[1,1152]{1,0:T(1,128)} %copy-done.23, bf16[1024,3584]{1,0:T(8,128)(2,1)} %get-tuple-element.43.dgu_ref, bf16[1024,1152]{1,0:T(8,128)(2,1)} %copy-done.16, ...), custom_call_target="tpu_custom_call" | custom-call | tf_op jit(solution)/shard_map/pallas_call | solution.py:769
  577.4 2.8 fusion
  585.6 9.5 %shard_map.184 = f32[256,512]{1,0:T(8,128)S(1)} custom-call(bf16[4,256,512]{2,1,0:T(8,128)(2,1)S(1)} %bitcast.332), custom_call_target="tpu_custom_call" | custom-call | tf_op jit(solution)/shard_map/pallas_call | solution.py:151
  603.4 3.5 reshape.609
  606.9 2.6 copy.162
  618.0 3.0 reshape.608
  621.0 3.6 copy.159
  624.6 3.0 reshape.607
  630.8 6.2 broadcast_select_fusion
  637.7 8.6 %collective-permute-done.4 = bf16[256,1152]{1,0:T(8,128)(2,1)S(1)} collective-permute-done((bf16[256,1152]{1,0:T(8,128)(2,1)S(1)}, bf16[256,1152]{1,0:T(8,128)(2,1)S(1)}, u32[]{:S(2)}, u32[]{:S(2)}) %collective-permute-start.4) | collective-permute-done | bytes 589856 | tf_op jit(solution)/shard_map/ppermute | solution.py:899
  650.0 4.1 broadcast_select_fusion.5
  654.1 7.5 select_add_fusion.refs_0_
  661.6 2.8 copy-done.2
  664.4 55.3 %shard_map.186 = bf16[1216,640]{1,0:T(8,128)(2,1)} custom-call(bf16[4,1216,640]{2,1,0:T(8,128)(2,1)S(1)} %bitcast.316), custom_call_target="tpu_custom_call" | custom-call | tf_op jit(solution)/shard_map/pallas_call | solution.py:151
  730.0 5.2 copy.95
  735.2 18.2 %reduce-scatter.12.cloned.1.call-done = bf16[304,640]{1,0:T(8,128)(2,1)} async-done(((bf16[1216,640]{1,0:T(8,128)(2,1)}), bf16[304,640]{1,0:T(8,128)(2,1)}) %reduce-scatter.12.cloned.1.call-update) | async-done | bytes 389136 | tf_op jit(solution)/shard_map/reduce_scatter | solution.py:873
  754.4 9.1 %all_gather.27 = bf16[288,512]{1,0:T(8,128)(2,1)S(1)} all-gather(bf16[288,128]{1,0:T(8,128)(2,1)S(1)} %slice.315), channel_id=1, replica_groups=mesh['section'=2,'wide'=4,'narrow'=4] {'narrow'}, dimensions={1}, use_global_device_ids=true | all-gather | bytes 368640 | tf_op jit(solution)/shard_map/all_gather | solution.py:1013
  (575 shorter events, 159.9 us)
Async XLA Ops:
  7.2 49.4 %all-gather.15.cloned.1.call-start = ((), (), s32[]{:S(2)}) async-start(), calls=%async_computation.14 | async-start | bytes 2048000 | tf_op jit(solution)/shard_map/all_gather | solution.py:922
  9.4 5.2 collective-permute-start.1
  11.0 3.6 collective-permute-start
  15.6 183.5 %all-gather.7.cloned.1.call-start = ((), (), s32[]{:S(2)}) async-start(), calls=%async_computation.5 | async-start | bytes 9289728 | tf_op jit(solution)/shard_map/all_gather | solution.py:925
  15.7 2.8 collective-permute-start.2
  20.3 210.3 %all-gather.9.cloned.1.call-start = ((), (), s32[]{:S(2)}) async-start(), calls=%async_computation.6 | async-start | bytes 4644864 | tf_op jit(solution)/shard_map/all_gather | solution.py:927
  20.4 2.0 collective-permute-start.3
  23.5 256.7 %all-gather.11.cloned.1.call-start = ((), (), s32[]{:S(2)}) async-start(), calls=%async_computation.7 | async-start | bytes 9289728 | tf_op jit(solution)/shard_map/all_gather | solution.py:925
  24.1 289.7 %all-gather.13.cloned.1.call-start = ((), (), s32[]{:S(2)}) async-start(), calls=%async_computation.8 | async-start | bytes 4644864 | tf_op jit(solution)/shard_map/all_gather | solution.py:927
  25.0 33.2 %copy-start.146 = (f32[256]{0:T(256)}, f32[256]{0:T(256)S(1)}, u32[]{:S(2)}) copy-start(f32[256]{0:T(256)S(1)} %fusion.53) | copy-start | bytes 3076
  25.0 114.9 %copy-start.158 = (f32[128]{0:T(128)}, f32[128]{0:T(128)S(1)}, u32[]{:S(2)}) copy-start(f32[128]{0:T(128)S(1)} %multiply_power_fusion) | copy-start | bytes 1540
  26.3 124.7 %copy-start.127 = (f32[256]{0:T(256)}, f32[256]{0:T(256)S(1)}, u32[]{:S(2)}) copy-start(f32[256]{0:T(256)S(1)} %fusion.145) | copy-start | bytes 3076
  27.9 316.1 %copy-start.11 = (f32[256,1152]{1,0:T(8,128)}, f32[256,1152]{1,0:T(8,128)S(1)}, u32[]{:S(2)}) copy-start(f32[256,1152]{1,0:T(8,128)S(1)} %convert_multiply_fusion.5.dy_ref) | copy-start | bytes 3538948
  27.9 437.6 %reduce-scatter.6.cloned.1.call-start = ((), (), s32[]{:S(2)}) async-start(), calls=%async_computation.9 | async-start | bytes 2580480 | tf_op jit(solution)/shard_map/reduce_scatter | solution.py:873
  98.9 40.8 %copy-start.84 = (f32[256,512]{1,0:T(8,128)}, f32[256,512]{1,0:T(8,128)S(1)}, u32[]{:S(2)}) copy-start(f32[256,512]{1,0:T(8,128)S(1)} %fusion.69) | copy-start | bytes 1572868
  99.1 40.6 %copy-start.148 = (f32[256]{0:T(256)}, f32[256]{0:T(256)S(1)}, u32[]{:S(2)}) copy-start(f32[256]{0:T(256)S(1)} %multiply_reduce_fusion.17) | copy-start | bytes 3076
  155.0 12.3 %copy-start.54 = (bf16[2,4,4,144,256]{4,3,2,1,0:T(8,128)(2,1)S(1)}, bf16[2,4,4,144,256]{4,3,2,1,0:T(8,128)(2,1)}, u32[]{:S(2)}) copy-start(bf16[2,4,4,144,256]{4,3,2,1,0:T(8,128)(2,1)} %get-tuple-element.93) | copy-start | bytes 7077892
  155.2 37.0 %copy-start.105 = (bf16[256,4,128]{0,2,1:T(8,128)(2,1)}, bf16[256,4,128]{0,2,1:T(8,128)(2,1)S(1)}, u32[]{:S(2)}) copy-start(bf16[256,4,128]{0,2,1:T(8,128)(2,1)S(1)} %get-tuple-element.115) | copy-start | bytes 786436
  155.2 37.0 %copy-start.107 = (bf16[256,4,128]{0,2,1:T(8,128)(2,1)}, bf16[256,4,128]{0,2,1:T(8,128)(2,1)S(1)}, u32[]{:S(2)}) copy-start(bf16[256,4,128]{0,2,1:T(8,128)(2,1)S(1)} %get-tuple-element.116) | copy-start | bytes 786436
  167.3 26.1 %copy-start.12 = (bf16[4,256,512]{2,1,0:T(8,128)(2,1)}, bf16[4,256,512]{2,1,0:T(8,128)(2,1)S(1)}, u32[]{:S(2)}) copy-start(bf16[4,256,512]{2,1,0:T(8,128)(2,1)S(1)} %shard_map.170) | copy-start | bytes 3145732
  171.3 27.8 %copy-start.23 = (f32[1,1152]{1,0:T(1,128)}, f32[1,1152]{1,0:T(1,128)S(1)}, u32[]{:S(2)}) copy-start(f32[1,1152]{1,0:T(1,128)S(1)} %slice.235.gain_ref) | copy-start | bytes 13828
  192.0 88.2 %copy-start.24 = (f32[1,1152]{1,0:T(1,128)}, f32[1,1152]{1,0:T(1,128)S(1)}, u32[]{:S(2)}) copy-start(f32[1,1152]{1,0:T(1,128)S(1)} %slice.258.gain_ref) | copy-start | bytes 13828
  197.8 31.3 %copy-start.150 = (f32[256]{0:T(256)}, f32[256]{0:T(256)S(1)}, u32[]{:S(2)}) copy-start(f32[256]{0:T(256)S(1)} %get-tuple-element.149) | copy-start | bytes 3076
  199.1 31.6 %copy-start.4 = (f32[256,1152]{1,0:T(8,128)}, f32[256,1152]{1,0:T(8,128)S(1)}, u32[]{:S(2)}) copy-start(f32[256,1152]{1,0:T(8,128)S(1)} %fusion.23.h_ref) | copy-start | bytes 3538948
  234.9 23.4 %copy-start.70 = (bf16[2,4,4,144,128]{4,1,3,0,2:T(4,128)(2,1)S(1)}, bf16[2,4,4,144,128]{4,1,3,0,2:T(4,128)(2,1)}, u32[]{:S(2)}) copy-start(bf16[2,4,4,144,128]{4,1,3,0,2:T(4,128)(2,1)} %copy.121) | copy-start | bytes 3538948
  258.3 12.9 %copy-start.119 = (f32[256]{0:T(256)}, f32[256]{0:T(256)S(1)}, u32[]{:S(2)}) copy-start(f32[256]{0:T(256)S(1)} %fusion.149) | copy-start | bytes 3076
  258.9 12.3 %copy-start.86 = (f32[256,512]{1,0:T(8,128)}, f32[256,512]{1,0:T(8,128)S(1)}, u32[]{:S(2)}) copy-start(f32[256,512]{1,0:T(8,128)S(1)} %fusion.65) | copy-start | bytes 1572868
  258.9 12.3 %copy-start.88 = (bf16[1024,1152]{1,0:T(8,128)(2,1)S(1)}, bf16[1024,1152]{1,0:T(8,128)(2,1)}, u32[]{:S(2)}) copy-start(bf16[1024,1152]{1,0:T(8,128)(2,1)} %copy.68) | copy-start | bytes 7077892
  280.2 33.6 %copy-start.5 = (f32[256,1152]{1,0:T(8,128)}, f32[256,1152]{1,0:T(8,128)S(1)}, u32[]{:S(2)}) copy-start(f32[256,1152]{1,0:T(8,128)S(1)} %convert_add_fusion.h_ref) | copy-start | bytes 3538948
  383.2 186.1 %reduce-scatter.8.cloned.1.call-start = ((), (), s32[]{:S(2)}) async-start(), calls=%async_computation.10 | async-start | bytes 5160960 | tf_op jit(solution)/shard_map/reduce_scatter | solution.py:873
  425.8 221.7 %reduce-scatter.10.cloned.1.call-start = ((), (), s32[]{:S(2)}) async-start(), calls=%async_computation.11 | async-start | bytes 2580480 | tf_op jit(solution)/shard_map/reduce_scatter | solution.py:873
  444.5 10.7 %copy-start.160 = (f32[128]{0:T(128)S(1)}, f32[128]{0:T(128)}, u32[]{:S(2)}) copy-start(f32[128]{0:T(128)} %copy-done.158) | copy-start | bytes 1540
  444.5 11.2 %copy-start.87 = (f32[256,512]{1,0:T(8,128)S(1)}, f32[256,512]{1,0:T(8,128)}, u32[]{:S(2)}) copy-start(f32[256,512]{1,0:T(8,128)} %copy-done.86) | copy-start | bytes 1572868
  444.6 11.2 %copy-start.126 = (f32[256]{0:T(256)S(1)}, f32[256]{0:T(256)}, u32[]{:S(2)}) copy-start(f32[256]{0:T(256)} %mul.794) | copy-start | bytes 3076
  444.6 11.2 %copy-start.132 = (f32[256]{0:T(256)S(1)}, f32[256]{0:T(256)}, u32[]{:S(2)}) copy-start(f32[256]{0:T(256)} %copy-done.131) | copy-start | bytes 3076
  444.6 11.9 %copy-start.61 = (bf16[4,256,768]{1,2,0:T(8,128)(2,1)S(1)}, bf16[4,256,768]{1,2,0:T(8,128)(2,1)}, u32[]{:S(2)}) copy-start(bf16[4,256,768]{1,2,0:T(8,128)(2,1)} %copy-done.60) | copy-start | bytes 4718596
  505.8 218.9 %reduce-scatter.14.cloned.1.call-start = ((), (), s32[]{:S(2)}) async-start(), calls=%async_computation.13 | async-start | bytes 5160960 | tf_op jit(solution)/shard_map/reduce_scatter | solution.py:873
  569.3 184.2 %reduce-scatter.12.cloned.1.call-start = ((), (), s32[]{:S(2)}) async-start(), calls=%async_computation.12 | async-start | bytes 1945600 | tf_op jit(solution)/shard_map/reduce_scatter | solution.py:873
  585.5 9.7 %copy-start.161 = (f32[128]{0:T(128)S(1)}, f32[128]{0:T(128)}, u32[]{:S(2)}) copy-start(f32[128]{0:T(128)} %copy-done.158) | copy-start | bytes 1540
  585.6 10.2 %copy-start.63 = (bf16[4,256,768]{1,2,0:T(8,128)(2,1)S(1)}, bf16[4,256,768]{1,2,0:T(8,128)(2,1)}, u32[]{:S(2)}) copy-start(bf16[4,256,768]{1,2,0:T(8,128)(2,1)} %copy-done.62) | copy-start | bytes 4718596
  637.0 17.1 %collective-permute-start.6 = (bf16[4,4,304,640]{3,2,1,0:T(8,128)(2,1)}, bf16[4,4,304,640]{3,2,1,0:T(8,128)(2,1)}, u32[]{:S(2)}, u32[]{:S(2)}) collective-permute-start(bf16[4,4,304,640]{3,2,1,0:T(8,128)(2,1)} %broadcast_select_fusion), channel_id=1, source_target_pairs={{0,16},{16,0},{1,17},{17,1},{2,18},{18,2},{3,19},{19,3},{4,20},{20... | collective-permute-start | bytes 18677768 | tf_op jit(solution)/shard_map/ppermute | solution.py:899
  637.2 12.8 %copy-start.147 = (f32[256]{0:T(256)S(1)}, f32[256]{0:T(256)}, u32[]{:S(2)}) copy-start(f32[256]{0:T(256)} %copy-done.146) | copy-start | bytes 3076
  637.2 9.2 %collective-permute-start.4 = (bf16[256,1152]{1,0:T(8,128)(2,1)S(1)}, bf16[256,1152]{1,0:T(8,128)(2,1)S(1)}, u32[]{:S(2)}, u32[]{:S(2)}) collective-permute-start(bf16[256,1152]{1,0:T(8,128)(2,1)S(1)} %broadcast_select_fusion.7), channel_id=1, source_target_pairs={{0,16},{16,0},{1,17},{17,1},{2,18},{18,2},{3,19},{19,3},{4,20},{20... | collective-permute-start | bytes 1769480 | tf_op jit(solution)/shard_map/ppermute | solution.py:899
  649.5 72.5 %collective-permute-start.8 = (bf16[288,896]{1,0:T(8,128)(2,1)}, bf16[288,896]{1,0:T(8,128)(2,1)}, u32[]{:S(2)}, u32[]{:S(2)}) collective-permute-start(bf16[288,896]{1,0:T(8,128)(2,1)} %broadcast_select_fusion.11), channel_id=1, source_target_pairs={{0,16},{16,0},{1,17},{17,1},{2,18},{18,2},{3,19},{19,3},{4,20},{20... | collective-permute-start | bytes 1548296 | tf_op jit(solution)/shard_map/ppermute | solution.py:899
  654.1 72.3 %collective-permute-start.5 = (f32[256,1152]{1,0:T(8,128)}, f32[256,1152]{1,0:T(8,128)}, u32[]{:S(2)}, u32[]{:S(2)}) collective-permute-start(f32[256,1152]{1,0:T(8,128)} %get-tuple-element.87), channel_id=1, source_target_pairs={{0,16},{16,0},{1,17},{17,1},{2,18},{18,2},{3,19},{19,3},{4,20},{20... | collective-permute-start | bytes 3538952 | tf_op jit(solution)/shard_map/ppermute | solution.py:899
  725.1 4.4 collective-permute-start.7
  730.0 36.4 %copy-start.1 = (bf16[1,288,512]{2,1,0:T(8,128)(2,1)S(1)}, bf16[1,288,512]{2,1,0:T(8,128)(2,1)}, u32[]{:S(2)}) copy-start(bf16[1,288,512]{2,1,0:T(8,128)(2,1)} %param.16) | copy-start | bytes 884740
  753.4 10.9 %copy-start.102 = (bf16[304,640]{1,0:T(8,128)(2,1)S(1)}, bf16[304,640]{1,0:T(8,128)(2,1)}, u32[]{:S(2)}) copy-start(bf16[304,640]{1,0:T(8,128)(2,1)} %reduce-scatter.12.cloned.1.call-done) | copy-start | bytes 1167364
  (137 other events, 302.9 us)
Sparse Core Ops, SparseCore 0:
  15.7 40.8 all-gather.14
  58.3 79.8 all-gather.6
  139.8 45.0 all-gather.8
  186.9 79.6 all-gather.10
  268.7 45.0 all-gather.12
  383.3 40.8 reduce-scatter.5
  426.6 75.1 reduce-scatter.7
  505.9 41.8 reduce-scatter.9
  569.4 73.7 reduce-scatter.13
  719.9 33.5 reduce-scatter.11

commit v3 on v2

v3 whole, which is shorter than its diff:
```python
import functools

import jax
import jax.numpy as jnp
from jax import lax
from jax.experimental import pallas as pl
from jax.experimental.pallas import tpu as pltpu
from jax.sharding import PartitionSpec as P

WINDOW = 512
EPSILON = 1e-06
NEGATIVE = -1e30
ROPE_BASE = 10000.0
MESH = pl.DeviceIdType.MESH
MIB = 2**20
GAIN_COLUMNS = 128
F32 = jnp.float32
BF16 = jnp.bfloat16


def dot(a, b, dims):
    return lax.dot_general(a, b, ((dims[0], dims[1]), ((), ())), preferred_element_type=F32)


def nn(a, b):
    return dot(a, b, ((1,), (0,)))


def nt(a, b):
    return dot(a, b, ((1,), (1,)))


def tn(a, b):
    return dot(a, b, ((0,), (0,)))


def normed(operand, gain_vec):
    return (
        operand
        * lax.rsqrt(jnp.mean(operand * operand, axis=-1, keepdims=True) + EPSILON)
        * gain_vec
    )


def geglu(gate, up):
    return jax.nn.gelu(gate, approximate=True) * up


def neighbours():
    me = lax.axis_index("narrow")
    return me, jnp.bitwise_xor(me, 1), jnp.bitwise_xor(me, 2)


def meet(nx, ny):
    barrier = pltpu.get_barrier_semaphore()
    for other in (nx, ny):
        pl.semaphore_signal(barrier, inc=1, device_id={"narrow": other}, device_id_type=MESH)
    pl.semaphore_wait(barrier, 2)


def remote(src, dst, send_sem, recv_sem, other):
    return pltpu.make_async_remote_copy(
        src_ref=src,
        dst_ref=dst,
        send_sem=send_sem,
        recv_sem=recv_sem,
        device_id={"narrow": other},
        device_id_type=MESH,
    )


def tables(positions, head_width):
    half_width = head_width // 2
    frequency = ROPE_BASE ** (-jnp.arange(half_width, dtype=F32) * (2.0 / head_width))
    angles = positions.astype(F32)[:, None] * frequency[None, :]
    return jnp.concatenate([jnp.cos(angles), jnp.sin(angles)], axis=1)


def rotate(operand, cosine, sine_table):
    half_width = operand.shape[-1] // 2
    front_half = operand[..., :half_width]
    back_half = operand[..., half_width:]
    return jnp.concatenate(
        [
            front_half * cosine - back_half * sine_table,
            back_half * cosine + front_half * sine_table,
        ],
        axis=-1,
    )


GELU_SCALE = 0.7978845608028654
GELU_CUBE = 0.044715


def vmem_spec():
    return pl.BlockSpec(memory_space=pltpu.VMEM)


def any_spec():
    return pl.BlockSpec(memory_space=pl.ANY)


def rows_of(block, count):
    return pl.ds(pl.multiple_of(block * count, count), count)


def columns_of(tile, width, offset=0):
    return pl.ds(pl.multiple_of(tile * width + offset, 128), width)


def inverse_rms(value):
    return lax.rsqrt(jnp.mean(value * value, axis=-1, keepdims=True) + EPSILON)


def normed_gradient(value, gain, grad):
    inverse = inverse_rms(value)
    unit = value * inverse
    scaled = grad * gain
    by_value = inverse * (scaled - unit * jnp.mean(scaled * unit, axis=-1, keepdims=True))
    return by_value, jnp.sum(grad * unit, axis=0, keepdims=True)


def halves_of(ref, count, base=0):
    half = count // 2

    def part(block, which):
        return ref.at[pl.ds(pl.multiple_of(base + block * count + which * half, half), half)]

    return part


class Spread:
    def __init__(self, part, send, recv):
        self.me, self.nx, self.ny = neighbours()
        self.far = jnp.bitwise_xor(self.me, 3)

        def copy(block, which, at, other):
            ref = part(block, which)
            return remote(ref, ref, send.at[at], recv.at[at], other)

        self.to_x1 = copy(self.me, 0, 0, self.nx)
        self.to_y2 = copy(self.me, 1, 1, self.ny)
        self.to_x2 = copy(self.me, 1, 2, self.nx)
        self.to_y1 = copy(self.me, 0, 3, self.ny)
        self.on_y = copy(self.nx, 0, 4, self.ny)
        self.on_x = copy(self.ny, 1, 5, self.nx)

    def start(self):
        for copy in (self.to_x1, self.to_y2, self.to_x2, self.to_y1):
            copy.start()

    def pass_on(self):
        self.to_x1.wait_recv()
        self.on_y.start()
        self.to_y2.wait_recv()
        self.on_x.start()

    def x_here(self):
        self.to_x2.wait_recv()

    def y_here(self):
        self.to_y1.wait_recv()

    def far_here(self):
        self.on_y.wait_recv()
        self.on_x.wait_recv()

    def all_here(self):
        self.x_here()
        self.y_here()
        self.far_here()

    def finish(self):
        for copy in (self.to_x1, self.to_y2, self.to_x2, self.to_y1, self.on_y, self.on_x):
            copy.wait_send()


class Fold:
    def __init__(self, part, land, passing, send, recv):
        self.me, self.nx, self.ny = neighbours()
        self.far = jnp.bitwise_xor(self.me, 3)
        self.part, self.land, self.passing = part, land, passing

        def copy(src, at, other):
            return remote(src, land.at[at], send.at[at], recv.at[at], other)

        self.far_x = copy(part(self.far, 0), 0, self.nx)
        self.far_y = copy(part(self.far, 1), 1, self.ny)
        self.near_x = copy(part(self.nx, 0), 2, self.nx)
        self.near_y = copy(part(self.ny, 1), 3, self.ny)
        self.on_y = copy(passing.at[0], 4, self.ny)
        self.on_x = copy(passing.at[1], 5, self.nx)

    def send_far(self):
        self.far_x.start()
        self.far_y.start()

    def send_near(self):
        self.near_x.start()
        self.near_y.start()

    def pass_on(self):
        self.far_x.wait_recv()
        self.passing[0] = (self.part(self.ny, 0)[...].astype(F32) + self.land[0].astype(F32)).astype(BF16)
        self.on_y.start()
        self.far_y.wait_recv()
        self.passing[1] = (self.part(self.nx, 1)[...].astype(F32) + self.land[1].astype(F32)).astype(BF16)
        self.on_x.start()

    def total(self, own):
        half = own.shape[0] // 2
        for copy in (self.near_x, self.near_y, self.on_y, self.on_x):
            copy.wait_recv()
        first = own[:half] + (self.land[2].astype(F32) + self.land[4].astype(F32))
        second = own[half:] + (self.land[3].astype(F32) + self.land[5].astype(F32))
        return jnp.concatenate([first, second], axis=0)

    def finish(self):
        for copy in (self.far_x, self.far_y, self.near_x, self.near_y, self.on_y, self.on_x):
            copy.wait_send()


class Deal:
    def __init__(self, src, place, send, recv):
        me, nx, ny = neighbours()
        far = jnp.bitwise_xor(me, 3)
        self.copies = [
            remote(src(other), place(me), send.at[at], recv.at[at], other)
            for at, other in enumerate((far, nx, ny))
        ]

    def start(self):
        for copy in self.copies:
            copy.start()

    def here(self):
        for copy in self.copies:
            copy.wait_recv()

    def finish(self):
        for copy in self.copies:
            copy.wait_send()


def greet(*others):
    barrier = pltpu.get_barrier_semaphore()
    for other in others:
        pl.semaphore_signal(barrier, inc=1, device_id=other, device_id_type=MESH)
    return lambda: pl.semaphore_wait(barrier, len(others))


def spread_spec():
    return [pltpu.SemaphoreType.DMA((6,)), pltpu.SemaphoreType.DMA((6,))]


def fold_spec(count, width):
    return [
        pltpu.VMEM((6, count // 2, width), BF16),
        pltpu.VMEM((2, count // 2, width), BF16),
        pltpu.SemaphoreType.DMA((6,)),
        pltpu.SemaphoreType.DMA((6,)),
    ]


def params(collective_id, mib):
    return pltpu.CompilerParams(
        collective_id=collective_id, has_side_effects=True, vmem_limit_bytes=mib * MIB
    )


TILE = 256


def up_kernel(h_ref, gain_ref, w_ref, *refs):
    sharing = len(refs) > 11
    if sharing:
        xn_ref, o_ref, rows_out, gu_out, act_out, xn_out, o_out, *refs = refs
        rows, w, gu, act, load, store, send, recv, *share_refs = refs
        share = Share(xn_ref, o_ref, *share_refs)
    else:
        rows_out, gu_out, act_out, rows, w, gu, act, load, store, send, recv = refs
    count = h_ref.shape[0]
    hidden = act.shape[1]
    weights = pltpu.make_async_copy(w_ref.at[:, pl.ds(0, 2 * hidden)], w, load)
    weights.start()
    me, nx, ny = neighbours()
    met = greet({"narrow": nx}, {"narrow": ny}, {"narrow": jnp.bitwise_xor(me, 3)})
    value = h_ref[...]
    rows[rows_of(me, count), :] = (value * inverse_rms(value) * gain_ref[...]).astype(BF16)
    spread = Spread(halves_of(rows, count), send, recv)
    met()
    spread.start()
    weights.wait()

    def one(block, at):
        here = rows_of(block, count)

        def tile(j, _):
            left = rows[here, :]
            gate = nn(left, w[:, columns_of(j, TILE)])
            up = nn(left, w[:, columns_of(j, TILE, hidden)])
            inner = jnp.tanh(GELU_SCALE * (gate + GELU_CUBE * (gate * gate * gate)))
            gu[here, columns_of(j, TILE)] = gate.astype(BF16)
            gu[here, columns_of(j, TILE, hidden)] = up.astype(BF16)
            act[here, columns_of(j, TILE)] = (0.5 * gate * (1.0 + inner) * up).astype(BF16)
            return 0

        lax.fori_loop(0, hidden // TILE, tile, 0)
        copies = [
            pltpu.make_async_copy(ref.at[here], out.at[here], store.at[k, at])
            for k, (ref, out) in enumerate(((gu, gu_out), (act, act_out), (rows, rows_out)))
        ]
        for copy in copies:
            copy.start()
        return copies

    copies = one(me, 0)
    spread.pass_on()
    if sharing:
        share.start_rows()
        share.start_deal()
    spread.x_here()
    copies += one(nx, 1)
    spread.y_here()
    copies += one(ny, 2)
    spread.far_here()
    if sharing:
        share.spread.pass_on()
    copies += one(spread.far, 3)
    spread.finish()
    if sharing:
        share.all_here()
        share.finish()
        xn, o, loads = share_refs[:3]
        copies += [pltpu.make_async_copy(xn, xn_out, loads.at[2]), pltpu.make_async_copy(o, o_out, loads.at[3])]
        for copy in copies[-2:]:
            copy.start()
    for copy in copies:
        copy.wait()


def feed_up(h, gain, w_gu, hidden, shared, collective_id):
    count, model = h.shape
    total = 4 * count
    shapes = [(total, model), (total, 2 * hidden), (total, hidden)]
    shapes = [jax.ShapeDtypeStruct(shape, BF16) for shape in shapes]
    if shared:
        shapes += share_shapes(*shared)
    return pl.pallas_call(
        up_kernel,
        out_shape=shapes,
        in_specs=[vmem_spec(), vmem_spec(), any_spec()] + [vmem_spec()] * len(shared),
        out_specs=[any_spec()] * len(shapes),
        scratch_shapes=[
            pltpu.VMEM((total, model), BF16),
            pltpu.VMEM((model, 2 * hidden), BF16),
            pltpu.VMEM((total, 2 * hidden), BF16),
            pltpu.VMEM((total, hidden), BF16),
            pltpu.SemaphoreType.DMA,
            pltpu.SemaphoreType.DMA((3, 4)),
            *spread_spec(),
            *(share_spec(count, model, shared[1].shape[1] // 4) if shared else []),
        ],
        compiler_params=params(collective_id, 48),
    )(h, gain, w_gu, *shared)


def down_kernel(
    h_ref, gain_ref, act_ref, w_ref, x_out, f_out, act, w, parts, load, land, passing, send, recv
):
    count, model = h_ref.shape
    me, nx, ny = neighbours()
    met = greet({"narrow": nx}, {"narrow": ny})
    far = jnp.bitwise_xor(me, 3)
    first = w_ref.shape[1] - w.shape[1]
    weights = pltpu.make_async_copy(w_ref.at[:, pl.ds(first, w.shape[1])], w, load.at[0])
    weights.start()
    arrivals = []
    for at, block in enumerate((far, nx, ny, me)):
        here = rows_of(block, count)
        arrivals.append(pltpu.make_async_copy(act_ref.at[here], act.at[here], load.at[1 + at]))
        arrivals[-1].start()
    fold = Fold(halves_of(parts, count), land, passing, send, recv)
    weights.wait()
    met()

    def one(block, at):
        arrivals[at].wait()
        return nt(act[rows_of(block, count), :], w[...])

    parts[rows_of(far, count), :] = one(far, 0).astype(BF16)
    fold.send_far()
    parts[rows_of(nx, count), :] = one(nx, 1).astype(BF16)
    parts[rows_of(ny, count), :] = one(ny, 2).astype(BF16)
    fold.send_near()
    f_out[...] = one(me, 3)
    fold.pass_on()
    total = fold.total(f_out[...])
    f_out[...] = total
    x_out[...] = (h_ref[...] + total * inverse_rms(total) * gain_ref[...]).astype(BF16)
    fold.finish()


def feed_down(h, gain, act, w_dt, collective_id):
    count, model = h.shape
    return pl.pallas_call(
        down_kernel,
        out_shape=[
            jax.ShapeDtypeStruct((count, model), BF16),
            jax.ShapeDtypeStruct((count, model), F32),
        ],
        in_specs=[vmem_spec(), vmem_spec(), any_spec(), any_spec()],
        out_specs=[vmem_spec(), vmem_spec()],
        scratch_shapes=[
            pltpu.VMEM(act.shape, BF16),
            pltpu.VMEM((model, act.shape[1]), BF16),
            pltpu.VMEM((4 * count, model), BF16),
            pltpu.SemaphoreType.DMA((5,)),
            *fold_spec(count, model),
        ],
        compiler_params=params(collective_id, 40),
    )(h, gain, act, w_dt)


def swap_sum(make, tiles, ours, theirs, came, send, recv, out, out_sems, between=None):
    other = {"section": 1 - lax.axis_index("section")}
    sends = []
    for at, (first, width) in enumerate(tiles):
        columns = pl.ds(first, width)
        theirs[:, columns] = make(False, first, width).astype(BF16)
        copy = pltpu.make_async_remote_copy(
            src_ref=theirs.at[:, columns],
            dst_ref=came.at[:, columns],
            send_sem=send.at[at],
            recv_sem=recv.at[at],
            device_id=other,
            device_id_type=MESH,
        )
        copy.start()
        sends.append(copy)
    if between is not None:
        between()
    stores = []
    for at, (first, width) in enumerate(tiles):
        columns = pl.ds(first, width)
        own = make(True, first, width)
        sends[at].wait_recv()
        ours[:, columns] = (own + came[:, columns].astype(F32)).astype(BF16)
        copy = pltpu.make_async_copy(ours.at[:, columns], out.at[:, columns], out_sems.at[at])
        copy.start()
        stores.append(copy)
    return sends, stores


def column_tiles(width):
    return [(first, min(TILE, width - first)) for first in range(0, width, TILE)]


def back_up_kernel(dy_ref, f_ref, gain_ref, gu_ref, act_ref, w_ref, *refs):
    if len(refs) == 18:
        extra_ref, *refs = refs
    else:
        extra_ref = None
    (
        dgu_out, dw_out, dgain_out, df, gu, act, w, ours, theirs, came,
        load, store, send, recv, swap_send, swap_recv, out_sems,
    ) = refs
    if extra_ref is not None:
        first = ours.shape[1]
        extra = pltpu.make_async_copy(
            extra_ref, dw_out.at[:, pl.ds(first, extra_ref.shape[1])], load.at[0, 1]
        )
        extra.start()
    count, model = dy_ref.shape
    hidden = act.shape[1]
    me, nx, ny = neighbours()
    core = lax.axis_index("section")
    met = greet({"narrow": nx}, {"narrow": ny}, {"section": 1 - core})
    far = jnp.bitwise_xor(me, 3)
    start = w_ref.shape[1] - hidden
    weights = pltpu.make_async_copy(w_ref.at[:, pl.ds(start, hidden)], w, load.at[0, 0])
    weights.start()
    arrivals = []
    for at, block in enumerate((me, nx, ny, far)):
        here = rows_of(block, count)
        pair = [
            pltpu.make_async_copy(gu_ref.at[here], gu.at[here], load.at[1, at]),
            pltpu.make_async_copy(act_ref.at[here], act.at[here], load.at[2, at]),
        ]
        for copy in pair:
            copy.start()
        arrivals.append(pair)
    dy = dy_ref[...].astype(BF16).astype(F32)
    by_value, by_gain = normed_gradient(f_ref[...], gain_ref[...], dy)
    df[rows_of(me, count), :] = by_value.astype(BF16)
    spread = Spread(halves_of(df, count), send, recv)
    met()
    spread.start()
    dgain_out[...] = by_gain
    weights.wait()

    def one(block, at):
        here = rows_of(block, count)
        for copy in arrivals[at]:
            copy.wait()

        def tile(j, _):
            dact = nn(df[here, :], w[:, columns_of(j, TILE)])
            gate = gu[here, columns_of(j, TILE)].astype(F32)
            up = gu[here, columns_of(j, TILE, hidden)].astype(F32)
            square = gate * gate
            inner = jnp.tanh(GELU_SCALE * gate * (1.0 + GELU_CUBE * square))
            half = 0.5 * (1.0 + inner)
            slope = half + 0.5 * GELU_SCALE * gate * (1.0 - inner * inner) * (
                1.0 + 3.0 * GELU_CUBE * square
            )
            gu[here, columns_of(j, TILE)] = (dact * up * slope).astype(BF16)
            gu[here, columns_of(j, TILE, hidden)] = (dact * gate * half).astype(BF16)
            return 0

        lax.fori_loop(0, hidden // TILE, tile, 0)
        copy = pltpu.make_async_copy(gu.at[here], dgu_out.at[here], store.at[at])
        copy.start()
        return copy

    copies = [one(me, 0)]
    spread.pass_on()
    spread.x_here()
    copies.append(one(nx, 1))
    spread.y_here()
    copies.append(one(ny, 2))
    spread.far_here()
    copies.append(one(far, 3))

    def make(mine, first, width):
        side = core if mine else 1 - core
        start = pl.multiple_of(side * (hidden // 2) + first, 128)
        return tn(df[...], act[:, pl.ds(start, width)])

    sends, stores = swap_sum(
        make, column_tiles(hidden // 2), ours, theirs, came, swap_send, swap_recv, dw_out, out_sems
    )
    spread.finish()
    for copy in sends:
        copy.wait_send()
    for copy in copies + stores:
        copy.wait()
    if extra_ref is not None:
        extra.wait()


def feed_back_up(dy, f, gain, gu, act, w_dt, extra, collective_id):
    count, model = dy.shape
    total, hidden = act.shape
    tiles = len(column_tiles(hidden // 2))
    extras = () if extra is None else (extra,)
    return pl.pallas_call(
        back_up_kernel,
        out_shape=[
            jax.ShapeDtypeStruct(gu.shape, BF16),
            jax.ShapeDtypeStruct((model, hidden // 2 + sum(e.shape[1] for e in extras)), BF16),
            jax.ShapeDtypeStruct((1, model), F32),
        ],
        in_specs=[vmem_spec()] * 3 + [any_spec()] * (3 + len(extras)),
        out_specs=[any_spec(), any_spec(), vmem_spec()],
        scratch_shapes=[
            pltpu.VMEM((total, model), BF16),
            pltpu.VMEM(gu.shape, BF16),
            pltpu.VMEM(act.shape, BF16),
            pltpu.VMEM((model, hidden), BF16),
            pltpu.VMEM((model, hidden // 2), BF16),
            pltpu.VMEM((model, hidden // 2), BF16),
            pltpu.VMEM((model, hidden // 2), BF16),
            pltpu.SemaphoreType.DMA((3, 4)),
            pltpu.SemaphoreType.DMA((4,)),
            *spread_spec(),
            pltpu.SemaphoreType.DMA((tiles,)),
            pltpu.SemaphoreType.DMA((tiles,)),
            pltpu.SemaphoreType.DMA((tiles,)),
        ],
        compiler_params=params(collective_id, 48),
    )(dy, f, gain, gu, act, w_dt, *extras)


def back_down_kernel(
    dy_ref, h_ref, gain_ref, dgu_ref, rows_ref, w_ref, dh_out, dw_out, dgain_out,
    dgu, rows, w, parts, ours, theirs, came, load, land, passing, send, recv, swap_send, swap_recv, out_sems,
):
    count, model = dy_ref.shape
    hidden = dgu.shape[1] // 2
    me, nx, ny = neighbours()
    core = lax.axis_index("section")
    far = jnp.bitwise_xor(me, 3)
    met = greet({"narrow": nx}, {"narrow": ny}, {"section": 1 - core})
    weights = pltpu.make_async_copy(w_ref.at[:, pl.ds(0, 2 * hidden)], w, load.at[0])
    weights.start()
    arrivals = []
    for at, block in enumerate((far, nx, ny, me)):
        here = rows_of(block, count)
        arrivals.append(pltpu.make_async_copy(dgu_ref.at[here], dgu.at[here], load.at[1 + at]))
        arrivals[-1].start()
    kept = pltpu.make_async_copy(rows_ref, rows, load.at[5])
    kept.start()
    fold = Fold(halves_of(parts, count), land, passing, send, recv)
    weights.wait()
    met()
    step = model // 3

    def one(block, at, out, here):
        arrivals[at].wait()

        def tile(j, _):
            part = nt(dgu[rows_of(block, count), :], w[pl.ds(pl.multiple_of(j * step, step), step), :])
            out[here, columns_of(j, step)] = part.astype(out.dtype)
            return 0

        lax.fori_loop(0, 3, tile, 0)

    one(far, 0, parts, rows_of(far, count))
    fold.send_far()
    one(nx, 1, parts, rows_of(nx, count))
    one(ny, 2, parts, rows_of(ny, count))
    fold.send_near()
    one(me, 3, dh_out, pl.ds(0, count))
    fold.pass_on()
    kept.wait()

    def make(mine, first, width):
        side = core if mine else 1 - core
        start = pl.multiple_of(side * hidden + first, 128)
        return tn(rows[...], dgu[:, pl.ds(start, width)])

    sends, stores = swap_sum(
        make, column_tiles(hidden), ours, theirs, came, swap_send, swap_recv, dw_out, out_sems
    )
    total = fold.total(dh_out[...])
    by_value, by_gain = normed_gradient(h_ref[...], gain_ref[...], total)
    dh_out[...] = dy_ref[...].astype(BF16).astype(F32) + by_value
    dgain_out[...] = by_gain
    fold.finish()
    for copy in sends:
        copy.wait_send()
    for copy in stores:
        copy.wait()


def feed_back_down(dy, h, gain, dgu, rows, w_gu, collective_id):
    count, model = dy.shape
    total, hidden = dgu.shape[0], dgu.shape[1] // 2
    tiles = len(column_tiles(hidden))
    return pl.pallas_call(
        back_down_kernel,
        out_shape=[
            jax.ShapeDtypeStruct((count, model), F32),
            jax.ShapeDtypeStruct((model, hidden), BF16),
            jax.ShapeDtypeStruct((1, model), F32),
        ],
        in_specs=[vmem_spec()] * 3 + [any_spec()] * 3,
        out_specs=[vmem_spec(), any_spec(), vmem_spec()],
        scratch_shapes=[
            pltpu.VMEM(dgu.shape, BF16),
            pltpu.VMEM(rows.shape, BF16),
            pltpu.VMEM((model, 2 * hidden), BF16),
            pltpu.VMEM((total, model), BF16),
            pltpu.VMEM((model, hidden), BF16),
            pltpu.VMEM((model, hidden), BF16),
            pltpu.VMEM((model, hidden), BF16),
            pltpu.SemaphoreType.DMA((6,)),
            *fold_spec(count, model),
            pltpu.SemaphoreType.DMA((tiles,)),
            pltpu.SemaphoreType.DMA((tiles,)),
            pltpu.SemaphoreType.DMA((tiles,)),
        ],
        compiler_params=params(collective_id, 56),
    )(dy, h, gain, dgu, rows, w_gu)


def pack_kernel(p_ref, o_ref, local, send, recv, peer_send, peer_recv):
    model = p_ref.shape[0]
    half = model // 2
    core = lax.axis_index("section")
    first = core * half
    me, nx, ny = neighbours()
    met = greet({"narrow": nx}, {"narrow": ny}, {"section": 1 - core})
    width = o_ref.shape[2]
    own = pltpu.make_async_copy(p_ref.at[:, pl.ds(0, width)], o_ref.at[me], local)
    own.start()

    def part(block, which):
        start = pl.multiple_of(first + which * (half // 2), half // 2)
        return o_ref.at[block, pl.ds(start, half // 2)]

    spread = Spread(part, send, recv)
    own.wait()
    met()
    spread.start()
    copies = []

    def across(block, at):
        ref = o_ref.at[block, pl.ds(pl.multiple_of(first, half), half)]
        copy = pltpu.make_async_remote_copy(
            src_ref=ref,
            dst_ref=ref,
            send_sem=peer_send.at[at],
            recv_sem=peer_recv.at[at],
            device_id={"section": 1 - core},
            device_id_type=MESH,
        )
        copy.start()
        copies.append(copy)

    spread.pass_on()
    spread.x_here()
    across(nx, 0)
    spread.y_here()
    across(ny, 1)
    spread.far_here()
    across(spread.far, 2)
    for copy in copies:
        copy.wait_recv()
    spread.finish()
    for copy in copies:
        copy.wait_send()


def gather_pack(pack, width, collective_id):
    return pl.pallas_call(
        pack_kernel,
        out_shape=jax.ShapeDtypeStruct((4, pack.shape[0], width), pack.dtype),
        in_specs=[any_spec()],
        out_specs=vmem_spec(),
        scratch_shapes=[
            pltpu.SemaphoreType.DMA,
            *spread_spec(),
            pltpu.SemaphoreType.DMA((3,)),
            pltpu.SemaphoreType.DMA((3,)),
        ],
        compiler_params=params(collective_id, 24),
    )(pack)


class Share:
    def __init__(self, xn_ref, o_ref, xn, o, loads, spread_send, spread_recv, deal_send, deal_recv):
        count, head = xn_ref.shape[0], o.shape[1]
        me = lax.axis_index("narrow")
        self.loads = [
            pltpu.make_async_copy(xn_ref, xn.at[rows_of(me, count)], loads.at[0]),
            pltpu.make_async_copy(o_ref.at[:, columns_of(me, head)], o.at[rows_of(me, count)], loads.at[1]),
        ]
        self.spread = Spread(halves_of(xn, count), spread_send, spread_recv)
        self.deal = Deal(
            lambda other: o_ref.at[:, columns_of(other, head)],
            lambda mine: o.at[rows_of(mine, count)],
            deal_send,
            deal_recv,
        )

    def start_rows(self):
        self.loads[0].start()
        self.loads[0].wait()
        self.spread.start()

    def start_deal(self):
        self.loads[1].start()
        self.deal.start()

    def all_here(self):
        self.spread.all_here()
        self.deal.here()

    def finish(self):
        self.spread.finish()
        self.deal.finish()
        self.loads[1].wait()


def share_spec(count, model, head):
    return [
        pltpu.VMEM((4 * count, model), BF16),
        pltpu.VMEM((4 * count, head), BF16),
        pltpu.SemaphoreType.DMA((4,)),
        *spread_spec(),
        pltpu.SemaphoreType.DMA((3,)),
        pltpu.SemaphoreType.DMA((3,)),
    ]


def share_shapes(xn, o):
    total = 4 * xn.shape[0]
    return [
        jax.ShapeDtypeStruct((total, xn.shape[1]), BF16),
        jax.ShapeDtypeStruct((total, o.shape[1] // 4), BF16),
    ]


def gain_kernel(g_ref, o_ref, land, total, send, recv):
    core, wide = lax.axis_index("section"), lax.axis_index("wide")
    wides = land.shape[0] - 3
    me, nx, ny = neighbours()
    far = jnp.bitwise_xor(me, 3)
    stages = [
        [{"narrow": nx}, {"narrow": ny}, {"narrow": far}],
        [{"section": 1 - core}],
        [{"wide": lax.rem(wide + step, wides)} for step in range(1, wides)],
    ]
    met = greet(*stages[0], *stages[1], *stages[2])
    total[0] = g_ref[...]
    met()
    at = 0
    copies = []
    for stage, others in enumerate(stages):
        mine = []
        for other in others:
            mine.append(
                pltpu.make_async_remote_copy(
                    src_ref=total.at[stage],
                    dst_ref=land.at[at],
                    send_sem=send.at[at],
                    recv_sem=recv.at[at],
                    device_id=other,
                    device_id_type=MESH,
                )
            )
            mine[-1].start()
            at += 1
        value = total[stage]
        for place, copy in enumerate(mine, at - len(mine)):
            copy.wait_recv()
            value = value + land[place]
        total[stage + 1] = value
        copies += mine
    o_ref[...] = total[3]
    for copy in copies:
        copy.wait_send()


def sum_gains(block, wides, collective_id):
    return pl.pallas_call(
        gain_kernel,
        out_shape=jax.ShapeDtypeStruct(block.shape, F32),
        in_specs=[vmem_spec()],
        out_specs=vmem_spec(),
        scratch_shapes=[
            pltpu.VMEM((wides + 3, *block.shape), F32),
            pltpu.VMEM((4, *block.shape), F32),
            pltpu.SemaphoreType.DMA((wides + 3,)),
            pltpu.SemaphoreType.DMA((wides + 3,)),
        ],
        compiler_params=params(collective_id, 16),
    )(block)


def turn_back(grad, cosine, sine_table):
    half = grad.shape[1] // 2
    front, back = grad[:, :half], grad[:, half:]
    return jnp.concatenate(
        [front * cosine + back * sine_table, back * cosine - front * sine_table], axis=1
    )


def pack_loads(pack_ref, head, wq, wot, wkv, sems):
    kv_part = wkv.shape[1] // 4
    loads = []
    for at, (w, first, width) in enumerate(
        ((wq, 0, head), (wot, head, head), (wkv, 2 * head, kv_part))
    ):
        loads.append(
            [
                pltpu.make_async_copy(
                    pack_ref.at[n, :, pl.ds(first, width)], w.at[:, pl.ds(n * width, width)], sems.at[at, n]
                )
                for n in range(4)
            ]
        )
    return loads


def start_all(copies):
    for copy in copies:
        copy.start()


def wait_all(copies):
    for copy in copies:
        copy.wait()


def window_mask(me, count, window, length):
    rows_at = me * count + lax.broadcasted_iota(jnp.int32, (count, 1), 0)
    cols_at = me * count - WINDOW + lax.broadcasted_iota(jnp.int32, (1, window), 1)
    return (
        (cols_at <= rows_at)
        & (rows_at - cols_at < WINDOW)
        & (cols_at >= 0)
        & ((cols_at < length) | (cols_at == rows_at))
    )


def attend_kernel(length_ref, x_ref, gains_ref, head_ref, trig_ref, pack_ref, *refs):
    (
        h_out, xn_out, q_out, k_out, win_out, lse_out, o_out, a_out, *refs
    ) = refs
    sharing = len(refs) > 9
    if sharing:
        xn_all_out, o_all_out, *refs = refs
    kv, wq, wot, wkv, load, send, recv, *share_refs = refs
    count, model = x_ref.shape
    head = k_out.shape[1]
    heads = q_out.shape[1] // head
    me, nx, ny = neighbours()
    met = greet({"narrow": nx}, {"narrow": ny}, {"narrow": jnp.bitwise_xor(me, 3)})
    q_loads, out_loads, kv_loads = pack_loads(pack_ref, head, wq, wot, wkv, load)
    start_all(kv_loads + q_loads + out_loads)
    scaling = head ** (-0.5)
    cosine, sine_table = trig_ref[:, : head // 2], trig_ref[:, head // 2 :]
    x = x_ref[...].astype(F32)
    xn_out[...] = (x * inverse_rms(x) * gains_ref[0:1, :]).astype(BF16)
    kv[pl.ds(0, WINDOW), :] = jnp.zeros((WINDOW, 2 * head), BF16)
    wait_all(kv_loads)
    raw = nn(xn_out[...], wkv[...])
    k_raw = raw[:, :head]
    k_out[...] = k_raw
    k_rot = rotate(k_raw * inverse_rms(k_raw) * head_ref[1:2, :], cosine, sine_table)
    here = pl.ds(pl.multiple_of(WINDOW + me * count, count), count)
    kv[here, :head] = k_rot.astype(BF16)
    kv[here, head:] = raw[:, head:].astype(BF16)
    spread = Spread(halves_of(kv, count, WINDOW), send, recv)
    met()
    spread.start()
    if sharing:
        share = Share(xn_out, o_out, *share_refs)
    wait_all(q_loads)
    q_out[...] = nn(xn_out[...], wq[...])
    spread.pass_on()
    if sharing:
        share.start_rows()
    spread.all_here()
    window = win_out.shape[0]
    win_out[...] = kv[pl.ds(pl.multiple_of(me * count, count), window), :]
    visible = window_mask(me, count, window, length_ref[0])
    k_win, v_win = win_out[:, :head], win_out[:, head:]
    q_gain = head_ref[0:1, :]

    def one_head(i, _):
        columns = columns_of(i, head)
        q_raw = q_out[:, columns]
        qr = rotate(q_raw * inverse_rms(q_raw) * q_gain, cosine, sine_table).astype(BF16)
        scores = jnp.where(visible, nt(qr, k_win) * scaling, NEGATIVE)
        most = jnp.max(scores, axis=-1, keepdims=True)
        exponent = jnp.exp(scores - most)
        total = jnp.sum(exponent, axis=-1, keepdims=True)
        lse_out[i] = most + jnp.log(total)
        o_out[:, columns] = nn((exponent / total).astype(BF16), v_win).astype(BF16)
        return 0

    lax.fori_loop(0, heads, one_head, 0)
    if sharing:
        share.start_deal()
        share.spread.pass_on()
    wait_all(out_loads)
    a = nt(o_out[...], wot[...])
    a_out[...] = a
    h_out[...] = x_ref[...].astype(F32) + a * inverse_rms(a) * gains_ref[1:2, :]
    spread.finish()
    if sharing:
        share.all_here()
        share.finish()
        xn, o, loads = share_refs[:3]
        stores = [
            pltpu.make_async_copy(xn, xn_all_out, loads.at[2]),
            pltpu.make_async_copy(o, o_all_out, loads.at[3]),
        ]
        start_all(stores)
        wait_all(stores)


def attend(length, x, gains, head_gains, trig, pack, head, sharing, collective_id):
    count, model = x.shape
    kv_width = 2 * head
    width = 4 * head
    window = count + WINDOW
    xn_shape = jax.ShapeDtypeStruct((count, model), BF16)
    o_shape = jax.ShapeDtypeStruct((count, width), BF16)
    shapes = [
        jax.ShapeDtypeStruct((count, model), F32),
        xn_shape,
        jax.ShapeDtypeStruct((count, width), F32),
        jax.ShapeDtypeStruct((count, head), F32),
        jax.ShapeDtypeStruct((window, kv_width), BF16),
        jax.ShapeDtypeStruct((4, count, 1), F32),
        o_shape,
        jax.ShapeDtypeStruct((count, model), F32),
    ]
    outs = [vmem_spec()] * 8
    if sharing:
        shapes += share_shapes(xn_shape, o_shape)
        outs += [any_spec()] * 2
    return pl.pallas_call(
        attend_kernel,
        out_shape=shapes,
        in_specs=[pl.BlockSpec(memory_space=pltpu.SMEM)] + [vmem_spec()] * 4 + [any_spec()],
        out_specs=outs,
        scratch_shapes=[
            pltpu.VMEM((4 * count + WINDOW, kv_width), BF16),
            pltpu.VMEM((model, width), BF16),
            pltpu.VMEM((model, width), BF16),
            pltpu.VMEM((model, kv_width), BF16),
            pltpu.SemaphoreType.DMA((3, 4)),
            *spread_spec(),
            *(share_spec(count, model, head) if sharing else []),
        ],
        compiler_params=params(collective_id, 40),
    )(length, x, gains, head_gains, trig, pack)


def attend_back_kernel(
    length_ref, dh_ref, a_ref, x_ref, gains_ref, head_ref, trig_ref, q_ref, k_ref, win_ref, lse_ref,
    pack_ref, xn_ref, o_ref,
    dx_out, dw_out, dgain_out, dhead_out,
    da, do, dq, dk, dv, parts, dq_all, dkv, dkv_all, wq, wot, wkv, xn, o, ours, theirs, came,
    pack_load, load, send, recv, land, passing, fold_send, fold_recv, q_send, q_recv, kv_send, kv_recv, swap_send, swap_recv, out_sem,
):
    count = dh_ref.shape[0]
    head = k_ref.shape[1]
    heads = q_ref.shape[1] // head
    kv_part = dkv_all.shape[1]
    me, nx, ny = neighbours()
    core = lax.axis_index("section")
    far = jnp.bitwise_xor(me, 3)
    met = greet({"narrow": nx}, {"narrow": ny}, {"narrow": far}, {"section": 1 - core})
    q_loads, out_loads, kv_loads = pack_loads(pack_ref, head, wq, wot, wkv, pack_load)
    loads = [
        pltpu.make_async_copy(src, dst, load.at[at])
        for at, (src, dst) in enumerate(((xn_ref, xn), (o_ref, o)))
    ]
    start_all(out_loads + q_loads + kv_loads + loads)
    here = rows_of(me, count)
    scaling = head ** (-0.5)
    cosine, sine_table = trig_ref[:, : head // 2], trig_ref[:, head // 2 :]

    dh = dh_ref[...]
    by_value, dg1 = normed_gradient(a_ref[...], gains_ref[1:2, :], dh)
    da[here, :] = by_value.astype(BF16)
    dgain_out[1:2, :] = dg1
    spread = Spread(halves_of(da, count), send, recv)
    met()
    spread.start()
    wait_all(out_loads)
    do[...] = nn(da[here, :], wot[...]).astype(BF16)

    visible = window_mask(me, count, win_ref.shape[0], length_ref[0])
    k_win, v_win = win_ref[:, :head], win_ref[:, head:]
    dk[...] = jnp.zeros_like(dk)
    dv[...] = jnp.zeros_like(dv)
    dhead_out[...] = jnp.zeros_like(dhead_out)
    q_gain, k_gain = head_ref[0:1, :], head_ref[1:2, :]

    def one_head(i, _):
        columns = columns_of(i, head)
        raw = q_ref[:, columns]
        inverse = inverse_rms(raw)
        unit = raw * inverse
        qr = rotate(unit * q_gain, cosine, sine_table).astype(BF16)
        scores = jnp.where(visible, nt(qr, k_win) * scaling, NEGATIVE)
        probs = jnp.exp(scores - lse_ref[i])
        do_head = do[:, columns]
        dp = nt(do_head, v_win)
        ds = (probs * (dp - jnp.sum(probs * dp, axis=-1, keepdims=True))).astype(BF16)
        dk[...] += tn(ds, qr)
        dv[...] += tn(probs.astype(BF16), do_head)
        grad = turn_back(nn(ds, k_win) * scaling, cosine, sine_table)
        scaled = grad * q_gain
        dq_raw = inverse * (scaled - unit * jnp.mean(scaled * unit, axis=-1, keepdims=True))
        dq[:, columns] = dq_raw.astype(BF16)
        dhead_out[0:1, :] += jnp.sum(grad * unit, axis=0, keepdims=True)
        return 0

    lax.fori_loop(0, heads, one_head, 0)
    parts[...] = jnp.zeros_like(parts)
    window = pl.ds(pl.multiple_of(me * count, count), win_ref.shape[0])
    parts[window, :head] = (dk[...] * scaling).astype(BF16)
    parts[window, head:] = dv[...].astype(BF16)
    fold = Fold(halves_of(parts, count, WINDOW), land, passing, fold_send, fold_recv)
    fold.send_far()
    fold.send_near()
    deal_q = Deal(
        lambda other: dq.at[:, columns_of(other, head)],
        lambda mine: dq_all.at[rows_of(mine, count)],
        q_send,
        q_recv,
    )
    deal_q.start()
    dq_all[here, :] = dq[:, columns_of(me, head)]
    spread.pass_on()
    wait_all(q_loads)
    dx_out[...] = nt(dq[...], wq[...])
    fold.pass_on()
    spread.all_here()
    wait_all(loads)
    first = core == 0
    swaps = []

    def exchange(at, columns, a, b):
        ours[:, columns] = jnp.where(first, a, b).astype(BF16)
        theirs[:, columns] = jnp.where(first, b, a).astype(BF16)
        copy = pltpu.make_async_remote_copy(
            src_ref=theirs.at[:, columns],
            dst_ref=came.at[:, columns],
            send_sem=swap_send.at[at],
            recv_sem=swap_recv.at[at],
            device_id={"section": 1 - core},
            device_id_type=MESH,
        )
        copy.start()
        swaps.append(copy)

    by_out = tn(da[...], o[...])
    deal_q.here()
    exchange(0, pl.ds(0, head), tn(xn[...], dq_all[...]), by_out)
    own = jnp.concatenate([dk[WINDOW:, :] * scaling, dv[WINDOW:, :]], axis=1)
    total = fold.total(own)
    grad = turn_back(total[:, :head], cosine, sine_table)
    dk_raw, dk_gain = normed_gradient(k_ref[...], k_gain, grad)
    dhead_out[1:2, :] = dk_gain
    dkv[:, :head] = dk_raw.astype(BF16)
    dkv[:, head:] = total[:, head:].astype(BF16)
    deal_kv = Deal(
        lambda other: dkv.at[:, columns_of(other, kv_part)],
        lambda mine: dkv_all.at[rows_of(mine, count)],
        kv_send,
        kv_recv,
    )
    deal_kv.start()
    dkv_all[here, :] = dkv[:, columns_of(me, kv_part)]
    wait_all(kv_loads)
    dxn = dx_out[...] + nt(dkv[...], wkv[...])
    by_value, dg0 = normed_gradient(x_ref[...].astype(F32), gains_ref[0:1, :], dxn)
    dx_out[...] = dh_ref[...] + by_value
    dgain_out[0:1, :] = dg0

    deal_kv.here()
    by_kv = tn(xn[...], dkv_all[...])
    exchange(1, pl.ds(head, kv_part), by_kv, jnp.zeros_like(by_kv))
    for copy in swaps:
        copy.wait_recv()
    ours[...] = (ours[...].astype(F32) + came[...].astype(F32)).astype(BF16)
    out = pltpu.make_async_copy(ours, dw_out, out_sem)
    out.start()
    spread.finish()
    fold.finish()
    deal_q.finish()
    deal_kv.finish()
    for copy in swaps:
        copy.wait_send()
    out.wait()


def attend_back(length, dh, a, x, gains, head_gains, trig, q_raw, k_raw, window, lse, pack, xn, o, collective_id):
    count, model = dh.shape
    head = k_raw.shape[1]
    width = q_raw.shape[1]
    kv_part = pack.shape[2] - 2 * head
    deal = pltpu.SemaphoreType.DMA((3,))
    dw = pltpu.VMEM((model, head + kv_part), BF16)
    return pl.pallas_call(
        attend_back_kernel,
        out_shape=[
            jax.ShapeDtypeStruct((count, model), F32),
            jax.ShapeDtypeStruct((model, head + kv_part), BF16),
            jax.ShapeDtypeStruct((2, model), F32),
            jax.ShapeDtypeStruct((2, head), F32),
        ],
        in_specs=[pl.BlockSpec(memory_space=pltpu.SMEM)] + [vmem_spec()] * 10 + [any_spec()] * 3,
        out_specs=[vmem_spec(), any_spec(), vmem_spec(), vmem_spec()],
        scratch_shapes=[
            pltpu.VMEM((4 * count, model), BF16),
            pltpu.VMEM((count, width), BF16),
            pltpu.VMEM((count, width), BF16),
            pltpu.VMEM((window.shape[0], head), F32),
            pltpu.VMEM((window.shape[0], head), F32),
            pltpu.VMEM((4 * count + WINDOW, 2 * head), BF16),
            pltpu.VMEM((4 * count, head), BF16),
            pltpu.VMEM((count, 2 * head), BF16),
            pltpu.VMEM((4 * count, kv_part), BF16),
            pltpu.VMEM((model, width), BF16),
            pltpu.VMEM((model, width), BF16),
            pltpu.VMEM((model, 2 * head), BF16),
            pltpu.VMEM(xn.shape, BF16),
            pltpu.VMEM(o.shape, BF16),
            dw,
            dw,
            dw,
            pltpu.SemaphoreType.DMA((3, 4)),
            pltpu.SemaphoreType.DMA((2,)),
            *spread_spec(),
            *fold_spec(count, 2 * head),
            deal,
            deal,
            deal,
            deal,
            pltpu.SemaphoreType.DMA((2,)),
            pltpu.SemaphoreType.DMA((2,)),
            pltpu.SemaphoreType.DMA,
        ],
        compiler_params=params(collective_id, 48),
    )(length, dh, a, x, gains, head_gains, trig, q_raw, k_raw, window, lse, pack, xn, o)


def after(value, *others):
    return pl.pallas_call(
        lambda *refs: None,
        out_shape=jax.ShapeDtypeStruct(value.shape, value.dtype),
        in_specs=[any_spec()] * (1 + len(others)),
        out_specs=any_spec(),
        input_output_aliases={0: 0},
    )(value, *others)


def feed_forward(h, gains, weights, shared, layer):
    w_up, w_down, hidden = weights
    rows, gu, act, *shared = feed_up(h, gains[2:3], w_up, hidden, shared, 10 + layer)
    out, f = feed_down(h, gains[3:4], act, w_down, 12 + layer)
    return out, (h, rows, gu, act, f), shared


def scatter(member):
    return lax.psum_scatter(member, "wide", scatter_dimension=0, tiled=True)


def feed_backward(dy, gains, weights, kept, extra, layer):
    w_up, w_down, _ = weights
    h, rows, gu, act, f = kept
    dgu, d_down, dg3 = feed_back_up(dy, f, gains[3:4], gu, act, w_down, extra, 14 + layer)
    dh, d_up, dg2 = feed_back_down(dy, h, gains[2:3], dgu, rows, w_up, 16 + layer)
    return dh, (dg2, dg3), scatter(d_up), scatter(d_down)


def on_device(
    inputs, cotangent, lengths, norm_gains, head_gains, w_q, w_kv, w_o, w_gate_up, w_down
):
    core = lax.axis_index("section")
    narrow = lax.axis_index("narrow")
    n_narrow = lax.axis_size("narrow")
    is_zero = core == 0
    rows, model = inputs.shape[1], inputs.shape[2]
    block = w_q.shape[1]
    head_width = w_q.shape[2]
    n_wide = lax.axis_size("wide")
    hidden = w_down.shape[1]
    kv_part = w_kv.shape[2] // n_narrow

    def swap(value):
        return lax.ppermute(value, "section", [(0, 1), (1, 0)])

    def by_core(first, second):
        return jnp.where(is_zero, first, second)

    half = block // 2

    def by_halves(member):
        keep = lax.dynamic_slice_in_dim(member, core * half, half, 0)
        give = lax.dynamic_slice_in_dim(member, (1 - core) * half, half, 0)
        came = swap(give)
        return by_core(keep, came), by_core(came, keep)

    pad = -hidden % TILE
    kv_own = lax.dynamic_slice_in_dim(w_kv[0], narrow * kv_part, kv_part, 1)
    pack_width = 2 * head_width + kv_part
    gain_columns = jnp.zeros((block, GAIN_COLUMNS), BF16)
    gain_columns = lax.dynamic_update_slice(gain_columns, norm_gains[0].T, (0, 0))
    gain_columns = lax.dynamic_update_slice(gain_columns, head_gains[0].T, (0, 4))
    pack = by_halves(jnp.concatenate([w_q[0], w_o[0].T, kv_own, gain_columns], axis=1))

    gate_up = jnp.pad(w_gate_up[0], ((0, 0), (0, 0), (0, pad))).reshape(block, -1)
    down = jnp.pad(w_down[0].T, ((0, 0), (0, pad)))
    feed = by_halves(jnp.concatenate([gate_up, down], axis=1))
    padded = hidden + pad

    def gather(member):
        return lax.all_gather(member, ("wide", "section"), axis=0, tiled=True)

    pack = gather(jnp.concatenate(pack, axis=1))
    both = gather(feed[0])
    feeds = [
        (both, both, padded),
        (gather(feed[1][:, : 2 * padded]), gather(feed[1][:, 2 * padded :]), padded),
    ]
    full_width = pack_width + GAIN_COLUMNS
    packs = [pack[:, :full_width], pack[:, full_width:]]

    def gains_of(section):
        columns = packs[section][:, pack_width:].astype(F32)
        heads = columns.reshape(n_wide, block, -1)[:, : head_width // n_wide, 4:6]
        return columns[:, :4].T, heads.transpose(2, 0, 1).reshape(2, head_width)

    start = narrow * rows
    positions = start + jnp.arange(rows, dtype=jnp.int32)
    trig = tables(positions, head_width)
    length = lax.dynamic_index_in_dim(lengths[:, 0], core, 0, keepdims=False)

    x = lax.dynamic_index_in_dim(inputs, core, 0, keepdims=False)
    length_one = length.reshape(1)
    outs, kept, gains = [], [], []
    for section in range(2):
        layer_gains, head_gain = gains_of(section)
        gains.append((layer_gains, head_gain))
        own_pack = packs[section] if section == 0 else after(packs[1], kept[0][0][0])
        whole = gather_pack(own_pack, pack_width, 6)
        h, xn, q_raw, k_raw, window, lse, o, a, *shared = attend(
            length_one, x, layer_gains, head_gain, trig, whole, head_width, section == 0, 8 + section
        )
        kept_a = (h, a, x, q_raw, k_raw, window, lse, whole)
        x, kept_f, more = feed_forward(
            h, layer_gains, feeds[section], () if section == 0 else (xn, o), section
        )
        outs.append(x)
        kept.append((kept_a, kept_f, shared or more))

    real = (positions < length).astype(F32)[:, None]
    dy = lax.dynamic_index_in_dim(cotangent, core, 0, keepdims=False).astype(F32) * real
    dxs, gain_grads = [None, None], [None, None]
    up_sums, down_sums, attention_sums = [None, None], [None, None], [None, None]
    extra = None
    for section in (1, 0):
        kept_a, kept_f, (xn, o) = kept[section]
        layer_gains, head_gain = gains[section]
        if section == 0:
            dy = after(dy, down_sums[1])
        dh, dg23, up_sums[section], down_sums[section] = feed_backward(
            dy, layer_gains, feeds[section], kept_f, extra, section
        )
        if section == 0:
            dh = after(dh, up_sums[1])
        _, a, x, q_raw, k_raw, window, lse, whole = kept_a
        dx, extra, dg01, dhead = attend_back(
            length_one, dh, a, x, layer_gains, head_gain, trig, q_raw, k_raw, window, lse, whole, xn, o, 1
        )
        dxs[section] = dx
        head_row = jnp.pad(dhead.reshape(1, -1), ((0, 0), (0, model - dhead.size)))
        gain_grads[section] = jnp.concatenate([dg01, *dg23, head_row, jnp.zeros((3, model), F32)])
        dy = dx
    extra = after(extra, up_sums[0])
    split = down_sums[1].shape[1]
    attention_sums = (scatter(extra), down_sums[0][:, split:])
    down_sums[0] = down_sums[0][:, :split]

    def own_section(first, second):
        came = swap(by_core(second, first))
        stays = by_core(first, second)
        return by_core(stays, came).astype(F32), by_core(came, stays).astype(F32)

    grad_gate_up = jnp.stack(own_section(*up_sums), axis=1)[:, :, :hidden]
    grad_down = jnp.concatenate(own_section(*down_sums), axis=1)[:, :hidden].T
    by_qkv, by_out = own_section(*attention_sums)
    grad_q = by_qkv[:, :head_width]
    grad_o = by_out[:, :head_width].T
    grad_kv = lax.all_gather(
        by_qkv[:, head_width:].astype(BF16), "narrow", axis=1, tiled=True
    ).astype(F32)
    gain_sums = sum_gains(jnp.concatenate(gain_grads), n_wide, 7)
    gain_sums = lax.dynamic_slice_in_dim(gain_sums, core * 8, 8, 0)
    wide = lax.axis_index("wide")
    grad_norm = lax.dynamic_slice_in_dim(gain_sums[:4], wide * block, block, 1)
    grad_head = gain_sums[4, : 2 * head_width].reshape(2, head_width)
    head_block = head_width // n_wide
    grad_head = lax.dynamic_slice_in_dim(grad_head, wide * head_block, head_block, 1)

    def by_section(first, second):
        stays, came = by_core(first, second), swap(by_core(second, first))
        return jnp.stack([by_core(stays, came), by_core(came, stays)])

    return (
        by_section(*outs)[None],
        by_section(*dxs)[None],
        grad_norm[None],
        grad_head[None],
        grad_q[None],
        grad_kv[None],
        grad_o[None],
        grad_gate_up[None],
        grad_down[None],
    )


def solution(mesh):
    return jax.shard_map(
        on_device,
        mesh=mesh,
        in_specs=(
            P(None, ("wide", "narrow"), None),
            P(None, ("wide", "narrow"), None),
            P(None, "wide"),
            P("section", None, "wide"),
            P("section", None, "wide"),
            P("section", "wide", "narrow"),
            P("section", "wide", None),
            P("section", "narrow", "wide"),
            P("section", "wide", None, "narrow"),
            P("section", "narrow", "wide"),
        ),
        out_specs=(
            P("section", None, ("wide", "narrow"), None),
            P("section", None, ("wide", "narrow"), None),
            P("section", None, "wide"),
            P("section", None, "wide"),
            P("section", "wide", "narrow"),
            P("section", "wide", None),
            P("section", "narrow", "wide"),
            P("section", "wide", None, "narrow"),
            P("section", "narrow", "wide"),
        ),
        check_vma=False,
    )
```

time: 780 us -> 720 us (0.923)
  Pallas kernels: 427 us -> 511 us
  local copies, waits for them, and re-layouts: 155 us -> 80.6 us
  matrix products: 40.6 us -> 0 us
  other arithmetic: 57.3 us -> 28 us
    pallas_call x9, Pallas kernels: 219 us -> 304 us  [the longest x2 92.5 us: attend_back(): pl.pallas_call(attend_back_kernel, out_shape=[jax.ShapeDtypeStruct((count...]
    dot_general x30 -> x0, matrix products: 40.6 us -> none  [the longest x18 26.7 us: dot(): lax.dot_general(a, b, ((dims[0], dims[1]), ((), ())), preferred_element_t...]
    reshape x16 -> x2, local copies, waits for them, and re-layouts: 36.3 us -> 0.17 us  [gains_of(): return (columns[:, :4].T, heads.transpose(2, 0, 1).reshape(2, head_width))]
    unnamed x346 -> x146, local copies, waits for them, and re-layouts: 81.3 us -> 63.1 us
    reduce_scatter x5, waiting for transfers between devices: 18.3 us -> 28.5 us  [scatter(): return lax.psum_scatter(member, 'wide', scatter_dimension=0, tiled=True)]
    dot_general x2 -> x0, local copies, waits for them, and re-layouts: 9.11 us -> none  [dot(): lax.dot_general(a, b, ((dims[0], dims[1]), ((), ())), preferred_element_t...]
    add x7 -> x0, other arithmetic: 7.98 us -> none  [the longest x1 7.5 us: on_device(): pack_sum = by_core(*packs) + swap(by_core(*packs[::-1]))]
    select_n x10 -> x9, other arithmetic: 16.7 us -> 12 us  [by_core(): return jnp.where(is_zero, first, second)]
  transfers between devices with their start and end apart: 19 -> 16, of which waited for: 6 -> 6; matrix products, arithmetic and copies ran while one was open for 25% -> 6% of each run, Pallas kernels for 47% -> 63%
where the time goes in v3:
time: 720 us; the launch traced here: 713 us
  Pallas kernels  511 us (71%)
  local copies, waits for them, and re-layouts  80.6 us (11%)
  waiting for transfers between devices  66.8 us (9%)
  other arithmetic  28 us (4%)
  between operations  15 us (2%)
  blocking collectives  9.09 us (1%)
    pallas_call x2, Pallas kernels, attend_back(): pl.pallas_call(attend_back_kernel, out_shape=[jax.ShapeDtypeStruct((count...  92.5 us
    pallas_call x2, Pallas kernels, feed_back_down(): pl.pallas_call(back_down_kernel, out_shape=[jax.ShapeDtypeStruct((count,...  85.1 us
    pallas_call x2, Pallas kernels, feed_up(): pl.pallas_call(up_kernel, out_shape=shapes, in_specs=[vmem_spec(), vmem_s...  76.9 us
    pallas_call x2, Pallas kernels, feed_back_up(): pl.pallas_call(back_up_kernel, out_shape=[jax.ShapeDtypeStruct(gu.shape,...  76.2 us
    unnamed x146, local copies, waits for them, and re-layouts  63.1 us
    pallas_call x2, Pallas kernels, gather_pack(): pl.pallas_call(pack_kernel, out_shape=jax.ShapeDtypeStruct((4, pack.shape...  58.2 us
    pallas_call x2, Pallas kernels, attend(): pl.pallas_call(attend_kernel, out_shape=shapes, in_specs=[pl.BlockSpec(me...  56.6 us
    pallas_call x2, Pallas kernels, feed_down(): pl.pallas_call(down_kernel, out_shape=[jax.ShapeDtypeStruct((count, model...  45.8 us
  transfers between devices with their start and end apart: 16, of which 6 were waited for; matrix products, arithmetic and copies ran while one was open for 6% of the time, Pallas kernels for 63%

profile of v3, /device:TPU:0, one launch (start us, length us, event | category | flops | bytes accessed | tf_op | source)
XLA Modules:
  0.0 713.3 jit_solution(8181556051538741317)
XLA Ops:
  13.6 1.3 collective-permute-done
  16.9 1.6 pad.16
  20.5 3.0 collective-permute-done.1
  23.5 1.7 broadcast_select_fusion
  29.5 31.6 %all-gather.5.cloned.1.call-done = bf16[1152,1536]{1,0:T(8,128)(2,1)} async-done(((bf16[144,1536]{1,0:T(8,128)(2,1)}), bf16[1152,1536]{1,0:T(8,128)(2,1)}) %all-gather.5.cloned.1.call-update) | async-done | bytes 3538960 | tf_op jit(solution)/shard_map/all_gather | solution.py:1281
  65.7 3.4 fusion.8
  69.1 29.5 %shard_map.169.pack_ref = bf16[4,1152,640]{2,1,0:T(8,128)(2,1)S(1)} custom-call(bf16[1152,768]{1,0:T(8,128)(2,1)S(1)} %get-tuple-element.139.p_ref), custom_call_target="tpu_custom_call" | custom-call | tf_op jit(solution)/shard_map/pallas_call | solution.py:728
  98.6 2.4 copy-done.2
  101.8 39.1 %shard_map.170 = (f32[256,1152]{1,0:T(8,128)S(1)}, bf16[256,1152]{1,0:T(8,128)(2,1)}, f32[256,1024]{1,0:T(8,128)S(1)}, f32[256,256]{1,0:T(8,128)S(1)}, bf16[768,...) custom-call(s32[1]{0:T(128)} %bitcast.length_ref, ...), custom_call_target="tpu_custom_call" | custom-call | tf_op jit(solution)/shard_map/pallas_call | solution.py:999
  142.0 1.4 copy-done.19
  148.1 1.5 copy-done.8
  149.6 28.7 %shard_map.174.pack_ref = bf16[4,1152,640]{2,1,0:T(8,128)(2,1)S(1)} custom-call(bf16[1152,768]{1,0:T(8,128)(2,1)S(1)} %copy-done.8), custom_call_target="tpu_custom_call" | custom-call | tf_op jit(solution)/shard_map/pallas_call | solution.py:728
  178.3 2.5 copy-done.3
  182.8 30.4 %shard_map.171 = (bf16[1024,1152]{1,0:T(8,128)(2,1)S(1)}, bf16[1024,3584]{1,0:T(8,128)(2,1)}, bf16[1024,1792]{1,0:T(8,128)(2,1)}) custom-call(f32[256,1152]{1,0:T(8,128)S(1)} %copy-done.5, f32[1,1152]{1,0:T(1,128)S(1)} %get-tuple-element.152.gain_ref, bf16[1152,5376]{1,0:T(8,128)(2,1)} %all-gather.7.cloned.1.call-done.w_ref), custom_call_target="tpu_custom_call" | custom-call | tf_op jit(solution)/shard_map/pallas_call | solution.py:350
  213.2 1.4 copy-done.17
  214.7 2.1 copy-done.9
  216.8 24.3 %shard_map.172 = (bf16[256,1152]{1,0:T(8,128)(2,1)S(1)}, f32[256,1152]{1,0:T(8,128)S(1)}) custom-call(f32[256,1152]{1,0:T(8,128)S(1)} %copy-done.5, f32[1,1152]{1,0:T(1,128)S(1)} %get-tuple-element.153.gain_ref, bf16[1024,1792]{1,0:T(8,128)(2,1)S(1)} %copy-done.9, bf16[1152,5376]{1,0:T(8,128)(2,1)} %all-gather.7.cloned.1.call-done.w_ref), custom_call_target="tpu_custom_call" | custom-call | tf_op jit(solution)/shard_map/pallas_call | solution.py:407
  242.2 17.5 %shard_map.175 = (f32[256,1152]{1,0:T(8,128)S(1)}, bf16[256,1152]{1,0:T(8,128)(2,1)S(1)}, f32[256,1024]{1,0:T(8,128)S(1)}, f32[256,256]{1,0:T(8,128)S(1)}, bf16[...) custom-call(s32[1]{0:T(128)} %bitcast.length_ref, ...), custom_call_target="tpu_custom_call" | custom-call | tf_op jit(solution)/shard_map/pallas_call | solution.py:999
  265.7 1.5 copy-done.38
  268.3 46.4 %shard_map.176 = (bf16[1024,1152]{1,0:T(8,128)(2,1)S(1)}, bf16[1024,3584]{1,0:T(8,128)(2,1)}, bf16[1024,1792]{1,0:T(8,128)(2,1)}, bf16[1024,1152]{1,0:T(8,128)(2,1)}, bf16[1024,256]{1,0:T(8,128)(2,1)S(1)}) custom-call(f32[256,1152]{1,0:T(8,128)S(1)} %get-tuple-element.60.h_ref, f32[1,1152]{1,0:T(1,128)S(1)} %get-tuple-element.150.gain_ref, ...), custom_call_target="tpu_custom_call" | custom-call | tf_op jit(solution)/shard_map/pallas_call | solution.py:350
  314.7 1.4 copy-done.18
  316.9 2.2 copy-done.7
  319.1 2.0 copy-done.10
  321.1 21.5 %shard_map.177 = (bf16[256,1152]{1,0:T(8,128)(2,1)S(1)}, f32[256,1152]{1,0:T(8,128)S(1)}) custom-call(f32[256,1152]{1,0:T(8,128)S(1)} %get-tuple-element.60.h_ref, f32[1,1152]{1,0:T(1,128)S(1)} %get-tuple-element.151.gain_ref, bf16[1024,1792]{1,0:T(8,128)(2,1)S(1)} %copy-done.10, bf16[1152,1792]{1,0:T(8,128)(2,1)S(1)} %copy-done.7), custom_call_target="tpu_custom_call" | custom-call | tf_op jit(solution)/shard_map/pallas_call | solution.py:407
  343.4 37.8 %shard_map.178 = (bf16[1024,3584]{1,0:T(8,128)(2,1)}, bf16[1152,896]{1,0:T(8,128)(2,1)S(1)}, f32[1,1152]{1,0:T(1,128)S(1)}) custom-call(f32[256,1152]{1,0:T(8,128)S(1)} %convert_multiply_fusion.dy_ref, f32[256,1152]{1,0:T(8,128)S(1)} %get-tuple-element.65.f_ref, f32[1,1152]{1,0:T(1,128)S(1)} %get-tuple-element.151.gain_ref, ...), custom_call_target="tpu_custom_call" | custom-call | tf_op jit(solution)/shard_map/pallas_call | solution.py:558
  381.2 1.3 copy-done.22
  382.6 42.7 %shard_map.179 = (f32[256,1152]{1,0:T(8,128)}, bf16[1152,1792]{1,0:T(8,128)(2,1)}, f32[1,1152]{1,0:T(1,128)}) custom-call(f32[256,1152]{1,0:T(8,128)} %copy-done.11, f32[256,1152]{1,0:T(8,128)} %copy-done.12, f32[1,1152]{1,0:T(1,128)} %copy-done.52, bf16[1024,3584]{1,0:T(8,128)(2,1)} %get-tuple-element.67.dgu_ref, bf16[1024,1152]{1,0:T(8,128)(2,1)} %copy-done.18, ...), custom_call_target="tpu_custom_call" | custom-call | tf_op jit(solution)/shard_map/pallas_call | solution.py:652
  430.6 46.1 %shard_map.180 = (f32[256,1152]{1,0:T(8,128)S(1)}, bf16[1152,384]{1,0:T(8,128)(2,1)S(1)}, f32[2,1152]{1,0:T(2,128)S(1)}, f32[2,256]{1,0:T(2,128)S(1)}) custom-call(s32[1]{0:T(128)} %bitcast.length_ref, f32[256,1152]{1,0:T(8,128)} %get-tuple-element.69.dh_ref, f32[256,1152]{1,0:T(8,128)} %copy-done.26, bf16[256,1152]{1,0:T(8,128)(2,1)S(1)} %get-tuple-element.59.x_ref, ...), custom_call_target="tpu_custom_call" | custom-call | tf_op jit(solution)/shard_map/pallas_call | solution.py:1166
  479.4 1.3 copy-done.6
  480.6 1.2 copy-done.32
  481.8 38.4 %shard_map.182 = (bf16[1024,3584]{1,0:T(8,128)(2,1)}, bf16[1152,1280]{1,0:T(8,128)(2,1)S(1)}, f32[1,1152]{1,0:T(1,128)S(1)}) custom-call(f32[256,1152]{1,0:T(8,128)S(1)} %copy-done.6, f32[256,1152]{1,0:T(8,128)S(1)} %copy-done.24, f32[1,1152]{1,0:T(1,128)S(1)} %get-tuple-element.153.gain_ref, bf16[1024,3584]{1,0:T(8,128)(2,1)} %get-tuple-element.80.gu_ref, ...), custom_call_target="tpu_custom_call" | custom-call | tf_op jit(solution)/shard_map/pallas_call | solution.py:558
  520.2 1.6 copy-done.16
  521.9 42.5 %shard_map.183 = (f32[256,1152]{1,0:T(8,128)}, bf16[1152,1792]{1,0:T(8,128)(2,1)}, f32[1,1152]{1,0:T(1,128)}) custom-call(f32[256,1152]{1,0:T(8,128)} %shard_map.181.dy_ref, f32[256,1152]{1,0:T(8,128)} %copy-done.4, f32[1,1152]{1,0:T(1,128)} %copy-done.51, bf16[1024,3584]{1,0:T(8,128)(2,1)} %get-tuple-element.82.dgu_ref, bf16[1024,1152]{1,0:T(8,128)(2,1)} %copy-done.17, ...), custom_call_target="tpu_custom_call" | custom-call | tf_op jit(solution)/shard_map/pallas_call | solution.py:652
  566.3 2.2 collective-permute-done.2
  570.8 1.2 copy-done.28
  575.2 46.3 %shard_map.185 = (f32[256,1152]{1,0:T(8,128)S(1)}, bf16[1152,384]{1,0:T(8,128)(2,1)S(1)}, f32[2,1152]{1,0:T(2,128)S(1)}, f32[2,256]{1,0:T(2,128)S(1)}) custom-call(s32[1]{0:T(128)} %bitcast.length_ref, f32[256,1152]{1,0:T(8,128)} %shard_map.184.dh_ref, f32[256,1152]{1,0:T(8,128)} %copy-done.25, bf16[256,1152]{1,0:T(8,128)(2,1)S(1)} %copy-done.14, ...), custom_call_target="tpu_custom_call" | custom-call | tf_op jit(solution)/shard_map/pallas_call | solution.py:1166
  625.1 20.0 %shard_map.186 = f32[16,1152]{1,0:T(8,128)S(1)} custom-call(f32[16,1152]{1,0:T(8,128)S(1)} %concatenate.23.g_ref), custom_call_target="tpu_custom_call" | custom-call | tf_op jit(solution)/shard_map/pallas_call | solution.py:839
  646.5 1.9 broadcast_select_fusion.10
  648.6 10.8 %reduce-scatter.10.cloned.1.call-done.refs_1_ = bf16[288,1792]{1,0:T(8,128)(2,1)} async-done(((bf16[1152,1792]{1,0:T(8,128)(2,1)}), bf16[288,1792]{1,0:T(8,128)(2,1)}) %reduce-scatter.10.cloned.1.call-update) | async-done | bytes 1032208 | tf_op jit(solution)/shard_map/reduce_scatter | solution.py:1228
  659.4 2.3 broadcast_select_fusion.2
  661.7 1.5 select_bitcast_fusion.1
  663.2 1.6 maximum_bitcast_fusion
  664.8 1.2 broadcast_select_fusion.9
  666.0 1.4 convert_bitcast_fusion
  668.2 1.5 select_bitcast_fusion.3
  669.7 17.6 %reduce-scatter.12.cloned.1.call-done = bf16[288,384]{1,0:T(8,128)(2,1)} async-done(((bf16[1152,384]{1,0:T(8,128)(2,1)}), bf16[288,384]{1,0:T(8,128)(2,1)}) %reduce-scatter.12.cloned.1.call-update) | async-done | bytes 221200 | tf_op jit(solution)/shard_map/reduce_scatter | solution.py:1228
  688.7 5.2 copy.47
  695.6 9.1 %all_gather.19 = bf16[288,512]{1,0:T(8,128)(2,1)S(1)} all-gather(bf16[288,128]{1,0:T(8,128)(2,1)S(1)} %slice.119), channel_id=1, replica_groups=mesh['section'=2,'wide'=4,'narrow'=4] {'narrow'}, dimensions={1}, use_global_device_ids=true | all-gather | bytes 368640 | tf_op jit(solution)/shard_map/all_gather | solution.py:1358
  (222 shorter events, 63.2 us)
Async XLA Ops:
  7.2 22.0 %copy-start = (bf16[2,256,1152]{2,1,0:T(8,128)(2,1)S(1)}, bf16[2,256,1152]{2,1,0:T(8,128)(2,1)}, u32[]{:S(2)}) copy-start(bf16[2,256,1152]{2,1,0:T(8,128)(2,1)} %param.10) | copy-start | bytes 3538948
  7.2 9.6 %copy-start.59 = (bf16[1,288,2,1728]{3,2,1,0:T(2,128)(2,1)S(1)}, bf16[1,288,2,1728]{3,2,1,0:T(2,128)(2,1)}, u32[]{:S(2)}) copy-start(bf16[1,288,2,1728]{3,2,1,0:T(2,128)(2,1)} %param.18) | copy-start | bytes 5971972
  7.2 53.9 %all-gather.5.cloned.1.call-start = ((), (), s32[]{:S(2)}) async-start(), calls=%async_computation.5 | async-start | bytes 3981312 | tf_op jit(solution)/shard_map/all_gather | solution.py:1281
  13.2 1.8 collective-permute-start
  16.8 165.9 %all-gather.7.cloned.1.call-start = ((), (), s32[]{:S(2)}) async-start(), calls=%async_computation.6 | async-start | bytes 13934592 | tf_op jit(solution)/shard_map/all_gather | solution.py:1281
  20.0 3.4 collective-permute-start.1
  25.2 240.5 %all-gather.9.cloned.1.call-start = ((), (), s32[]{:S(2)}) async-start(), calls=%async_computation.7 | async-start | bytes 9289728 | tf_op jit(solution)/shard_map/all_gather | solution.py:1281
  25.2 2.2 copy-start.66
  26.4 290.6 %all-gather.11.cloned.1.call-start = ((), (), s32[]{:S(2)}) async-start(), calls=%async_computation.8 | async-start | bytes 4644864 | tf_op jit(solution)/shard_map/all_gather | solution.py:1281
  27.3 2.0 copy-start.63
  27.3 451.4 %reduce-scatter.6.cloned.1.call-start = ((), (), s32[]{:S(2)}) async-start(), calls=%async_computation.9 | async-start | bytes 2580480 | tf_op jit(solution)/shard_map/reduce_scatter | solution.py:1228
  29.3 72.5 %copy-start.13 = (bf16[256,1152]{1,0:T(8,128)(2,1)}, bf16[256,1152]{1,0:T(8,128)(2,1)S(1)}, u32[]{:S(2)}) copy-start(bf16[256,1152]{1,0:T(8,128)(2,1)S(1)} %dynamic-slice_bitcast_fusion.x_ref) | copy-start | bytes 1769476
  29.5 313.9 %copy-start.11 = (f32[256,1152]{1,0:T(8,128)}, f32[256,1152]{1,0:T(8,128)S(1)}, u32[]{:S(2)}) copy-start(f32[256,1152]{1,0:T(8,128)S(1)} %convert_multiply_fusion.dy_ref) | copy-start | bytes 3538948
  98.6 2.4 copy-start.2
  148.1 1.5 copy-start.8
  149.6 33.2 %copy-start.5 = (f32[256,1152]{1,0:T(8,128)S(1)}, f32[256,1152]{1,0:T(8,128)}, u32[]{:S(2)}) copy-start(f32[256,1152]{1,0:T(8,128)} %copy-done.4) | copy-start | bytes 3538948
  178.3 2.5 copy-start.3
  181.9 31.3 %copy-start.51 = (f32[1,1152]{1,0:T(1,128)}, f32[1,1152]{1,0:T(1,128)S(1)}, u32[]{:S(2)}) copy-start(f32[1,1152]{1,0:T(1,128)S(1)} %get-tuple-element.152.gain_ref) | copy-start | bytes 13828
  182.7 83.0 %copy-start.52 = (f32[1,1152]{1,0:T(1,128)}, f32[1,1152]{1,0:T(1,128)S(1)}, u32[]{:S(2)}) copy-start(f32[1,1152]{1,0:T(1,128)S(1)} %get-tuple-element.150.gain_ref) | copy-start | bytes 13828
  182.7 59.4 %slice-start = ((s8[5898240]{0:T(1024)(128)(4,1)}), s8[4194304]{0:T(1024)(128)(4,1)S(1)}, s32[]{:S(2)}) async-start(s8[5898240]{0:T(1024)(128)(4,1)} %bitcast.84), calls=%async_computation.14 | async-start | bytes 8388608
  214.7 2.1 copy-start.9
  216.8 25.4 %slice-start.1 = ((s8[5898240]{0:T(1024)(128)(4,1)}), s8[1703936]{0:T(1024)(128)(4,1)S(1)}, s32[]{:S(2)}) async-start(s8[5898240]{0:T(1024)(128)(4,1)} %bitcast.84), calls=%async_computation.15 | async-start | bytes 3407872
  265.6 51.3 %copy-start.12 = (f32[256,1152]{1,0:T(8,128)}, f32[256,1152]{1,0:T(8,128)S(1)}, u32[]{:S(2)}) copy-start(f32[256,1152]{1,0:T(8,128)S(1)} %get-tuple-element.60.h_ref) | copy-start | bytes 3538948
  265.7 1.5 copy-start.38
  316.9 2.2 copy-start.7
  319.1 2.0 copy-start.10
  382.5 187.2 %reduce-scatter.8.cloned.1.call-start = ((), (), s32[]{:S(2)}) async-start(), calls=%async_computation.10 | async-start | bytes 5160960 | tf_op jit(solution)/shard_map/reduce_scatter | solution.py:1228
  425.3 221.2 %reduce-scatter.14.cloned.1.call-start = ((), (), s32[]{:S(2)}) async-start(), calls=%async_computation.13 | async-start | bytes 3686400 | tf_op jit(solution)/shard_map/reduce_scatter | solution.py:1228
  477.7 1.7 copy-start.24
  520.2 1.6 copy-start.16
  521.8 137.6 %reduce-scatter.10.cloned.1.call-start = ((), (), s32[]{:S(2)}) async-start(), calls=%async_computation.11 | async-start | bytes 5160960 | tf_op jit(solution)/shard_map/reduce_scatter | solution.py:1228
  564.4 122.9 %reduce-scatter.12.cloned.1.call-start = ((), (), s32[]{:S(2)}) async-start(), calls=%async_computation.12 | async-start | bytes 1105920 | tf_op jit(solution)/shard_map/reduce_scatter | solution.py:1228
  566.3 2.2 collective-permute-start.2
  621.6 3.4 copy-start.15
  621.6 2.2 copy-start.57
  621.6 2.2 copy-start.58
  622.7 2.3 copy-start.64
  622.7 2.3 copy-start.65
  622.7 23.7 %copy-start.55 = (bf16[288,896]{1,0:T(8,128)(2,1)S(1)}, bf16[288,896]{1,0:T(8,128)(2,1)}, u32[]{:S(2)}) copy-start(bf16[288,896]{1,0:T(8,128)(2,1)} %reduce-scatter.6.cloned.1.call-done.refs_1_) | copy-start | bytes 1548292
  622.7 39.0 %collective-permute-start.3 = (f32[256,1152]{1,0:T(8,128)}, f32[256,1152]{1,0:T(8,128)}, u32[]{:S(2)}, u32[]{:S(2)}) collective-permute-start(f32[256,1152]{1,0:T(8,128)} %broadcast_select_fusion.4), channel_id=1, source_target_pairs={{0,16},{16,0},{1,17},{17,1},{2,18},{18,2},{3,19},{19,3},{4,20},{20... | collective-permute-start | bytes 3538952 | tf_op jit(solution)/shard_map/ppermute | solution.py:1254
  648.4 16.4 %collective-permute-start.6 = (bf16[288,896]{1,0:T(8,128)(2,1)}, bf16[288,896]{1,0:T(8,128)(2,1)}, u32[]{:S(2)}, u32[]{:S(2)}) collective-permute-start(bf16[288,896]{1,0:T(8,128)(2,1)} %broadcast_select_fusion.10), channel_id=1, source_target_pairs={{0,16},{16,0},{1,17},{17,1},{2,18},{18,2},{3,19},{19,3},{4,20},{20... | collective-permute-start | bytes 1548296 | tf_op jit(solution)/shard_map/ppermute | solution.py:1254
  661.7 5.7 collective-permute-start.5
  663.2 1.6 copy-start.56
  666.0 1.6 copy-start.53
  666.0 2.3 copy-start.54
  688.3 5.6 collective-permute-start.4
  688.7 5.2 copy-start.62
  688.7 17.7 %copy-start.1 = (bf16[2,256,1152]{2,1,0:T(8,128)(2,1)S(1)}, bf16[2,256,1152]{2,1,0:T(8,128)(2,1)}, u32[]{:S(2)}) copy-start(bf16[2,256,1152]{2,1,0:T(8,128)(2,1)} %param.10) | copy-start | bytes 3538948
  (37 other events, 38.3 us)
Sparse Core Ops, SparseCore 0:
  16.9 44.1 all-gather.4
  63.3 114.3 all-gather.6
  179.4 79.6 all-gather.8
  260.5 45.0 all-gather.10
  382.6 41.0 reduce-scatter.5
  426.0 75.0 reduce-scatter.7
  522.0 54.6 reduce-scatter.13
  579.1 80.2 reduce-scatter.9
  661.9 25.4 reduce-scatter.11

commit v4 on v3

--- a/solution.py
+++ b/solution.py
@@ -106,6 +106,8 @@
 
 
 def columns_of(tile, width, offset=0):
+    if isinstance(tile, int):
+        return pl.ds(tile * width + offset, width)
     return pl.ds(pl.multiple_of(tile * width + offset, 128), width)
 
 
@@ -296,7 +298,7 @@
     def one(block, at):
         here = rows_of(block, count)
 
-        def tile(j, _):
+        def tile(j):
             left = rows[here, :]
             gate = nn(left, w[:, columns_of(j, TILE)])
             up = nn(left, w[:, columns_of(j, TILE, hidden)])
@@ -304,9 +306,9 @@
             gu[here, columns_of(j, TILE)] = gate.astype(BF16)
             gu[here, columns_of(j, TILE, hidden)] = up.astype(BF16)
             act[here, columns_of(j, TILE)] = (0.5 * gate * (1.0 + inner) * up).astype(BF16)
-            return 0
-
-        lax.fori_loop(0, hidden // TILE, tile, 0)
+
+        for j in range(hidden // TILE):
+            tile(j)
         copies = [
             pltpu.make_async_copy(ref.at[here], out.at[here], store.at[k, at])
             for k, (ref, out) in enumerate(((gu, gu_out), (act, act_out), (rows, rows_out)))
@@ -362,7 +364,7 @@
             *spread_spec(),
             *(share_spec(count, model, shared[1].shape[1] // 4) if shared else []),
         ],
-        compiler_params=params(collective_id, 48),
+        compiler_params=params(collective_id, 60),
     )(h, gain, w_gu, *shared)
 
 
@@ -419,7 +421,7 @@
             pltpu.SemaphoreType.DMA((5,)),
             *fold_spec(count, model),
         ],
-        compiler_params=params(collective_id, 40),
+        compiler_params=params(collective_id, 60),
     )(h, gain, act, w_dt)
 
 
@@ -454,12 +456,27 @@
 
 
 def column_tiles(width):
-    return [(first, min(TILE, width - first)) for first in range(0, width, TILE)]
+    return [(first, min(2 * TILE, width - first)) for first in range(0, width, 2 * TILE)]
+
+
+def gate_up_gradient(df, here, w, gu, hidden):
+    for j in range(hidden // TILE):
+        dact = nn(df[here, :], w[:, columns_of(j, TILE)])
+        gate = gu[here, columns_of(j, TILE)].astype(F32)
+        up = gu[here, columns_of(j, TILE, hidden)].astype(F32)
+        square = gate * gate
+        inner = jnp.tanh(GELU_SCALE * gate * (1.0 + GELU_CUBE * square))
+        half = 0.5 * (1.0 + inner)
+        slope = half + 0.5 * GELU_SCALE * gate * (1.0 - inner * inner) * (
+            1.0 + 3.0 * GELU_CUBE * square
+        )
+        gu[here, columns_of(j, TILE)] = (dact * up * slope).astype(BF16)
+        gu[here, columns_of(j, TILE, hidden)] = (dact * gate * half).astype(BF16)
 
 
 def back_up_kernel(dy_ref, f_ref, gain_ref, gu_ref, act_ref, w_ref, *refs):
-    if len(refs) == 18:
-        extra_ref, *refs = refs
+    if len(refs) == 19:
+        extra_ref, _, *refs = refs
     else:
         extra_ref = None
     (
@@ -505,21 +522,7 @@
         for copy in arrivals[at]:
             copy.wait()
 
-        def tile(j, _):
-            dact = nn(df[here, :], w[:, columns_of(j, TILE)])
-            gate = gu[here, columns_of(j, TILE)].astype(F32)
-            up = gu[here, columns_of(j, TILE, hidden)].astype(F32)
-            square = gate * gate
-            inner = jnp.tanh(GELU_SCALE * gate * (1.0 + GELU_CUBE * square))
-            half = 0.5 * (1.0 + inner)
-            slope = half + 0.5 * GELU_SCALE * gate * (1.0 - inner * inner) * (
-                1.0 + 3.0 * GELU_CUBE * square
-            )
-            gu[here, columns_of(j, TILE)] = (dact * up * slope).astype(BF16)
-            gu[here, columns_of(j, TILE, hidden)] = (dact * gate * half).astype(BF16)
-            return 0
-
-        lax.fori_loop(0, hidden // TILE, tile, 0)
+        gate_up_gradient(df, here, w, gu, hidden)
         copy = pltpu.make_async_copy(gu.at[here], dgu_out.at[here], store.at[at])
         copy.start()
         return copy
@@ -550,16 +553,138 @@
         extra.wait()
 
 
+def turn_kernel(
+    h_ref, gain_ref, dy_ref, act_ref, w_ref, gu_ref, x_out, dgu_out, dw_out, dgain_out,
+    act, w, parts, df, gu, ours, theirs, came, load, store, land, passing, fold_send, fold_recv, send, recv,
+    swap_send, swap_recv, out_sems,
+):
+    count, model = h_ref.shape
+    hidden = act.shape[1]
+    me, nx, ny = neighbours()
+    core = lax.axis_index("section")
+    far = jnp.bitwise_xor(me, 3)
+    met = greet({"narrow": nx}, {"narrow": ny}, {"section": 1 - core})
+    first = w_ref.shape[1] - hidden
+    weights = pltpu.make_async_copy(w_ref.at[:, pl.ds(first, hidden)], w, load.at[0, 0])
+    weights.start()
+    blocks = (far, nx, ny, me)
+    for at, block in enumerate(blocks):
+        here = rows_of(block, count)
+        pltpu.make_async_copy(act_ref.at[here], act.at[here], load.at[1, at]).start()
+    for at, block in enumerate(blocks):
+        here = rows_of(block, count)
+        pltpu.make_async_copy(gu_ref.at[here], gu.at[here], load.at[2, at]).start()
+
+    def here_now(row, at):
+        here = rows_of(blocks[at], count)
+        src, dst = ((act_ref, act), (gu_ref, gu))[row - 1]
+        pltpu.make_async_copy(src.at[here], dst.at[here], load.at[row, at]).wait()
+        return here
+
+    fold = Fold(halves_of(parts, count), land, passing, fold_send, fold_recv)
+    weights.wait()
+    met()
+
+    def part(at):
+        here = here_now(1, at)
+        return here, nt(act[here, :], w[...])
+
+    here, value = part(0)
+    parts[here, :] = value.astype(BF16)
+    fold.send_far()
+    for at in (1, 2):
+        here, value = part(at)
+        parts[here, :] = value.astype(BF16)
+    fold.send_near()
+    _, value = part(3)
+    fold.pass_on()
+    f = fold.total(value)
+    gain = gain_ref[...]
+    by_value, by_gain = normed_gradient(f, gain, dy_ref[...])
+    df[rows_of(me, count), :] = by_value.astype(BF16)
+    spread = Spread(halves_of(df, count), send, recv)
+    spread.start()
+    dgain_out[...] = by_gain
+    x_out[...] = (h_ref[...] + f * inverse_rms(f) * gain).astype(BF16)
+
+    def one(at):
+        here = here_now(2, at)
+        gate_up_gradient(df, here, w, gu, hidden)
+        copy = pltpu.make_async_copy(gu.at[here], dgu_out.at[here], store.at[at])
+        copy.start()
+        return copy
+
+    copies = [one(3)]
+    spread.pass_on()
+    spread.x_here()
+    copies.append(one(1))
+    spread.y_here()
+    copies.append(one(2))
+    spread.far_here()
+    copies.append(one(0))
+
+    def make(mine, first, width):
+        side = core if mine else 1 - core
+        start = pl.multiple_of(side * (hidden // 2) + first, 128)
+        return tn(df[...], act[:, pl.ds(start, width)])
+
+    sends, stores = swap_sum(
+        make, column_tiles(hidden // 2), ours, theirs, came, swap_send, swap_recv, dw_out, out_sems
+    )
+    spread.finish()
+    fold.finish()
+    for copy in sends:
+        copy.wait_send()
+    for copy in copies + stores:
+        copy.wait()
+
+
+def feed_turn(h, gain, dy, act, w_dt, gu, collective_id):
+    count, model = h.shape
+    total, hidden = act.shape
+    tiles = pltpu.SemaphoreType.DMA((len(column_tiles(hidden // 2)),))
+    dw = pltpu.VMEM((model, hidden // 2), BF16)
+    return pl.pallas_call(
+        turn_kernel,
+        out_shape=[
+            jax.ShapeDtypeStruct((count, model), BF16),
+            jax.ShapeDtypeStruct(gu.shape, BF16),
+            jax.ShapeDtypeStruct((model, hidden // 2), BF16),
+            jax.ShapeDtypeStruct((1, model), F32),
+        ],
+        in_specs=[vmem_spec()] * 3 + [any_spec()] * 3,
+        out_specs=[vmem_spec(), any_spec(), any_spec(), vmem_spec()],
+        scratch_shapes=[
+            pltpu.VMEM(act.shape, BF16),
+            pltpu.VMEM((model, hidden), BF16),
+            pltpu.VMEM((total, model), BF16),
+            pltpu.VMEM((total, model), BF16),
+            pltpu.VMEM(gu.shape, BF16),
+            dw,
+            dw,
+            dw,
+            pltpu.SemaphoreType.DMA((3, 4)),
+            pltpu.SemaphoreType.DMA((4,)),
+            *fold_spec(count, model),
+            *spread_spec(),
+            tiles,
+            tiles,
+            tiles,
+        ],
+        compiler_params=params(collective_id, 60),
+    )(h, gain, dy, act, w_dt, gu)
+
+
 def feed_back_up(dy, f, gain, gu, act, w_dt, extra, collective_id):
     count, model = dy.shape
     total, hidden = act.shape
     tiles = len(column_tiles(hidden // 2))
-    extras = () if extra is None else (extra,)
+    extras = () if extra is None else extra
     return pl.pallas_call(
         back_up_kernel,
         out_shape=[
             jax.ShapeDtypeStruct(gu.shape, BF16),
-            jax.ShapeDtypeStruct((model, hidden // 2 + sum(e.shape[1] for e in extras)), BF16),
+            jax.ShapeDtypeStruct((model, hidden // 2 + sum(e.shape[1] for e in extras[:1])), BF16),
             jax.ShapeDtypeStruct((1, model), F32),
         ],
         in_specs=[vmem_spec()] * 3 + [any_spec()] * (3 + len(extras)),
@@ -579,7 +704,7 @@
             pltpu.SemaphoreType.DMA((tiles,)),
             pltpu.SemaphoreType.DMA((tiles,)),
         ],
-        compiler_params=params(collective_id, 48),
+        compiler_params=params(collective_id, 60),
     )(dy, f, gain, gu, act, w_dt, *extras)
 
 
@@ -605,17 +730,10 @@
     fold = Fold(halves_of(parts, count), land, passing, send, recv)
     weights.wait()
     met()
-    step = model // 3
 
     def one(block, at, out, here):
         arrivals[at].wait()
-
-        def tile(j, _):
-            part = nt(dgu[rows_of(block, count), :], w[pl.ds(pl.multiple_of(j * step, step), step), :])
-            out[here, columns_of(j, step)] = part.astype(out.dtype)
-            return 0
-
-        lax.fori_loop(0, 3, tile, 0)
+        out[here, :] = nt(dgu[rows_of(block, count), :], w[...]).astype(out.dtype)
 
     one(far, 0, parts, rows_of(far, count))
     fold.send_far()
@@ -672,51 +790,50 @@
             pltpu.SemaphoreType.DMA((tiles,)),
             pltpu.SemaphoreType.DMA((tiles,)),
         ],
-        compiler_params=params(collective_id, 56),
+        compiler_params=params(collective_id, 60),
     )(dy, h, gain, dgu, rows, w_gu)
 
 
-def pack_kernel(p_ref, o_ref, local, send, recv, peer_send, peer_recv):
-    model = p_ref.shape[0]
-    half = model // 2
+def pack_kernel(p_ref, o_ref, g_ref, local, send, recv, peer_send, peer_recv):
+    half = p_ref.shape[0] // 2
+    width = o_ref.shape[3]
     core = lax.axis_index("section")
-    first = core * half
     me, nx, ny = neighbours()
     met = greet({"narrow": nx}, {"narrow": ny}, {"section": 1 - core})
-    width = o_ref.shape[2]
-    own = pltpu.make_async_copy(p_ref.at[:, pl.ds(0, width)], o_ref.at[me], local)
-    own.start()
-
-    def part(block, which):
-        start = pl.multiple_of(first + which * (half // 2), half // 2)
-        return o_ref.at[block, pl.ds(start, half // 2)]
-
-    spread = Spread(part, send, recv)
-    own.wait()
+    owns = [
+        pltpu.make_async_copy(p_ref.at[:, pl.ds(0, width)], o_ref.at[core, me], local.at[0]),
+        pltpu.make_async_copy(p_ref.at[:, pl.ds(width, g_ref.shape[2])], g_ref.at[core], local.at[1]),
+    ]
+    for copy in owns:
+        copy.start()
+    spread = Spread(lambda block, which: o_ref.at[core, block, pl.ds(which * half, half)], send, recv)
+    for copy in owns:
+        copy.wait()
     met()
     spread.start()
     copies = []
 
-    def across(block, at):
-        ref = o_ref.at[block, pl.ds(pl.multiple_of(first, half), half)]
+    def across(ref):
         copy = pltpu.make_async_remote_copy(
             src_ref=ref,
             dst_ref=ref,
-            send_sem=peer_send.at[at],
-            recv_sem=peer_recv.at[at],
+            send_sem=peer_send.at[len(copies)],
+            recv_sem=peer_recv.at[len(copies)],
             device_id={"section": 1 - core},
             device_id_type=MESH,
         )
         copy.start()
         copies.append(copy)
 
+    across(g_ref.at[core])
+    across(o_ref.at[core, me])
     spread.pass_on()
     spread.x_here()
-    across(nx, 0)
+    across(o_ref.at[core, nx])
     spread.y_here()
-    across(ny, 1)
+    across(o_ref.at[core, ny])
     spread.far_here()
-    across(spread.far, 2)
+    across(o_ref.at[core, spread.far])
     for copy in copies:
         copy.wait_recv()
     spread.finish()
@@ -725,19 +842,87 @@
 
 
 def gather_pack(pack, width, collective_id):
+    model = pack.shape[0]
     return pl.pallas_call(
         pack_kernel,
-        out_shape=jax.ShapeDtypeStruct((4, pack.shape[0], width), pack.dtype),
+        out_shape=[
+            jax.ShapeDtypeStruct((2, 4, model, width), pack.dtype),
+            jax.ShapeDtypeStruct((2, model, pack.shape[1] - width), pack.dtype),
+        ],
         in_specs=[any_spec()],
-        out_specs=vmem_spec(),
+        out_specs=[vmem_spec()] * 2,
         scratch_shapes=[
+            pltpu.SemaphoreType.DMA((2,)),
+            *spread_spec(),
+            pltpu.SemaphoreType.DMA((5,)),
+            pltpu.SemaphoreType.DMA((5,)),
+        ],
+        compiler_params=params(collective_id, 32),
+    )(pack)
+
+
+def finish_kernel(zero_ref, one_ref, dep_ref, q_out, kv_out, o_out, give, came, kv, send, recv, kv_send, kv_recv):
+    core = lax.axis_index("section")
+    me, nx, ny = neighbours()
+    others = (nx, ny, jnp.bitwise_xor(me, 3))
+    met = greet({"section": 1 - core}, *[{"narrow": other} for other in others])
+    head = q_out.shape[1]
+    first = core == 0
+    zero, one = zero_ref[...], one_ref[...]
+    give[...] = jnp.where(first, one, zero)
+    keep = jnp.where(first, zero, one)
+    met()
+    across = pltpu.make_async_remote_copy(
+        src_ref=give,
+        dst_ref=came,
+        send_sem=send,
+        recv_sem=recv,
+        device_id={"section": 1 - core},
+        device_id_type=MESH,
+    )
+    across.start()
+    across.wait_recv()
+    by_qkv = jnp.where(first, keep, came[...])
+    by_out = jnp.where(first, came[...], keep)
+    kv[me] = by_qkv[:, head:]
+    copies = []
+    for at, other in enumerate(others):
+        copies.append(remote(kv.at[me], kv.at[me], kv_send.at[at], kv_recv.at[at], other))
+        copies[-1].start()
+    q_out[...] = by_qkv[:, :head].astype(F32)
+    o_out[...] = by_out[:, :head].astype(F32)
+    for copy in copies:
+        copy.wait_recv()
+    width = kv.shape[2]
+    for n in range(4):
+        kv_out[:, n * width : (n + 1) * width] = kv[n].astype(F32)
+    across.wait_send()
+    for copy in copies:
+        copy.wait_send()
+
+
+def finish_attention(zero, one, dep, head, collective_id):
+    block, width = zero.shape
+    return pl.pallas_call(
+        finish_kernel,
+        out_shape=[
+            jax.ShapeDtypeStruct((block, head), F32),
+            jax.ShapeDtypeStruct((block, 4 * (width - head)), F32),
+            jax.ShapeDtypeStruct((block, head), F32),
+        ],
+        in_specs=[vmem_spec()] * 2 + [any_spec()],
+        out_specs=[vmem_spec()] * 3,
+        scratch_shapes=[
+            pltpu.VMEM((block, width), BF16),
+            pltpu.VMEM((block, width), BF16),
+            pltpu.VMEM((4, block, width - head), BF16),
             pltpu.SemaphoreType.DMA,
-            *spread_spec(),
+            pltpu.SemaphoreType.DMA,
             pltpu.SemaphoreType.DMA((3,)),
             pltpu.SemaphoreType.DMA((3,)),
         ],
-        compiler_params=params(collective_id, 24),
-    )(pack)
+        compiler_params=params(collective_id, 16),
+    )(zero, one, dep)
 
 
 class Share:
@@ -859,7 +1044,7 @@
     )
 
 
-def pack_loads(pack_ref, head, wq, wot, wkv, sems):
+def pack_loads(pack_ref, layer, head, wq, wot, wkv, sems):
     kv_part = wkv.shape[1] // 4
     loads = []
     for at, (w, first, width) in enumerate(
@@ -868,7 +1053,7 @@
         loads.append(
             [
                 pltpu.make_async_copy(
-                    pack_ref.at[n, :, pl.ds(first, width)], w.at[:, pl.ds(n * width, width)], sems.at[at, n]
+                    pack_ref.at[layer, n, :, pl.ds(first, width)], w.at[:, pl.ds(n * width, width)], sems.at[at, n]
                 )
                 for n in range(4)
             ]
@@ -897,7 +1082,7 @@
     )
 
 
-def attend_kernel(length_ref, x_ref, gains_ref, head_ref, trig_ref, pack_ref, *refs):
+def attend_kernel(layer, length_ref, x_ref, gains_ref, head_ref, trig_ref, pack_ref, *refs):
     (
         h_out, xn_out, q_out, k_out, win_out, lse_out, o_out, a_out, *refs
     ) = refs
@@ -910,7 +1095,7 @@
     heads = q_out.shape[1] // head
     me, nx, ny = neighbours()
     met = greet({"narrow": nx}, {"narrow": ny}, {"narrow": jnp.bitwise_xor(me, 3)})
-    q_loads, out_loads, kv_loads = pack_loads(pack_ref, head, wq, wot, wkv, load)
+    q_loads, out_loads, kv_loads = pack_loads(pack_ref, layer, head, wq, wot, wkv, load)
     start_all(kv_loads + q_loads + out_loads)
     scaling = head ** (-0.5)
     cosine, sine_table = trig_ref[:, : head // 2], trig_ref[:, head // 2 :]
@@ -942,7 +1127,7 @@
     k_win, v_win = win_out[:, :head], win_out[:, head:]
     q_gain = head_ref[0:1, :]
 
-    def one_head(i, _):
+    def one_head(i):
         columns = columns_of(i, head)
         q_raw = q_out[:, columns]
         qr = rotate(q_raw * inverse_rms(q_raw) * q_gain, cosine, sine_table).astype(BF16)
@@ -952,9 +1137,9 @@
         total = jnp.sum(exponent, axis=-1, keepdims=True)
         lse_out[i] = most + jnp.log(total)
         o_out[:, columns] = nn((exponent / total).astype(BF16), v_win).astype(BF16)
-        return 0
-
-    lax.fori_loop(0, heads, one_head, 0)
+
+    for i in range(heads):
+        one_head(i)
     if sharing:
         share.start_deal()
         share.spread.pass_on()
@@ -975,11 +1160,12 @@
         wait_all(stores)
 
 
-def attend(length, x, gains, head_gains, trig, pack, head, sharing, collective_id):
+def attend(length, x, gains, head_gains, trig, pack, head, layer, collective_id):
     count, model = x.shape
     kv_width = 2 * head
     width = 4 * head
     window = count + WINDOW
+    sharing = True
     xn_shape = jax.ShapeDtypeStruct((count, model), BF16)
     o_shape = jax.ShapeDtypeStruct((count, width), BF16)
     shapes = [
@@ -997,7 +1183,7 @@
         shapes += share_shapes(xn_shape, o_shape)
         outs += [any_spec()] * 2
     return pl.pallas_call(
-        attend_kernel,
+        functools.partial(attend_kernel, layer),
         out_shape=shapes,
         in_specs=[pl.BlockSpec(memory_space=pltpu.SMEM)] + [vmem_spec()] * 4 + [any_spec()],
         out_specs=outs,
@@ -1015,12 +1201,14 @@
 
 
 def attend_back_kernel(
-    length_ref, dh_ref, a_ref, x_ref, gains_ref, head_ref, trig_ref, q_ref, k_ref, win_ref, lse_ref,
-    pack_ref, xn_ref, o_ref,
+    layer, length_ref, dh_ref, a_ref, x_ref, gains_ref, head_ref, trig_ref, q_ref, k_ref, win_ref, lse_ref,
+    pack_ref, xn_ref, o_ref, *refs
+):
+    (
     dx_out, dw_out, dgain_out, dhead_out,
     da, do, dq, dk, dv, parts, dq_all, dkv, dkv_all, wq, wot, wkv, xn, o, ours, theirs, came,
     pack_load, load, send, recv, land, passing, fold_send, fold_recv, q_send, q_recv, kv_send, kv_recv, swap_send, swap_recv, out_sem,
-):
+    ) = refs[-36:]
     count = dh_ref.shape[0]
     head = k_ref.shape[1]
     heads = q_ref.shape[1] // head
@@ -1029,7 +1217,7 @@
     core = lax.axis_index("section")
     far = jnp.bitwise_xor(me, 3)
     met = greet({"narrow": nx}, {"narrow": ny}, {"narrow": far}, {"section": 1 - core})
-    q_loads, out_loads, kv_loads = pack_loads(pack_ref, head, wq, wot, wkv, pack_load)
+    q_loads, out_loads, kv_loads = pack_loads(pack_ref, layer, head, wq, wot, wkv, pack_load)
     loads = [
         pltpu.make_async_copy(src, dst, load.at[at])
         for at, (src, dst) in enumerate(((xn_ref, xn), (o_ref, o)))
@@ -1056,7 +1244,7 @@
     dhead_out[...] = jnp.zeros_like(dhead_out)
     q_gain, k_gain = head_ref[0:1, :], head_ref[1:2, :]
 
-    def one_head(i, _):
+    def one_head(i):
         columns = columns_of(i, head)
         raw = q_ref[:, columns]
         inverse = inverse_rms(raw)
@@ -1074,9 +1262,9 @@
         dq_raw = inverse * (scaled - unit * jnp.mean(scaled * unit, axis=-1, keepdims=True))
         dq[:, columns] = dq_raw.astype(BF16)
         dhead_out[0:1, :] += jnp.sum(grad * unit, axis=0, keepdims=True)
-        return 0
-
-    lax.fori_loop(0, heads, one_head, 0)
+
+    for i in range(heads):
+        one_head(i)
     parts[...] = jnp.zeros_like(parts)
     window = pl.ds(pl.multiple_of(me * count, count), win_ref.shape[0])
     parts[window, :head] = (dk[...] * scaling).astype(BF16)
@@ -1156,22 +1344,22 @@
     out.wait()
 
 
-def attend_back(length, dh, a, x, gains, head_gains, trig, q_raw, k_raw, window, lse, pack, xn, o, collective_id):
+def attend_back(length, dh, a, x, gains, head_gains, trig, q_raw, k_raw, window, lse, pack, xn, o, deps, layer, collective_id):
     count, model = dh.shape
     head = k_raw.shape[1]
     width = q_raw.shape[1]
-    kv_part = pack.shape[2] - 2 * head
+    kv_part = pack.shape[3] - 2 * head
     deal = pltpu.SemaphoreType.DMA((3,))
     dw = pltpu.VMEM((model, head + kv_part), BF16)
     return pl.pallas_call(
-        attend_back_kernel,
+        functools.partial(attend_back_kernel, layer),
         out_shape=[
             jax.ShapeDtypeStruct((count, model), F32),
             jax.ShapeDtypeStruct((model, head + kv_part), BF16),
             jax.ShapeDtypeStruct((2, model), F32),
             jax.ShapeDtypeStruct((2, head), F32),
         ],
-        in_specs=[pl.BlockSpec(memory_space=pltpu.SMEM)] + [vmem_spec()] * 10 + [any_spec()] * 3,
+        in_specs=[pl.BlockSpec(memory_space=pltpu.SMEM)] + [vmem_spec()] * 10 + [any_spec()] * (3 + len(deps)),
         out_specs=[vmem_spec(), any_spec(), vmem_spec(), vmem_spec()],
         scratch_shapes=[
             pltpu.VMEM((4 * count, model), BF16),
@@ -1204,7 +1392,7 @@
             pltpu.SemaphoreType.DMA,
         ],
         compiler_params=params(collective_id, 48),
-    )(length, dh, a, x, gains, head_gains, trig, q_raw, k_raw, window, lse, pack, xn, o)
+    )(length, dh, a, x, gains, head_gains, trig, q_raw, k_raw, window, lse, pack, xn, o, *deps)
 
 
 def after(value, *others):
@@ -1217,23 +1405,8 @@
     )(value, *others)
 
 
-def feed_forward(h, gains, weights, shared, layer):
-    w_up, w_down, hidden = weights
-    rows, gu, act, *shared = feed_up(h, gains[2:3], w_up, hidden, shared, 10 + layer)
-    out, f = feed_down(h, gains[3:4], act, w_down, 12 + layer)
-    return out, (h, rows, gu, act, f), shared
-
-
 def scatter(member):
     return lax.psum_scatter(member, "wide", scatter_dimension=0, tiled=True)
-
-
-def feed_backward(dy, gains, weights, kept, extra, layer):
-    w_up, w_down, _ = weights
-    h, rows, gu, act, f = kept
-    dgu, d_down, dg3 = feed_back_up(dy, f, gains[3:4], gu, act, w_down, extra, 14 + layer)
-    dh, d_up, dg2 = feed_back_down(dy, h, gains[2:3], dgu, rows, w_up, 16 + layer)
-    return dh, (dg2, dg3), scatter(d_up), scatter(d_down)
 
 
 def on_device(
@@ -1258,39 +1431,39 @@
 
     half = block // 2
 
-    def by_halves(member):
-        keep = lax.dynamic_slice_in_dim(member, core * half, half, 0)
-        give = lax.dynamic_slice_in_dim(member, (1 - core) * half, half, 0)
-        came = swap(give)
-        return by_core(keep, came), by_core(came, keep)
-
     pad = -hidden % TILE
     kv_own = lax.dynamic_slice_in_dim(w_kv[0], narrow * kv_part, kv_part, 1)
     pack_width = 2 * head_width + kv_part
     gain_columns = jnp.zeros((block, GAIN_COLUMNS), BF16)
     gain_columns = lax.dynamic_update_slice(gain_columns, norm_gains[0].T, (0, 0))
     gain_columns = lax.dynamic_update_slice(gain_columns, head_gains[0].T, (0, 4))
-    pack = by_halves(jnp.concatenate([w_q[0], w_o[0].T, kv_own, gain_columns], axis=1))
-
-    gate_up = jnp.pad(w_gate_up[0], ((0, 0), (0, 0), (0, pad))).reshape(block, -1)
-    down = jnp.pad(w_down[0].T, ((0, 0), (0, pad)))
-    feed = by_halves(jnp.concatenate([gate_up, down], axis=1))
+    pack = jnp.concatenate([w_q[0], w_o[0].T, kv_own, gain_columns], axis=1)
+
+    late = after(core.reshape(1), pack)[0]
+
+    def half_of(side):
+        gate_up = lax.dynamic_slice_in_dim(w_gate_up[0], side * half, half, 0)
+        gate_up = jnp.pad(gate_up, ((0, 0), (0, 0), (0, pad))).reshape(half, -1)
+        down = lax.dynamic_slice_in_dim(w_down[0].T, side * half, half, 0)
+        return jnp.concatenate([gate_up, jnp.pad(down, ((0, 0), (0, pad)))], axis=1)
+
+    keep, came = half_of(late), swap(half_of(1 - late))
+    feed = by_core(keep, came), by_core(came, keep)
     padded = hidden + pad
 
     def gather(member):
         return lax.all_gather(member, ("wide", "section"), axis=0, tiled=True)
 
-    pack = gather(jnp.concatenate(pack, axis=1))
     both = gather(feed[0])
     feeds = [
         (both, both, padded),
         (gather(feed[1][:, : 2 * padded]), gather(feed[1][:, 2 * padded :]), padded),
     ]
-    full_width = pack_width + GAIN_COLUMNS
-    packs = [pack[:, :full_width], pack[:, full_width:]]
+    pack = lax.all_gather(pack, "wide", axis=0, tiled=True)
+    packs, gain_packs = gather_pack(pack, pack_width, 6)
 
     def gains_of(section):
-        columns = packs[section][:, pack_width:].astype(F32)
+        columns = gain_packs[section].astype(F32)
         heads = columns.reshape(n_wide, block, -1)[:, : head_width // n_wide, 4:6]
         return columns[:, :4].T, heads.transpose(2, 0, 1).reshape(2, head_width)
 
@@ -1305,17 +1478,15 @@
     for section in range(2):
         layer_gains, head_gain = gains_of(section)
         gains.append((layer_gains, head_gain))
-        own_pack = packs[section] if section == 0 else after(packs[1], kept[0][0][0])
-        whole = gather_pack(own_pack, pack_width, 6)
         h, xn, q_raw, k_raw, window, lse, o, a, *shared = attend(
-            length_one, x, layer_gains, head_gain, trig, whole, head_width, section == 0, 8 + section
+            length_one, x, layer_gains, head_gain, trig, packs, head_width, section, 8 + section
         )
-        kept_a = (h, a, x, q_raw, k_raw, window, lse, whole)
-        x, kept_f, more = feed_forward(
-            h, layer_gains, feeds[section], () if section == 0 else (xn, o), section
-        )
-        outs.append(x)
-        kept.append((kept_a, kept_f, shared or more))
+        w_up, w_down, _ = feeds[section]
+        mid_rows, gu, act = feed_up(h, layer_gains[2:3], w_up, padded, (), 10 + section)
+        kept.append(((a, x, q_raw, k_raw, window, lse), (h, mid_rows, gu, act), shared))
+        if section == 0:
+            x, f = feed_down(h, layer_gains[3:4], act, w_down, 12)
+            outs.append(x)
 
     real = (positions < length).astype(F32)[:, None]
     dy = lax.dynamic_index_in_dim(cotangent, core, 0, keepdims=False).astype(F32) * real
@@ -1323,24 +1494,30 @@
     up_sums, down_sums, attention_sums = [None, None], [None, None], [None, None]
     extra = None
     for section in (1, 0):
-        kept_a, kept_f, (xn, o) = kept[section]
+        kept_a, (h, mid_rows, gu, act), (xn, o) = kept[section]
         layer_gains, head_gain = gains[section]
-        if section == 0:
-            dy = after(dy, down_sums[1])
-        dh, dg23, up_sums[section], down_sums[section] = feed_backward(
-            dy, layer_gains, feeds[section], kept_f, extra, section
-        )
-        if section == 0:
-            dh = after(dh, up_sums[1])
-        _, a, x, q_raw, k_raw, window, lse, whole = kept_a
+        w_up, w_down, _ = feeds[section]
+        if section:
+            out, dgu, d_down, dg3 = feed_turn(h, layer_gains[3:4], dy, act, w_down, gu, 13)
+            outs.append(out)
+        else:
+            dgu, d_down, dg3 = feed_back_up(
+                dy, f, layer_gains[3:4], gu, act, w_down, (extra, down_sums[1]), 14
+            )
+        down_sums[section] = scatter(d_down)
+        dh, d_up, dg2 = feed_back_down(dy, h, layer_gains[2:3], dgu, mid_rows, w_up, 16 + section)
+        up_sums[section] = scatter(d_up)
+        dg23 = (dg2, dg3)
+        a, x, q_raw, k_raw, window, lse = kept_a
         dx, extra, dg01, dhead = attend_back(
-            length_one, dh, a, x, layer_gains, head_gain, trig, q_raw, k_raw, window, lse, whole, xn, o, 1
+            length_one, dh, a, x, layer_gains, head_gain, trig, q_raw, k_raw, window, lse, packs, xn, o,
+            () if section else (up_sums[1],), section, 18 + section,
         )
         dxs[section] = dx
         head_row = jnp.pad(dhead.reshape(1, -1), ((0, 0), (0, model - dhead.size)))
         gain_grads[section] = jnp.concatenate([dg01, *dg23, head_row, jnp.zeros((3, model), F32)])
         dy = dx
-    extra = after(extra, up_sums[0])
+    outs = [after(out, extra) for out in outs]
     split = down_sums[1].shape[1]
     attention_sums = (scatter(extra), down_sums[0][:, split:])
     down_sums[0] = down_sums[0][:, :split]
@@ -1352,12 +1529,8 @@
 
     grad_gate_up = jnp.stack(own_section(*up_sums), axis=1)[:, :, :hidden]
     grad_down = jnp.concatenate(own_section(*down_sums), axis=1)[:, :hidden].T
-    by_qkv, by_out = own_section(*attention_sums)
-    grad_q = by_qkv[:, :head_width]
-    grad_o = by_out[:, :head_width].T
-    grad_kv = lax.all_gather(
-        by_qkv[:, head_width:].astype(BF16), "narrow", axis=1, tiled=True
-    ).astype(F32)
+    grad_q, grad_kv, grad_o = finish_attention(*attention_sums, grad_gate_up, head_width, 1)
+    grad_o = grad_o.T
     gain_sums = sum_gains(jnp.concatenate(gain_grads), n_wide, 7)
     gain_sums = lax.dynamic_slice_in_dim(gain_sums, core * 8, 8, 0)
     wide = lax.axis_index("wide")

time: 720 us -> 682 us (0.947)
  local copies, waits for them, and re-layouts: 80.6 us -> 57.2 us
  Pallas kernels: 511 us -> 496 us
  blocking collectives: 9.09 us -> 0 us
  waiting for transfers between devices: 66.8 us -> 74.4 us
    pallas_call x6 -> x7, Pallas kernels: 207 us -> 291 us  [the longest x2 96.5 us: attend_back(): pl.pallas_call(functools.partial(attend_back_kernel, layer), out_shape=[j...]
    pallas_call x2 -> x1, Pallas kernels: 76.2 us -> 34.4 us  [feed_back_up(): pl.pallas_call(back_up_kernel, out_shape=[jax.ShapeDtypeStruct(gu.shape,...]
    all_gather x0 -> x1, waiting for transfers between devices: none -> 31 us  [on_device(): pack = lax.all_gather(pack, 'wide', axis=0, tiled=True)]
    all_gather x4 -> x3, waiting for transfers between devices: 31.6 us -> 7.94 us  [gather(): return lax.all_gather(member, ('wide', 'section'), axis=0, tiled=True)]
    unnamed x146 -> x104, local copies, waits for them, and re-layouts: 63.1 us -> 39.9 us
    pallas_call x2, Pallas kernels: 85.1 us -> 65 us  [feed_back_down(): pl.pallas_call(back_down_kernel, out_shape=[jax.ShapeDtypeStruct((count,...]
    pallas_call x2, Pallas kernels: 76.9 us -> 56.9 us  [feed_up(): pl.pallas_call(up_kernel, out_shape=shapes, in_specs=[vmem_spec(), vmem_s...]
    pallas_call x2 -> x1, Pallas kernels: 45.8 us -> 28.2 us  [feed_down(): pl.pallas_call(down_kernel, out_shape=[jax.ShapeDtypeStruct((count, model...]
  transfers between devices with their start and end apart: 16 -> 14, of which waited for: 6 -> 5; matrix products, arithmetic and copies ran while one was open for 6% -> 6% of each run, Pallas kernels for 63% -> 64%
where the time goes in v4:
time: 682 us; the launch traced here: 676 us
  Pallas kernels  496 us (73%)
  waiting for transfers between devices  74.4 us (11%)
  local copies, waits for them, and re-layouts  57.2 us (8%)
  other arithmetic  29.5 us (4%)
  between operations  16 us (2%)
    pallas_call x2, Pallas kernels, attend_back(): pl.pallas_call(functools.partial(attend_back_kernel, layer), out_shape=[j...  96.5 us
    pallas_call x2, Pallas kernels, attend(): pl.pallas_call(functools.partial(attend_kernel, layer), out_shape=shapes,...  77.5 us
    pallas_call x2, Pallas kernels, feed_back_down(): pl.pallas_call(back_down_kernel, out_shape=[jax.ShapeDtypeStruct((count,...  65 us
    pallas_call x2, Pallas kernels, feed_up(): pl.pallas_call(up_kernel, out_shape=shapes, in_specs=[vmem_spec(), vmem_s...  56.9 us
    pallas_call x1, Pallas kernels, feed_turn(): pl.pallas_call(turn_kernel, out_shape=[jax.ShapeDtypeStruct((count, model...  54.6 us
    pallas_call x1, Pallas kernels, gather_pack(): pl.pallas_call(pack_kernel, out_shape=[jax.ShapeDtypeStruct((2, 4, model,...  53.9 us
    unnamed x104, local copies, waits for them, and re-layouts  39.9 us
    pallas_call x1, Pallas kernels, feed_back_up(): pl.pallas_call(back_up_kernel, out_shape=[jax.ShapeDtypeStruct(gu.shape,...  34.4 us
  transfers between devices with their start and end apart: 14, of which 5 were waited for; matrix products, arithmetic and copies ran while one was open for 6% of the time, Pallas kernels for 64%

profile of v4, /device:TPU:0, one launch (start us, length us, event | category | flops | bytes accessed | tf_op | source)
XLA Modules:
  0.0 676.1 jit_solution(15569141016826165376)
XLA Ops:
  10.6 1.8 pad_maximum_fusion.2.refs_1_
  14.2 3.0 dynamic-slice_bitcast_fusion.1
  18.1 1.1 copy-done.41
  19.3 1.2 fusion.4
  22.0 2.3 collective-permute-done
  24.4 3.0 broadcast_select_fusion
  27.5 1.1 slice.93
  31.7 1.2 convert_multiply_fusion.dy_ref
  32.9 31.0 %all-gather.5.cloned.1.call-done.p_ref = bf16[1152,768]{1,0:T(8,128)(2,1)} async-done(((bf16[288,768]{1,0:T(8,128)(2,1)}), bf16[1152,768]{1,0:T(8,128)(2,1)}) %all-gather.5.cloned.1.call-update) | async-done | bytes 1769488 | tf_op jit(solution)/shard_map/all_gather | solution.py:1462
  63.9 1.5 copy-done.15
  65.4 53.9 %shard_map.169 = (bf16[2,4,1152,640]{3,2,1,0:T(8,128)(2,1)S(1)}, bf16[2,1152,128]{2,1,0:T(8,128)(2,1)S(1)}) custom-call(bf16[1152,768]{1,0:T(8,128)(2,1)S(1)} %copy-done.15), custom_call_target="tpu_custom_call" | custom-call | tf_op jit(solution)/shard_map/pallas_call | solution.py:846
  119.3 4.3 copy-done.2
  125.4 39.9 %shard_map.170 = (f32[256,1152]{1,0:T(8,128)S(1)}, bf16[256,1152]{1,0:T(8,128)(2,1)}, f32[256,1024]{1,0:T(8,128)S(1)}, f32[256,256]{1,0:T(8,128)S(1)}, bf16[768,...) custom-call(s32[1]{0:T(128)} %bitcast.length_ref, ...), custom_call_target="tpu_custom_call" | custom-call | tf_op jit(solution)/shard_map/pallas_call | solution.py:1185
  166.4 1.4 copy-done.13
  172.3 7.9 %all-gather.7.cloned.1.call-done.w_ref = bf16[1152,5376]{1,0:T(8,128)(2,1)} async-done(((bf16[144,5376]{1,0:T(8,128)(2,1)}), bf16[1152,5376]{1,0:T(8,128)(2,1)}) %all-gather.7.cloned.1.call-update) | async-done | bytes 12386320 | tf_op jit(solution)/shard_map/all_gather | solution.py:1455
  180.2 28.5 %shard_map.172 = (bf16[1024,1152]{1,0:T(8,128)(2,1)}, bf16[1024,3584]{1,0:T(8,128)(2,1)}, bf16[1024,1792]{1,0:T(8,128)(2,1)}) custom-call(f32[256,1152]{1,0:T(8,128)} %copy-done.9, f32[1,1152]{1,0:T(1,128)} %get-tuple-element.131.gain_ref, bf16[1152,5376]{1,0:T(8,128)(2,1)} %all-gather.7.cloned.1.call-done.w_ref), custom_call_target="tpu_custom_call" | custom-call | tf_op jit(solution)/shard_map/pallas_call | solution.py:352
  208.7 28.2 %shard_map.173 = (bf16[256,1152]{1,0:T(8,128)(2,1)}, f32[256,1152]{1,0:T(8,128)}) custom-call(f32[256,1152]{1,0:T(8,128)} %copy-done.9, f32[1,1152]{1,0:T(1,128)} %get-tuple-element.132.gain_ref, bf16[1024,1792]{1,0:T(8,128)(2,1)} %get-tuple-element.62.act_ref, bf16[1152,5376]{1,0:T(8,128)(2,1)} %all-gather.7.cloned.1.call-done.w_ref), custom_call_target="tpu_custom_call" | custom-call | tf_op jit(solution)/shard_map/pallas_call | solution.py:409
  236.9 1.1 copy-done.6
  238.0 37.6 %shard_map.174 = (f32[256,1152]{1,0:T(8,128)S(1)}, bf16[256,1152]{1,0:T(8,128)(2,1)}, f32[256,1024]{1,0:T(8,128)S(1)}, f32[256,256]{1,0:T(8,128)S(1)}, bf16[768,...) custom-call(s32[1]{0:T(128)} %bitcast.length_ref, ...), custom_call_target="tpu_custom_call" | custom-call | tf_op jit(solution)/shard_map/pallas_call | solution.py:1185
  276.6 1.4 copy-done.14
  282.5 28.4 %shard_map.175 = (bf16[1024,1152]{1,0:T(8,128)(2,1)}, bf16[1024,3584]{1,0:T(8,128)(2,1)}, bf16[1024,1792]{1,0:T(8,128)(2,1)}) custom-call(f32[256,1152]{1,0:T(8,128)} %copy-done.10, f32[1,1152]{1,0:T(1,128)} %get-tuple-element.129.gain_ref, bf16[1152,3584]{1,0:T(8,128)(2,1)} %all-gather.9.cloned.1.call-done.w_ref), custom_call_target="tpu_custom_call" | custom-call | tf_op jit(solution)/shard_map/pallas_call | solution.py:352
  310.9 54.6 %shard_map.176 = (bf16[256,1152]{1,0:T(8,128)(2,1)}, bf16[1024,3584]{1,0:T(8,128)(2,1)}, bf16[1152,896]{1,0:T(8,128)(2,1)}, f32[1,1152]{1,0:T(1,128)}) custom-call(f32[256,1152]{1,0:T(8,128)} %copy-done.10, f32[1,1152]{1,0:T(1,128)} %get-tuple-element.130.gain_ref, f32[256,1152]{1,0:T(8,128)} %convert_multiply_fusion.dy_ref, ...), custom_call_target="tpu_custom_call" | custom-call | tf_op jit(solution)/shard_map/pallas_call | solution.py:647
  365.6 32.5 %shard_map.177 = (f32[256,1152]{1,0:T(8,128)}, bf16[1152,1792]{1,0:T(8,128)(2,1)}, f32[1,1152]{1,0:T(1,128)}) custom-call(f32[256,1152]{1,0:T(8,128)} %convert_multiply_fusion.dy_ref, f32[256,1152]{1,0:T(8,128)} %copy-done.10, f32[1,1152]{1,0:T(1,128)} %get-tuple-element.129.gain_ref, bf16[1024,3584]{1,0:T(8,128)(2,1)} %get-tuple-element.67.dgu_ref, ...), custom_call_target="tpu_custom_call" | custom-call | tf_op jit(solution)/shard_map/pallas_call | solution.py:770
  399.3 1.2 copy-done.19
  400.5 1.1 copy-done.22
  401.6 1.1 copy-done.28
  404.7 48.1 %shard_map.178 = (f32[256,1152]{1,0:T(8,128)S(1)}, bf16[1152,384]{1,0:T(8,128)(2,1)S(1)}, f32[2,1152]{1,0:T(2,128)S(1)}, f32[2,256]{1,0:T(2,128)S(1)}) custom-call(s32[1]{0:T(128)} %bitcast.length_ref, f32[256,1152]{1,0:T(8,128)} %get-tuple-element.69.dh_ref, f32[256,1152]{1,0:T(8,128)} %copy-done.17, bf16[256,1152]{1,0:T(8,128)(2,1)S(1)} %copy-done.7, ...), custom_call_target="tpu_custom_call" | custom-call | tf_op jit(solution)/shard_map/pallas_call | solution.py:1354
  454.7 34.4 %shard_map.179 = (bf16[1024,3584]{1,0:T(8,128)(2,1)}, bf16[1152,1280]{1,0:T(8,128)(2,1)}, f32[1,1152]{1,0:T(1,128)}) custom-call(f32[256,1152]{1,0:T(8,128)} %copy-done.3, f32[256,1152]{1,0:T(8,128)} %get-tuple-element.78.f_ref, f32[1,1152]{1,0:T(1,128)} %get-tuple-element.132.gain_ref, bf16[1024,3584]{1,0:T(8,128)(2,1)} %get-tuple-element.79.gu_ref, ...), custom_call_target="tpu_custom_call" | custom-call | tf_op jit(solution)/shard_map/pallas_call | solution.py:683
  489.2 32.5 %shard_map.180 = (f32[256,1152]{1,0:T(8,128)}, bf16[1152,1792]{1,0:T(8,128)(2,1)}, f32[1,1152]{1,0:T(1,128)}) custom-call(f32[256,1152]{1,0:T(8,128)} %copy-done.3, f32[256,1152]{1,0:T(8,128)} %copy-done.9, f32[1,1152]{1,0:T(1,128)} %get-tuple-element.131.gain_ref, bf16[1024,3584]{1,0:T(8,128)(2,1)} %get-tuple-element.82.dgu_ref, ...), custom_call_target="tpu_custom_call" | custom-call | tf_op jit(solution)/shard_map/pallas_call | solution.py:770
  522.8 1.2 copy-done.11
  526.0 48.4 %shard_map.181 = (f32[256,1152]{1,0:T(8,128)}, bf16[1152,384]{1,0:T(8,128)(2,1)}, f32[2,1152]{1,0:T(2,128)S(1)}, f32[2,256]{1,0:T(2,128)S(1)}) custom-call(s32[1]{0:T(128)} %bitcast.length_ref, f32[256,1152]{1,0:T(8,128)} %get-tuple-element.84.dh_ref, f32[256,1152]{1,0:T(8,128)} %copy-done.16, bf16[256,1152]{1,0:T(8,128)(2,1)S(1)} %dynamic-slice_bitcast_fusion.2.x_ref, ...), custom_call_target="tpu_custom_call" | custom-call | tf_op jit(solution)/shard_map/pallas_call | solution.py:1354
  575.2 20.2 %shard_map.184 = f32[16,1152]{1,0:T(8,128)S(1)} custom-call(f32[16,1152]{1,0:T(8,128)S(1)} %concatenate.23.g_ref), custom_call_target="tpu_custom_call" | custom-call | tf_op jit(solution)/shard_map/pallas_call | solution.py:1024
  595.5 1.3 broadcast_select_fusion.6
  597.2 1.1 broadcast_select_fusion.4
  600.0 1.1 maximum_bitcast_fusion.1
  601.1 1.1 broadcast_select_fusion.10
  602.7 25.0 %reduce-scatter.14.cloned.1.call-done = bf16[288,1792]{1,0:T(8,128)(2,1)} async-done(((bf16[1152,1792]{1,0:T(8,128)(2,1)}), bf16[288,1792]{1,0:T(8,128)(2,1)}) %reduce-scatter.14.cloned.1.call-update) | async-done | bytes 1032208 | tf_op jit(solution)/shard_map/reduce_scatter | solution.py:1409
  627.8 1.2 collective-permute-start.3
  629.0 1.8 select_bitcast_fusion.1
  630.9 1.8 maximum_bitcast_fusion
  632.7 1.2 broadcast_select_fusion.9
  633.9 1.4 convert_bitcast_fusion
  635.7 1.6 copy.44
  637.3 1.6 copy.45
  638.9 8.7 %fusion.8 = (f32[1,288,2,1728]{3,2,1,0:T(2,128)}, f32[288,2,1728]{2,1,0:T(2,128)}) fusion(bf16[288,1,1792]{2,1,0:T(2,128)(2,1)S(1)} %copy.45, bf16[288,1,1792]{2,1,0:T(2,128)(2,1)S(1)} %copy.44), kind=kLoop, calls=%fused_computation.56 | loop fusion | flops 3981312 | bytes 10027008 | tf_op jit(solution)/shard_map/broadcast_in_dim | solution.py:1554
  647.5 7.9 %reduce-scatter.10.cloned.1.call-done.zero_ref = bf16[288,384]{1,0:T(8,128)(2,1)} async-done(((bf16[1152,384]{1,0:T(8,128)(2,1)}), bf16[288,384]{1,0:T(8,128)(2,1)}) %reduce-scatter.10.cloned.1.call-update) | async-done | bytes 221200 | tf_op jit(solution)/shard_map/reduce_scatter | solution.py:1409
  655.4 2.2 copy-done.5
  658.5 8.6 %shard_map.185 = (f32[288,256]{1,0:T(8,128)S(1)}, f32[288,512]{1,0:T(8,128)S(1)}, f32[288,256]{1,0:T(8,128)S(1)}) custom-call(bf16[288,384]{1,0:T(8,128)(2,1)S(1)} %copy-done.35, bf16[288,384]{1,0:T(8,128)(2,1)S(1)} %slice.95.one_ref, f32[288,2,1728]{2,1,0:T(2,128)S(1)} %copy-done.5), custom_call_target="tpu_custom_call" | custom-call | tf_op jit(solution)/shard_map/pallas_call | solution.py:906
  (166 shorter events, 37.5 us)
Async XLA Ops:
  7.2 24.5 %copy-start = (bf16[2,256,1152]{2,1,0:T(8,128)(2,1)S(1)}, bf16[2,256,1152]{2,1,0:T(8,128)(2,1)}, u32[]{:S(2)}) copy-start(bf16[2,256,1152]{2,1,0:T(8,128)(2,1)} %param.10) | copy-start | bytes 3538948
  7.2 56.7 %all-gather.5.cloned.1.call-start = ((), (), s32[]{:S(2)}) async-start(), calls=%async_computation.5 | async-start | bytes 2211840 | tf_op jit(solution)/shard_map/all_gather | solution.py:1462
  18.0 1.2 copy-start.41
  20.6 3.8 collective-permute-start
  21.0 159.2 %all-gather.7.cloned.1.call-start = ((), (), s32[]{:S(2)}) async-start(), calls=%async_computation.6 | async-start | bytes 13934592 | tf_op jit(solution)/shard_map/all_gather | solution.py:1455
  27.4 255.1 %all-gather.9.cloned.1.call-start = ((), (), s32[]{:S(2)}) async-start(), calls=%async_computation.7 | async-start | bytes 9289728 | tf_op jit(solution)/shard_map/all_gather | solution.py:1455
  28.5 1.2 copy-start.47
  28.6 282.4 %all-gather.11.cloned.1.call-start = ((), (), s32[]{:S(2)}) async-start(), calls=%async_computation.8 | async-start | bytes 4644864 | tf_op jit(solution)/shard_map/all_gather | solution.py:1455
  29.5 425.2 %reduce-scatter.6.cloned.1.call-start = ((), (), s32[]{:S(2)}) async-start(), calls=%async_computation.9 | async-start | bytes 2580480 | tf_op jit(solution)/shard_map/reduce_scatter | solution.py:1409
  30.3 1.4 copy-start.42
  63.9 1.5 copy-start.15
  119.2 4.3 copy-start.2
  165.3 1.0 copy-start.9
  166.3 1.4 copy-start.13
  170.3 38.4 %copy-start.25 = (bf16[1024,256]{1,0:T(8,128)(2,1)}, bf16[1024,256]{1,0:T(8,128)(2,1)S(1)}, u32[]{:S(2)}) copy-start(bf16[1024,256]{1,0:T(8,128)(2,1)S(1)} %get-tuple-element.91.o_ref) | copy-start | bytes 1572868
  236.9 1.1 copy-start.6
  275.5 1.0 copy-start.10
  276.6 1.4 copy-start.14
  278.0 1.0 copy-start.17
  279.0 1.0 copy-start.18
  282.5 28.4 %copy-start.29 = (bf16[1024,256]{1,0:T(8,128)(2,1)}, bf16[1024,256]{1,0:T(8,128)(2,1)S(1)}, u32[]{:S(2)}) copy-start(bf16[1024,256]{1,0:T(8,128)(2,1)S(1)} %get-tuple-element.76.o_ref) | copy-start | bytes 1572868
  365.6 156.2 %reduce-scatter.8.cloned.1.call-start = ((), (), s32[]{:S(2)}) async-start(), calls=%async_computation.10 | async-start | bytes 5160960 | tf_op jit(solution)/shard_map/reduce_scatter | solution.py:1409
  398.2 1.1 copy-start.7
  398.2 202.9 %reduce-scatter.12.cloned.1.call-start = ((), (), s32[]{:S(2)}) async-start(), calls=%async_computation.12 | async-start | bytes 3686400 | tf_op jit(solution)/shard_map/reduce_scatter | solution.py:1409
  399.3 1.2 copy-start.19
  400.5 1.1 copy-start.22
  401.6 1.1 copy-start.28
  402.7 1.0 copy-start.30
  452.8 1.0 copy-start.3
  489.2 138.6 %reduce-scatter.14.cloned.1.call-start = ((), (), s32[]{:S(2)}) async-start(), calls=%async_computation.13 | async-start | bytes 5160960 | tf_op jit(solution)/shard_map/reduce_scatter | solution.py:1409
  521.7 1.1 copy-start.24
  521.7 133.6 %reduce-scatter.10.cloned.1.call-start = ((), (), s32[]{:S(2)}) async-start(), calls=%async_computation.11 | async-start | bytes 1105920 | tf_op jit(solution)/shard_map/reduce_scatter | solution.py:1409
  522.8 1.2 copy-start.11
  524.0 1.0 copy-start.26
  574.4 21.0 %copy-start.8 = (bf16[256,1152]{1,0:T(8,128)(2,1)S(1)}, bf16[256,1152]{1,0:T(8,128)(2,1)}, u32[]{:S(2)}) copy-start(bf16[256,1152]{1,0:T(8,128)(2,1)} %shard_map.182) | copy-start | bytes 1769476
  595.4 1.4 copy-start.4
  595.5 1.8 copy-start.37
  596.8 3.0 collective-permute-start.1
  597.2 2.6 copy-start.36
  598.4 30.6 %collective-permute-start.2 = (f32[256,1152]{1,0:T(8,128)}, f32[256,1152]{1,0:T(8,128)}, u32[]{:S(2)}, u32[]{:S(2)}) collective-permute-start(f32[256,1152]{1,0:T(8,128)} %broadcast_select_fusion.4), channel_id=1, source_target_pairs={{0,16},{16,0},{1,17},{17,1},{2,18},{18,2},{3,19},{19,3},{4,20},{20... | collective-permute-start | bytes 3538952 | tf_op jit(solution)/shard_map/ppermute | solution.py:1427
  600.0 1.2 copy-start.38
  600.0 27.8 %copy-start.12 = (bf16[288,1792]{1,0:T(8,128)(2,1)S(1)}, bf16[288,1792]{1,0:T(8,128)(2,1)}, u32[]{:S(2)}) copy-start(bf16[288,1792]{1,0:T(8,128)(2,1)} %reduce-scatter.8.cloned.1.call-done.refs_0_) | copy-start | bytes 3096580
  602.2 30.5 %collective-permute-start.4 = (bf16[288,896]{1,0:T(8,128)(2,1)S(1)}, bf16[288,896]{1,0:T(8,128)(2,1)}, u32[]{:S(2)}, u32[]{:S(2)}) collective-permute-start(bf16[288,896]{1,0:T(8,128)(2,1)S(1)} %broadcast_select_fusion.10), channel_id=1, source_target_pairs={{0,16},{16,0},{1,17},{17,1},{2,18},{18,2},{3,19},{19,3},{4,20},{20... | collective-permute-start | bytes 1548296 | tf_op jit(solution)/shard_map/ppermute | solution.py:1427
  627.8 7.5 %collective-permute-start.3 = (bf16[288,1792]{1,0:T(8,128)(2,1)S(1)}, bf16[288,1792]{1,0:T(8,128)(2,1)S(1)}, u32[]{:S(2)}, u32[]{:S(2)}) collective-permute-start(bf16[288,1792]{1,0:T(8,128)(2,1)S(1)} %broadcast_select_fusion.2), channel_id=1, source_target_pairs={{0,16},{16,0},{1,17},{17,1},{2,18},{18,2},{3,19},{19,3},{4,20},{20... | collective-permute-start | bytes 3096584 | tf_op jit(solution)/shard_map/ppermute | solution.py:1427
  630.9 1.8 copy-start.40
  633.9 1.6 copy-start.39
  655.4 2.2 copy-start.5
  658.5 10.8 %copy-start.1 = (bf16[2,256,1152]{2,1,0:T(8,128)(2,1)S(1)}, bf16[2,256,1152]{2,1,0:T(8,128)(2,1)}, u32[]{:S(2)}) copy-start(bf16[2,256,1152]{2,1,0:T(8,128)(2,1)} %param.10) | copy-start | bytes 3538948
  (14 other events, 11.5 us)
Sparse Core Ops, SparseCore 0:
  21.2 42.7 all-gather.4
  66.1 114.0 all-gather.6
  181.8 79.1 all-gather.8
  262.6 45.0 all-gather.10
  365.7 41.7 reduce-scatter.5
  409.8 75.0 reduce-scatter.7
  489.3 55.6 reduce-scatter.11
  547.4 80.2 reduce-scatter.13
  630.0 25.2 reduce-scatter.9

commit v5 on v4

--- a/solution.py
+++ b/solution.py
@@ -221,6 +221,129 @@
     def finish(self):
         for copy in (self.far_x, self.far_y, self.near_x, self.near_y, self.on_y, self.on_x):
             copy.wait_send()
+
+
+class LineFold:
+    def __init__(self, own, land, out, columns, send, recv):
+        self.own, self.land, self.out, self.columns = own, land, out, columns
+        self.send, self.recv = send, recv
+        self.wides = own.shape[0]
+        self.wide = lax.axis_index("wide")
+
+    def place(self, way):
+        return self.wide if way == 0 else self.wides - 1 - self.wide
+
+    def copy(self, way, step):
+        return pltpu.make_async_remote_copy(
+            src_ref=self.out.at[self.slot(way, step), :, self.columns],
+            dst_ref=self.land.at[way, step, :, self.columns],
+            send_sem=self.send.at[way, step],
+            recv_sem=self.recv.at[way, step],
+            device_id={"wide": self.wide + 1 if way == 0 else self.wide - 1},
+            device_id_type=MESH,
+        )
+
+    def slot(self, way, step):
+        return jnp.clip(step - self.wide, 0, self.wides - 2) if way == 0 else step
+
+    def sends(self, way, step):
+        place = self.place(way)
+        return (place <= step) & (place < self.wides - 1)
+
+    def gets(self, way, step):
+        place = self.place(way)
+        return (place >= 1) & (place - 1 <= step)
+
+    def step(self, step):
+        for way in (0, 1):
+            ahead = self.wides - 1 - step
+            block = self.wide + ahead if way == 0 else self.wide - ahead
+            block = jnp.clip(block, 0, self.wides - 1)
+            begins = self.place(way) == 0
+
+            @pl.when(self.sends(way, step) & begins)
+            def _():
+                self.out[self.slot(way, step), :, self.columns] = self.own[block, :, self.columns]
+                self.copy(way, step).start()
+
+            if step:
+
+                @pl.when(self.sends(way, step) & jnp.logical_not(begins))
+                def _():
+                    self.copy(way, step - 1).wait_recv()
+                    total = self.own[block, :, self.columns].astype(F32)
+                    total = total + self.land[way, step - 1, :, self.columns].astype(F32)
+                    self.out[self.slot(way, step), :, self.columns] = total.astype(BF16)
+                    self.copy(way, step).start()
+
+    def finish(self, result):
+        last = self.wides - 2
+        result[:, self.columns] = self.own[self.wide, :, self.columns]
+        for way in (0, 1):
+
+            @pl.when(self.gets(way, last))
+            def _():
+                self.copy(way, last).wait_recv()
+                total = result[:, self.columns].astype(F32)
+                total = total + self.land[way, last, :, self.columns].astype(F32)
+                result[:, self.columns] = total.astype(BF16)
+
+    def close(self):
+        for step in range(self.wides - 1):
+            for way in (0, 1):
+                pl.when(self.sends(way, step))(self.copy(way, step).wait_send)
+
+
+def line_spec(wides, block, columns, pieces):
+    hops = pltpu.SemaphoreType.DMA((pieces, 2, wides - 1))
+    return [
+        pltpu.VMEM((wides, block, columns), BF16),
+        pltpu.VMEM((2, wides - 1, block, columns), BF16),
+        pltpu.VMEM((wides - 1, block, columns), BF16),
+        pltpu.VMEM((block, columns), BF16),
+        pltpu.SemaphoreType.DMA((wides + 1,)),
+        hops,
+        hops,
+    ]
+
+
+class LineSum:
+    def __init__(self, src, dst, own, land, out, result, loads, send, recv):
+        self.src, self.dst, self.own, self.result, self.loads = src, dst, own, result, loads
+        pieces = send.shape[0]
+        columns = own.shape[2]
+        width = -(-columns // (128 * pieces)) * 128
+        self.folds = [
+            LineFold(own, land, out, pl.ds(first, min(width, columns - first)), send.at[p], recv.at[p])
+            for p, first in enumerate(range(0, columns, width))
+        ]
+        self.steps = own.shape[0] - 1
+
+    def load(self):
+        wides, rows, columns = self.own.shape
+        for w in range(wides):
+            part = self.src.at[pl.ds(w * rows, rows), pl.ds(0, columns)]
+            pltpu.make_async_copy(part, self.own.at[w], self.loads.at[w]).start()
+
+    def begin(self):
+        wides, rows, columns = self.own.shape
+        for w in range(wides):
+            part = self.src.at[pl.ds(w * rows, rows), pl.ds(0, columns)]
+            pltpu.make_async_copy(part, self.own.at[w], self.loads.at[w]).wait()
+        for fold in self.folds:
+            fold.step(0)
+
+    def step(self, step, piece):
+        self.folds[piece].step(step)
+
+    def end(self):
+        for fold in self.folds:
+            fold.finish(self.result)
+        copy = pltpu.make_async_copy(self.result, self.dst, self.loads.at[self.own.shape[0]])
+        copy.start()
+        for fold in self.folds:
+            fold.close()
+        copy.wait()
 
 
 class Deal:
@@ -794,21 +917,38 @@
     )(dy, h, gain, dgu, rows, w_gu)
 
 
-def pack_kernel(p_ref, o_ref, g_ref, local, send, recv, peer_send, peer_recv):
-    half = p_ref.shape[0] // 2
-    width = o_ref.shape[3]
+def pack_kernel(*refs):
+    *p_refs, o_ref, g_ref, local, send, recv, peer_send, peer_recv = refs
+    model, width = o_ref.shape[2:]
+    half = model // 2
+    rest = g_ref.shape[2]
     core = lax.axis_index("section")
     me, nx, ny = neighbours()
     met = greet({"narrow": nx}, {"narrow": ny}, {"section": 1 - core})
-    owns = [
-        pltpu.make_async_copy(p_ref.at[:, pl.ds(0, width)], o_ref.at[core, me], local.at[0]),
-        pltpu.make_async_copy(p_ref.at[:, pl.ds(width, g_ref.shape[2])], g_ref.at[core], local.at[1]),
-    ]
-    for copy in owns:
-        copy.start()
+    rows = p_refs[0].shape[0]
+
+    def owns(run):
+        wides = model // rows
+        for at in range(wides):
+            for distance, p_ref in enumerate(p_refs, -(len(p_refs) // 2)):
+                wide = at - distance
+                if not 0 <= wide < wides:
+                    continue
+                place = pl.ds(at * rows, rows)
+                both = [
+                    (p_ref.at[:, pl.ds(0, width)], o_ref.at[core, me, place], local.at[0, at]),
+                    (p_ref.at[:, pl.ds(width, rest)], g_ref.at[core, place], local.at[1, at]),
+                ]
+                for src, dst, sem in both:
+                    copy = pltpu.make_async_copy(src, dst, sem)
+                    if wides == 1:
+                        run(copy)()
+                    else:
+                        pl.when(lax.axis_index("wide") == wide)(run(copy))
+
+    owns(lambda copy: copy.start)
     spread = Spread(lambda block, which: o_ref.at[core, block, pl.ds(which * half, half)], send, recv)
-    for copy in owns:
-        copy.wait()
+    owns(lambda copy: copy.wait)
     met()
     spread.start()
     copies = []
@@ -841,39 +981,40 @@
         copy.wait_send()
 
 
-def gather_pack(pack, width, collective_id):
-    model = pack.shape[0]
+def gather_pack(packs, model, width, collective_id):
+    pack = packs[0]
     return pl.pallas_call(
         pack_kernel,
         out_shape=[
             jax.ShapeDtypeStruct((2, 4, model, width), pack.dtype),
             jax.ShapeDtypeStruct((2, model, pack.shape[1] - width), pack.dtype),
         ],
-        in_specs=[any_spec()],
+        in_specs=[any_spec()] * len(packs),
         out_specs=[vmem_spec()] * 2,
         scratch_shapes=[
-            pltpu.SemaphoreType.DMA((2,)),
+            pltpu.SemaphoreType.DMA((2, model // pack.shape[0])),
             *spread_spec(),
             pltpu.SemaphoreType.DMA((5,)),
             pltpu.SemaphoreType.DMA((5,)),
         ],
         compiler_params=params(collective_id, 32),
-    )(pack)
-
-
-def finish_kernel(zero_ref, one_ref, dep_ref, q_out, kv_out, o_out, give, came, kv, send, recv, kv_send, kv_recv):
+    )(*packs)
+
+
+def finish_kernel(
+    zero_ref, one_ref, early_ref, dep_ref, q_out, kv_out, o_out, came, kv, send, recv, kv_send, kv_recv
+):
     core = lax.axis_index("section")
     me, nx, ny = neighbours()
     others = (nx, ny, jnp.bitwise_xor(me, 3))
     met = greet({"section": 1 - core}, *[{"narrow": other} for other in others])
     head = q_out.shape[1]
     first = core == 0
-    zero, one = zero_ref[...], one_ref[...]
-    give[...] = jnp.where(first, one, zero)
-    keep = jnp.where(first, zero, one)
+    by_qkv = jnp.where(first, zero_ref[...], early_ref[...])
+    kv[me] = by_qkv[:, head:]
     met()
     across = pltpu.make_async_remote_copy(
-        src_ref=give,
+        src_ref=zero_ref,
         dst_ref=came,
         send_sem=send,
         recv_sem=recv,
@@ -881,16 +1022,13 @@
         device_id_type=MESH,
     )
     across.start()
-    across.wait_recv()
-    by_qkv = jnp.where(first, keep, came[...])
-    by_out = jnp.where(first, came[...], keep)
-    kv[me] = by_qkv[:, head:]
     copies = []
     for at, other in enumerate(others):
         copies.append(remote(kv.at[me], kv.at[me], kv_send.at[at], kv_recv.at[at], other))
         copies[-1].start()
     q_out[...] = by_qkv[:, :head].astype(F32)
-    o_out[...] = by_out[:, :head].astype(F32)
+    across.wait_recv()
+    o_out[...] = jnp.where(first, came[:, :head], one_ref[:, :head]).astype(F32)
     for copy in copies:
         copy.wait_recv()
     width = kv.shape[2]
@@ -901,7 +1039,7 @@
         copy.wait_send()
 
 
-def finish_attention(zero, one, dep, head, collective_id):
+def finish_attention(zero, one, early, dep, head, collective_id):
     block, width = zero.shape
     return pl.pallas_call(
         finish_kernel,
@@ -910,10 +1048,9 @@
             jax.ShapeDtypeStruct((block, 4 * (width - head)), F32),
             jax.ShapeDtypeStruct((block, head), F32),
         ],
-        in_specs=[vmem_spec()] * 2 + [any_spec()],
+        in_specs=[vmem_spec()] * 3 + [any_spec()],
         out_specs=[vmem_spec()] * 3,
         scratch_shapes=[
-            pltpu.VMEM((block, width), BF16),
             pltpu.VMEM((block, width), BF16),
             pltpu.VMEM((4, block, width - head), BF16),
             pltpu.SemaphoreType.DMA,
@@ -922,7 +1059,30 @@
             pltpu.SemaphoreType.DMA((3,)),
         ],
         compiler_params=params(collective_id, 16),
-    )(zero, one, dep)
+    )(zero, one, early, dep)
+
+
+def pair_kernel(zero_ref, one_ref, came_zero_ref, came_one_ref, out_ref, flag_ref):
+    hidden = out_ref.shape[2]
+    first = lax.axis_index("section") == 0
+    keep = jnp.where(first, zero_ref[:, :hidden], one_ref[:, :hidden])
+    came = jnp.where(first, came_zero_ref[:, :hidden], came_one_ref[:, :hidden])
+    out_ref[:, 0, :] = jnp.where(first, keep, came).astype(F32)
+    out_ref[:, 1, :] = jnp.where(first, came, keep).astype(F32)
+    flag_ref[...] = jnp.zeros_like(flag_ref)
+
+
+def pair_up(zero, one, came_zero, came_one, hidden):
+    return pl.pallas_call(
+        pair_kernel,
+        out_shape=[
+            jax.ShapeDtypeStruct((zero.shape[0], 2, hidden), F32),
+            jax.ShapeDtypeStruct((8, 128), F32),
+        ],
+        in_specs=[vmem_spec()] * 4,
+        out_specs=[vmem_spec()] * 2,
+        compiler_params=pltpu.CompilerParams(vmem_limit_bytes=40 * MIB),
+    )(zero, one, came_zero, came_one)
 
 
 class Share:
@@ -979,61 +1139,58 @@
     ]
 
 
-def gain_kernel(g_ref, o_ref, land, total, send, recv):
+def gain_stages():
+    wides = lax.axis_size("wide")
     core, wide = lax.axis_index("section"), lax.axis_index("wide")
-    wides = land.shape[0] - 3
     me, nx, ny = neighbours()
-    far = jnp.bitwise_xor(me, 3)
-    stages = [
-        [{"narrow": nx}, {"narrow": ny}, {"narrow": far}],
+    return [
+        [{"narrow": nx}, {"narrow": ny}, {"narrow": jnp.bitwise_xor(me, 3)}],
         [{"section": 1 - core}],
         [{"wide": lax.rem(wide + step, wides)} for step in range(1, wides)],
     ]
-    met = greet(*stages[0], *stages[1], *stages[2])
-    total[0] = g_ref[...]
-    met()
-    at = 0
-    copies = []
-    for stage, others in enumerate(stages):
-        mine = []
-        for other in others:
-            mine.append(
-                pltpu.make_async_remote_copy(
-                    src_ref=total.at[stage],
-                    dst_ref=land.at[at],
-                    send_sem=send.at[at],
-                    recv_sem=recv.at[at],
-                    device_id=other,
-                    device_id_type=MESH,
-                )
+
+
+class GainSum:
+    def __init__(self, land, total, send, recv):
+        self.land, self.total, self.send, self.recv = land, total, send, recv
+        self.copies = []
+        self.waiting = []
+
+    def start(self, stage):
+        for other in gain_stages()[stage]:
+            at = len(self.copies)
+            copy = pltpu.make_async_remote_copy(
+                src_ref=self.total.at[stage],
+                dst_ref=self.land.at[at],
+                send_sem=self.send.at[at],
+                recv_sem=self.recv.at[at],
+                device_id=other,
+                device_id_type=MESH,
             )
-            mine[-1].start()
-            at += 1
-        value = total[stage]
-        for place, copy in enumerate(mine, at - len(mine)):
-            copy.wait_recv()
-            value = value + land[place]
-        total[stage + 1] = value
-        copies += mine
-    o_ref[...] = total[3]
-    for copy in copies:
-        copy.wait_send()
-
-
-def sum_gains(block, wides, collective_id):
-    return pl.pallas_call(
-        gain_kernel,
-        out_shape=jax.ShapeDtypeStruct(block.shape, F32),
-        in_specs=[vmem_spec()],
-        out_specs=vmem_spec(),
-        scratch_shapes=[
-            pltpu.VMEM((wides + 3, *block.shape), F32),
-            pltpu.VMEM((4, *block.shape), F32),
-            pltpu.SemaphoreType.DMA((wides + 3,)),
-            pltpu.SemaphoreType.DMA((wides + 3,)),
-        ],
-        compiler_params=params(collective_id, 16),
-    )(block)
+            copy.start()
+            self.copies.append(copy)
+            self.waiting.append(at)
+
+    def add(self, stage):
+        value = self.total[stage]
+        for at in self.waiting:
+            self.copies[at].wait_recv()
+            value = value + self.land[at]
+        self.waiting = []
+        self.total[stage + 1] = value
+
+    def close(self):
+        for copy in self.copies:
+            copy.wait_send()
+
+
+def gain_spec(wides, shape):
+    return [
+        pltpu.VMEM((wides + 3, *shape), F32),
+        pltpu.VMEM((4, *shape), F32),
+        pltpu.SemaphoreType.DMA((wides + 3,)),
+        pltpu.SemaphoreType.DMA((wides + 3,)),
+    ]
 
 
 def turn_back(grad, cosine, sine_table):
@@ -1204,11 +1361,17 @@
     layer, length_ref, dh_ref, a_ref, x_ref, gains_ref, head_ref, trig_ref, q_ref, k_ref, win_ref, lse_ref,
     pack_ref, xn_ref, o_ref, *refs
 ):
+    if layer == 0:
+        block_ref, lined_ref, *refs = refs
+        block_out, lined_out, came_out, small_out = refs[4:8]
+        refs = refs[:4] + refs[8:]
+        gain_refs, line_refs = refs[36:40], refs[40:]
+        refs = refs[:36]
     (
     dx_out, dw_out, dgain_out, dhead_out,
     da, do, dq, dk, dv, parts, dq_all, dkv, dkv_all, wq, wot, wkv, xn, o, ours, theirs, came,
     pack_load, load, send, recv, land, passing, fold_send, fold_recv, q_send, q_recv, kv_send, kv_recv, swap_send, swap_recv, out_sem,
-    ) = refs[-36:]
+    ) = refs
     count = dh_ref.shape[0]
     head = k_ref.shape[1]
     heads = q_ref.shape[1] // head
@@ -1216,7 +1379,17 @@
     me, nx, ny = neighbours()
     core = lax.axis_index("section")
     far = jnp.bitwise_xor(me, 3)
-    met = greet({"narrow": nx}, {"narrow": ny}, {"narrow": far}, {"section": 1 - core})
+    lined = layer == 0 and len(line_refs) > 0
+    if layer == 0:
+        met = greet(*sum(gain_stages(), []))
+        sums = GainSum(*gain_refs)
+    else:
+        met = greet({"narrow": nx}, {"narrow": ny}, {"narrow": far}, {"section": 1 - core})
+    if lined:
+        line = LineSum(lined_ref, lined_out, *line_refs[:7])
+        small = LineSum(ours, small_out, *line_refs[7:14])
+        came_line, came_send, came_recv, came_store = line_refs[14:]
+        line.load()
     q_loads, out_loads, kv_loads = pack_loads(pack_ref, layer, head, wq, wot, wkv, pack_load)
     loads = [
         pltpu.make_async_copy(src, dst, load.at[at])
@@ -1234,6 +1407,8 @@
     spread = Spread(halves_of(da, count), send, recv)
     met()
     spread.start()
+    if lined:
+        line.begin()
     wait_all(out_loads)
     do[...] = nn(da[here, :], wot[...]).astype(BF16)
 
@@ -1265,6 +1440,8 @@
 
     for i in range(heads):
         one_head(i)
+    if lined:
+        line.step(1, 0)
     parts[...] = jnp.zeros_like(parts)
     window = pl.ds(pl.multiple_of(me * count, count), win_ref.shape[0])
     parts[window, :head] = (dk[...] * scaling).astype(BF16)
@@ -1326,15 +1503,59 @@
     by_value, dg0 = normed_gradient(x_ref[...].astype(F32), gains_ref[0:1, :], dxn)
     dx_out[...] = dh_ref[...] + by_value
     dgain_out[0:1, :] = dg0
+    if lined:
+        line.step(1, 1)
+    if layer == 0:
+        own_total = sums.total.at[0]
+        own_total[...] = block_ref[...]
+        own_total[0:2, :] = dgain_out[...]
+        own_total[4:5, :head] = dhead_out[0:1, :]
+        own_total[4:5, head : 2 * head] = dhead_out[1:2, :]
+        sums.start(0)
 
     deal_kv.here()
     by_kv = tn(xn[...], dkv_all[...])
+    if layer == 0:
+        sums.add(0)
+        sums.start(1)
     exchange(1, pl.ds(head, kv_part), by_kv, jnp.zeros_like(by_kv))
     for copy in swaps:
         copy.wait_recv()
     ours[...] = (ours[...].astype(F32) + came[...].astype(F32)).astype(BF16)
     out = pltpu.make_async_copy(ours, dw_out, out_sem)
     out.start()
+    if layer == 0:
+        sums.add(1)
+        sums.start(2)
+    if lined:
+        small.load()
+        for step in range(2, line.steps):
+            for piece in (0, 1):
+                line.step(step, piece)
+        small.begin()
+        line.end()
+        cross = pltpu.make_async_remote_copy(
+            src_ref=line.result,
+            dst_ref=came_line,
+            send_sem=came_send,
+            recv_sem=came_recv,
+            device_id={"section": 1 - core},
+            device_id_type=MESH,
+        )
+        cross.start()
+        for step in range(1, small.steps):
+            for piece in range(len(small.folds)):
+                small.step(step, piece)
+        cross.wait_recv()
+        keep = pltpu.make_async_copy(came_line, came_out, came_store)
+        keep.start()
+        small.end()
+        keep.wait()
+        cross.wait_send()
+    if layer == 0:
+        sums.add(2)
+        block_out[...] = sums.total[3]
+        sums.close()
     spread.finish()
     fold.finish()
     deal_q.finish()
@@ -1349,6 +1570,10 @@
     head = k_raw.shape[1]
     width = q_raw.shape[1]
     kv_part = pack.shape[3] - 2 * head
+    if layer == 0:
+        wides = lax.axis_size("wide")
+        block, lined = deps
+        rows = model // wides
     deal = pltpu.SemaphoreType.DMA((3,))
     dw = pltpu.VMEM((model, head + kv_part), BF16)
     return pl.pallas_call(
@@ -1358,9 +1583,20 @@
             jax.ShapeDtypeStruct((model, head + kv_part), BF16),
             jax.ShapeDtypeStruct((2, model), F32),
             jax.ShapeDtypeStruct((2, head), F32),
+            *(
+                [
+                    jax.ShapeDtypeStruct(block.shape, F32),
+                    jax.ShapeDtypeStruct((rows, lined.shape[1]), BF16),
+                    jax.ShapeDtypeStruct((rows, lined.shape[1]), BF16),
+                    jax.ShapeDtypeStruct((rows, head + kv_part), BF16),
+                ]
+                if layer == 0
+                else []
+            ),
         ],
-        in_specs=[pl.BlockSpec(memory_space=pltpu.SMEM)] + [vmem_spec()] * 10 + [any_spec()] * (3 + len(deps)),
-        out_specs=[vmem_spec(), any_spec(), vmem_spec(), vmem_spec()],
+        in_specs=[pl.BlockSpec(memory_space=pltpu.SMEM)] + [vmem_spec()] * 10 + [any_spec()] * 3 + ([vmem_spec(), any_spec()] if layer == 0 else []),
+        out_specs=[vmem_spec(), any_spec(), vmem_spec(), vmem_spec()]
+        + ([vmem_spec()] + [any_spec()] * 3 if layer == 0 else []),
         scratch_shapes=[
             pltpu.VMEM((4 * count, model), BF16),
             pltpu.VMEM((count, width), BF16),
@@ -1390,8 +1626,21 @@
             pltpu.SemaphoreType.DMA((2,)),
             pltpu.SemaphoreType.DMA((2,)),
             pltpu.SemaphoreType.DMA,
+            *(gain_spec(wides, block.shape) if layer == 0 else []),
+            *(
+                [
+                    *line_spec(wides, rows, lined.shape[1], 2),
+                    *line_spec(wides, rows, head + kv_part, 2),
+                    pltpu.VMEM((rows, lined.shape[1]), BF16),
+                    pltpu.SemaphoreType.DMA,
+                    pltpu.SemaphoreType.DMA,
+                    pltpu.SemaphoreType.DMA,
+                ]
+                if layer == 0 and rows % 16 == 0
+                else []
+            ),
         ],
-        compiler_params=params(collective_id, 48),
+        compiler_params=params(collective_id, 56 if layer == 0 else 48),
     )(length, dh, a, x, gains, head_gains, trig, q_raw, k_raw, window, lse, pack, xn, o, *deps)
 
 
@@ -1440,6 +1689,7 @@
     pack = jnp.concatenate([w_q[0], w_o[0].T, kv_own, gain_columns], axis=1)
 
     late = after(core.reshape(1), pack)[0]
+    pack = (lax.all_gather(pack, "wide", axis=0, tiled=True),)
 
     def half_of(side):
         gate_up = lax.dynamic_slice_in_dim(w_gate_up[0], side * half, half, 0)
@@ -1459,8 +1709,7 @@
         (both, both, padded),
         (gather(feed[1][:, : 2 * padded]), gather(feed[1][:, 2 * padded :]), padded),
     ]
-    pack = lax.all_gather(pack, "wide", axis=0, tiled=True)
-    packs, gain_packs = gather_pack(pack, pack_width, 6)
+    packs, gain_packs = gather_pack(pack, model, pack_width, 6)
 
     def gains_of(section):
         columns = gain_packs[section].astype(F32)
@@ -1487,6 +1736,10 @@
         if section == 0:
             x, f = feed_down(h, layer_gains[3:4], act, w_down, 12)
             outs.append(x)
+
+    def by_section(first, second):
+        stays, came = by_core(first, second), swap(by_core(second, first))
+        return jnp.stack([by_core(stays, came), by_core(came, stays)])
 
     real = (positions < length).astype(F32)[:, None]
     dy = lax.dynamic_index_in_dim(cotangent, core, 0, keepdims=False).astype(F32) * real
@@ -1506,20 +1759,32 @@
             )
         down_sums[section] = scatter(d_down)
         dh, d_up, dg2 = feed_back_down(dy, h, layer_gains[2:3], dgu, mid_rows, w_up, 16 + section)
-        up_sums[section] = scatter(d_up)
-        dg23 = (dg2, dg3)
+        if section or block % 16:
+            up_sums[section] = scatter(d_up)
         a, x, q_raw, k_raw, window, lse = kept_a
-        dx, extra, dg01, dhead = attend_back(
+        if section == 0:
+            zeros = jnp.zeros((2, model), F32)
+            gain_grads[0] = jnp.concatenate([zeros, dg2, dg3, zeros, zeros])
+            section_out = by_section(*outs)
+            deps = (jnp.concatenate(gain_grads), after(d_up, up_sums[1], section_out))
+        dx, extra, dg01, dhead, *more = attend_back(
             length_one, dh, a, x, layer_gains, head_gain, trig, q_raw, k_raw, window, lse, packs, xn, o,
-            () if section else (up_sums[1],), section, 18 + section,
+            () if section else deps, section, 18 + section,
         )
         dxs[section] = dx
-        head_row = jnp.pad(dhead.reshape(1, -1), ((0, 0), (0, model - dhead.size)))
-        gain_grads[section] = jnp.concatenate([dg01, *dg23, head_row, jnp.zeros((3, model), F32)])
+        if section:
+            head_row = jnp.pad(dhead.reshape(1, -1), ((0, 0), (0, model - dhead.size)))
+            gain_grads[1] = jnp.concatenate([dg01, dg2, dg3, head_row, jnp.zeros((3, model), F32)])
+        else:
+            gain_sums, up_lined, came_up, attention_lined = more
+            if block % 16 == 0:
+                up_sums[0] = up_lined
+            else:
+                came_up = swap(up_sums[0])
         dy = dx
-    outs = [after(out, extra) for out in outs]
     split = down_sums[1].shape[1]
-    attention_sums = (scatter(extra), down_sums[0][:, split:])
+    attention_zero = scatter(extra) if block % 16 else attention_lined
+    attention_sums = (attention_zero, down_sums[0][:, split:])
     down_sums[0] = down_sums[0][:, :split]
 
     def own_section(first, second):
@@ -1527,11 +1792,12 @@
         stays = by_core(first, second)
         return by_core(stays, came).astype(F32), by_core(came, stays).astype(F32)
 
-    grad_gate_up = jnp.stack(own_section(*up_sums), axis=1)[:, :, :hidden]
+    grad_gate_up, flag = pair_up(*up_sums, came_up, swap(up_sums[1]), hidden)
     grad_down = jnp.concatenate(own_section(*down_sums), axis=1)[:, :hidden].T
-    grad_q, grad_kv, grad_o = finish_attention(*attention_sums, grad_gate_up, head_width, 1)
+    grad_q, grad_kv, grad_o = finish_attention(
+        *attention_sums, swap(attention_sums[1]), flag, head_width, 1
+    )
     grad_o = grad_o.T
-    gain_sums = sum_gains(jnp.concatenate(gain_grads), n_wide, 7)
     gain_sums = lax.dynamic_slice_in_dim(gain_sums, core * 8, 8, 0)
     wide = lax.axis_index("wide")
     grad_norm = lax.dynamic_slice_in_dim(gain_sums[:4], wide * block, block, 1)
@@ -1539,12 +1805,8 @@
     head_block = head_width // n_wide
     grad_head = lax.dynamic_slice_in_dim(grad_head, wide * head_block, head_block, 1)
 
-    def by_section(first, second):
-        stays, came = by_core(first, second), swap(by_core(second, first))
-        return jnp.stack([by_core(stays, came), by_core(came, stays)])
-
     return (
-        by_section(*outs)[None],
+        section_out[None],
         by_section(*dxs)[None],
         grad_norm[None],
         grad_head[None],

time: 682 us -> 675 us (0.990)
  Pallas kernels: 496 us -> 543 us
  waiting for transfers between devices: 74.4 us -> 41.3 us
  other arithmetic: 29.5 us -> 17.6 us
  local copies, waits for them, and re-layouts: 57.2 us -> 46.3 us
    pallas_call x2, Pallas kernels: 96.5 us -> 157 us  [attend_back(): pl.pallas_call(functools.partial(attend_back_kernel, layer), out_shape=[j...]
    reduce_scatter x5 -> x3, waiting for transfers between devices: 32.9 us -> 0.01 us  [scatter(): return lax.psum_scatter(member, 'wide', scatter_dimension=0, tiled=True)]
    pallas_call x1, Pallas kernels: 20.2 us -> 4.15 us  [pair_up(): pl.pallas_call(pair_kernel, out_shape=[jax.ShapeDtypeStruct((zero.shape[0...]
    unnamed x104 -> x87, local copies, waits for them, and re-layouts: 39.9 us -> 29.7 us
    broadcast_in_dim x2 -> x0, other arithmetic: 9.79 us -> none  [the longest x1 8.66 us: on_device(): grad_gate_up[None]]
  transfers between devices with their start and end apart: 14 -> 13, of which waited for: 5 -> 4; matrix products, arithmetic and copies ran while one was open for 6% -> 4% of each run, Pallas kernels for 64% -> 72%
where the time goes in v5:
time: 675 us; the launch traced here: 669 us
  Pallas kernels  543 us (80%)
  local copies, waits for them, and re-layouts  46.3 us (7%)
  waiting for transfers between devices  41.3 us (6%)
  other arithmetic  17.6 us (3%)
  between operations  16.3 us (2%)
    pallas_call x2, Pallas kernels, attend_back(): pl.pallas_call(functools.partial(attend_back_kernel, layer), out_shape=[j...  157 us
    pallas_call x2, Pallas kernels, attend(): pl.pallas_call(functools.partial(attend_kernel, layer), out_shape=shapes,...  77.6 us
    pallas_call x2, Pallas kernels, feed_back_down(): pl.pallas_call(back_down_kernel, out_shape=[jax.ShapeDtypeStruct((count,...  65.4 us
    pallas_call x1, Pallas kernels, feed_turn(): pl.pallas_call(turn_kernel, out_shape=[jax.ShapeDtypeStruct((count, model...  58.8 us
    pallas_call x2, Pallas kernels, feed_up(): pl.pallas_call(up_kernel, out_shape=shapes, in_specs=[vmem_spec(), vmem_s...  56.8 us
    pallas_call x1, Pallas kernels, gather_pack(): pl.pallas_call(pack_kernel, out_shape=[jax.ShapeDtypeStruct((2, 4, model,...  53.9 us
    pallas_call x1, Pallas kernels, feed_back_up(): pl.pallas_call(back_up_kernel, out_shape=[jax.ShapeDtypeStruct(gu.shape,...  34 us
    all_gather x1, waiting for transfers between devices, on_device(): pack = (lax.all_gather(pack, 'wide', axis=0, tiled=True),)  30.9 us
  transfers between devices with their start and end apart: 13, of which 4 were waited for; matrix products, arithmetic and copies ran while one was open for 4% of the time, Pallas kernels for 72%

profile of v5, /device:TPU:0, one launch (start us, length us, event | category | flops | bytes accessed | tf_op | source)
XLA Modules:
  0.0 669.1 jit_solution(11002944073340241368)
XLA Ops:
  10.6 1.8 pad_maximum_fusion.2.refs_1_
  14.2 3.0 dynamic-slice_bitcast_fusion.1
  18.1 1.1 copy-done.34
  19.3 1.2 fusion.3
  22.0 2.3 collective-permute-done
  24.4 3.0 broadcast_select_fusion
  27.5 1.1 slice.86
  31.8 1.2 convert_multiply_fusion.dy_ref
  33.0 30.9 %all-gather.5.cloned.1.call-done.refs_0_ = bf16[1152,768]{1,0:T(8,128)(2,1)} async-done(((bf16[288,768]{1,0:T(8,128)(2,1)}), bf16[1152,768]{1,0:T(8,128)(2,1)}) %all-gather.5.cloned.1.call-update) | async-done | bytes 1769488 | tf_op jit(solution)/shard_map/all_gather | solution.py:1692
  63.9 1.5 copy-done.14
  65.4 53.9 %shard_map.169 = (bf16[2,4,1152,640]{3,2,1,0:T(8,128)(2,1)S(1)}, bf16[2,1152,128]{2,1,0:T(8,128)(2,1)S(1)}) custom-call(bf16[1152,768]{1,0:T(8,128)(2,1)S(1)} %copy-done.14), custom_call_target="tpu_custom_call" | custom-call | tf_op jit(solution)/shard_map/pallas_call | solution.py:986
  119.3 4.2 copy-done.2
  124.7 40.1 %shard_map.170 = (f32[256,1152]{1,0:T(8,128)S(1)}, bf16[256,1152]{1,0:T(8,128)(2,1)}, f32[256,1024]{1,0:T(8,128)S(1)}, f32[256,256]{1,0:T(8,128)S(1)}, bf16[768,...) custom-call(s32[1]{0:T(128)} %bitcast.length_ref, ...), custom_call_target="tpu_custom_call" | custom-call | tf_op jit(solution)/shard_map/pallas_call | solution.py:1342
  164.8 1.1 copy-done.5
  165.9 1.4 copy-done.12
  167.3 1.0 copy-done.15
  168.3 1.0 copy-done.17
  173.9 6.3 all-gather.7.cloned.1.call-done.w_ref
  180.2 28.5 %shard_map.172 = (bf16[1024,1152]{1,0:T(8,128)(2,1)}, bf16[1024,3584]{1,0:T(8,128)(2,1)}, bf16[1024,1792]{1,0:T(8,128)(2,1)}) custom-call(f32[256,1152]{1,0:T(8,128)} %copy-done.5, f32[1,1152]{1,0:T(1,128)} %get-tuple-element.135.gain_ref, bf16[1152,5376]{1,0:T(8,128)(2,1)} %all-gather.7.cloned.1.call-done.w_ref), custom_call_target="tpu_custom_call" | custom-call | tf_op jit(solution)/shard_map/pallas_call | solution.py:475
  208.7 28.1 %shard_map.173 = (bf16[256,1152]{1,0:T(8,128)(2,1)}, f32[256,1152]{1,0:T(8,128)}) custom-call(f32[256,1152]{1,0:T(8,128)} %copy-done.5, f32[1,1152]{1,0:T(1,128)} %get-tuple-element.136.gain_ref, bf16[1024,1792]{1,0:T(8,128)(2,1)} %get-tuple-element.65.act_ref, bf16[1152,5376]{1,0:T(8,128)(2,1)} %all-gather.7.cloned.1.call-done.w_ref), custom_call_target="tpu_custom_call" | custom-call | tf_op jit(solution)/shard_map/pallas_call | solution.py:532
  236.8 1.1 copy-done.7
  237.9 37.5 %shard_map.174 = (f32[256,1152]{1,0:T(8,128)S(1)}, bf16[256,1152]{1,0:T(8,128)(2,1)}, f32[256,1024]{1,0:T(8,128)S(1)}, f32[256,256]{1,0:T(8,128)S(1)}, bf16[768,...) custom-call(s32[1]{0:T(128)} %bitcast.length_ref, ...), custom_call_target="tpu_custom_call" | custom-call | tf_op jit(solution)/shard_map/pallas_call | solution.py:1342
  275.4 1.0 copy-done.6
  276.4 1.4 copy-done.13
  277.8 1.0 copy-done.16
  279.6 28.3 %shard_map.175 = (bf16[1024,1152]{1,0:T(8,128)(2,1)}, bf16[1024,3584]{1,0:T(8,128)(2,1)}, bf16[1024,1792]{1,0:T(8,128)(2,1)}) custom-call(f32[256,1152]{1,0:T(8,128)} %copy-done.6, f32[1,1152]{1,0:T(1,128)} %get-tuple-element.133.gain_ref, bf16[1152,3584]{1,0:T(8,128)(2,1)} %all-gather.9.cloned.1.call-done.w_ref), custom_call_target="tpu_custom_call" | custom-call | tf_op jit(solution)/shard_map/pallas_call | solution.py:475
  307.9 58.8 %shard_map.176 = (bf16[256,1152]{1,0:T(8,128)(2,1)}, bf16[1024,3584]{1,0:T(8,128)(2,1)}, bf16[1152,896]{1,0:T(8,128)(2,1)}, f32[1,1152]{1,0:T(1,128)}) custom-call(f32[256,1152]{1,0:T(8,128)} %copy-done.6, f32[1,1152]{1,0:T(1,128)} %get-tuple-element.134.gain_ref, f32[256,1152]{1,0:T(8,128)} %convert_multiply_fusion.dy_ref, ...), custom_call_target="tpu_custom_call" | custom-call | tf_op jit(solution)/shard_map/pallas_call | solution.py:770
  366.8 32.6 %shard_map.177 = (f32[256,1152]{1,0:T(8,128)}, bf16[1152,1792]{1,0:T(8,128)(2,1)}, f32[1,1152]{1,0:T(1,128)}) custom-call(f32[256,1152]{1,0:T(8,128)} %convert_multiply_fusion.dy_ref, f32[256,1152]{1,0:T(8,128)} %copy-done.6, f32[1,1152]{1,0:T(1,128)} %get-tuple-element.133.gain_ref, bf16[1024,3584]{1,0:T(8,128)(2,1)} %get-tuple-element.71.dgu_ref, ...), custom_call_target="tpu_custom_call" | custom-call | tf_op jit(solution)/shard_map/pallas_call | solution.py:893
  400.5 1.0 copy-done.25
  401.5 48.2 %shard_map.178 = (f32[256,1152]{1,0:T(8,128)S(1)}, bf16[1152,384]{1,0:T(8,128)(2,1)S(1)}, f32[2,1152]{1,0:T(2,128)S(1)}, f32[2,256]{1,0:T(2,128)S(1)}) custom-call(s32[1]{0:T(128)} %bitcast.length_ref, f32[256,1152]{1,0:T(8,128)} %get-tuple-element.73.dh_ref, f32[256,1152]{1,0:T(8,128)} %copy-done.16, bf16[256,1152]{1,0:T(8,128)(2,1)S(1)} %copy-done.8, ...), custom_call_target="tpu_custom_call" | custom-call | tf_op jit(solution)/shard_map/pallas_call | solution.py:1579
  449.7 1.0 copy-done.3
  451.7 34.0 %shard_map.179 = (bf16[1024,3584]{1,0:T(8,128)(2,1)}, bf16[1152,1280]{1,0:T(8,128)(2,1)}, f32[1,1152]{1,0:T(1,128)}) custom-call(f32[256,1152]{1,0:T(8,128)} %copy-done.3, f32[256,1152]{1,0:T(8,128)} %get-tuple-element.82.f_ref, f32[1,1152]{1,0:T(1,128)} %get-tuple-element.136.gain_ref, bf16[1024,3584]{1,0:T(8,128)(2,1)} %get-tuple-element.83.gu_ref, ...), custom_call_target="tpu_custom_call" | custom-call | tf_op jit(solution)/shard_map/pallas_call | solution.py:806
  485.7 1.0 copy-done.32
  487.6 1.6 collective-permute-done.1
  489.4 1.6 pad_maximum_fusion
  491.0 32.8 %shard_map.180 = (f32[256,1152]{1,0:T(8,128)}, bf16[1152,1792]{1,0:T(8,128)(2,1)}, f32[1,1152]{1,0:T(1,128)}) custom-call(f32[256,1152]{1,0:T(8,128)} %copy-done.3, f32[256,1152]{1,0:T(8,128)} %copy-done.5, f32[1,1152]{1,0:T(1,128)} %get-tuple-element.135.gain_ref, bf16[1024,3584]{1,0:T(8,128)(2,1)} %get-tuple-element.86.dgu_ref, ...), custom_call_target="tpu_custom_call" | custom-call | tf_op jit(solution)/shard_map/pallas_call | solution.py:893
  523.9 2.0 concatenate.27.refs_0_
  525.9 108.4 %shard_map.182 = (f32[256,1152]{1,0:T(8,128)}, bf16[1152,384]{1,0:T(8,128)(2,1)}, f32[2,1152]{1,0:T(2,128)}, f32[2,256]{1,0:T(2,128)}, f32[16,1152]{1,0:T(8,128)...) custom-call(s32[1]{0:T(128)} %bitcast.length_ref, ...), custom_call_target="tpu_custom_call" | custom-call | tf_op jit(solution)/shard_map/pallas_call | solution.py:1579
  634.4 1.1 broadcast_select_fusion.2
  635.6 1.8 collective-permute-start.2
  638.8 1.4 dynamic-slice_bitcast_fusion.6
  640.2 1.2 copy-done.19
  641.4 4.1 shard_map.183
  645.5 1.3 broadcast_select_fusion.8
  647.1 1.5 select_bitcast_fusion.1
  649.1 1.6 maximum_bitcast_fusion
  650.6 7.5 %shard_map.184 = (f32[288,256]{1,0:T(8,128)S(1)}, f32[288,512]{1,0:T(8,128)S(1)}, f32[288,256]{1,0:T(8,128)S(1)}) custom-call(bf16[288,384]{1,0:T(8,128)(2,1)S(1)} %copy-done.28, bf16[288,384]{1,0:T(8,128)(2,1)S(1)} %slice.88.one_ref, bf16[288,384]{1,0:T(8,128)(2,1)S(1)} %collective-permute-done.3.early_ref, f32[8,128]{1,0:T(8,128)S(1)} %get-tuple-element.110.dep_ref), custom_call_target="tpu_custom_call" | custom-call | tf_op jit(solution)/shard_map/pallas_call | solution.py:1044
  658.3 1.4 convert_bitcast_fusion
  (140 shorter events, 23.6 us)
Async XLA Ops:
  7.2 24.5 %copy-start = (bf16[2,256,1152]{2,1,0:T(8,128)(2,1)S(1)}, bf16[2,256,1152]{2,1,0:T(8,128)(2,1)}, u32[]{:S(2)}) copy-start(bf16[2,256,1152]{2,1,0:T(8,128)(2,1)} %param.10) | copy-start | bytes 3538948
  7.2 56.7 %all-gather.5.cloned.1.call-start = ((), (), s32[]{:S(2)}) async-start(), calls=%async_computation.3 | async-start | bytes 2211840 | tf_op jit(solution)/shard_map/all_gather | solution.py:1692
  18.0 1.2 copy-start.34
  20.6 3.8 collective-permute-start
  21.0 159.1 %all-gather.7.cloned.1.call-start = ((), (), s32[]{:S(2)}) async-start(), calls=%async_computation.4 | async-start | bytes 13934592 | tf_op jit(solution)/shard_map/all_gather | solution.py:1705
  27.4 252.2 %all-gather.9.cloned.1.call-start = ((), (), s32[]{:S(2)}) async-start(), calls=%async_computation.5 | async-start | bytes 9289728 | tf_op jit(solution)/shard_map/all_gather | solution.py:1705
  28.6 1.3 copy-start.39
  28.6 279.3 %all-gather.11.cloned.1.call-start = ((), (), s32[]{:S(2)}) async-start(), calls=%async_computation.6 | async-start | bytes 4644864 | tf_op jit(solution)/shard_map/all_gather | solution.py:1705
  29.5 2.3 copy-start.35
  29.5 422.2 %reduce-scatter.4.cloned.1.call-start = ((), (), s32[]{:S(2)}) async-start(), calls=%async_computation.7 | async-start | bytes 2580480 | tf_op jit(solution)/shard_map/reduce_scatter | solution.py:1658
  31.7 367.8 %copy-start.9 = (f32[256,256]{1,0:T(8,128)}, f32[256,256]{1,0:T(8,128)S(1)}, u32[]{:S(2)}) copy-start(f32[256,256]{1,0:T(8,128)S(1)} %pad_maximum_fusion.3.trig_ref) | copy-start | bytes 786436
  31.8 92.9 %copy-start.10 = (bf16[256,1152]{1,0:T(8,128)(2,1)}, bf16[256,1152]{1,0:T(8,128)(2,1)S(1)}, u32[]{:S(2)}) copy-start(bf16[256,1152]{1,0:T(8,128)(2,1)S(1)} %dynamic-slice_bitcast_fusion.2.x_ref) | copy-start | bytes 1769476
  63.9 1.5 copy-start.14
  119.2 4.2 copy-start.2
  124.3 40.5 %copy-start.29 = (f32[2,256]{1,0:T(2,128)}, f32[2,256]{1,0:T(2,128)S(1)}, u32[]{:S(2)}) copy-start(f32[2,256]{1,0:T(2,128)S(1)} %copy.33.head_ref) | copy-start | bytes 6148
  124.7 40.1 %copy-start.27 = (f32[4,1152]{1,0:T(4,128)}, f32[4,1152]{1,0:T(4,128)S(1)}, u32[]{:S(2)}) copy-start(f32[4,1152]{1,0:T(4,128)S(1)} %convert_bitcast_fusion.2.gains_ref) | copy-start | bytes 55300
  164.8 1.1 copy-start.5
  165.9 1.4 copy-start.12
  167.3 1.0 copy-start.15
  168.3 1.0 copy-start.17
  169.4 0.9 copy-start.21
  236.8 1.1 copy-start.7
  275.4 1.0 copy-start.6
  276.4 1.4 copy-start.13
  277.8 1.0 copy-start.16
  366.8 159.1 %reduce-scatter.6.cloned.1.call-start = ((), (), s32[]{:S(2)}) async-start(), calls=%async_computation.8 | async-start | bytes 5160960 | tf_op jit(solution)/shard_map/reduce_scatter | solution.py:1658
  399.4 1.1 copy-start.8
  399.4 246.1 %reduce-scatter.8.cloned.1.call-start = ((), (), s32[]{:S(2)}) async-start(), calls=%async_computation.9 | async-start | bytes 3686400 | tf_op jit(solution)/shard_map/reduce_scatter | solution.py:1658
  400.5 1.0 copy-start.25
  449.7 1.0 copy-start.3
  485.7 1.1 copy-start.32
  486.9 2.4 collective-permute-start.1
  491.0 32.9 %copy-start.36 = (f32[1,1152]{1,0:T(1,128)S(1)}, f32[1,1152]{1,0:T(1,128)}, u32[]{:S(2)}) copy-start(f32[1,1152]{1,0:T(1,128)} %get-tuple-element.100) | copy-start | bytes 13828
  491.0 32.9 %copy-start.37 = (f32[1,1152]{1,0:T(1,128)S(1)}, f32[1,1152]{1,0:T(1,128)}, u32[]{:S(2)}) copy-start(f32[1,1152]{1,0:T(1,128)} %get-tuple-element.99) | copy-start | bytes 13828
  491.0 32.9 %copy-start.38 = (f32[1,1152]{1,0:T(1,128)S(1)}, f32[1,1152]{1,0:T(1,128)}, u32[]{:S(2)}) copy-start(f32[1,1152]{1,0:T(1,128)} %get-tuple-element.97) | copy-start | bytes 13828
  525.9 108.5 %copy-start.11 = (bf16[288,1792]{1,0:T(8,128)(2,1)S(1)}, bf16[288,1792]{1,0:T(8,128)(2,1)}, u32[]{:S(2)}) copy-start(bf16[288,1792]{1,0:T(8,128)(2,1)} %reduce-scatter.6.cloned.1.call-done.refs_1_.one_ref) | copy-start | bytes 3096580
  525.9 108.5 %copy-start.4 = (f32[256,1152]{1,0:T(8,128)S(1)}, f32[256,1152]{1,0:T(8,128)}, u32[]{:S(2)}) copy-start(f32[256,1152]{1,0:T(8,128)} %copy-done.3) | copy-start | bytes 3538948
  634.3 5.9 collective-permute-start.4
  634.4 5.8 copy-start.18
  635.6 11.4 %collective-permute-start.2 = (f32[256,1152]{1,0:T(8,128)}, f32[256,1152]{1,0:T(8,128)}, u32[]{:S(2)}, u32[]{:S(2)}) collective-permute-start(f32[256,1152]{1,0:T(8,128)} %broadcast_select_fusion.2), channel_id=1, source_target_pairs={{0,16},{16,0},{1,17},{17,1},{2,18},{18,2},{3,19},{19,3},{4,20},{20... | collective-permute-start | bytes 3538952 | tf_op jit(solution)/shard_map/ppermute | solution.py:1676
  640.2 1.2 copy-start.19
  645.5 1.6 copy-start.30
  646.9 1.7 copy-start.33
  646.9 11.2 %collective-permute-start.5 = (bf16[288,896]{1,0:T(8,128)(2,1)S(1)}, bf16[288,896]{1,0:T(8,128)(2,1)S(1)}, u32[]{:S(2)}, u32[]{:S(2)}) collective-permute-start(bf16[288,896]{1,0:T(8,128)(2,1)S(1)} %broadcast_select_fusion.8), channel_id=1, source_target_pairs={{0,16},{16,0},{1,17},{17,1},{2,18},{18,2},{3,19},{19,3},{4,20},{20... | collective-permute-start | bytes 1548296 | tf_op jit(solution)/shard_map/ppermute | solution.py:1676
  648.6 2.0 collective-permute-start.3
  649.1 1.6 copy-start.28
  649.1 9.1 %copy-start.31 = (bf16[288,896]{1,0:T(8,128)(2,1)S(1)}, bf16[288,896]{1,0:T(8,128)(2,1)}, u32[]{:S(2)}) copy-start(bf16[288,896]{1,0:T(8,128)(2,1)} %reduce-scatter.4.cloned.1.call-done.refs_1_) | copy-start | bytes 1548292
  658.3 3.7 copy-start.1
  (5 other events, 4.1 us)
Sparse Core Ops, SparseCore 0:
  21.2 42.7 all-gather.4
  66.1 113.9 all-gather.6
  181.8 79.1 all-gather.8
  262.5 45.0 all-gather.10
  366.9 41.7 reduce-scatter.3
  411.0 75.0 reduce-scatter.5
  488.4 66.4 reduce-scatter.7

commit v6 on v5

--- a/solution.py
+++ b/solution.py
@@ -13,7 +13,7 @@
 ROPE_BASE = 10000.0
 MESH = pl.DeviceIdType.MESH
 MIB = 2**20
-GAIN_COLUMNS = 128
+GAIN_ROWS = 16
 F32 = jnp.float32
 BF16 = jnp.bfloat16
 
@@ -339,11 +339,13 @@
     def end(self):
         for fold in self.folds:
             fold.finish(self.result)
-        copy = pltpu.make_async_copy(self.result, self.dst, self.loads.at[self.own.shape[0]])
-        copy.start()
+        if self.dst is not None:
+            copy = pltpu.make_async_copy(self.result, self.dst, self.loads.at[self.own.shape[0]])
+            copy.start()
         for fold in self.folds:
             fold.close()
-        copy.wait()
+        if self.dst is not None:
+            copy.wait()
 
 
 class Deal:
@@ -598,6 +600,8 @@
 
 
 def back_up_kernel(dy_ref, f_ref, gain_ref, gu_ref, act_ref, w_ref, *refs):
+    if len(refs) == 18:
+        refs = refs[1:]
     if len(refs) == 19:
         extra_ref, _, *refs = refs
     else:
@@ -802,12 +806,12 @@
     count, model = dy.shape
     total, hidden = act.shape
     tiles = len(column_tiles(hidden // 2))
-    extras = () if extra is None else extra
+    extras = extra
     return pl.pallas_call(
         back_up_kernel,
         out_shape=[
             jax.ShapeDtypeStruct(gu.shape, BF16),
-            jax.ShapeDtypeStruct((model, hidden // 2 + sum(e.shape[1] for e in extras[:1])), BF16),
+            jax.ShapeDtypeStruct((model, hidden // 2 + sum(e.shape[1] for e in extras[:-1])), BF16),
             jax.ShapeDtypeStruct((1, model), F32),
         ],
         in_specs=[vmem_spec()] * 3 + [any_spec()] * (3 + len(extras)),
@@ -917,38 +921,28 @@
     )(dy, h, gain, dgu, rows, w_gu)
 
 
-def pack_kernel(*refs):
-    *p_refs, o_ref, g_ref, local, send, recv, peer_send, peer_recv = refs
+def pack_kernel(p_ref, o_ref, g_ref, local, send, recv, peer_send, peer_recv):
     model, width = o_ref.shape[2:]
     half = model // 2
-    rest = g_ref.shape[2]
+    wides, extra = g_ref.shape[1:3]
+    rows = model // wides
     core = lax.axis_index("section")
     me, nx, ny = neighbours()
     met = greet({"narrow": nx}, {"narrow": ny}, {"section": 1 - core})
-    rows = p_refs[0].shape[0]
-
-    def owns(run):
-        wides = model // rows
-        for at in range(wides):
-            for distance, p_ref in enumerate(p_refs, -(len(p_refs) // 2)):
-                wide = at - distance
-                if not 0 <= wide < wides:
-                    continue
-                place = pl.ds(at * rows, rows)
-                both = [
-                    (p_ref.at[:, pl.ds(0, width)], o_ref.at[core, me, place], local.at[0, at]),
-                    (p_ref.at[:, pl.ds(width, rest)], g_ref.at[core, place], local.at[1, at]),
-                ]
-                for src, dst, sem in both:
-                    copy = pltpu.make_async_copy(src, dst, sem)
-                    if wides == 1:
-                        run(copy)()
-                    else:
-                        pl.when(lax.axis_index("wide") == wide)(run(copy))
-
-    owns(lambda copy: copy.start)
+    whole = p_ref.shape[0] == model
+    owns = []
+    if whole:
+        owns.append(pltpu.make_async_copy(p_ref, o_ref.at[core, me], local.at[0, 0]))
+    else:
+        for w in range(wides):
+            first = w * (rows + extra)
+            place = o_ref.at[core, me, pl.ds(w * rows, rows)]
+            owns.append(pltpu.make_async_copy(p_ref.at[pl.ds(first, rows)], place, local.at[0, w]))
+            part = p_ref.at[pl.ds(first + rows, extra)]
+            owns.append(pltpu.make_async_copy(part, g_ref.at[core, w], local.at[1, w]))
+    start_all(owns)
     spread = Spread(lambda block, which: o_ref.at[core, block, pl.ds(which * half, half)], send, recv)
-    owns(lambda copy: copy.wait)
+    wait_all(owns)
     met()
     spread.start()
     copies = []
@@ -965,7 +959,8 @@
         copy.start()
         copies.append(copy)
 
-    across(g_ref.at[core])
+    if not whole:
+        across(g_ref.at[core])
     across(o_ref.at[core, me])
     spread.pass_on()
     spread.x_here()
@@ -981,24 +976,24 @@
         copy.wait_send()
 
 
-def gather_pack(packs, model, width, collective_id):
-    pack = packs[0]
+def gather_pack(pack, model, wides, collective_id):
+    width = pack.shape[1]
     return pl.pallas_call(
         pack_kernel,
         out_shape=[
             jax.ShapeDtypeStruct((2, 4, model, width), pack.dtype),
-            jax.ShapeDtypeStruct((2, model, pack.shape[1] - width), pack.dtype),
+            jax.ShapeDtypeStruct((2, wides, GAIN_ROWS, width), pack.dtype),
         ],
-        in_specs=[any_spec()] * len(packs),
+        in_specs=[any_spec()],
         out_specs=[vmem_spec()] * 2,
         scratch_shapes=[
-            pltpu.SemaphoreType.DMA((2, model // pack.shape[0])),
+            pltpu.SemaphoreType.DMA((2, wides)),
             *spread_spec(),
             pltpu.SemaphoreType.DMA((5,)),
             pltpu.SemaphoreType.DMA((5,)),
         ],
         compiler_params=params(collective_id, 32),
-    )(*packs)
+    )(pack)
 
 
 def finish_kernel(
@@ -1362,10 +1357,10 @@
     pack_ref, xn_ref, o_ref, *refs
 ):
     if layer == 0:
-        block_ref, lined_ref, *refs = refs
-        block_out, lined_out, came_out, small_out = refs[4:8]
-        refs = refs[:4] + refs[8:]
-        gain_refs, line_refs = refs[36:40], refs[40:]
+        block_ref, dx_one_ref, lined_ref, early_ref, *refs = refs
+        block_out, both_out, lined_out, came_out, q_out, kv_out, o_out = refs[4:11]
+        refs = refs[:4] + refs[11:]
+        gain_refs, (dx_give, dx_send, dx_recv), line_refs = refs[36:40], refs[40:43], refs[43:]
         refs = refs[:36]
     (
     dx_out, dw_out, dgain_out, dhead_out,
@@ -1387,8 +1382,23 @@
         met = greet({"narrow": nx}, {"narrow": ny}, {"narrow": far}, {"section": 1 - core})
     if lined:
         line = LineSum(lined_ref, lined_out, *line_refs[:7])
-        small = LineSum(ours, small_out, *line_refs[7:14])
-        came_line, came_send, came_recv, came_store = line_refs[14:]
+        early = LineSum(early_ref, None, *line_refs[7:14])
+        late = LineSum(ours, None, *line_refs[14:21])
+        came_line, came_store, came_early, came_late, kv_all, cross_send, cross_recv, narrow_send, narrow_recv = (
+            line_refs[21:]
+        )
+
+        def across(at, src, dst):
+            return pltpu.make_async_remote_copy(
+                src_ref=src,
+                dst_ref=dst,
+                send_sem=cross_send.at[at],
+                recv_sem=cross_recv.at[at],
+                device_id={"section": 1 - core},
+                device_id_type=MESH,
+            )
+
+        early.load()
         line.load()
     q_loads, out_loads, kv_loads = pack_loads(pack_ref, layer, head, wq, wot, wkv, pack_load)
     loads = [
@@ -1408,6 +1418,7 @@
     met()
     spread.start()
     if lined:
+        early.begin()
         line.begin()
     wait_all(out_loads)
     do[...] = nn(da[here, :], wot[...]).astype(BF16)
@@ -1440,8 +1451,6 @@
 
     for i in range(heads):
         one_head(i)
-    if lined:
-        line.step(1, 0)
     parts[...] = jnp.zeros_like(parts)
     window = pl.ds(pl.multiple_of(me * count, count), win_ref.shape[0])
     parts[window, :head] = (dk[...] * scaling).astype(BF16)
@@ -1458,6 +1467,9 @@
     deal_q.start()
     dq_all[here, :] = dq[:, columns_of(me, head)]
     spread.pass_on()
+    if lined:
+        early.step(1, 0)
+        line.step(1, 0)
     wait_all(q_loads)
     dx_out[...] = nt(dq[...], wq[...])
     fold.pass_on()
@@ -1480,6 +1492,8 @@
         copy.start()
         swaps.append(copy)
 
+    if lined:
+        line.step(1, 1)
     by_out = tn(da[...], o[...])
     deal_q.here()
     exchange(0, pl.ds(0, head), tn(xn[...], dq_all[...]), by_out)
@@ -1503,8 +1517,23 @@
     by_value, dg0 = normed_gradient(x_ref[...].astype(F32), gains_ref[0:1, :], dxn)
     dx_out[...] = dh_ref[...] + by_value
     dgain_out[0:1, :] = dg0
+    if layer == 0:
+        zero = core == 0
+        both_out[core] = jnp.where(zero, dx_out[...], dx_one_ref[...])
+        dx_give[...] = jnp.where(zero, dx_one_ref[...], dx_out[...])
+        dx_copy = pltpu.make_async_remote_copy(
+            src_ref=dx_give,
+            dst_ref=both_out.at[core],
+            send_sem=dx_send,
+            recv_sem=dx_recv,
+            device_id={"section": 1 - core},
+            device_id_type=MESH,
+        )
+        dx_copy.start()
     if lined:
-        line.step(1, 1)
+        line.step(2, 0)
+        for step in range(2, early.steps):
+            early.step(step, 0)
     if layer == 0:
         own_total = sums.total.at[0]
         own_total[...] = block_ref[...]
@@ -1528,30 +1557,47 @@
         sums.add(1)
         sums.start(2)
     if lined:
-        small.load()
+        late.load()
+        late.begin()
         for step in range(2, line.steps):
-            for piece in (0, 1):
-                line.step(step, piece)
-        small.begin()
+            if step > 2:
+                line.step(step, 0)
+            late.step(step - 1, 0)
+            line.step(step, 1)
+        early.end()
+        crosses = [across(0, early.result, came_early)]
+        crosses[0].start()
+        late.step(late.steps - 1, 0)
+        late.end()
+        crosses.append(across(1, late.result, came_late))
+        crosses[1].start()
+        crosses[0].wait_recv()
+        by_qkv = jnp.where(zero, late.result[...], came_early[...])
+        kv_all[me] = by_qkv[:, head:]
+        narrows = [
+            remote(kv_all.at[me], kv_all.at[me], narrow_send.at[at], narrow_recv.at[at], other)
+            for at, other in enumerate((nx, ny, far))
+        ]
+        start_all(narrows)
+        q_out[...] = by_qkv[:, :head].astype(F32)
+        crosses[1].wait_recv()
+        o_out[...] = jnp.where(zero, came_late[:, :head], early.result[:, :head]).astype(F32)
+        for copy in narrows:
+            copy.wait_recv()
+        for n in range(4):
+            kv_out[:, n * kv_part : (n + 1) * kv_part] = kv_all[n].astype(F32)
         line.end()
-        cross = pltpu.make_async_remote_copy(
-            src_ref=line.result,
-            dst_ref=came_line,
-            send_sem=came_send,
-            recv_sem=came_recv,
-            device_id={"section": 1 - core},
-            device_id_type=MESH,
-        )
-        cross.start()
-        for step in range(1, small.steps):
-            for piece in range(len(small.folds)):
-                small.step(step, piece)
-        cross.wait_recv()
+        crosses.append(across(2, line.result, came_line))
+        crosses[2].start()
+        crosses[2].wait_recv()
         keep = pltpu.make_async_copy(came_line, came_out, came_store)
         keep.start()
-        small.end()
+        for copy in crosses + narrows:
+            copy.wait_send()
         keep.wait()
-        cross.wait_send()
+    if layer == 0:
+        dx_copy.wait_recv()
+        dx_copy.wait_send()
     if layer == 0:
         sums.add(2)
         block_out[...] = sums.total[3]
@@ -1572,7 +1618,7 @@
     kv_part = pack.shape[3] - 2 * head
     if layer == 0:
         wides = lax.axis_size("wide")
-        block, lined = deps
+        block, dx_one, lined, early = deps
         rows = model // wides
     deal = pltpu.SemaphoreType.DMA((3,))
     dw = pltpu.VMEM((model, head + kv_part), BF16)
@@ -1586,17 +1632,20 @@
             *(
                 [
                     jax.ShapeDtypeStruct(block.shape, F32),
+                    jax.ShapeDtypeStruct((2, count, model), F32),
                     jax.ShapeDtypeStruct((rows, lined.shape[1]), BF16),
                     jax.ShapeDtypeStruct((rows, lined.shape[1]), BF16),
-                    jax.ShapeDtypeStruct((rows, head + kv_part), BF16),
+                    jax.ShapeDtypeStruct((rows, head), F32),
+                    jax.ShapeDtypeStruct((rows, 4 * kv_part), F32),
+                    jax.ShapeDtypeStruct((rows, head), F32),
                 ]
                 if layer == 0
                 else []
             ),
         ],
-        in_specs=[pl.BlockSpec(memory_space=pltpu.SMEM)] + [vmem_spec()] * 10 + [any_spec()] * 3 + ([vmem_spec(), any_spec()] if layer == 0 else []),
+        in_specs=[pl.BlockSpec(memory_space=pltpu.SMEM)] + [vmem_spec()] * 10 + [any_spec()] * 3 + ([vmem_spec()] * 2 + [any_spec()] * 2 if layer == 0 else []),
         out_specs=[vmem_spec(), any_spec(), vmem_spec(), vmem_spec()]
-        + ([vmem_spec()] + [any_spec()] * 3 if layer == 0 else []),
+        + ([vmem_spec()] * 2 + [any_spec()] * 2 + [vmem_spec()] * 3 if layer == 0 else []),
         scratch_shapes=[
             pltpu.VMEM((4 * count, model), BF16),
             pltpu.VMEM((count, width), BF16),
@@ -1626,21 +1675,36 @@
             pltpu.SemaphoreType.DMA((2,)),
             pltpu.SemaphoreType.DMA((2,)),
             pltpu.SemaphoreType.DMA,
-            *(gain_spec(wides, block.shape) if layer == 0 else []),
+            *(
+                [
+                    *gain_spec(wides, block.shape),
+                    pltpu.VMEM((count, model), F32),
+                    pltpu.SemaphoreType.DMA,
+                    pltpu.SemaphoreType.DMA,
+                ]
+                if layer == 0
+                else []
+            ),
             *(
                 [
                     *line_spec(wides, rows, lined.shape[1], 2),
-                    *line_spec(wides, rows, head + kv_part, 2),
+                    *line_spec(wides, rows, head + kv_part, 1),
+                    *line_spec(wides, rows, head + kv_part, 1),
                     pltpu.VMEM((rows, lined.shape[1]), BF16),
                     pltpu.SemaphoreType.DMA,
-                    pltpu.SemaphoreType.DMA,
-                    pltpu.SemaphoreType.DMA,
+                    pltpu.VMEM((rows, head + kv_part), BF16),
+                    pltpu.VMEM((rows, head + kv_part), BF16),
+                    pltpu.VMEM((4, rows, kv_part), BF16),
+                    pltpu.SemaphoreType.DMA((3,)),
+                    pltpu.SemaphoreType.DMA((3,)),
+                    pltpu.SemaphoreType.DMA((3,)),
+                    pltpu.SemaphoreType.DMA((3,)),
                 ]
                 if layer == 0 and rows % 16 == 0
                 else []
             ),
         ],
-        compiler_params=params(collective_id, 56 if layer == 0 else 48),
+        compiler_params=params(collective_id, 60 if layer == 0 else 48),
     )(length, dh, a, x, gains, head_gains, trig, q_raw, k_raw, window, lse, pack, xn, o, *deps)
 
 
@@ -1683,13 +1747,15 @@
     pad = -hidden % TILE
     kv_own = lax.dynamic_slice_in_dim(w_kv[0], narrow * kv_part, kv_part, 1)
     pack_width = 2 * head_width + kv_part
-    gain_columns = jnp.zeros((block, GAIN_COLUMNS), BF16)
-    gain_columns = lax.dynamic_update_slice(gain_columns, norm_gains[0].T, (0, 0))
-    gain_columns = lax.dynamic_update_slice(gain_columns, head_gains[0].T, (0, 4))
-    pack = jnp.concatenate([w_q[0], w_o[0].T, kv_own, gain_columns], axis=1)
-
+    pack = [w_q[0], w_o[0].T, kv_own]
+    pack = jnp.concatenate(pack, axis=1)
+    if block % 16 == 0:
+        gain_rows = jnp.zeros((GAIN_ROWS, pack_width), BF16)
+        gain_rows = lax.dynamic_update_slice(gain_rows, norm_gains[0], (0, 0))
+        gain_rows = lax.dynamic_update_slice(gain_rows, head_gains[0], (4, 0))
+        pack = jnp.concatenate([pack, gain_rows], axis=0)
     late = after(core.reshape(1), pack)[0]
-    pack = (lax.all_gather(pack, "wide", axis=0, tiled=True),)
+    pack = lax.all_gather(pack, "wide", axis=0, tiled=True)
 
     def half_of(side):
         gate_up = lax.dynamic_slice_in_dim(w_gate_up[0], side * half, half, 0)
@@ -1709,12 +1775,22 @@
         (both, both, padded),
         (gather(feed[1][:, : 2 * padded]), gather(feed[1][:, 2 * padded :]), padded),
     ]
-    packs, gain_packs = gather_pack(pack, model, pack_width, 6)
+    packs, gain_packs = gather_pack(pack, model, n_wide, 6)
+    if block % 16:
+        norm_own = lax.all_gather(norm_gains[0], "wide", axis=1, tiled=True)
+        head_own = lax.all_gather(head_gains[0], "wide", axis=1, tiled=True)
+        norm_came, head_came = swap(norm_own), swap(head_own)
 
     def gains_of(section):
-        columns = gain_packs[section].astype(F32)
-        heads = columns.reshape(n_wide, block, -1)[:, : head_width // n_wide, 4:6]
-        return columns[:, :4].T, heads.transpose(2, 0, 1).reshape(2, head_width)
+        if block % 16:
+            mine = core == section
+            norm_part = jnp.where(mine, norm_own, norm_came)
+            head_part = jnp.where(mine, head_own, head_came)
+        else:
+            tail = gain_packs[section]
+            norm_part = tail[:, :4, :block].transpose(1, 0, 2).reshape(4, model)
+            head_part = tail[:, 4:6, : head_width // n_wide].transpose(1, 0, 2).reshape(2, head_width)
+        return norm_part.astype(F32), head_part.astype(F32)
 
     start = narrow * rows
     positions = start + jnp.arange(rows, dtype=jnp.int32)
@@ -1755,7 +1831,8 @@
             outs.append(out)
         else:
             dgu, d_down, dg3 = feed_back_up(
-                dy, f, layer_gains[3:4], gu, act, w_down, (extra, down_sums[1]), 14
+                dy, f, layer_gains[3:4], gu, act, w_down,
+                (extra, down_sums[1]) if block % 16 else (down_sums[1],), 14,
             )
         down_sums[section] = scatter(d_down)
         dh, d_up, dg2 = feed_back_down(dy, h, layer_gains[2:3], dgu, mid_rows, w_up, 16 + section)
@@ -1766,7 +1843,8 @@
             zeros = jnp.zeros((2, model), F32)
             gain_grads[0] = jnp.concatenate([zeros, dg2, dg3, zeros, zeros])
             section_out = by_section(*outs)
-            deps = (jnp.concatenate(gain_grads), after(d_up, up_sums[1], section_out))
+            lined = after(d_up, up_sums[1], section_out)
+            deps = (jnp.concatenate(gain_grads), dxs[1], lined, extra)
         dx, extra, dg01, dhead, *more = attend_back(
             length_one, dh, a, x, layer_gains, head_gain, trig, q_raw, k_raw, window, lse, packs, xn, o,
             () if section else deps, section, 18 + section,
@@ -1776,28 +1854,28 @@
             head_row = jnp.pad(dhead.reshape(1, -1), ((0, 0), (0, model - dhead.size)))
             gain_grads[1] = jnp.concatenate([dg01, dg2, dg3, head_row, jnp.zeros((3, model), F32)])
         else:
-            gain_sums, up_lined, came_up, attention_lined = more
+            gain_sums, input_grad, up_lined, came_up, grad_q, grad_kv, grad_o = more
             if block % 16 == 0:
                 up_sums[0] = up_lined
             else:
                 came_up = swap(up_sums[0])
         dy = dx
-    split = down_sums[1].shape[1]
-    attention_zero = scatter(extra) if block % 16 else attention_lined
-    attention_sums = (attention_zero, down_sums[0][:, split:])
-    down_sums[0] = down_sums[0][:, :split]
-
     def own_section(first, second):
         came = swap(by_core(second, first))
         stays = by_core(first, second)
         return by_core(stays, came).astype(F32), by_core(came, stays).astype(F32)
 
-    grad_gate_up, flag = pair_up(*up_sums, came_up, swap(up_sums[1]), hidden)
+    if block % 16:
+        split = down_sums[1].shape[1]
+        attention_sums = (scatter(extra), down_sums[0][:, split:])
+        down_sums[0] = down_sums[0][:, :split]
+        grad_q, grad_kv, grad_o = finish_attention(
+            *attention_sums, swap(attention_sums[1]), up_sums[0], head_width, 2
+        )
+    grad_o = grad_o.T
+    grad_gate_up, _ = pair_up(*up_sums, came_up, swap(up_sums[1]), hidden)
+    down_sums[0] = after(down_sums[0], gain_sums)
     grad_down = jnp.concatenate(own_section(*down_sums), axis=1)[:, :hidden].T
-    grad_q, grad_kv, grad_o = finish_attention(
-        *attention_sums, swap(attention_sums[1]), flag, head_width, 1
-    )
-    grad_o = grad_o.T
     gain_sums = lax.dynamic_slice_in_dim(gain_sums, core * 8, 8, 0)
     wide = lax.axis_index("wide")
     grad_norm = lax.dynamic_slice_in_dim(gain_sums[:4], wide * block, block, 1)
@@ -1807,7 +1885,7 @@
 
     return (
         section_out[None],
-        by_section(*dxs)[None],
+        input_grad[None],
         grad_norm[None],
         grad_head[None],
         grad_q[None],

time: 675 us -> 675 us (level)
    pallas_call x2, Pallas kernels: 157 us -> 169 us  [attend_back(): pl.pallas_call(functools.partial(attend_back_kernel, layer), out_shape=[j...]
    pallas_call x1 -> x0, Pallas kernels: 7.5 us -> none  [finish_attention(): pl.pallas_call(finish_kernel, out_shape=[jax.ShapeDtypeStruct((block, hea...]
    unnamed x87 -> x89, local copies, waits for them, and re-layouts: 29.7 us -> 28.7 us
  transfers between devices with their start and end apart: 13 -> 11, of which waited for: 4 -> 4; matrix products, arithmetic and copies ran while one was open for 4% -> 3% of each run, Pallas kernels for 72% -> 73%
where the time goes in v6:
time: 675 us; the launch traced here: 666 us
  Pallas kernels  547 us (81%)
  local copies, waits for them, and re-layouts  47 us (7%)
  waiting for transfers between devices  37.6 us (6%)
  between operations  16.2 us (2%)
  other arithmetic  13.7 us (2%)
    pallas_call x2, Pallas kernels, attend_back(): pl.pallas_call(functools.partial(attend_back_kernel, layer), out_shape=[j...  169 us
    pallas_call x2, Pallas kernels, attend(): pl.pallas_call(functools.partial(attend_kernel, layer), out_shape=shapes,...  77.9 us
    pallas_call x2, Pallas kernels, feed_back_down(): pl.pallas_call(back_down_kernel, out_shape=[jax.ShapeDtypeStruct((count,...  65.1 us
    pallas_call x2, Pallas kernels, feed_up(): pl.pallas_call(up_kernel, out_shape=shapes, in_specs=[vmem_spec(), vmem_s...  56.7 us
    pallas_call x1, Pallas kernels, feed_turn(): pl.pallas_call(turn_kernel, out_shape=[jax.ShapeDtypeStruct((count, model...  54.6 us
    pallas_call x1, Pallas kernels, gather_pack(): pl.pallas_call(pack_kernel, out_shape=[jax.ShapeDtypeStruct((2, 4, model,...  53.4 us
    pallas_call x1, Pallas kernels, feed_back_up(): pl.pallas_call(back_up_kernel, out_shape=[jax.ShapeDtypeStruct(gu.shape,...  34.2 us
    pallas_call x1, Pallas kernels, feed_down(): pl.pallas_call(down_kernel, out_shape=[jax.ShapeDtypeStruct((count, model...  33.1 us
  transfers between devices with their start and end apart: 11, of which 4 were waited for; matrix products, arithmetic and copies ran while one was open for 3% of the time, Pallas kernels for 73%

profile of v6, /device:TPU:0, one launch (start us, length us, event | category | flops | bytes accessed | tf_op | source)
XLA Modules:
  0.0 665.8 jit_solution(11071683514557250664)
XLA Ops:
  7.2 1.0 dynamic-slice_bitcast_fusion.5
  8.9 1.5 dynamic_update_slice.7
  10.4 1.8 pad_maximum_fusion.2.refs_1_
  14.0 3.0 dynamic-slice_bitcast_fusion.1
  18.2 1.2 fusion.3
  20.9 2.3 collective-permute-done
  23.3 3.0 broadcast_select_fusion
  26.4 1.1 slice.88
  30.4 1.2 convert_multiply_fusion.dy_ref
  31.6 27.7 %all-gather.5.cloned.1.call-done.p_ref = bf16[1216,640]{1,0:T(8,128)(2,1)} async-done(((bf16[304,640]{1,0:T(8,128)(2,1)}), bf16[1216,640]{1,0:T(8,128)(2,1)}) %all-gather.5.cloned.1.call-update) | async-done | bytes 1556496 | tf_op jit(solution)/shard_map/all_gather | solution.py:1758
  59.3 1.4 copy-done.13
  60.7 53.4 %shard_map.169 = (bf16[2,4,1152,640]{3,2,1,0:T(8,128)(2,1)S(1)}, bf16[2,4,16,640]{3,2,1,0:T(8,128)(2,1)S(1)}) custom-call(bf16[1216,640]{1,0:T(8,128)(2,1)S(1)} %copy-done.13), custom_call_target="tpu_custom_call" | custom-call | tf_op jit(solution)/shard_map/pallas_call | solution.py:981
  114.2 4.2 copy-done.2
  121.7 40.3 %shard_map.170 = (f32[256,1152]{1,0:T(8,128)S(1)}, bf16[256,1152]{1,0:T(8,128)(2,1)}, f32[256,1024]{1,0:T(8,128)S(1)}, f32[256,256]{1,0:T(8,128)S(1)}, bf16[768,...) custom-call(s32[1]{0:T(128)} %bitcast.length_ref, ...), custom_call_target="tpu_custom_call" | custom-call | tf_op jit(solution)/shard_map/pallas_call | solution.py:1337
  162.0 1.1 copy-done.3
  163.1 1.4 copy-done.11
  164.5 1.0 copy-done.15
  165.5 1.0 copy-done.16
  166.5 0.9 copy-done.20
  169.8 5.8 all-gather.7.cloned.1.call-done.w_ref
  175.6 28.5 %shard_map.172 = (bf16[1024,1152]{1,0:T(8,128)(2,1)}, bf16[1024,3584]{1,0:T(8,128)(2,1)}, bf16[1024,1792]{1,0:T(8,128)(2,1)}) custom-call(f32[256,1152]{1,0:T(8,128)} %copy-done.3, f32[1,1152]{1,0:T(1,128)} %slice.67.gain_ref, bf16[1152,5376]{1,0:T(8,128)(2,1)} %all-gather.7.cloned.1.call-done.w_ref), custom_call_target="tpu_custom_call" | custom-call | tf_op jit(solution)/shard_map/pallas_call | solution.py:477
  204.1 33.1 %shard_map.173 = (bf16[256,1152]{1,0:T(8,128)(2,1)}, f32[256,1152]{1,0:T(8,128)}) custom-call(f32[256,1152]{1,0:T(8,128)} %copy-done.3, f32[1,1152]{1,0:T(1,128)} %slice.65.gain_ref, bf16[1024,1792]{1,0:T(8,128)(2,1)} %get-tuple-element.63.act_ref, bf16[1152,5376]{1,0:T(8,128)(2,1)} %all-gather.7.cloned.1.call-done.w_ref), custom_call_target="tpu_custom_call" | custom-call | tf_op jit(solution)/shard_map/pallas_call | solution.py:534
  237.2 1.1 copy-done.6
  238.3 37.6 %shard_map.174 = (f32[256,1152]{1,0:T(8,128)S(1)}, bf16[256,1152]{1,0:T(8,128)(2,1)}, f32[256,1024]{1,0:T(8,128)S(1)}, f32[256,256]{1,0:T(8,128)S(1)}, bf16[768,...) custom-call(s32[1]{0:T(128)} %bitcast.length_ref, ...), custom_call_target="tpu_custom_call" | custom-call | tf_op jit(solution)/shard_map/pallas_call | solution.py:1337
  275.9 1.0 copy-done.4
  276.9 1.4 copy-done.12
  278.3 1.0 copy-done.14
  280.1 28.2 %shard_map.175 = (bf16[1024,1152]{1,0:T(8,128)(2,1)}, bf16[1024,3584]{1,0:T(8,128)(2,1)}, bf16[1024,1792]{1,0:T(8,128)(2,1)}) custom-call(f32[256,1152]{1,0:T(8,128)} %copy-done.4, f32[1,1152]{1,0:T(1,128)} %slice.74.gain_ref, bf16[1152,3584]{1,0:T(8,128)(2,1)} %all-gather.9.cloned.1.call-done.w_ref), custom_call_target="tpu_custom_call" | custom-call | tf_op jit(solution)/shard_map/pallas_call | solution.py:477
  308.3 54.6 %shard_map.176 = (bf16[256,1152]{1,0:T(8,128)(2,1)}, bf16[1024,3584]{1,0:T(8,128)(2,1)}, bf16[1152,896]{1,0:T(8,128)(2,1)}, f32[1,1152]{1,0:T(1,128)}) custom-call(f32[256,1152]{1,0:T(8,128)} %copy-done.4, f32[1,1152]{1,0:T(1,128)} %slice.72.gain_ref, f32[256,1152]{1,0:T(8,128)} %convert_multiply_fusion.dy_ref, ...), custom_call_target="tpu_custom_call" | custom-call | tf_op jit(solution)/shard_map/pallas_call | solution.py:774
  363.1 32.6 %shard_map.177 = (f32[256,1152]{1,0:T(8,128)}, bf16[1152,1792]{1,0:T(8,128)(2,1)}, f32[1,1152]{1,0:T(1,128)}) custom-call(f32[256,1152]{1,0:T(8,128)} %convert_multiply_fusion.dy_ref, f32[256,1152]{1,0:T(8,128)} %copy-done.4, f32[1,1152]{1,0:T(1,128)} %slice.74.gain_ref, bf16[1024,3584]{1,0:T(8,128)(2,1)} %get-tuple-element.69.dgu_ref, ...), custom_call_target="tpu_custom_call" | custom-call | tf_op jit(solution)/shard_map/pallas_call | solution.py:897
  395.7 1.0 copy-done.7
  396.7 1.0 copy-done.24
  397.8 48.1 %shard_map.178 = (f32[256,1152]{1,0:T(8,128)S(1)}, bf16[1152,384]{1,0:T(8,128)(2,1)S(1)}, f32[2,1152]{1,0:T(2,128)S(1)}, f32[2,256]{1,0:T(2,128)S(1)}) custom-call(s32[1]{0:T(128)} %bitcast.length_ref, f32[256,1152]{1,0:T(8,128)} %get-tuple-element.71.dh_ref, f32[256,1152]{1,0:T(8,128)} %copy-done.14, bf16[256,1152]{1,0:T(8,128)(2,1)S(1)} %copy-done.7, ...), custom_call_target="tpu_custom_call" | custom-call | tf_op jit(solution)/shard_map/pallas_call | solution.py:1625
  445.9 1.0 copy-done.5
  446.9 0.9 copy-done.19
  447.8 34.2 %shard_map.179 = (bf16[1024,3584]{1,0:T(8,128)(2,1)}, bf16[1152,896]{1,0:T(8,128)(2,1)}, f32[1,1152]{1,0:T(1,128)}) custom-call(f32[256,1152]{1,0:T(8,128)} %copy-done.5, f32[256,1152]{1,0:T(8,128)} %get-tuple-element.80.f_ref, f32[1,1152]{1,0:T(1,128)} %slice.65.gain_ref, bf16[1024,3584]{1,0:T(8,128)(2,1)} %get-tuple-element.81.gu_ref, ...), custom_call_target="tpu_custom_call" | custom-call | tf_op jit(solution)/shard_map/pallas_call | solution.py:810
  482.1 1.0 copy-done.31
  483.9 1.6 collective-permute-done.1
  485.6 1.6 pad_maximum_fusion
  487.2 32.6 %shard_map.180 = (f32[256,1152]{1,0:T(8,128)}, bf16[1152,1792]{1,0:T(8,128)(2,1)}, f32[1,1152]{1,0:T(1,128)}) custom-call(f32[256,1152]{1,0:T(8,128)} %copy-done.5, f32[256,1152]{1,0:T(8,128)} %copy-done.3, f32[1,1152]{1,0:T(1,128)} %slice.67.gain_ref, bf16[1024,3584]{1,0:T(8,128)(2,1)} %get-tuple-element.83.dgu_ref, ...), custom_call_target="tpu_custom_call" | custom-call | tf_op jit(solution)/shard_map/pallas_call | solution.py:897
  519.8 2.0 concatenate.31.refs_0_
  521.8 120.7 %shard_map.182 = (f32[256,1152]{1,0:T(8,128)}, bf16[1152,384]{1,0:T(8,128)(2,1)}, f32[2,1152]{1,0:T(2,128)}, f32[2,256]{1,0:T(2,128)}, f32[16,1152]{1,0:T(8,128)...) custom-call(s32[1]{0:T(128)} %bitcast.length_ref, ...), custom_call_target="tpu_custom_call" | custom-call | tf_op jit(solution)/shard_map/pallas_call | solution.py:1625
  643.4 2.5 collective-permute-start.3
  647.3 1.4 dynamic-slice_bitcast_fusion.6
  648.7 1.2 broadcast_select_fusion.5
  649.9 1.4 convert_bitcast_fusion
  652.1 2.9 shard_map.183
  655.1 1.4 copy.37
  (138 shorter events, 19.7 us)
Async XLA Ops:
  7.2 23.1 %copy-start = (bf16[2,256,1152]{2,1,0:T(8,128)(2,1)S(1)}, bf16[2,256,1152]{2,1,0:T(8,128)(2,1)}, u32[]{:S(2)}) copy-start(bf16[2,256,1152]{2,1,0:T(8,128)(2,1)} %param.10) | copy-start | bytes 3538948
  7.2 52.1 %all-gather.5.cloned.1.call-start = ((), (), s32[]{:S(2)}) async-start(), calls=%async_computation.3 | async-start | bytes 1945600 | tf_op jit(solution)/shard_map/all_gather | solution.py:1758
  16.9 1.2 copy-start.32
  19.5 3.8 collective-permute-start
  20.0 155.6 %all-gather.7.cloned.1.call-start = ((), (), s32[]{:S(2)}) async-start(), calls=%async_computation.4 | async-start | bytes 13934592 | tf_op jit(solution)/shard_map/all_gather | solution.py:1771
  26.3 253.8 %all-gather.9.cloned.1.call-start = ((), (), s32[]{:S(2)}) async-start(), calls=%async_computation.5 | async-start | bytes 9289728 | tf_op jit(solution)/shard_map/all_gather | solution.py:1771
  27.4 1.0 copy-start.40
  27.5 280.9 %all-gather.11.cloned.1.call-start = ((), (), s32[]{:S(2)}) async-start(), calls=%async_computation.6 | async-start | bytes 4644864 | tf_op jit(solution)/shard_map/all_gather | solution.py:1771
  28.4 2.0 copy-start.34
  28.4 419.4 %reduce-scatter.4.cloned.1.call-start = ((), (), s32[]{:S(2)}) async-start(), calls=%async_computation.7 | async-start | bytes 2580480 | tf_op jit(solution)/shard_map/reduce_scatter | solution.py:1722
  30.3 365.4 %copy-start.8 = (f32[256,256]{1,0:T(8,128)}, f32[256,256]{1,0:T(8,128)S(1)}, u32[]{:S(2)}) copy-start(f32[256,256]{1,0:T(8,128)S(1)} %pad_maximum_fusion.3.trig_ref) | copy-start | bytes 786436
  30.4 91.3 %copy-start.9 = (bf16[256,1152]{1,0:T(8,128)(2,1)}, bf16[256,1152]{1,0:T(8,128)(2,1)S(1)}, u32[]{:S(2)}) copy-start(bf16[256,1152]{1,0:T(8,128)(2,1)S(1)} %dynamic-slice_bitcast_fusion.2.x_ref) | copy-start | bytes 1769476
  59.3 1.4 copy-start.13
  114.1 4.3 copy-start.2
  118.5 43.5 %copy-start.26 = (f32[4,1152]{1,0:T(4,128)}, f32[4,1152]{1,0:T(4,128)S(1)}, u32[]{:S(2)}) copy-start(f32[4,1152]{1,0:T(4,128)S(1)} %convert_element_type.60.gains_ref) | copy-start | bytes 55300
  118.7 43.4 %copy-start.27 = (f32[2,256]{1,0:T(2,128)}, f32[2,256]{1,0:T(2,128)S(1)}, u32[]{:S(2)}) copy-start(f32[2,256]{1,0:T(2,128)S(1)} %reshape.85.head_ref) | copy-start | bytes 6148
  162.0 1.1 copy-start.3
  163.1 1.4 copy-start.11
  164.5 1.0 copy-start.15
  165.5 1.0 copy-start.16
  166.5 0.9 copy-start.20
  237.2 1.1 copy-start.6
  275.9 1.0 copy-start.4
  276.9 1.4 copy-start.12
  278.3 1.0 copy-start.14
  363.0 158.8 %reduce-scatter.6.cloned.1.call-start = ((), (), s32[]{:S(2)}) async-start(), calls=%async_computation.8 | async-start | bytes 5160960 | tf_op jit(solution)/shard_map/reduce_scatter | solution.py:1722
  395.6 1.1 copy-start.7
  395.7 246.8 %reduce-scatter.8.cloned.1.call-start = ((), (), s32[]{:S(2)}) async-start(), calls=%async_computation.9 | async-start | bytes 2580480 | tf_op jit(solution)/shard_map/reduce_scatter | solution.py:1722
  396.7 1.0 copy-start.24
  445.9 1.0 copy-start.5
  446.9 0.9 copy-start.19
  482.0 1.1 copy-start.31
  483.2 2.3 collective-permute-start.1
  487.2 32.6 %copy-start.37 = (f32[1,1152]{1,0:T(1,128)S(1)}, f32[1,1152]{1,0:T(1,128)}, u32[]{:S(2)}) copy-start(f32[1,1152]{1,0:T(1,128)} %get-tuple-element.97) | copy-start | bytes 13828
  487.2 32.6 %copy-start.38 = (f32[1,1152]{1,0:T(1,128)S(1)}, f32[1,1152]{1,0:T(1,128)}, u32[]{:S(2)}) copy-start(f32[1,1152]{1,0:T(1,128)} %get-tuple-element.96) | copy-start | bytes 13828
  487.2 32.6 %copy-start.39 = (f32[1,1152]{1,0:T(1,128)S(1)}, f32[1,1152]{1,0:T(1,128)}, u32[]{:S(2)}) copy-start(f32[1,1152]{1,0:T(1,128)} %get-tuple-element.94) | copy-start | bytes 13828
  521.8 120.7 %copy-start.29 = (bf16[288,896]{1,0:T(8,128)(2,1)S(1)}, bf16[288,896]{1,0:T(8,128)(2,1)}, u32[]{:S(2)}) copy-start(bf16[288,896]{1,0:T(8,128)(2,1)} %reduce-scatter.4.cloned.1.call-done.refs_0_) | copy-start | bytes 1548292
  642.5 3.4 copy-start.10
  642.5 6.2 copy-start.28
  643.4 5.3 collective-permute-start.3
  645.9 5.4 collective-permute-start.2
  649.9 1.6 copy-start.17
  649.9 2.3 copy-start.18
  652.1 2.9 copy-start.30
  655.1 1.4 copy-start.36
  655.1 2.1 copy-start.33
  655.1 3.7 copy-start.1
  656.5 1.5 copy-start.35
  (4 other events, 3.1 us)
Sparse Core Ops, SparseCore 0:
  20.1 39.2 all-gather.4
  61.6 113.9 all-gather.6
  177.2 79.2 all-gather.8
  258.0 45.0 all-gather.10
  363.1 41.2 reduce-scatter.3
  406.7 75.0 reduce-scatter.5
  484.1 43.6 reduce-scatter.7

commit v7 on v6

--- a/solution.py
+++ b/solution.py
@@ -1186,6 +1186,57 @@
         pltpu.SemaphoreType.DMA((wides + 3,)),
         pltpu.SemaphoreType.DMA((wides + 3,)),
     ]
+
+
+def trade_kernel(keep_ref, give_ref, zero_ref, one_ref, came, send, recv):
+    core = lax.axis_index("section")
+    met = greet({"section": 1 - core})
+    met()
+    copy = pltpu.make_async_remote_copy(
+        src_ref=give_ref,
+        dst_ref=came,
+        send_sem=send,
+        recv_sem=recv,
+        device_id={"section": 1 - core},
+        device_id_type=MESH,
+    )
+    copy.start()
+
+    @pl.when(core == 0)
+    def _():
+        zero_ref[...] = keep_ref[...]
+
+    @pl.when(core == 1)
+    def _():
+        one_ref[...] = keep_ref[...]
+
+    copy.wait_recv()
+
+    @pl.when(core == 0)
+    def _():
+        one_ref[...] = came[...]
+
+    @pl.when(core == 1)
+    def _():
+        zero_ref[...] = came[...]
+
+    copy.wait_send()
+
+
+def trade(keep, give, collective_id):
+    shape = jax.ShapeDtypeStruct(keep.shape, keep.dtype)
+    return pl.pallas_call(
+        trade_kernel,
+        out_shape=[shape, shape],
+        in_specs=[vmem_spec()] * 2,
+        out_specs=[vmem_spec()] * 2,
+        scratch_shapes=[
+            pltpu.VMEM(keep.shape, keep.dtype),
+            pltpu.SemaphoreType.DMA,
+            pltpu.SemaphoreType.DMA,
+        ],
+        compiler_params=params(collective_id, 16),
+    )(keep, give)
 
 
 def turn_back(grad, cosine, sine_table):
@@ -1763,8 +1814,7 @@
         down = lax.dynamic_slice_in_dim(w_down[0].T, side * half, half, 0)
         return jnp.concatenate([gate_up, jnp.pad(down, ((0, 0), (0, pad)))], axis=1)
 
-    keep, came = half_of(late), swap(half_of(1 - late))
-    feed = by_core(keep, came), by_core(came, keep)
+    feed = trade(half_of(late), half_of(1 - late), 7)
     padded = hidden + pad
 
     def gather(member):

time: 675 us -> 666 us (0.987)
  waiting for transfers between devices: 37.6 us -> 29.4 us
    unnamed x89 -> x87, local copies, waits for them, and re-layouts: 28.7 us -> 28.7 us
  transfers between devices with their start and end apart: 11 -> 10, of which waited for: 4 -> 3; matrix products, arithmetic and copies ran while one was open for 3% -> 3% of each run, Pallas kernels for 73% -> 75%
where the time goes in v7:
time: 666 us; the launch traced here: 657 us
  Pallas kernels  552 us (83%)
  local copies, waits for them, and re-layouts  47 us (7%)
  waiting for transfers between devices  29.4 us (4%)
  between operations  16.3 us (2%)
  other arithmetic  9.08 us (1%)
    pallas_call x2, Pallas kernels, attend_back(): pl.pallas_call(functools.partial(attend_back_kernel, layer), out_shape=[j...  169 us
    pallas_call x2, Pallas kernels, attend(): pl.pallas_call(functools.partial(attend_kernel, layer), out_shape=shapes,...  78 us
    pallas_call x2, Pallas kernels, feed_back_down(): pl.pallas_call(back_down_kernel, out_shape=[jax.ShapeDtypeStruct((count,...  65.2 us
    pallas_call x2, Pallas kernels, feed_up(): pl.pallas_call(up_kernel, out_shape=shapes, in_specs=[vmem_spec(), vmem_s...  56.7 us
    pallas_call x1, Pallas kernels, feed_turn(): pl.pallas_call(turn_kernel, out_shape=[jax.ShapeDtypeStruct((count, model...  54.6 us
    pallas_call x1, Pallas kernels, gather_pack(): pl.pallas_call(pack_kernel, out_shape=[jax.ShapeDtypeStruct((2, 4, model,...  53.4 us
    pallas_call x1, Pallas kernels, feed_back_up(): pl.pallas_call(back_up_kernel, out_shape=[jax.ShapeDtypeStruct(gu.shape,...  34.1 us
    pallas_call x1, Pallas kernels, feed_down(): pl.pallas_call(down_kernel, out_shape=[jax.ShapeDtypeStruct((count, model...  33.1 us
  transfers between devices with their start and end apart: 10, of which 3 were waited for; matrix products, arithmetic and copies ran while one was open for 3% of the time, Pallas kernels for 75%

profile of v7, /device:TPU:0, one launch (start us, length us, event | category | flops | bytes accessed | tf_op | source)
XLA Modules:
  0.0 657.1 jit_solution(12071068509485600246)
XLA Ops:
  7.2 1.0 dynamic-slice_bitcast_fusion.5
  8.9 1.5 dynamic_update_slice.7
  10.4 1.8 pad_maximum_fusion.2.refs_1_
  14.1 3.0 dynamic-slice_bitcast_fusion
  19.5 4.7 shard_map.172
  24.2 1.1 slice.75
  25.4 0.8 slice.76
  28.2 1.3 convert_multiply_fusion.dy_ref
  29.5 22.4 %all-gather.5.cloned.1.call-done.p_ref = bf16[1216,640]{1,0:T(8,128)(2,1)} async-done(((bf16[304,640]{1,0:T(8,128)(2,1)}), bf16[1216,640]{1,0:T(8,128)(2,1)}) %all-gather.5.cloned.1.call-update) | async-done | bytes 1556496 | tf_op jit(solution)/shard_map/all_gather | solution.py:1809
  51.9 1.4 copy-done.13
  53.3 53.4 %shard_map.169 = (bf16[2,4,1152,640]{3,2,1,0:T(8,128)(2,1)S(1)}, bf16[2,4,16,640]{3,2,1,0:T(8,128)(2,1)S(1)}) custom-call(bf16[1216,640]{1,0:T(8,128)(2,1)S(1)} %copy-done.13), custom_call_target="tpu_custom_call" | custom-call | tf_op jit(solution)/shard_map/pallas_call | solution.py:981
  106.7 4.2 copy-done.2
  114.2 40.4 %shard_map.170 = (f32[256,1152]{1,0:T(8,128)S(1)}, bf16[256,1152]{1,0:T(8,128)(2,1)}, f32[256,1024]{1,0:T(8,128)S(1)}, f32[256,256]{1,0:T(8,128)S(1)}, bf16[768,...) custom-call(s32[1]{0:T(128)} %bitcast.length_ref, ...), custom_call_target="tpu_custom_call" | custom-call | tf_op jit(solution)/shard_map/pallas_call | solution.py:1388
  154.6 1.0 copy-done.3
  155.6 1.4 copy-done.11
  157.0 1.0 copy-done.15
  158.0 1.0 copy-done.16
  159.0 0.9 copy-done.20
  159.9 0.8 copy-done.21
  162.3 5.2 all-gather.7.cloned.1.call-done.w_ref
  167.5 28.5 %shard_map.173 = (bf16[1024,1152]{1,0:T(8,128)(2,1)}, bf16[1024,3584]{1,0:T(8,128)(2,1)}, bf16[1024,1792]{1,0:T(8,128)(2,1)}) custom-call(f32[256,1152]{1,0:T(8,128)} %copy-done.3, f32[1,1152]{1,0:T(1,128)} %slice.67.gain_ref, bf16[1152,5376]{1,0:T(8,128)(2,1)} %all-gather.7.cloned.1.call-done.w_ref), custom_call_target="tpu_custom_call" | custom-call | tf_op jit(solution)/shard_map/pallas_call | solution.py:477
  196.0 33.1 %shard_map.174 = (bf16[256,1152]{1,0:T(8,128)(2,1)}, f32[256,1152]{1,0:T(8,128)}) custom-call(f32[256,1152]{1,0:T(8,128)} %copy-done.3, f32[1,1152]{1,0:T(1,128)} %slice.65.gain_ref, bf16[1024,1792]{1,0:T(8,128)(2,1)} %get-tuple-element.66.act_ref, bf16[1152,5376]{1,0:T(8,128)(2,1)} %all-gather.7.cloned.1.call-done.w_ref), custom_call_target="tpu_custom_call" | custom-call | tf_op jit(solution)/shard_map/pallas_call | solution.py:534
  229.1 1.1 copy-done.6
  230.2 37.6 %shard_map.175 = (f32[256,1152]{1,0:T(8,128)S(1)}, bf16[256,1152]{1,0:T(8,128)(2,1)}, f32[256,1024]{1,0:T(8,128)S(1)}, f32[256,256]{1,0:T(8,128)S(1)}, bf16[768,...) custom-call(s32[1]{0:T(128)} %bitcast.length_ref, ...), custom_call_target="tpu_custom_call" | custom-call | tf_op jit(solution)/shard_map/pallas_call | solution.py:1388
  267.9 1.0 copy-done.4
  268.9 1.4 copy-done.12
  270.3 1.0 copy-done.14
  272.1 28.2 %shard_map.176 = (bf16[1024,1152]{1,0:T(8,128)(2,1)}, bf16[1024,3584]{1,0:T(8,128)(2,1)}, bf16[1024,1792]{1,0:T(8,128)(2,1)}) custom-call(f32[256,1152]{1,0:T(8,128)} %copy-done.4, f32[1,1152]{1,0:T(1,128)} %slice.74.gain_ref, bf16[1152,3584]{1,0:T(8,128)(2,1)} %all-gather.9.cloned.1.call-done.w_ref), custom_call_target="tpu_custom_call" | custom-call | tf_op jit(solution)/shard_map/pallas_call | solution.py:477
  300.3 54.6 %shard_map.177 = (bf16[256,1152]{1,0:T(8,128)(2,1)}, bf16[1024,3584]{1,0:T(8,128)(2,1)}, bf16[1152,896]{1,0:T(8,128)(2,1)}, f32[1,1152]{1,0:T(1,128)}) custom-call(f32[256,1152]{1,0:T(8,128)} %copy-done.4, f32[1,1152]{1,0:T(1,128)} %slice.72.gain_ref, f32[256,1152]{1,0:T(8,128)} %convert_multiply_fusion.dy_ref, ...), custom_call_target="tpu_custom_call" | custom-call | tf_op jit(solution)/shard_map/pallas_call | solution.py:774
  355.0 32.6 %shard_map.178 = (f32[256,1152]{1,0:T(8,128)}, bf16[1152,1792]{1,0:T(8,128)(2,1)}, f32[1,1152]{1,0:T(1,128)}) custom-call(f32[256,1152]{1,0:T(8,128)} %convert_multiply_fusion.dy_ref, f32[256,1152]{1,0:T(8,128)} %copy-done.4, f32[1,1152]{1,0:T(1,128)} %slice.74.gain_ref, bf16[1024,3584]{1,0:T(8,128)(2,1)} %get-tuple-element.73.dgu_ref, ...), custom_call_target="tpu_custom_call" | custom-call | tf_op jit(solution)/shard_map/pallas_call | solution.py:897
  387.7 1.0 copy-done.7
  388.6 1.0 copy-done.24
  389.7 48.1 %shard_map.179 = (f32[256,1152]{1,0:T(8,128)S(1)}, bf16[1152,384]{1,0:T(8,128)(2,1)S(1)}, f32[2,1152]{1,0:T(2,128)S(1)}, f32[2,256]{1,0:T(2,128)S(1)}) custom-call(s32[1]{0:T(128)} %bitcast.length_ref, f32[256,1152]{1,0:T(8,128)} %get-tuple-element.75.dh_ref, f32[256,1152]{1,0:T(8,128)} %copy-done.14, bf16[256,1152]{1,0:T(8,128)(2,1)S(1)} %copy-done.7, ...), custom_call_target="tpu_custom_call" | custom-call | tf_op jit(solution)/shard_map/pallas_call | solution.py:1676
  437.8 1.0 copy-done.5
  438.8 1.0 copy-done.19
  439.8 34.1 %shard_map.180 = (bf16[1024,3584]{1,0:T(8,128)(2,1)}, bf16[1152,896]{1,0:T(8,128)(2,1)}, f32[1,1152]{1,0:T(1,128)}) custom-call(f32[256,1152]{1,0:T(8,128)} %copy-done.5, f32[256,1152]{1,0:T(8,128)} %get-tuple-element.84.f_ref, f32[1,1152]{1,0:T(1,128)} %slice.65.gain_ref, bf16[1024,3584]{1,0:T(8,128)(2,1)} %get-tuple-element.85.gu_ref, ...), custom_call_target="tpu_custom_call" | custom-call | tf_op jit(solution)/shard_map/pallas_call | solution.py:810
  474.0 1.0 copy-done.30
  475.8 1.6 collective-permute-done
  477.6 1.6 pad_maximum_fusion
  479.1 32.6 %shard_map.181 = (f32[256,1152]{1,0:T(8,128)}, bf16[1152,1792]{1,0:T(8,128)(2,1)}, f32[1,1152]{1,0:T(1,128)}) custom-call(f32[256,1152]{1,0:T(8,128)} %copy-done.5, f32[256,1152]{1,0:T(8,128)} %copy-done.3, f32[1,1152]{1,0:T(1,128)} %slice.67.gain_ref, bf16[1024,3584]{1,0:T(8,128)(2,1)} %get-tuple-element.87.dgu_ref, ...), custom_call_target="tpu_custom_call" | custom-call | tf_op jit(solution)/shard_map/pallas_call | solution.py:897
  511.8 2.0 concatenate.31.refs_0_
  513.8 120.5 %shard_map.183 = (f32[256,1152]{1,0:T(8,128)}, bf16[1152,384]{1,0:T(8,128)(2,1)}, f32[2,1152]{1,0:T(2,128)}, f32[2,256]{1,0:T(2,128)}, f32[16,1152]{1,0:T(8,128)...) custom-call(s32[1]{0:T(128)} %bitcast.length_ref, ...), custom_call_target="tpu_custom_call" | custom-call | tf_op jit(solution)/shard_map/pallas_call | solution.py:1676
  634.5 2.5 collective-permute-start.2
  638.4 1.4 dynamic-slice_bitcast_fusion.6
  639.8 1.3 broadcast_select_fusion.3
  641.2 1.4 convert_bitcast_fusion
  643.4 2.9 shard_map.184
  646.4 1.4 copy.37
  (134 shorter events, 17.1 us)
Async XLA Ops:
  7.2 20.9 %copy-start = (bf16[2,256,1152]{2,1,0:T(8,128)(2,1)S(1)}, bf16[2,256,1152]{2,1,0:T(8,128)(2,1)}, u32[]{:S(2)}) copy-start(bf16[2,256,1152]{2,1,0:T(8,128)(2,1)} %param.10) | copy-start | bytes 3538948
  7.2 44.7 %all-gather.5.cloned.1.call-start = ((), (), s32[]{:S(2)}) async-start(), calls=%async_computation.3 | async-start | bytes 1945600 | tf_op jit(solution)/shard_map/all_gather | solution.py:1809
  12.2 155.3 %all-gather.7.cloned.1.call-start = ((), (), s32[]{:S(2)}) async-start(), calls=%async_computation.4 | async-start | bytes 13934592 | tf_op jit(solution)/shard_map/all_gather | solution.py:1821
  18.0 1.2 copy-start.31
  24.2 247.9 %all-gather.9.cloned.1.call-start = ((), (), s32[]{:S(2)}) async-start(), calls=%async_computation.5 | async-start | bytes 9289728 | tf_op jit(solution)/shard_map/all_gather | solution.py:1821
  24.2 2.1 copy-start.39
  25.3 274.9 %all-gather.11.cloned.1.call-start = ((), (), s32[]{:S(2)}) async-start(), calls=%async_computation.6 | async-start | bytes 4644864 | tf_op jit(solution)/shard_map/all_gather | solution.py:1821
  26.2 2.0 copy-start.33
  26.2 413.6 %reduce-scatter.4.cloned.1.call-start = ((), (), s32[]{:S(2)}) async-start(), calls=%async_computation.7 | async-start | bytes 2580480 | tf_op jit(solution)/shard_map/reduce_scatter | solution.py:1773
  28.1 359.5 %copy-start.8 = (f32[256,256]{1,0:T(8,128)}, f32[256,256]{1,0:T(8,128)S(1)}, u32[]{:S(2)}) copy-start(f32[256,256]{1,0:T(8,128)S(1)} %pad_maximum_fusion.3.trig_ref) | copy-start | bytes 786436
  28.2 126.3 %copy-start.9 = (bf16[256,1152]{1,0:T(8,128)(2,1)}, bf16[256,1152]{1,0:T(8,128)(2,1)S(1)}, u32[]{:S(2)}) copy-start(bf16[256,1152]{1,0:T(8,128)(2,1)S(1)} %dynamic-slice_bitcast_fusion.2.x_ref) | copy-start | bytes 1769476
  51.9 1.4 copy-start.13
  106.7 4.2 copy-start.2
  111.1 43.5 %copy-start.26 = (f32[4,1152]{1,0:T(4,128)}, f32[4,1152]{1,0:T(4,128)S(1)}, u32[]{:S(2)}) copy-start(f32[4,1152]{1,0:T(4,128)S(1)} %convert_element_type.60.gains_ref) | copy-start | bytes 55300
  111.2 43.4 %copy-start.27 = (f32[2,256]{1,0:T(2,128)}, f32[2,256]{1,0:T(2,128)S(1)}, u32[]{:S(2)}) copy-start(f32[2,256]{1,0:T(2,128)S(1)} %reshape.85.head_ref) | copy-start | bytes 6148
  154.6 1.0 copy-start.3
  155.6 1.4 copy-start.11
  157.0 1.0 copy-start.15
  158.0 1.0 copy-start.16
  159.0 0.9 copy-start.20
  159.9 0.8 copy-start.21
  160.8 0.8 copy-start.22
  229.1 1.1 copy-start.6
  267.9 1.0 copy-start.4
  268.9 1.4 copy-start.12
  270.3 1.0 copy-start.14
  354.9 158.9 %reduce-scatter.6.cloned.1.call-start = ((), (), s32[]{:S(2)}) async-start(), calls=%async_computation.8 | async-start | bytes 5160960 | tf_op jit(solution)/shard_map/reduce_scatter | solution.py:1773
  387.6 1.1 copy-start.7
  387.6 246.8 %reduce-scatter.8.cloned.1.call-start = ((), (), s32[]{:S(2)}) async-start(), calls=%async_computation.9 | async-start | bytes 2580480 | tf_op jit(solution)/shard_map/reduce_scatter | solution.py:1773
  388.6 1.0 copy-start.24
  437.8 1.0 copy-start.5
  438.8 1.0 copy-start.19
  473.9 1.1 copy-start.30
  475.1 2.4 collective-permute-start
  479.1 32.6 %copy-start.36 = (f32[1,1152]{1,0:T(1,128)S(1)}, f32[1,1152]{1,0:T(1,128)}, u32[]{:S(2)}) copy-start(f32[1,1152]{1,0:T(1,128)} %get-tuple-element.101) | copy-start | bytes 13828
  479.1 32.7 %copy-start.37 = (f32[1,1152]{1,0:T(1,128)S(1)}, f32[1,1152]{1,0:T(1,128)}, u32[]{:S(2)}) copy-start(f32[1,1152]{1,0:T(1,128)} %get-tuple-element.100) | copy-start | bytes 13828
  479.1 32.7 %copy-start.38 = (f32[1,1152]{1,0:T(1,128)S(1)}, f32[1,1152]{1,0:T(1,128)}, u32[]{:S(2)}) copy-start(f32[1,1152]{1,0:T(1,128)} %get-tuple-element.98) | copy-start | bytes 13828
  513.8 120.6 %copy-start.28 = (bf16[288,896]{1,0:T(8,128)(2,1)S(1)}, bf16[288,896]{1,0:T(8,128)(2,1)}, u32[]{:S(2)}) copy-start(bf16[288,896]{1,0:T(8,128)(2,1)} %reduce-scatter.4.cloned.1.call-done.refs_0_) | copy-start | bytes 1548292
  634.3 2.6 copy-start.10
  634.5 5.4 collective-permute-start.2
  637.0 5.6 collective-permute-start.1
  641.1 1.6 copy-start.17
  641.2 2.3 copy-start.18
  643.4 2.9 copy-start.29
  646.4 1.4 copy-start.35
  646.4 2.2 copy-start.32
  646.4 3.0 copy-start.34
  646.4 3.7 copy-start.1
  (2 other events, 1.5 us)
Sparse Core Ops, SparseCore 0:
  12.3 39.5 all-gather.4
  53.5 113.9 all-gather.6
  169.2 79.2 all-gather.8
  249.9 45.0 all-gather.10
  355.1 41.3 reduce-scatter.3
  398.7 75.0 reduce-scatter.5
  476.1 43.6 reduce-scatter.7

commit v8 on v7

--- a/solution.py
+++ b/solution.py
@@ -336,8 +336,8 @@
     def step(self, step, piece):
         self.folds[piece].step(step)
 
-    def end(self):
-        for fold in self.folds:
+    def end(self, done=0):
+        for fold in self.folds[done:]:
             fold.finish(self.result)
         if self.dst is not None:
             copy = pltpu.make_async_copy(self.result, self.dst, self.loads.at[self.own.shape[0]])
@@ -1619,9 +1619,13 @@
         crosses = [across(0, early.result, came_early)]
         crosses[0].start()
         late.step(late.steps - 1, 0)
+        line.folds[0].finish(line.result)
+        half = line.folds[0].columns
+        crosses.append(across(1, line.result.at[:, half], came_line.at[:, half]))
+        crosses[1].start()
         late.end()
-        crosses.append(across(1, late.result, came_late))
-        crosses[1].start()
+        crosses.append(across(2, late.result, came_late))
+        crosses[2].start()
         crosses[0].wait_recv()
         by_qkv = jnp.where(zero, late.result[...], came_early[...])
         kv_all[me] = by_qkv[:, head:]
@@ -1631,16 +1635,19 @@
         ]
         start_all(narrows)
         q_out[...] = by_qkv[:, :head].astype(F32)
-        crosses[1].wait_recv()
+        crosses[2].wait_recv()
         o_out[...] = jnp.where(zero, came_late[:, :head], early.result[:, :head]).astype(F32)
         for copy in narrows:
             copy.wait_recv()
         for n in range(4):
             kv_out[:, n * kv_part : (n + 1) * kv_part] = kv_all[n].astype(F32)
-        line.end()
-        crosses.append(across(2, line.result, came_line))
-        crosses[2].start()
-        crosses[2].wait_recv()
+        rest = line.folds[1].columns
+        line.folds[1].finish(line.result)
+        crosses.append(across(3, line.result.at[:, rest], came_line.at[:, rest]))
+        crosses[3].start()
+        line.end(2)
+        crosses[1].wait_recv()
+        crosses[3].wait_recv()
         keep = pltpu.make_async_copy(came_line, came_out, came_store)
         keep.start()
         for copy in crosses + narrows:
@@ -1746,8 +1753,8 @@
                     pltpu.VMEM((rows, head + kv_part), BF16),
                     pltpu.VMEM((rows, head + kv_part), BF16),
                     pltpu.VMEM((4, rows, kv_part), BF16),
-                    pltpu.SemaphoreType.DMA((3,)),
-                    pltpu.SemaphoreType.DMA((3,)),
+                    pltpu.SemaphoreType.DMA((4,)),
+                    pltpu.SemaphoreType.DMA((4,)),
                     pltpu.SemaphoreType.DMA((3,)),
                     pltpu.SemaphoreType.DMA((3,)),
                 ]
@@ -1801,10 +1808,9 @@
     pack = [w_q[0], w_o[0].T, kv_own]
     pack = jnp.concatenate(pack, axis=1)
     if block % 16 == 0:
-        gain_rows = jnp.zeros((GAIN_ROWS, pack_width), BF16)
-        gain_rows = lax.dynamic_update_slice(gain_rows, norm_gains[0], (0, 0))
-        gain_rows = lax.dynamic_update_slice(gain_rows, head_gains[0], (4, 0))
-        pack = jnp.concatenate([pack, gain_rows], axis=0)
+        norm_rows = jnp.pad(norm_gains[0], ((0, 0), (0, pack_width - block)))
+        head_rows = jnp.pad(head_gains[0], ((0, GAIN_ROWS - 6), (0, pack_width - head_width // n_wide)))
+        pack = jnp.concatenate([pack, norm_rows, head_rows], axis=0)
     late = after(core.reshape(1), pack)[0]
     pack = lax.all_gather(pack, "wide", axis=0, tiled=True)
 

time: 666 us -> 662 us (level)
  no operation moved by 1% of the time
where the time goes in v8:
time: 662 us; the launch traced here: 653 us
  Pallas kernels  550 us (83%)
  local copies, waits for them, and re-layouts  44.8 us (7%)
  waiting for transfers between devices  29.4 us (4%)
  between operations  16.2 us (2%)
  other arithmetic  9.11 us (1%)
    pallas_call x2, Pallas kernels, attend_back(): pl.pallas_call(functools.partial(attend_back_kernel, layer), out_shape=[j...  167 us
    pallas_call x2, Pallas kernels, attend(): pl.pallas_call(functools.partial(attend_kernel, layer), out_shape=shapes,...  78 us
    pallas_call x2, Pallas kernels, feed_back_down(): pl.pallas_call(back_down_kernel, out_shape=[jax.ShapeDtypeStruct((count,...  65.1 us
    pallas_call x2, Pallas kernels, feed_up(): pl.pallas_call(up_kernel, out_shape=shapes, in_specs=[vmem_spec(), vmem_s...  56.7 us
    pallas_call x1, Pallas kernels, feed_turn(): pl.pallas_call(turn_kernel, out_shape=[jax.ShapeDtypeStruct((count, model...  54.6 us
    pallas_call x1, Pallas kernels, gather_pack(): pl.pallas_call(pack_kernel, out_shape=[jax.ShapeDtypeStruct((2, 4, model,...  53.4 us
    pallas_call x1, Pallas kernels, feed_back_up(): pl.pallas_call(back_up_kernel, out_shape=[jax.ShapeDtypeStruct(gu.shape,...  34.1 us
    pallas_call x1, Pallas kernels, feed_down(): pl.pallas_call(down_kernel, out_shape=[jax.ShapeDtypeStruct((count, model...  33.1 us
  transfers between devices with their start and end apart: 10, of which 3 were waited for; matrix products, arithmetic and copies ran while one was open for 3% of the time, Pallas kernels for 75%

profile of v8, /device:TPU:0, one launch (start us, length us, event | category | flops | bytes accessed | tf_op | source)
XLA Modules:
  0.0 653.1 jit_solution(717996080781376414)
XLA Ops:
  7.2 1.0 dynamic-slice_bitcast_fusion.5
  8.2 1.8 fusion.8.refs_1_
  11.9 3.0 dynamic-slice_bitcast_fusion
  14.9 0.8 pad.28
  17.3 4.7 shard_map.172
  22.1 1.1 slice.75
  23.2 0.8 slice.76
  26.1 1.3 convert_multiply_fusion.dy_ref
  27.3 22.4 %all-gather.5.cloned.1.call-done.p_ref = bf16[1216,640]{1,0:T(8,128)(2,1)} async-done(((bf16[304,640]{1,0:T(8,128)(2,1)}), bf16[1216,640]{1,0:T(8,128)(2,1)}) %all-gather.5.cloned.1.call-update) | async-done | bytes 1556496 | tf_op jit(solution)/shard_map/all_gather | solution.py:1815
  49.7 1.4 copy-done.13
  51.1 53.4 %shard_map.169 = (bf16[2,4,1152,640]{3,2,1,0:T(8,128)(2,1)S(1)}, bf16[2,4,16,640]{3,2,1,0:T(8,128)(2,1)S(1)}) custom-call(bf16[1216,640]{1,0:T(8,128)(2,1)S(1)} %copy-done.13), custom_call_target="tpu_custom_call" | custom-call | tf_op jit(solution)/shard_map/pallas_call | solution.py:981
  104.5 4.2 copy-done.2
  112.0 40.4 %shard_map.170 = (f32[256,1152]{1,0:T(8,128)S(1)}, bf16[256,1152]{1,0:T(8,128)(2,1)}, f32[256,1024]{1,0:T(8,128)S(1)}, f32[256,256]{1,0:T(8,128)S(1)}, bf16[768,...) custom-call(s32[1]{0:T(128)} %bitcast.length_ref, ...), custom_call_target="tpu_custom_call" | custom-call | tf_op jit(solution)/shard_map/pallas_call | solution.py:1388
  152.4 1.0 copy-done.3
  153.5 1.4 copy-done.11
  154.9 1.0 copy-done.15
  155.9 1.0 copy-done.16
  156.9 0.9 copy-done.20
  157.8 0.8 copy-done.21
  160.1 5.2 all-gather.7.cloned.1.call-done.w_ref
  165.4 28.5 %shard_map.173 = (bf16[1024,1152]{1,0:T(8,128)(2,1)}, bf16[1024,3584]{1,0:T(8,128)(2,1)}, bf16[1024,1792]{1,0:T(8,128)(2,1)}) custom-call(f32[256,1152]{1,0:T(8,128)} %copy-done.3, f32[1,1152]{1,0:T(1,128)} %slice.67.gain_ref, bf16[1152,5376]{1,0:T(8,128)(2,1)} %all-gather.7.cloned.1.call-done.w_ref), custom_call_target="tpu_custom_call" | custom-call | tf_op jit(solution)/shard_map/pallas_call | solution.py:477
  193.9 33.1 %shard_map.174 = (bf16[256,1152]{1,0:T(8,128)(2,1)}, f32[256,1152]{1,0:T(8,128)}) custom-call(f32[256,1152]{1,0:T(8,128)} %copy-done.3, f32[1,1152]{1,0:T(1,128)} %slice.65.gain_ref, bf16[1024,1792]{1,0:T(8,128)(2,1)} %get-tuple-element.66.act_ref, bf16[1152,5376]{1,0:T(8,128)(2,1)} %all-gather.7.cloned.1.call-done.w_ref), custom_call_target="tpu_custom_call" | custom-call | tf_op jit(solution)/shard_map/pallas_call | solution.py:534
  227.0 1.1 copy-done.6
  228.1 37.6 %shard_map.175 = (f32[256,1152]{1,0:T(8,128)S(1)}, bf16[256,1152]{1,0:T(8,128)(2,1)}, f32[256,1024]{1,0:T(8,128)S(1)}, f32[256,256]{1,0:T(8,128)S(1)}, bf16[768,...) custom-call(s32[1]{0:T(128)} %bitcast.length_ref, ...), custom_call_target="tpu_custom_call" | custom-call | tf_op jit(solution)/shard_map/pallas_call | solution.py:1388
  265.7 1.0 copy-done.4
  266.7 1.4 copy-done.12
  268.1 1.0 copy-done.14
  269.9 28.2 %shard_map.176 = (bf16[1024,1152]{1,0:T(8,128)(2,1)}, bf16[1024,3584]{1,0:T(8,128)(2,1)}, bf16[1024,1792]{1,0:T(8,128)(2,1)}) custom-call(f32[256,1152]{1,0:T(8,128)} %copy-done.4, f32[1,1152]{1,0:T(1,128)} %slice.74.gain_ref, bf16[1152,3584]{1,0:T(8,128)(2,1)} %all-gather.9.cloned.1.call-done.w_ref), custom_call_target="tpu_custom_call" | custom-call | tf_op jit(solution)/shard_map/pallas_call | solution.py:477
  298.1 54.6 %shard_map.177 = (bf16[256,1152]{1,0:T(8,128)(2,1)}, bf16[1024,3584]{1,0:T(8,128)(2,1)}, bf16[1152,896]{1,0:T(8,128)(2,1)}, f32[1,1152]{1,0:T(1,128)}) custom-call(f32[256,1152]{1,0:T(8,128)} %copy-done.4, f32[1,1152]{1,0:T(1,128)} %slice.72.gain_ref, f32[256,1152]{1,0:T(8,128)} %convert_multiply_fusion.dy_ref, ...), custom_call_target="tpu_custom_call" | custom-call | tf_op jit(solution)/shard_map/pallas_call | solution.py:774
  352.9 32.5 %shard_map.178 = (f32[256,1152]{1,0:T(8,128)}, bf16[1152,1792]{1,0:T(8,128)(2,1)}, f32[1,1152]{1,0:T(1,128)}) custom-call(f32[256,1152]{1,0:T(8,128)} %convert_multiply_fusion.dy_ref, f32[256,1152]{1,0:T(8,128)} %copy-done.4, f32[1,1152]{1,0:T(1,128)} %slice.74.gain_ref, bf16[1024,3584]{1,0:T(8,128)(2,1)} %get-tuple-element.73.dgu_ref, ...), custom_call_target="tpu_custom_call" | custom-call | tf_op jit(solution)/shard_map/pallas_call | solution.py:897
  385.5 1.0 copy-done.7
  386.5 1.0 copy-done.24
  387.5 48.1 %shard_map.179 = (f32[256,1152]{1,0:T(8,128)S(1)}, bf16[1152,384]{1,0:T(8,128)(2,1)S(1)}, f32[2,1152]{1,0:T(2,128)S(1)}, f32[2,256]{1,0:T(2,128)S(1)}) custom-call(s32[1]{0:T(128)} %bitcast.length_ref, f32[256,1152]{1,0:T(8,128)} %get-tuple-element.75.dh_ref, f32[256,1152]{1,0:T(8,128)} %copy-done.14, bf16[256,1152]{1,0:T(8,128)(2,1)S(1)} %copy-done.7, ...), custom_call_target="tpu_custom_call" | custom-call | tf_op jit(solution)/shard_map/pallas_call | solution.py:1683
  435.7 1.0 copy-done.5
  436.7 1.0 copy-done.19
  437.7 34.1 %shard_map.180 = (bf16[1024,3584]{1,0:T(8,128)(2,1)}, bf16[1152,896]{1,0:T(8,128)(2,1)}, f32[1,1152]{1,0:T(1,128)}) custom-call(f32[256,1152]{1,0:T(8,128)} %copy-done.5, f32[256,1152]{1,0:T(8,128)} %get-tuple-element.84.f_ref, f32[1,1152]{1,0:T(1,128)} %slice.65.gain_ref, bf16[1024,3584]{1,0:T(8,128)(2,1)} %get-tuple-element.85.gu_ref, ...), custom_call_target="tpu_custom_call" | custom-call | tf_op jit(solution)/shard_map/pallas_call | solution.py:810
  471.8 1.0 copy-done.30
  473.7 1.6 collective-permute-done
  475.4 1.6 pad_maximum_fusion
  477.0 32.6 %shard_map.181 = (f32[256,1152]{1,0:T(8,128)}, bf16[1152,1792]{1,0:T(8,128)(2,1)}, f32[1,1152]{1,0:T(1,128)}) custom-call(f32[256,1152]{1,0:T(8,128)} %copy-done.5, f32[256,1152]{1,0:T(8,128)} %copy-done.3, f32[1,1152]{1,0:T(1,128)} %slice.67.gain_ref, bf16[1024,3584]{1,0:T(8,128)(2,1)} %get-tuple-element.87.dgu_ref, ...), custom_call_target="tpu_custom_call" | custom-call | tf_op jit(solution)/shard_map/pallas_call | solution.py:897
  509.7 2.0 concatenate.31.refs_0_
  511.7 119.1 %shard_map.183 = (f32[256,1152]{1,0:T(8,128)}, bf16[1152,384]{1,0:T(8,128)(2,1)}, f32[2,1152]{1,0:T(2,128)}, f32[2,256]{1,0:T(2,128)}, f32[16,1152]{1,0:T(8,128)...) custom-call(s32[1]{0:T(128)} %bitcast.length_ref, ...), custom_call_target="tpu_custom_call" | custom-call | tf_op jit(solution)/shard_map/pallas_call | solution.py:1683
  630.9 2.0 collective-permute-start.2
  634.4 1.4 dynamic-slice_bitcast_fusion.6
  635.8 1.3 broadcast_select_fusion.3
  637.1 1.4 convert_bitcast_fusion
  639.4 2.9 shard_map.184
  642.4 1.4 copy.36
  (132 shorter events, 15.6 us)
Async XLA Ops:
  7.2 18.8 %copy-start = (bf16[2,256,1152]{2,1,0:T(8,128)(2,1)S(1)}, bf16[2,256,1152]{2,1,0:T(8,128)(2,1)}, u32[]{:S(2)}) copy-start(bf16[2,256,1152]{2,1,0:T(8,128)(2,1)} %param.10) | copy-start | bytes 3538948
  7.2 42.5 %all-gather.5.cloned.1.call-start = ((), (), s32[]{:S(2)}) async-start(), calls=%async_computation.3 | async-start | bytes 1945600 | tf_op jit(solution)/shard_map/all_gather | solution.py:1815
  10.0 155.3 %all-gather.7.cloned.1.call-start = ((), (), s32[]{:S(2)}) async-start(), calls=%async_computation.4 | async-start | bytes 13934592 | tf_op jit(solution)/shard_map/all_gather | solution.py:1827
  15.8 1.2 copy-start.31
  22.0 247.9 %all-gather.9.cloned.1.call-start = ((), (), s32[]{:S(2)}) async-start(), calls=%async_computation.5 | async-start | bytes 9289728 | tf_op jit(solution)/shard_map/all_gather | solution.py:1827
  22.1 2.1 copy-start.39
  23.2 274.9 %all-gather.11.cloned.1.call-start = ((), (), s32[]{:S(2)}) async-start(), calls=%async_computation.6 | async-start | bytes 4644864 | tf_op jit(solution)/shard_map/all_gather | solution.py:1827
  24.1 2.0 copy-start.33
  24.1 413.6 %reduce-scatter.4.cloned.1.call-start = ((), (), s32[]{:S(2)}) async-start(), calls=%async_computation.7 | async-start | bytes 2580480 | tf_op jit(solution)/shard_map/reduce_scatter | solution.py:1780
  26.0 359.5 %copy-start.8 = (f32[256,256]{1,0:T(8,128)}, f32[256,256]{1,0:T(8,128)S(1)}, u32[]{:S(2)}) copy-start(f32[256,256]{1,0:T(8,128)S(1)} %pad_maximum_fusion.2.trig_ref) | copy-start | bytes 786436
  26.1 126.3 %copy-start.9 = (bf16[256,1152]{1,0:T(8,128)(2,1)}, bf16[256,1152]{1,0:T(8,128)(2,1)S(1)}, u32[]{:S(2)}) copy-start(bf16[256,1152]{1,0:T(8,128)(2,1)S(1)} %dynamic-slice_bitcast_fusion.2.x_ref) | copy-start | bytes 1769476
  49.7 1.4 copy-start.13
  104.5 4.2 copy-start.2
  108.9 43.5 %copy-start.26 = (f32[4,1152]{1,0:T(4,128)}, f32[4,1152]{1,0:T(4,128)S(1)}, u32[]{:S(2)}) copy-start(f32[4,1152]{1,0:T(4,128)S(1)} %convert_element_type.64.gains_ref) | copy-start | bytes 55300
  109.0 43.4 %copy-start.27 = (f32[2,256]{1,0:T(2,128)}, f32[2,256]{1,0:T(2,128)S(1)}, u32[]{:S(2)}) copy-start(f32[2,256]{1,0:T(2,128)S(1)} %reshape.85.head_ref) | copy-start | bytes 6148
  152.4 1.0 copy-start.3
  153.5 1.4 copy-start.11
  154.9 1.0 copy-start.15
  155.9 1.0 copy-start.16
  156.9 0.9 copy-start.20
  157.8 0.8 copy-start.21
  158.6 0.8 copy-start.22
  227.0 1.1 copy-start.6
  265.7 1.0 copy-start.4
  266.7 1.4 copy-start.12
  268.1 1.0 copy-start.14
  352.8 158.9 %reduce-scatter.6.cloned.1.call-start = ((), (), s32[]{:S(2)}) async-start(), calls=%async_computation.8 | async-start | bytes 5160960 | tf_op jit(solution)/shard_map/reduce_scatter | solution.py:1780
  385.4 1.1 copy-start.7
  385.4 245.3 %reduce-scatter.8.cloned.1.call-start = ((), (), s32[]{:S(2)}) async-start(), calls=%async_computation.9 | async-start | bytes 2580480 | tf_op jit(solution)/shard_map/reduce_scatter | solution.py:1780
  386.5 1.0 copy-start.24
  435.7 1.0 copy-start.5
  436.7 1.0 copy-start.19
  471.8 1.1 copy-start.30
  472.9 2.4 collective-permute-start
  477.0 32.6 %copy-start.36 = (f32[1,1152]{1,0:T(1,128)S(1)}, f32[1,1152]{1,0:T(1,128)}, u32[]{:S(2)}) copy-start(f32[1,1152]{1,0:T(1,128)} %get-tuple-element.101) | copy-start | bytes 13828
  477.0 32.7 %copy-start.37 = (f32[1,1152]{1,0:T(1,128)S(1)}, f32[1,1152]{1,0:T(1,128)}, u32[]{:S(2)}) copy-start(f32[1,1152]{1,0:T(1,128)} %get-tuple-element.100) | copy-start | bytes 13828
  477.0 32.7 %copy-start.38 = (f32[1,1152]{1,0:T(1,128)S(1)}, f32[1,1152]{1,0:T(1,128)}, u32[]{:S(2)}) copy-start(f32[1,1152]{1,0:T(1,128)} %get-tuple-element.98) | copy-start | bytes 13828
  511.7 119.1 %copy-start.28 = (bf16[288,896]{1,0:T(8,128)(2,1)S(1)}, bf16[288,896]{1,0:T(8,128)(2,1)}, u32[]{:S(2)}) copy-start(bf16[288,896]{1,0:T(8,128)(2,1)} %reduce-scatter.4.cloned.1.call-done.refs_0_) | copy-start | bytes 1548292
  630.7 2.2 copy-start.10
  630.9 4.9 collective-permute-start.2
  632.9 5.6 collective-permute-start.1
  637.1 1.6 copy-start.17
  637.1 2.3 copy-start.18
  639.4 2.9 copy-start.29
  642.3 1.4 copy-start.35
  642.3 2.2 copy-start.32
  642.3 3.0 copy-start.34
  642.3 3.7 copy-start.1
  (2 other events, 1.5 us)
Sparse Core Ops, SparseCore 0:
  10.2 39.5 all-gather.4
  51.4 113.9 all-gather.6
  167.0 79.2 all-gather.8
  247.8 45.0 all-gather.10
  352.9 41.3 reduce-scatter.3
  396.6 75.0 reduce-scatter.5
  474.0 43.5 reduce-scatter.7

commit v9 on v8

--- a/solution.py
+++ b/solution.py
@@ -1057,27 +1057,32 @@
     )(zero, one, early, dep)
 
 
-def pair_kernel(zero_ref, one_ref, came_zero_ref, came_one_ref, out_ref, flag_ref):
+def pair_kernel(zero_ref, one_ref, came_zero_ref, came_one_ref, down_zero_ref, down_one_ref, down_came_ref, out_ref, down_ref):
     hidden = out_ref.shape[2]
     first = lax.axis_index("section") == 0
     keep = jnp.where(first, zero_ref[:, :hidden], one_ref[:, :hidden])
     came = jnp.where(first, came_zero_ref[:, :hidden], came_one_ref[:, :hidden])
     out_ref[:, 0, :] = jnp.where(first, keep, came).astype(F32)
     out_ref[:, 1, :] = jnp.where(first, came, keep).astype(F32)
-    flag_ref[...] = jnp.zeros_like(flag_ref)
-
-
-def pair_up(zero, one, came_zero, came_one, hidden):
+    width = down_came_ref.shape[1]
+    keep = jnp.where(first, down_zero_ref[...], down_one_ref[...])
+    came = down_came_ref[...]
+    down_ref[:, :width] = jnp.where(first, keep, came).astype(F32)
+    rest = hidden - width
+    down_ref[:, width:] = jnp.where(first, came[:, :rest], keep[:, :rest]).astype(F32)
+
+
+def pair_up(zero, one, came_zero, came_one, down_zero, down_one, down_came, hidden):
     return pl.pallas_call(
         pair_kernel,
         out_shape=[
             jax.ShapeDtypeStruct((zero.shape[0], 2, hidden), F32),
-            jax.ShapeDtypeStruct((8, 128), F32),
+            jax.ShapeDtypeStruct((zero.shape[0], hidden), F32),
         ],
-        in_specs=[vmem_spec()] * 4,
+        in_specs=[vmem_spec()] * 7,
         out_specs=[vmem_spec()] * 2,
         compiler_params=pltpu.CompilerParams(vmem_limit_bytes=40 * MIB),
-    )(zero, one, came_zero, came_one)
+    )(zero, one, came_zero, came_one, down_zero, down_one, down_came)
 
 
 class Share:
@@ -1623,6 +1628,10 @@
         half = line.folds[0].columns
         crosses.append(across(1, line.result.at[:, half], came_line.at[:, half]))
         crosses[1].start()
+        rest = line.folds[1].columns
+        line.folds[1].finish(line.result)
+        last = across(3, line.result.at[:, rest], came_line.at[:, rest])
+        last.start()
         late.end()
         crosses.append(across(2, late.result, came_late))
         crosses[2].start()
@@ -1641,15 +1650,12 @@
             copy.wait_recv()
         for n in range(4):
             kv_out[:, n * kv_part : (n + 1) * kv_part] = kv_all[n].astype(F32)
-        rest = line.folds[1].columns
-        line.folds[1].finish(line.result)
-        crosses.append(across(3, line.result.at[:, rest], came_line.at[:, rest]))
-        crosses[3].start()
-        line.end(2)
+        crosses.append(last)
         crosses[1].wait_recv()
         crosses[3].wait_recv()
         keep = pltpu.make_async_copy(came_line, came_out, came_store)
         keep.start()
+        line.end(2)
         for copy in crosses + narrows:
             copy.wait_send()
         keep.wait()
@@ -1916,11 +1922,6 @@
             else:
                 came_up = swap(up_sums[0])
         dy = dx
-    def own_section(first, second):
-        came = swap(by_core(second, first))
-        stays = by_core(first, second)
-        return by_core(stays, came).astype(F32), by_core(came, stays).astype(F32)
-
     if block % 16:
         split = down_sums[1].shape[1]
         attention_sums = (scatter(extra), down_sums[0][:, split:])
@@ -1929,9 +1930,11 @@
             *attention_sums, swap(attention_sums[1]), up_sums[0], head_width, 2
         )
     grad_o = grad_o.T
-    grad_gate_up, _ = pair_up(*up_sums, came_up, swap(up_sums[1]), hidden)
     down_sums[0] = after(down_sums[0], gain_sums)
-    grad_down = jnp.concatenate(own_section(*down_sums), axis=1)[:, :hidden].T
+    grad_gate_up, grad_down = pair_up(
+        *up_sums, came_up, swap(up_sums[1]), *down_sums, swap(by_core(down_sums[1], down_sums[0])), hidden
+    )
+    grad_down = grad_down.T
     gain_sums = lax.dynamic_slice_in_dim(gain_sums, core * 8, 8, 0)
     wide = lax.axis_index("wide")
     grad_norm = lax.dynamic_slice_in_dim(gain_sums[:4], wide * block, block, 1)

time: 662 us -> 663 us (level)
    unnamed x87 -> x97, local copies, waits for them, and re-layouts: 28.7 us -> 30 us
  transfers between devices with their start and end apart: 10 -> 10, of which waited for: 3 -> 3; matrix products, arithmetic and copies ran while one was open for 3% -> 4% of each run, Pallas kernels for 75% -> 75%
where the time goes in v9:
time: 663 us; the launch traced here: 654 us
  Pallas kernels  551 us (83%)
  local copies, waits for them, and re-layouts  46.8 us (7%)
  waiting for transfers between devices  29.1 us (4%)
  between operations  16.3 us (2%)
  other arithmetic  9.01 us (1%)
    pallas_call x2, Pallas kernels, attend_back(): pl.pallas_call(functools.partial(attend_back_kernel, layer), out_shape=[j...  166 us
    pallas_call x2, Pallas kernels, attend(): pl.pallas_call(functools.partial(attend_kernel, layer), out_shape=shapes,...  77.9 us
    pallas_call x2, Pallas kernels, feed_back_down(): pl.pallas_call(back_down_kernel, out_shape=[jax.ShapeDtypeStruct((count,...  65.1 us
    pallas_call x2, Pallas kernels, feed_up(): pl.pallas_call(up_kernel, out_shape=shapes, in_specs=[vmem_spec(), vmem_s...  57.2 us
    pallas_call x1, Pallas kernels, feed_turn(): pl.pallas_call(turn_kernel, out_shape=[jax.ShapeDtypeStruct((count, model...  54.7 us
    pallas_call x1, Pallas kernels, gather_pack(): pl.pallas_call(pack_kernel, out_shape=[jax.ShapeDtypeStruct((2, 4, model,...  53.4 us
    pallas_call x1, Pallas kernels, feed_back_up(): pl.pallas_call(back_up_kernel, out_shape=[jax.ShapeDtypeStruct(gu.shape,...  34.2 us
    pallas_call x1, Pallas kernels, feed_down(): pl.pallas_call(down_kernel, out_shape=[jax.ShapeDtypeStruct((count, model...  33.1 us
  transfers between devices with their start and end apart: 10, of which 3 were waited for; matrix products, arithmetic and copies ran while one was open for 4% of the time, Pallas kernels for 75%

profile of v9, /device:TPU:0, one launch (start us, length us, event | category | flops | bytes accessed | tf_op | source)
XLA Modules:
  0.0 653.7 jit_solution(16835867977189941416)
XLA Ops:
  7.2 1.0 dynamic-slice_bitcast_fusion.5
  8.2 1.8 fusion.8.refs_1_
  11.9 3.0 dynamic-slice_bitcast_fusion
  14.9 0.8 pad.28
  15.8 0.8 pad.30
  16.8 1.1 copy-done.36
  18.2 4.7 shard_map.172
  22.9 1.0 slice.71
  24.0 0.9 slice.72
  26.9 1.2 convert_multiply_fusion.dy_ref
  28.1 21.6 %all-gather.5.cloned.1.call-done.p_ref = bf16[1216,640]{1,0:T(8,128)(2,1)} async-done(((bf16[304,640]{1,0:T(8,128)(2,1)}), bf16[1216,640]{1,0:T(8,128)(2,1)}) %all-gather.5.cloned.1.call-update) | async-done | bytes 1556496 | tf_op jit(solution)/shard_map/all_gather | solution.py:1821
  49.7 1.4 copy-done.15
  51.1 53.4 %shard_map.169 = (bf16[2,4,1152,640]{3,2,1,0:T(8,128)(2,1)S(1)}, bf16[2,4,16,640]{3,2,1,0:T(8,128)(2,1)S(1)}) custom-call(bf16[1216,640]{1,0:T(8,128)(2,1)S(1)} %copy-done.15), custom_call_target="tpu_custom_call" | custom-call | tf_op jit(solution)/shard_map/pallas_call | solution.py:981
  104.5 4.2 copy-done.2
  112.6 40.3 %shard_map.170 = (f32[256,1152]{1,0:T(8,128)S(1)}, bf16[256,1152]{1,0:T(8,128)(2,1)}, f32[256,1024]{1,0:T(8,128)S(1)}, f32[256,256]{1,0:T(8,128)S(1)}, bf16[768,...) custom-call(s32[1]{0:T(128)} %bitcast.length_ref, ...), custom_call_target="tpu_custom_call" | custom-call | tf_op jit(solution)/shard_map/pallas_call | solution.py:1393
  153.0 1.0 copy-done.3
  154.0 1.4 copy-done.13
  155.4 1.0 copy-done.18
  156.4 0.9 copy-done.22
  159.7 5.7 all-gather.7.cloned.1.call-done.w_ref
  165.4 28.5 %shard_map.173 = (bf16[1024,1152]{1,0:T(8,128)(2,1)}, bf16[1024,3584]{1,0:T(8,128)(2,1)}, bf16[1024,1792]{1,0:T(8,128)(2,1)}) custom-call(f32[256,1152]{1,0:T(8,128)} %copy-done.3, f32[1,1152]{1,0:T(1,128)} %slice.63.gain_ref, bf16[1152,5376]{1,0:T(8,128)(2,1)} %all-gather.7.cloned.1.call-done.w_ref), custom_call_target="tpu_custom_call" | custom-call | tf_op jit(solution)/shard_map/pallas_call | solution.py:477
  193.9 33.1 %shard_map.174 = (bf16[256,1152]{1,0:T(8,128)(2,1)}, f32[256,1152]{1,0:T(8,128)}) custom-call(f32[256,1152]{1,0:T(8,128)} %copy-done.3, f32[1,1152]{1,0:T(1,128)} %slice.61.gain_ref, bf16[1024,1792]{1,0:T(8,128)(2,1)} %get-tuple-element.67.act_ref, bf16[1152,5376]{1,0:T(8,128)(2,1)} %all-gather.7.cloned.1.call-done.w_ref), custom_call_target="tpu_custom_call" | custom-call | tf_op jit(solution)/shard_map/pallas_call | solution.py:534
  227.1 1.1 copy-done.6
  228.2 37.6 %shard_map.175 = (f32[256,1152]{1,0:T(8,128)S(1)}, bf16[256,1152]{1,0:T(8,128)(2,1)}, f32[256,1024]{1,0:T(8,128)S(1)}, f32[256,256]{1,0:T(8,128)S(1)}, bf16[768,...) custom-call(s32[1]{0:T(128)} %bitcast.length_ref, ...), custom_call_target="tpu_custom_call" | custom-call | tf_op jit(solution)/shard_map/pallas_call | solution.py:1393
  265.7 1.0 copy-done.4
  266.8 1.4 copy-done.14
  269.7 28.7 %shard_map.176 = (bf16[1024,1152]{1,0:T(8,128)(2,1)}, bf16[1024,3584]{1,0:T(8,128)(2,1)}, bf16[1024,1792]{1,0:T(8,128)(2,1)}) custom-call(f32[256,1152]{1,0:T(8,128)} %copy-done.4, f32[1,1152]{1,0:T(1,128)} %slice.70.gain_ref, bf16[1152,3584]{1,0:T(8,128)(2,1)} %all-gather.9.cloned.1.call-done.w_ref), custom_call_target="tpu_custom_call" | custom-call | tf_op jit(solution)/shard_map/pallas_call | solution.py:477
  298.5 54.7 %shard_map.177 = (bf16[256,1152]{1,0:T(8,128)(2,1)}, bf16[1024,3584]{1,0:T(8,128)(2,1)}, bf16[1152,896]{1,0:T(8,128)(2,1)}, f32[1,1152]{1,0:T(1,128)}) custom-call(f32[256,1152]{1,0:T(8,128)} %copy-done.4, f32[1,1152]{1,0:T(1,128)} %slice.68.gain_ref, f32[256,1152]{1,0:T(8,128)} %convert_multiply_fusion.dy_ref, ...), custom_call_target="tpu_custom_call" | custom-call | tf_op jit(solution)/shard_map/pallas_call | solution.py:774
  353.2 32.6 %shard_map.178 = (f32[256,1152]{1,0:T(8,128)}, bf16[1152,1792]{1,0:T(8,128)(2,1)}, f32[1,1152]{1,0:T(1,128)}) custom-call(f32[256,1152]{1,0:T(8,128)} %convert_multiply_fusion.dy_ref, f32[256,1152]{1,0:T(8,128)} %copy-done.4, f32[1,1152]{1,0:T(1,128)} %slice.70.gain_ref, bf16[1024,3584]{1,0:T(8,128)(2,1)} %get-tuple-element.74.dgu_ref, ...), custom_call_target="tpu_custom_call" | custom-call | tf_op jit(solution)/shard_map/pallas_call | solution.py:897
  385.9 1.0 copy-done.7
  387.0 1.0 copy-done.28
  388.1 48.1 %shard_map.179 = (f32[256,1152]{1,0:T(8,128)S(1)}, bf16[1152,384]{1,0:T(8,128)(2,1)S(1)}, f32[2,1152]{1,0:T(2,128)S(1)}, f32[2,256]{1,0:T(2,128)S(1)}) custom-call(s32[1]{0:T(128)} %bitcast.length_ref, f32[256,1152]{1,0:T(8,128)} %get-tuple-element.76.dh_ref, f32[256,1152]{1,0:T(8,128)} %copy-done.16, bf16[256,1152]{1,0:T(8,128)(2,1)S(1)} %copy-done.7, ...), custom_call_target="tpu_custom_call" | custom-call | tf_op jit(solution)/shard_map/pallas_call | solution.py:1689
  436.2 1.0 copy-done.5
  437.2 1.0 copy-done.21
  438.1 34.2 %shard_map.180 = (bf16[1024,3584]{1,0:T(8,128)(2,1)}, bf16[1152,896]{1,0:T(8,128)(2,1)}, f32[1,1152]{1,0:T(1,128)}) custom-call(f32[256,1152]{1,0:T(8,128)} %copy-done.5, f32[256,1152]{1,0:T(8,128)} %get-tuple-element.85.f_ref, f32[1,1152]{1,0:T(1,128)} %slice.61.gain_ref, bf16[1024,3584]{1,0:T(8,128)(2,1)} %get-tuple-element.86.gu_ref, ...), custom_call_target="tpu_custom_call" | custom-call | tf_op jit(solution)/shard_map/pallas_call | solution.py:810
  472.3 1.0 copy-done.35
  474.1 1.6 collective-permute-done
  475.8 1.0 select_bitcast_fusion.1
  477.1 2.6 pad_maximum_fusion
  479.7 32.5 %shard_map.181 = (f32[256,1152]{1,0:T(8,128)}, bf16[1152,1792]{1,0:T(8,128)(2,1)}, f32[1,1152]{1,0:T(1,128)}) custom-call(f32[256,1152]{1,0:T(8,128)} %copy-done.5, f32[256,1152]{1,0:T(8,128)} %copy-done.3, f32[1,1152]{1,0:T(1,128)} %slice.63.gain_ref, bf16[1024,3584]{1,0:T(8,128)(2,1)} %get-tuple-element.88.dgu_ref, ...), custom_call_target="tpu_custom_call" | custom-call | tf_op jit(solution)/shard_map/pallas_call | solution.py:897
  512.3 2.0 concatenate.27.refs_0_
  514.3 117.6 %shard_map.183 = (f32[256,1152]{1,0:T(8,128)}, bf16[1152,384]{1,0:T(8,128)(2,1)}, f32[2,1152]{1,0:T(2,128)}, f32[2,256]{1,0:T(2,128)}, f32[16,1152]{1,0:T(8,128)...) custom-call(s32[1]{0:T(128)} %bitcast.length_ref, ...), custom_call_target="tpu_custom_call" | custom-call | tf_op jit(solution)/shard_map/pallas_call | solution.py:1689
  632.0 0.9 broadcast_select_fusion.2
  634.2 1.4 dynamic-slice_bitcast_fusion.6
  635.7 1.2 copy-done.19
  636.9 1.2 copy-done.20
  638.1 4.8 shard_map.185
  642.9 1.4 copy.36
  (140 shorter events, 16.1 us)
Async XLA Ops:
  7.2 19.6 %copy-start = (bf16[2,256,1152]{2,1,0:T(8,128)(2,1)S(1)}, bf16[2,256,1152]{2,1,0:T(8,128)(2,1)}, u32[]{:S(2)}) copy-start(bf16[2,256,1152]{2,1,0:T(8,128)(2,1)} %param.10) | copy-start | bytes 3538948
  7.2 42.5 %all-gather.5.cloned.1.call-start = ((), (), s32[]{:S(2)}) async-start(), calls=%async_computation.3 | async-start | bytes 1945600 | tf_op jit(solution)/shard_map/all_gather | solution.py:1821
  10.0 155.3 %all-gather.7.cloned.1.call-start = ((), (), s32[]{:S(2)}) async-start(), calls=%async_computation.4 | async-start | bytes 13934592 | tf_op jit(solution)/shard_map/all_gather | solution.py:1833
  16.6 1.2 copy-start.36
  22.9 246.9 %all-gather.9.cloned.1.call-start = ((), (), s32[]{:S(2)}) async-start(), calls=%async_computation.5 | async-start | bytes 9289728 | tf_op jit(solution)/shard_map/all_gather | solution.py:1833
  24.0 1.0 copy-start.44
  24.0 274.5 %all-gather.11.cloned.1.call-start = ((), (), s32[]{:S(2)}) async-start(), calls=%async_computation.6 | async-start | bytes 4644864 | tf_op jit(solution)/shard_map/all_gather | solution.py:1833
  24.9 2.0 copy-start.38
  24.9 413.2 %reduce-scatter.4.cloned.1.call-start = ((), (), s32[]{:S(2)}) async-start(), calls=%async_computation.7 | async-start | bytes 2580480 | tf_op jit(solution)/shard_map/reduce_scatter | solution.py:1786
  26.8 359.1 %copy-start.8 = (f32[256,256]{1,0:T(8,128)}, f32[256,256]{1,0:T(8,128)S(1)}, u32[]{:S(2)}) copy-start(f32[256,256]{1,0:T(8,128)S(1)} %pad_maximum_fusion.1.trig_ref) | copy-start | bytes 786436
  26.9 85.7 %copy-start.9 = (bf16[256,1152]{1,0:T(8,128)(2,1)}, bf16[256,1152]{1,0:T(8,128)(2,1)S(1)}, u32[]{:S(2)}) copy-start(bf16[256,1152]{1,0:T(8,128)(2,1)S(1)} %dynamic-slice_bitcast_fusion.2.x_ref) | copy-start | bytes 1769476
  49.7 1.4 copy-start.15
  104.5 4.2 copy-start.2
  108.9 44.0 %copy-start.30 = (f32[4,1152]{1,0:T(4,128)}, f32[4,1152]{1,0:T(4,128)S(1)}, u32[]{:S(2)}) copy-start(f32[4,1152]{1,0:T(4,128)S(1)} %convert_element_type.62.gains_ref) | copy-start | bytes 55300
  109.0 43.9 %copy-start.33 = (f32[2,256]{1,0:T(2,128)}, f32[2,256]{1,0:T(2,128)S(1)}, u32[]{:S(2)}) copy-start(f32[2,256]{1,0:T(2,128)S(1)} %reshape.85.head_ref) | copy-start | bytes 6148
  153.0 1.0 copy-start.3
  154.0 1.4 copy-start.13
  155.4 1.0 copy-start.18
  159.7 34.3 %copy-start.17 = (f32[256,1152]{1,0:T(8,128)}, f32[256,1152]{1,0:T(8,128)S(1)}, u32[]{:S(2)}) copy-start(f32[256,1152]{1,0:T(8,128)S(1)} %get-tuple-element.91.a_ref) | copy-start | bytes 3538948
  193.9 33.2 %copy-start.31 = (f32[4,1152]{1,0:T(4,128)S(1)}, f32[4,1152]{1,0:T(4,128)}, u32[]{:S(2)}) copy-start(f32[4,1152]{1,0:T(4,128)} %convert_element_type.69.gains_ref) | copy-start | bytes 55300
  227.1 1.1 copy-start.6
  265.7 1.0 copy-start.4
  266.8 1.4 copy-start.14
  269.7 28.7 %copy-start.16 = (f32[256,1152]{1,0:T(8,128)}, f32[256,1152]{1,0:T(8,128)S(1)}, u32[]{:S(2)}) copy-start(f32[256,1152]{1,0:T(8,128)S(1)} %get-tuple-element.77.a_ref) | copy-start | bytes 3538948
  353.2 123.6 %reduce-scatter.6.cloned.1.call-start = ((), (), s32[]{:S(2)}) async-start(), calls=%async_computation.8 | async-start | bytes 5160960 | tf_op jit(solution)/shard_map/reduce_scatter | solution.py:1786
  385.8 1.1 copy-start.7
  385.8 1.2 copy-start.26
  385.8 1.2 copy-start.32
  385.8 246.1 %reduce-scatter.8.cloned.1.call-start = ((), (), s32[]{:S(2)}) async-start(), calls=%async_computation.9 | async-start | bytes 2580480 | tf_op jit(solution)/shard_map/reduce_scatter | solution.py:1786
  387.0 1.0 copy-start.28
  436.1 1.0 copy-start.5
  472.3 1.1 copy-start.35
  473.4 2.3 collective-permute-start
  476.7 158.9 %collective-permute-start.1 = (bf16[288,1792]{1,0:T(8,128)(2,1)}, bf16[288,1792]{1,0:T(8,128)(2,1)S(1)}, u32[]{:S(2)}, u32[]{:S(2)}) collective-permute-start(bf16[288,1792]{1,0:T(8,128)(2,1)} %reduce-scatter.6.cloned.1.call-done.refs_1_.one_ref), channel_id=1, source_target_pairs={{0,16},{16,0},{1,17},{17,1},{2,18},{18,2},{3,19},{19,3},{4,20},{20... | collective-permute-start | bytes 3096584 | tf_op jit(solution)/shard_map/ppermute | solution.py:1804
  479.7 32.6 %copy-start.41 = (f32[1,1152]{1,0:T(1,128)S(1)}, f32[1,1152]{1,0:T(1,128)}, u32[]{:S(2)}) copy-start(f32[1,1152]{1,0:T(1,128)} %get-tuple-element.102) | copy-start | bytes 13828
  479.7 32.6 %copy-start.42 = (f32[1,1152]{1,0:T(1,128)S(1)}, f32[1,1152]{1,0:T(1,128)}, u32[]{:S(2)}) copy-start(f32[1,1152]{1,0:T(1,128)} %get-tuple-element.101) | copy-start | bytes 13828
  479.7 32.6 %copy-start.43 = (f32[1,1152]{1,0:T(1,128)S(1)}, f32[1,1152]{1,0:T(1,128)}, u32[]{:S(2)}) copy-start(f32[1,1152]{1,0:T(1,128)} %get-tuple-element.99) | copy-start | bytes 13828
  514.3 117.7 %copy-start.11 = (bf16[288,896]{1,0:T(8,128)(2,1)S(1)}, bf16[288,896]{1,0:T(8,128)(2,1)}, u32[]{:S(2)}) copy-start(bf16[288,896]{1,0:T(8,128)(2,1)} %reduce-scatter.4.cloned.1.call-done.refs_0_.down_one_ref) | copy-start | bytes 1548292
  631.9 3.7 copy-start.12
  632.0 3.7 copy-start.10
  632.9 2.8 collective-permute-start.2
  635.7 1.2 copy-start.19
  636.9 1.2 copy-start.20
  638.1 4.8 copy-start.34
  642.9 1.4 copy-start.40
  642.9 2.1 copy-start.37
  642.9 3.7 copy-start.1
  644.3 1.5 copy-start.39
  (7 other events, 5.8 us)
Sparse Core Ops, SparseCore 0:
  10.2 39.5 all-gather.4
  51.4 113.9 all-gather.6
  167.0 79.2 all-gather.8
  247.8 45.0 all-gather.10
  353.3 41.2 reduce-scatter.3
  396.8 74.9 reduce-scatter.5
  474.1 43.6 reduce-scatter.7
